TPU v7x, 32 devices: a whole 2x2x4 slice. The times are simulated.
32 devices in a mesh: subj: 4 (over x, core), row: 4 (over z), col: 2 (over y).
Axes of the slice: x: 2, y: 2, z: 4, core: 2. Of those that a mesh axis runs over, the one named last changes fastest.
Arguments:
- series: float32 [8, 5120, 1200], P('subj', ('row', 'col')), may hold values from -4000 to 4000
- block_start: int32 [5], replicated, may hold values from 0 to 4096, as said below
Outputs:
- connectome: float32 [5120, 5120], P(('row', 'col'), 'subj')
Inputs may be any that keep to these rules, and one draw needn't show every extreme that they name: `block_start`: each entry is a multiple of 1024 and no two entries are equal.
All inputs are finite; a program needn't handle non-finite values.
Results may differ from a plain program's by a relative error of at most 0.0012.
Values may be sent and summed in bfloat16 or wider, within the bound.
No kernel may reach another device: no remote copies, remote signals or barrier semaphores. Data moves between devices by JAX's collectives and lax.ppermute only.
A program may use at most 192 MiB of HBM per device.

v0:
```python
import jax
import jax.numpy as jnp
from jax import lax
from jax.sharding import PartitionSpec as P

clip_limit = 0.99
epsilon = 1e-05


def normalize(raw_rows):
    center = jnp.mean(raw_rows, axis=-1, keepdims=True)
    spread = jnp.mean((raw_rows - center) ** 2, axis=-1, keepdims=True)
    return ((raw_rows - center) * lax.rsqrt(spread + epsilon)).astype(jnp.bfloat16)


def fisher(products, length):
    scaled = jnp.clip(products / length, -clip_limit, clip_limit)
    return (0.5 * (jnp.log1p(scaled) - jnp.log1p(-scaled))).astype(jnp.bfloat16)


def on_device(series, block_start):
    local_subjects = series.shape[0]
    duration = series.shape[2]
    devices = lax.axis_size(("row", "col"))
    position = lax.axis_index(("row", "col"))
    normed = normalize(series)
    gathered = lax.all_gather(normed, ("row", "col"), axis=1, tiled=True)
    window = gathered.shape[1]
    blocks = block_start.shape[0]
    block_rows = window // blocks
    block_order = block_start // block_rows
    ordered = jnp.take(
        gathered.reshape(local_subjects, blocks, block_rows, duration), block_order, axis=1
    )
    ordered = ordered.reshape(local_subjects, window, duration)
    slab_rows = window // devices
    own_rows = lax.dynamic_slice_in_dim(ordered, position * slab_rows, slab_rows, 1)
    tile_cols = 2 * slab_rows
    initial = jnp.zeros((local_subjects, slab_rows, window), jnp.bfloat16)

    def add_tile(tile_index, buffer):
        columns = lax.dynamic_slice_in_dim(ordered, tile_index * tile_cols, tile_cols, 1)
        tile_scores = fisher(
            jnp.einsum("ast,agt->asg", own_rows, columns, preferred_element_type=jnp.float32),
            duration,
        )
        return lax.dynamic_update_slice_in_dim(buffer, tile_scores, tile_index * tile_cols, 2)

    upper = lax.fori_loop(position // 2, devices // 2, add_tile, initial)
    pieces = upper.reshape(local_subjects, slab_rows, devices, slab_rows).transpose(0, 3, 2, 1)
    targets = jnp.arange(devices, dtype=jnp.int32)
    pieces = jnp.where((targets > position)[None, None, :, None], pieces, jnp.zeros_like(pieces))
    incoming = lax.all_to_all(
        pieces.reshape(local_subjects, slab_rows, window),
        ("row", "col"),
        split_axis=2,
        concat_axis=2,
        tiled=True,
    )
    sources = jnp.arange(devices, dtype=jnp.int32)
    below = (sources < position)[None, None, :, None]
    merged = jnp.where(
        below,
        incoming.reshape(local_subjects, slab_rows, devices, slab_rows),
        upper.reshape(local_subjects, slab_rows, devices, slab_rows),
    )
    running = jnp.sum(merged.astype(jnp.float32), axis=0).reshape(slab_rows, window)
    summed = lax.psum_scatter(running, "subj", scatter_dimension=1, tiled=True)
    return summed / (local_subjects * lax.axis_size("subj"))


def solution(mesh):
    return jax.shard_map(
        on_device,
        mesh=mesh,
        in_specs=(P("subj", ("row", "col"), None), P()),
        out_specs=P(("row", "col"), "subj"),
        check_vma=False,
    )
```

profile of v0, /device:TPU:0, one launch (start us, length us, event | category | flops | bytes accessed | tf_op | source)
XLA Modules:
  0.0 1282.1 jit_solution(2078066351174969951)
XLA Ops:
  13.1 5.0 multiply_convert_fusion.1
  18.8 471.5 %all-gather.2.cloned.1.call-done = bf16[2,5120,1200]{1,2,0:T(8,128)(2,1)} async-done(((bf16[2,640,1200]{1,2,0:T(8,128)(2,1)}), bf16[2,5120,1200]{1,2,0:T(8,128)(2,1)}) %all-gather.2.cloned.1.call-update) | async-done | bytes 24576016 | tf_op jit(solution)/shard_map/all_gather | solution.py:27
  490.3 31.9 %copy.18 = bf16[2,5120,1200]{2,1,0:T(8,128)(2,1)} copy(bf16[2,5120,1200]{1,2,0:T(8,128)(2,1)} %all-gather.2.cloned.1.call-done) | data formatting | bytes 49152000 | tf_op jit(solution)/shard_map/all_gather | solution.py:27
  522.2 5.1 mini-gather-slice.5
  527.3 15.8 %fusion.11 = (bf16[2,5,1024,512]{3,2,1,0:T(8,128)(2,1)}, bf16[2,5,1024,512]{3,2,1,0:T(8,128)(2,1)}) fusion(bf16[2,5,1024,1200]{3,2,1,0:T(8,128)(2,1)} %bitcast.36), kind=kLoop, calls=%fused_computation.30 | loop fusion | bytes 41943040 | tf_op jit(solution)/shard_map/jit(_take)/gather | solution.py:32
  543.1 4.7 broadcast.75.clone
  547.9 21.4 %while.14 = (s32[]{:T(128)}, bf16[2,5,1024,512]{3,2,1,0:T(8,128)(2,1)}, s32[5,1]{0,1:T(1,128)S(1)}, bf16[5,2,1024,512]{3,2,1,0:T(8,128)(2,1)}, s32[]{:T(128)}) while((s32[]{:T(128)}, bf16[2,5,1024,512]{3,2,1,0:T(8,128)(2,1)}, s32[5,1]{0,1:T(1,128)S(1)}, bf16[5,2,1024,512]{3,2,1,0:T(8,128)(2,1)}, s32[]{:T(128)}) %tuple.60), condition=%wide.while_cond.1, body=%wide.while_body.1.sunk | while | flops 2 | bytes 4194901 | solution.py:32
  561.3 3.7 bitcast_dynamic-update-slice_fusion.5
  569.3 4.8 broadcast.75.clone.1
  574.1 21.5 %while.13 = (s32[]{:T(128)}, bf16[2,5,1024,512]{3,2,1,0:T(8,128)(2,1)}, s32[5,1]{0,1:T(1,128)S(1)}, bf16[5,2,1024,512]{3,2,1,0:T(8,128)(2,1)}, s32[]{:T(128)}) while((s32[]{:T(128)}, bf16[2,5,1024,512]{3,2,1,0:T(8,128)(2,1)}, s32[5,1]{0,1:T(1,128)S(1)}, bf16[5,2,1024,512]{3,2,1,0:T(8,128)(2,1)}, s32[]{:T(128)}) %tuple.61), condition=%wide.while_cond, body=%wide.while_body.sunk | while | flops 2 | bytes 4194901 | solution.py:32
  574.7 3.7 bitcast_dynamic-update-slice_fusion.4
  587.5 3.7 bitcast_dynamic-update-slice_fusion.4
  595.6 6.3 gather_fusion
  601.8 18.2 %pad_maximum_fusion = bf16[2,5,1024,1200]{3,2,0,1:T(8,128)(2,1)} fusion(bf16[2,5,1024,176]{3,2,0,1:T(8,128)(2,1)} %bitcast.40, bf16[2,5,1024,512]{3,2,0,1:T(8,128)(2,1)} %bitcast.38, bf16[2,5,1024,512]{3,2,0,1:T(8,128)(2,1)} %bitcast.39), kind=kLoop, calls=%fused_computation.11 | loop fusion | flops 73728000 | bytes 49152000
  620.0 18.2 %copy.19 = bf16[2,5,1024,1200]{3,2,1,0:T(8,128)(2,1)} copy(bf16[2,5,1024,1200]{3,2,0,1:T(8,128)(2,1)} %pad_maximum_fusion) | data formatting | bytes 49152000
  638.3 18.0 %bitcast_select_fusion = bf16[2,5120,1200]{2,1,0:T(8,128)(2,1)} fusion(bf16[2,5,1024,1200]{3,2,1,0:T(8,128)(2,1)} %copy.19, pred[5120]{0:T(1024)(128)(4,1)S(1)} %broadcast_in_dim.49), kind=kLoop, calls=%fused_computation.12 | loop fusion | flops 12288000 | bytes 49157120 | tf_op jit(solution)/shard_map/jit(_take)/select_n | solution.py:32
  656.2 32.5 %copy.20 = bf16[2,5120,1200]{1,2,0:T(8,128)(2,1)} copy(bf16[2,5120,1200]{2,1,0:T(8,128)(2,1)} %bitcast_select_fusion) | data formatting | bytes 49152000 | tf_op jit(solution)/shard_map/while | solution.py:49
  694.2 5.7 broadcast_in_dim.47
  700.0 64.9 %while.12 = (s32[]{:T(128)}, bf16[2,640,5120]{1,2,0:T(8,128)(2,1)}, bf16[2,5120,1200]{1,2,0:T(8,128)(2,1)}, bf16[2,640,1200]{1,2,0:T(8,128)(2,1)S(1)}, s32[]{:T(128)}, /*index=5*/s32[]{:T(128)}, s32[]{:T(128)}, s32[]{:T(128)}) while((s32[]{:T(128)}, bf16[2,640,5120]{1,2,0:T(8,128)(2,1)}, bf16[2,5120,1200]{1,2,0:T(8,128)(2,1)}, ...), condition=%wide.region_3.4_spmd, body=%wide.region_2.3_spmd.sunk | while | flops 3941990400 | bytes 12493955 | solution.py:49
  700.0 16.3 %fusion.18 = bf16[2,640,5120]{1,2,0:T(8,128)(2,1)} fusion(bf16[2,640,5120]{1,2,0:T(8,128)(2,1)} %get-tuple-element.200, s32[]{:T(128)S(6)} %select_n.55, bf16[2,640,1200]{1,2,0:T(8,128)(2,1)S(1)} %get-tuple-element.210, bf16[2,5120,1200]{1,2,0:T(8,128)(2,1)} %get-tuple-element.209), kind=kOutput, calls=%fused_computation.5.clone.1 | convolution fusion | flops 3941990400 | bytes 12493824 | tf_op jit(solution)/shard_map/while/body/ast,agt->asg/dot_general | solution.py:44
  716.2 16.2 %fusion.18 = bf16[2,640,5120]{1,2,0:T(8,128)(2,1)} fusion(bf16[2,640,5120]{1,2,0:T(8,128)(2,1)} %get-tuple-element.200, s32[]{:T(128)S(6)} %select_n.55, bf16[2,640,1200]{1,2,0:T(8,128)(2,1)S(1)} %get-tuple-element.210, bf16[2,5120,1200]{1,2,0:T(8,128)(2,1)} %get-tuple-element.209), kind=kOutput, calls=%fused_computation.5.clone.1 | convolution fusion | flops 3941990400 | bytes 12493824 | tf_op jit(solution)/shard_map/while/body/ast,agt->asg/dot_general | solution.py:44
  732.4 16.2 %fusion.18 = bf16[2,640,5120]{1,2,0:T(8,128)(2,1)} fusion(bf16[2,640,5120]{1,2,0:T(8,128)(2,1)} %get-tuple-element.200, s32[]{:T(128)S(6)} %select_n.55, bf16[2,640,1200]{1,2,0:T(8,128)(2,1)S(1)} %get-tuple-element.210, bf16[2,5120,1200]{1,2,0:T(8,128)(2,1)} %get-tuple-element.209), kind=kOutput, calls=%fused_computation.5.clone.1 | convolution fusion | flops 3941990400 | bytes 12493824 | tf_op jit(solution)/shard_map/while/body/ast,agt->asg/dot_general | solution.py:44
  748.6 16.2 %fusion.18 = bf16[2,640,5120]{1,2,0:T(8,128)(2,1)} fusion(bf16[2,640,5120]{1,2,0:T(8,128)(2,1)} %get-tuple-element.200, s32[]{:T(128)S(6)} %select_n.55, bf16[2,640,1200]{1,2,0:T(8,128)(2,1)S(1)} %get-tuple-element.210, bf16[2,5120,1200]{1,2,0:T(8,128)(2,1)} %get-tuple-element.209), kind=kOutput, calls=%fused_computation.5.clone.1 | convolution fusion | flops 3941990400 | bytes 12493824 | tf_op jit(solution)/shard_map/while/body/ast,agt->asg/dot_general | solution.py:44
  764.8 33.0 %copy.22 = bf16[2,640,8,640]{3,0,1,2:T(2,128)(2,1)} copy(bf16[2,640,8,640]{1,3,2,0:T(8,128)(2,1)} %bitcast.34) | data formatting | bytes 26214400 | tf_op jit(solution)/shard_map/reshape | solution.py:50
  797.8 15.2 %broadcast_select_fusion = bf16[2,640,8,640]{3,0,1,2:T(2,128)(2,1)} fusion(bf16[2,640,8,640]{3,0,1,2:T(2,128)(2,1)} %copy.22, pred[8]{0:T(512)(128)(4,1)S(1)} %copy-done.1), kind=kLoop, calls=%fused_computation.14 | loop fusion | flops 6553600 | bytes 26214408 | tf_op jit(solution)/shard_map/jit(_where)/select_n | solution.py:52
  812.9 5.4 all-to-all-start
  818.5 17.7 %copy.24 = bf16[2,640,5120]{2,1,0:T(8,128)(2,1)} copy(bf16[2,640,5120]{1,2,0:T(8,128)(2,1)} %get-tuple-element.27) | data formatting | bytes 26214400 | tf_op jit(solution)/shard_map/while | solution.py:49
  836.2 266.6 %all-to-all-done = bf16[2,640,5120]{1,0,2:T(2,128)(2,1)} async-done(((bf16[2,640,5120]{1,0,2:T(2,128)(2,1)}), bf16[2,640,5120]{1,0,2:T(2,128)(2,1)}, u32[]{:S(2)}, u32[]{:S(2)}) %all-to-all-start) | async-done | bytes 13107232 | tf_op jit(solution)/shard_map/all_to_all | solution.py:53
  1102.8 32.5 %copy.23 = bf16[2,640,5120]{2,1,0:T(8,128)(2,1)} copy(bf16[2,640,5120]{1,0,2:T(2,128)(2,1)} %all-to-all-done) | data formatting | bytes 26214400 | tf_op jit(solution)/shard_map/all_to_all | solution.py:53
  1135.3 19.1 %convert_reduce_fusion = f32[640,5120]{1,0:T(8,128)} fusion(bf16[2,640,5120]{2,1,0:T(8,128)(2,1)} %copy.23, bf16[2,640,5120]{2,1,0:T(8,128)(2,1)} %copy.24, pred[5120]{0:T(1024)(128)(4,1)S(1)} %broadcast_in_dim.44), kind=kLoop, calls=%fused_computation.13 | loop fusion | flops 16384000 | bytes 39326720 | tf_op jit(solution)/shard_map/reduce_sum | solution.py:67
  1154.4 14.0 %copy.27 = f32[640,5120]{0,1:T(8,128)} copy(f32[640,5120]{1,0:T(8,128)} %convert_reduce_fusion) | data formatting | bytes 26214400
  1168.5 101.7 %reduce-scatter.2.cloned.1.call-done = f32[640,1280]{0,1:T(8,128)} async-done(((f32[640,5120]{0,1:T(8,128)}), f32[640,1280]{0,1:T(8,128)}) %reduce-scatter.2.cloned.1.call-update) | async-done | bytes 3276816 | tf_op jit(solution)/shard_map/reduce_scatter | solution.py:68
  (44 shorter events, 49.6 us)
Async XLA Ops:
  6.5 483.8 %all-gather.2.cloned.1.call-start = ((), (), s32[]{:S(2)}) async-start(), calls=%async_computation.2 | async-start | bytes 27648000 | tf_op jit(solution)/shard_map/all_gather | solution.py:27
  9.6 8.5 copy-start.3
  694.2 5.7 copy-start
  764.8 33.0 %copy-start.1 = (pred[8]{0:T(512)(128)(4,1)S(1)}, pred[8]{0:T(512)(128)(4,1)}, u32[]{:S(2)}) copy-start(pred[8]{0:T(512)(128)(4,1)} %get-tuple-element.84) | copy-start | bytes 28
  812.9 5.5 copy-start.2
  812.9 289.9 %all-to-all-start = ((bf16[2,640,5120]{1,0,2:T(2,128)(2,1)}), bf16[2,640,5120]{1,0,2:T(2,128)(2,1)}, u32[]{:S(2)}, u32[]{:S(2)}) async-start(bf16[2,640,5120]{1,0,2:T(2,128)(2,1)} %bitcast.37), calls=%async_computation | async-start | bytes 26214400 | tf_op jit(solution)/shard_map/all_to_all | solution.py:53
  818.3 451.8 %reduce-scatter.2.cloned.1.call-start = ((), (), s32[]{:S(2)}) async-start(), calls=%async_computation.3 | async-start | bytes 16384000 | tf_op jit(solution)/shard_map/reduce_scatter | solution.py:68
Sparse Core Ops, SparseCore 0:
  18.2 472.0 all-gather.1
  1168.6 101.4 reduce-scatter.1
where the time goes:
time: 1290 us; the launch traced here: 1280 us
  waiting for transfers between devices  840 us (65%)
  local copies, waits for them, and re-layouts  274 us (21%)
  other arithmetic  84.7 us (7%)
  matrix products  64.9 us (5%)
  between operations  13.5 us (1%)
    all_gather x1, waiting for transfers between devices, on_device(): gathered = lax.all_gather(normed, ('row', 'col'), axis=1, tiled=True)  472 us
    all_to_all x1, waiting for transfers between devices, on_device(): lax.all_to_all(pieces.reshape(local_subjects, slab_rows, window), ('row',...  267 us
    reduce_scatter x1, waiting for transfers between devices, on_device(): summed = lax.psum_scatter(running, 'subj', scatter_dimension=1, tiled=True)  102 us
    dot_general x4, matrix products, add_tile(): jnp.einsum('ast,agt->asg', own_rows, columns, preferred_element_type=jnp....  64.9 us
    while x3, local copies, waits for them, and re-layouts, on_device(): upper = lax.fori_loop(position // 2, devices // 2, add_tile, initial)  53.6 us
    gather x20, local copies, waits for them, and re-layouts  42.9 us
    unnamed x12, local copies, waits for them, and re-layouts  41.8 us
    reshape x1, local copies, waits for them, and re-layouts, on_device(): upper.reshape(local_subjects, slab_rows, devices, slab_rows)  33 us
  transfers between devices with their start and end apart: 3, of which 3 were waited for; matrix products, arithmetic and copies ran while one was open for 1% of the time, Pallas kernels for 0%

commit v1 on v0

v1 whole, which is shorter than its diff:
```python
import functools
import math

import jax
import jax.numpy as jnp
import numpy as np
from jax import lax
from jax.experimental import pallas as pl
from jax.experimental.pallas import tpu as pltpu
from jax.sharding import PartitionSpec as P

clip_limit = 0.99
epsilon = 1e-05
SLABS = ("row", "col")


def cycle(rows, cols):
    if cols == 1:
        return list(range(rows))
    walk = [(r, 0) for r in range(rows)]
    for i, r in enumerate(reversed(range(rows))):
        back = list(range(1, cols))
        walk += [(r, c) for c in (back if i % 2 == 0 else back[::-1])]
    return [r * cols + c for r, c in walk]


def normalize_kernel(x_ref, o_ref):
    values = x_ref[...]
    center = jnp.mean(values, axis=-1, keepdims=True)
    away = values - center
    spread = jnp.mean(away * away, axis=-1, keepdims=True)
    o_ref[...] = (away * lax.rsqrt(spread + epsilon)).astype(jnp.bfloat16)


def normalize(series, subject, half, half_rows):
    duration = series.shape[2]
    step = max(d for d in range(16, 161, 16) if half_rows % d == 0)
    steps = half_rows // step
    return pl.pallas_call(
        normalize_kernel,
        grid=(steps,),
        in_specs=[pl.BlockSpec((None, step, duration), lambda i: (subject, half * steps + i, 0))],
        out_specs=pl.BlockSpec((step, duration), lambda i: (i, 0)),
        out_shape=jax.ShapeDtypeStruct((half_rows, duration), jnp.bfloat16),
    )(series)


def scores_kernel(
    source_ref, block_start_ref, place_ref, *refs, slab, half_rows, granule, block_rows, chips, chunk, duration
):
    count = source_ref.shape[0]
    pieces, (same_ref, other_ref, ordered, place_of, sem) = refs[: 2 * count], refs[2 * count :]
    blocks = block_start_ref.shape[0]
    for a in range(blocks):
        place_of[block_start_ref[a] // block_rows] = a

    for slot in range(count):
        for half in range(2):
            piece = pieces[2 * slot + half]
            first = source_ref[slot] * slab + half * half_rows

            def start(g, _, piece=piece, first=first):
                stored = first + g * granule
                block = stored // block_rows
                row = place_of[block] * block_rows + (stored - block * block_rows)
                pltpu.make_async_copy(
                    piece.at[pl.ds(pl.multiple_of(g * granule, granule), granule)],
                    ordered.at[pl.ds(pl.multiple_of(row, granule), granule)],
                    sem,
                ).start()
                return 0

            lax.fori_loop(0, half_rows // granule, start, 0)
    pltpu.make_async_copy(ordered, ordered, sem).wait()

    position, subj = place_ref[0], place_ref[1]
    chip, core = subj // 2, subj % 2
    limit = clip_limit * duration
    width = math.gcd(chunk, 256)
    for away in range(chips):
        for flip, out_ref in ((0, same_ref), (1, other_ref)):
            owner = (chip + away) % chips * 2 + (core + flip) % 2

            def tile(k, _, away=away, out_ref=out_ref, owner=owner):
                own = ordered[pl.ds(pl.multiple_of(position * slab, granule), slab)]
                first = pl.multiple_of(owner * chunk + k * width, width)
                columns = ordered[pl.ds(first, width)]
                products = lax.dot_general(
                    own, columns, (((1,), (1,)), ((), ())), preferred_element_type=jnp.float32
                )
                products = jnp.clip(products, -limit, limit)
                score = 0.5 * (jnp.log(duration + products) - jnp.log(duration - products))
                out_ref[away, :, pl.ds(pl.multiple_of(k * width, width), width)] = score.astype(jnp.bfloat16)
                return 0

            lax.fori_loop(0, chunk // width, tile, 0)


def scores(source, block_start, place, pieces, slab, window, chips):
    half_rows, duration = pieces[0].shape
    block_rows = window // block_start.shape[0]
    granule = math.gcd(half_rows, block_rows)
    chunk = window // (2 * chips)
    out = jax.ShapeDtypeStruct((chips, slab, chunk), jnp.bfloat16)
    smem = pl.BlockSpec(memory_space=pltpu.SMEM)
    return pl.pallas_call(
        functools.partial(
            scores_kernel,
            slab=slab,
            half_rows=half_rows,
            granule=granule,
            block_rows=block_rows,
            chips=chips,
            chunk=chunk,
            duration=duration,
        ),
        in_specs=[smem, smem, smem] + [pl.BlockSpec(memory_space=pl.ANY)] * len(pieces),
        out_shape=[out, out],
        scratch_shapes=[
            pltpu.VMEM((window, duration), jnp.bfloat16),
            pltpu.SMEM((block_start.shape[0],), jnp.int32),
            pltpu.SemaphoreType.DMA,
        ],
        compiler_params=pltpu.CompilerParams(vmem_limit_bytes=48 * 2**20),
        cost_estimate=pl.CostEstimate(
            flops=2 * slab * window * duration,
            bytes_accessed=2 * window * (duration + slab),
            transcendentals=2 * slab * window,
        ),
    )(source, block_start, place, *pieces)


def on_device(series, block_start):
    local_subjects, slab, duration = series.shape
    rows, cols = lax.axis_size("row"), lax.axis_size("col")
    count = rows * cols
    window = count * slab
    subjs = lax.axis_size("subj")
    chips = subjs // 2
    half_rows = slab // 2
    order = cycle(rows, cols)
    onward = [(order[i], order[(i + 1) % count]) for i in range(count)]
    backward = [(b, a) for a, b in onward]
    reach = count // 2
    offsets = [0]
    for d in range(1, reach):
        offsets += [d, -d]
    offsets.append(reach)
    table = np.zeros((count, count), np.int32)
    for i, device in enumerate(order):
        table[device] = [order[(i - d) % count] for d in offsets]
    position = lax.axis_index(SLABS)
    source = jnp.asarray(table)[position]
    place = jnp.stack([position, lax.axis_index("subj")]).astype(jnp.int32)

    def gather(own):
        got = [own]
        ahead, behind = list(own), list(own)
        for d in range(1, reach):
            ahead = [lax.ppermute(piece, SLABS, onward) for piece in ahead]
            behind = [lax.ppermute(piece, SLABS, backward) for piece in behind]
            got += [ahead, behind]
        got.append([lax.ppermute(ahead[0], SLABS, onward), lax.ppermute(behind[1], SLABS, backward)])
        return [piece for pair in got for piece in pair]

    swap = [(s, s ^ 1) for s in range(subjs)]

    def share(subject, own):
        same, other = scores(source, block_start, place, gather(own), slab, window, chips)
        crossed = lax.ppermute(other, "subj", swap)
        mine = same[0].astype(jnp.float32) + crossed[0].astype(jnp.float32)
        for d in range(1, chips):
            part = same[d].astype(jnp.float32) + crossed[d].astype(jnp.float32)
            mine = mine + lax.ppermute(part, "subj", [(s, (s + 2 * d) % subjs) for s in range(subjs)])
        return mine

    owns = [[normalize(series, a, half, half_rows) for half in range(2)] for a in range(local_subjects)]
    total = share(0, owns[0])
    for a in range(1, local_subjects):
        total = total + share(a, owns[a])
    return total / (local_subjects * subjs)


def solution(mesh):
    return jax.shard_map(
        on_device,
        mesh=mesh,
        in_specs=(P("subj", SLABS, None), P()),
        out_specs=P(SLABS, "subj"),
        check_vma=False,
    )
```

time: 1290 us -> 440 us (0.34)
  waiting for transfers between devices: 840 us -> 303 us
  local copies, waits for them, and re-layouts: 274 us -> 21.4 us
  other arithmetic: 84.7 us -> 3.75 us
  matrix products: 64.9 us -> 0 us
  Pallas kernels: 0 us -> 63.6 us
  starting transfers between devices: 5.44 us -> 46.9 us
  between operations: 13.5 us -> 0.18 us
    all_gather x1 -> x0, waiting for transfers between devices: 472 us -> none  [on_device(): gathered = lax.all_gather(normed, ('row', 'col'), axis=1, tiled=True)]
    ppermute x0 -> x32, waiting for transfers between devices: none -> 303 us  [the longest x2 136 us: share(): lax.ppermute(part, 'subj', [(s, (s + 2 * d) % subjs) for s in range(subjs)])]
    all_to_all x1 -> x0, waiting for transfers between devices: 267 us -> none  [on_device(): lax.all_to_all(pieces.reshape(local_subjects, slab_rows, window), ('row',...]
    reduce_scatter x1 -> x0, waiting for transfers between devices: 102 us -> none  [on_device(): summed = lax.psum_scatter(running, 'subj', scatter_dimension=1, tiled=True)]
    gather x23 -> x0, local copies, waits for them, and re-layouts: 70 us -> none
    dot_general x4 -> x0, matrix products: 64.9 us -> none  [add_tile(): jnp.einsum('ast,agt->asg', own_rows, columns, preferred_element_type=jnp....]
    pallas_call x0 -> x6, Pallas kernels: none -> 63.6 us  [the longest x2 53.7 us: scores(): pl.pallas_call(functools.partial(scores_kernel, slab=slab, half_rows=half...]
    while x3 -> x0, local copies, waits for them, and re-layouts: 53.6 us -> none  [on_device(): upper = lax.fori_loop(position // 2, devices // 2, add_tile, initial)]
  transfers between devices with their start and end apart: 3 -> 32, of which waited for: 3 -> 16; matrix products, arithmetic and copies ran while one was open for 1% -> 0% of each run, Pallas kernels for 0% -> 14%
where the time goes in v1:
time: 440 us; the launch traced here: 439 us
  waiting for transfers between devices  303 us (69%)
  Pallas kernels  63.6 us (14%)
  starting transfers between devices  46.9 us (11%)
  local copies, waits for them, and re-layouts  21.4 us (5%)
    ppermute x2, waiting for transfers between devices, share(): lax.ppermute(part, 'subj', [(s, (s + 2 * d) % subjs) for s in range(subjs)])  136 us
    ppermute x12, waiting for transfers between devices, gather(): behind = [lax.ppermute(piece, SLABS, backward) for piece in behind]  100 us
    pallas_call x2, Pallas kernels, scores(): pl.pallas_call(functools.partial(scores_kernel, slab=slab, half_rows=half...  53.7 us
    ppermute x12, waiting for transfers between devices, gather(): ahead = [lax.ppermute(piece, SLABS, onward) for piece in ahead]  47.7 us
    ppermute x12, starting transfers between devices, gather(): behind = [lax.ppermute(piece, SLABS, backward) for piece in behind]  22.2 us
    unnamed x51, local copies, waits for them, and re-layouts  20.7 us
    ppermute x2, waiting for transfers between devices, gather(): lax.ppermute(ahead[0], SLABS, onward)  16 us
    ppermute x12, starting transfers between devices, gather(): ahead = [lax.ppermute(piece, SLABS, onward) for piece in ahead]  15.7 us
  transfers between devices with their start and end apart: 32, of which 16 were waited for; matrix products, arithmetic and copies ran while one was open for 0% of the time, Pallas kernels for 14%

profile of v1, /device:TPU:0, one launch (start us, length us, event | category | flops | bytes accessed | tf_op | source)
XLA Modules:
  0.0 439.3 jit_solution(9291353103833753672)
XLA Ops:
  0.0 8.0 %copy.4.x_ref = f32[2,640,1200]{2,1,0:T(8,128)} copy(f32[2,640,1200]{1,2,0:T(8,128)} %param.3) | data formatting | bytes 12288000 | tf_op args[0]
  8.0 2.5 shard_map.37.refs_0_
  10.5 3.0 collective-permute-start.2
  13.5 2.5 shard_map.38.refs_1_
  18.0 2.5 shard_map.40.refs_0_
  22.5 2.5 shard_map.41.refs_1_
  25.0 7.8 %collective-permute-done.2.refs_4_ = bf16[320,1200]{1,0:T(8,128)(2,1)S(1)} collective-permute-done((bf16[320,1200]{1,0:T(8,128)(2,1)}, bf16[320,1200]{1,0:T(8,128)(2,1)S(1)}, u32[]{:S(2)}, u32[]{:S(2)}) %collective-permute-start.2) | collective-permute-done | bytes 768032 | tf_op jit(solution)/shard_map/ppermute | solution.py:161
  32.8 2.1 collective-permute-start.16
  36.4 13.9 %collective-permute-done.3.refs_5_ = bf16[320,1200]{1,0:T(8,128)(2,1)S(1)} collective-permute-done((bf16[320,1200]{1,0:T(8,128)(2,1)}, bf16[320,1200]{1,0:T(8,128)(2,1)S(1)}, u32[]{:S(2)}, u32[]{:S(2)}) %collective-permute-start.3) | collective-permute-done | bytes 768032 | tf_op jit(solution)/shard_map/ppermute | solution.py:161
  50.4 2.1 collective-permute-start.17
  54.1 13.9 %collective-permute-done.18.refs_4_ = bf16[320,1200]{1,0:T(8,128)(2,1)} collective-permute-done((bf16[320,1200]{1,0:T(8,128)(2,1)}, bf16[320,1200]{1,0:T(8,128)(2,1)}, u32[]{:S(2)}, u32[]{:S(2)}) %collective-permute-start.18) | collective-permute-done | bytes 768032 | tf_op jit(solution)/shard_map/ppermute | solution.py:161
  68.0 2.1 collective-permute-start.4
  71.5 13.9 %collective-permute-done.19.refs_5_ = bf16[320,1200]{1,0:T(8,128)(2,1)S(1)} collective-permute-done((bf16[320,1200]{1,0:T(8,128)(2,1)}, bf16[320,1200]{1,0:T(8,128)(2,1)S(1)}, u32[]{:S(2)}, u32[]{:S(2)}) %collective-permute-start.19) | collective-permute-done | bytes 768032 | tf_op jit(solution)/shard_map/ppermute | solution.py:161
  85.5 2.1 collective-permute-start.5
  90.0 13.0 %collective-permute-done.6.refs_8_ = bf16[320,1200]{1,0:T(8,128)(2,1)S(1)} collective-permute-done((bf16[320,1200]{1,0:T(8,128)(2,1)S(1)}, bf16[320,1200]{1,0:T(8,128)(2,1)S(1)}, u32[]{:S(2)}, u32[]{:S(2)}) %collective-permute-start.6) | collective-permute-done | bytes 768032 | tf_op jit(solution)/shard_map/ppermute | solution.py:161
  103.0 2.0 collective-permute-start.23
  107.5 13.2 %collective-permute-done.7.refs_9_ = bf16[320,1200]{1,0:T(8,128)(2,1)} collective-permute-done((bf16[320,1200]{1,0:T(8,128)(2,1)S(1)}, bf16[320,1200]{1,0:T(8,128)(2,1)}, u32[]{:S(2)}, u32[]{:S(2)}) %collective-permute-start.7) | collective-permute-done | bytes 768032 | tf_op jit(solution)/shard_map/ppermute | solution.py:161
  120.7 2.1 collective-permute-start.21
  126.2 14.0 %collective-permute-done.20.refs_6_ = bf16[320,1200]{1,0:T(8,128)(2,1)S(1)} collective-permute-done((bf16[320,1200]{1,0:T(8,128)(2,1)S(1)}, bf16[320,1200]{1,0:T(8,128)(2,1)S(1)}, u32[]{:S(2)}, u32[]{:S(2)}) %collective-permute-start.20) | collective-permute-done | bytes 768032 | tf_op jit(solution)/shard_map/ppermute | solution.py:160
  143.1 12.7 %collective-permute-done.22.refs_8_ = bf16[320,1200]{1,0:T(8,128)(2,1)} collective-permute-done((bf16[320,1200]{1,0:T(8,128)(2,1)}, bf16[320,1200]{1,0:T(8,128)(2,1)}, u32[]{:S(2)}, u32[]{:S(2)}) %collective-permute-start.22) | collective-permute-done | bytes 768032 | tf_op jit(solution)/shard_map/ppermute | solution.py:161
  159.4 15.9 %collective-permute-done.8.refs_10_ = bf16[320,1200]{1,0:T(8,128)(2,1)S(1)} collective-permute-done((bf16[320,1200]{1,0:T(8,128)(2,1)S(1)}, bf16[320,1200]{1,0:T(8,128)(2,1)S(1)}, u32[]{:S(2)}, u32[]{:S(2)}) %collective-permute-start.8) | collective-permute-done | bytes 768032 | tf_op jit(solution)/shard_map/ppermute | solution.py:160
  175.3 17.6 %collective-permute-done.24.refs_10_ = bf16[320,1200]{1,0:T(8,128)(2,1)} collective-permute-done((bf16[320,1200]{1,0:T(8,128)(2,1)S(1)}, bf16[320,1200]{1,0:T(8,128)(2,1)}, u32[]{:S(2)}, u32[]{:S(2)}) %collective-permute-start.24) | collective-permute-done | bytes 768032 | tf_op jit(solution)/shard_map/ppermute | solution.py:160
  193.0 2.0 collective-permute-start.29
  196.7 11.8 %collective-permute-done.26.refs_12_ = bf16[320,1200]{1,0:T(8,128)(2,1)} collective-permute-done((bf16[320,1200]{1,0:T(8,128)(2,1)}, bf16[320,1200]{1,0:T(8,128)(2,1)}, u32[]{:S(2)}, u32[]{:S(2)}) %collective-permute-start.26) | collective-permute-done | bytes 768032 | tf_op jit(solution)/shard_map/ppermute | solution.py:161
  208.5 2.1 collective-permute-start.9
  212.1 16.0 %collective-permute-done.28.refs_14_ = bf16[320,1200]{1,0:T(8,128)(2,1)} collective-permute-done((bf16[320,1200]{1,0:T(8,128)(2,1)}, bf16[320,1200]{1,0:T(8,128)(2,1)}, u32[]{:S(2)}, u32[]{:S(2)}) %collective-permute-start.28) | collective-permute-done | bytes 768032 | tf_op jit(solution)/shard_map/ppermute | solution.py:163
  236.2 26.8 %shard_map.42 = (bf16[2,640,1280]{2,1,0:T(8,128)(2,1)}, bf16[2,640,1280]{2,1,0:T(8,128)(2,1)}) custom-call(s32[8]{0:T(128)S(1)} %dynamic-slice_bitcast_fusion.source_ref, s32[5]{0:T(128)S(1)} %copy-done.14, s32[2]{0:T(128)S(1)} %pad_add_fusion.place_ref, bf16[320,1200]{1,0:T(8,128)(2,1)S(1)} %copy-done.2, bf16[320,1200]{1,0:T(8,128)(2,1)S(1)} %copy-done.3, ...), custom_call_target="tpu_custom_call" | custom-call | flops 7864320000 | bytes 18841600 | tf_op jit(solution)/shard_map/pallas_call | solution.py:106
  265.5 26.9 %shard_map.39 = (bf16[2,640,1280]{2,1,0:T(8,128)(2,1)}, bf16[2,640,1280]{2,1,0:T(8,128)(2,1)}) custom-call(s32[8]{0:T(128)S(1)} %dynamic-slice_bitcast_fusion.source_ref, s32[5]{0:T(128)S(1)} %copy-done.14, s32[2]{0:T(128)S(1)} %pad_add_fusion.place_ref, bf16[320,1200]{1,0:T(8,128)(2,1)S(1)} %copy-done, bf16[320,1200]{1,0:T(8,128)(2,1)S(1)} %copy-done.1, ...), custom_call_target="tpu_custom_call" | custom-call | flops 7864320000 | bytes 18841600 | tf_op jit(solution)/shard_map/pallas_call | solution.py:106
  294.8 3.8 collective-permute-done.14
  300.6 66.5 %collective-permute-done.31 = f32[640,1280]{1,0:T(8,128)S(1)} collective-permute-done((f32[640,1280]{1,0:T(8,128)S(1)}, f32[640,1280]{1,0:T(8,128)S(1)}, u32[]{:S(2)}, u32[]{:S(2)}) %collective-permute-start.31) | collective-permute-done | bytes 3276832 | tf_op jit(solution)/shard_map/ppermute | solution.py:174
  367.1 69.3 %collective-permute-done.15 = f32[640,1280]{1,0:T(8,128)S(1)} collective-permute-done((f32[640,1280]{1,0:T(8,128)S(1)}, f32[640,1280]{1,0:T(8,128)S(1)}, u32[]{:S(2)}, u32[]{:S(2)}) %collective-permute-start.15) | collective-permute-done | bytes 3276832 | tf_op jit(solution)/shard_map/ppermute | solution.py:174
  436.4 2.9 fusion.1
  (94 shorter events, 41.9 us)
Async XLA Ops:
  10.5 22.3 %collective-permute-start.2 = (bf16[320,1200]{1,0:T(8,128)(2,1)}, bf16[320,1200]{1,0:T(8,128)(2,1)S(1)}, u32[]{:S(2)}, u32[]{:S(2)}) collective-permute-start(bf16[320,1200]{1,0:T(8,128)(2,1)} %shard_map.37.refs_0_), channel_id=1, source_target_pairs={{2,0},{4,2},{6,4},{7,6},{5,7},{3,5},{1,3},{0,1},{10,8},{12,10},{14... | collective-permute-start | bytes 2304008 | tf_op jit(solution)/shard_map/ppermute | solution.py:161
  13.5 21.4 %collective-permute-start = (bf16[320,1200]{1,0:T(8,128)(2,1)}, bf16[320,1200]{1,0:T(8,128)(2,1)S(1)}, u32[]{:S(2)}, u32[]{:S(2)}) collective-permute-start(bf16[320,1200]{1,0:T(8,128)(2,1)} %shard_map.37.refs_0_), channel_id=1, source_target_pairs={{0,2},{2,4},{4,6},{6,7},{7,5},{5,3},{3,1},{1,0},{8,10},{10,12},{12... | collective-permute-start | bytes 2304008 | tf_op jit(solution)/shard_map/ppermute | solution.py:160
  16.0 34.3 %collective-permute-start.3 = (bf16[320,1200]{1,0:T(8,128)(2,1)}, bf16[320,1200]{1,0:T(8,128)(2,1)S(1)}, u32[]{:S(2)}, u32[]{:S(2)}) collective-permute-start(bf16[320,1200]{1,0:T(8,128)(2,1)} %shard_map.38.refs_1_), channel_id=1, source_target_pairs={{2,0},{4,2},{6,4},{7,6},{5,7},{3,5},{1,3},{0,1},{10,8},{12,10},{14... | collective-permute-start | bytes 2304008 | tf_op jit(solution)/shard_map/ppermute | solution.py:161
  18.0 34.5 %collective-permute-start.1 = (bf16[320,1200]{1,0:T(8,128)(2,1)}, bf16[320,1200]{1,0:T(8,128)(2,1)}, u32[]{:S(2)}, u32[]{:S(2)}) collective-permute-start(bf16[320,1200]{1,0:T(8,128)(2,1)} %shard_map.38.refs_1_), channel_id=1, source_target_pairs={{0,2},{2,4},{4,6},{6,7},{7,5},{5,3},{3,1},{1,0},{8,10},{10,12},{12... | collective-permute-start | bytes 2304008 | tf_op jit(solution)/shard_map/ppermute | solution.py:160
  20.5 47.5 %collective-permute-start.18 = (bf16[320,1200]{1,0:T(8,128)(2,1)}, bf16[320,1200]{1,0:T(8,128)(2,1)}, u32[]{:S(2)}, u32[]{:S(2)}) collective-permute-start(bf16[320,1200]{1,0:T(8,128)(2,1)} %shard_map.40.refs_0_), channel_id=1, source_target_pairs={{2,0},{4,2},{6,4},{7,6},{5,7},{3,5},{1,3},{0,1},{10,8},{12,10},{14... | collective-permute-start | bytes 2304008 | tf_op jit(solution)/shard_map/ppermute | solution.py:161
  32.8 37.3 %collective-permute-start.16 = (bf16[320,1200]{1,0:T(8,128)(2,1)S(1)}, bf16[320,1200]{1,0:T(8,128)(2,1)S(1)}, u32[]{:S(2)}, u32[]{:S(2)}) collective-permute-start(bf16[320,1200]{1,0:T(8,128)(2,1)S(1)} %copy-done.2), channel_id=1, source_target_pairs={{0,2},{2,4},{4,6},{6,7},{7,5},{5,3},{3,1},{1,0},{8,10},{10,12},{12... | collective-permute-start | bytes 2304008 | tf_op jit(solution)/shard_map/ppermute | solution.py:160
  34.9 50.6 %collective-permute-start.19 = (bf16[320,1200]{1,0:T(8,128)(2,1)}, bf16[320,1200]{1,0:T(8,128)(2,1)S(1)}, u32[]{:S(2)}, u32[]{:S(2)}) collective-permute-start(bf16[320,1200]{1,0:T(8,128)(2,1)} %shard_map.41.refs_1_), channel_id=1, source_target_pairs={{2,0},{4,2},{6,4},{7,6},{5,7},{3,5},{1,3},{0,1},{10,8},{12,10},{14... | collective-permute-start | bytes 2304008 | tf_op jit(solution)/shard_map/ppermute | solution.py:161
  50.4 37.2 %collective-permute-start.17 = (bf16[320,1200]{1,0:T(8,128)(2,1)}, bf16[320,1200]{1,0:T(8,128)(2,1)S(1)}, u32[]{:S(2)}, u32[]{:S(2)}) collective-permute-start(bf16[320,1200]{1,0:T(8,128)(2,1)} %shard_map.41.refs_1_), channel_id=1, source_target_pairs={{0,2},{2,4},{4,6},{6,7},{7,5},{5,3},{3,1},{1,0},{8,10},{10,12},{12... | collective-permute-start | bytes 2304008 | tf_op jit(solution)/shard_map/ppermute | solution.py:160
  52.5 50.5 %collective-permute-start.6 = (bf16[320,1200]{1,0:T(8,128)(2,1)S(1)}, bf16[320,1200]{1,0:T(8,128)(2,1)S(1)}, u32[]{:S(2)}, u32[]{:S(2)}) collective-permute-start(bf16[320,1200]{1,0:T(8,128)(2,1)S(1)} %collective-permute-done.2.refs_4_), channel_id=1, source_target_pairs={{2,0},{4,2},{6,4},{7,6},{5,7},{3,5},{1,3},{0,1},{10,8},{12,10},{14... | collective-permute-start | bytes 2304008 | tf_op jit(solution)/shard_map/ppermute | solution.py:161
  68.0 37.9 %collective-permute-start.4 = (bf16[320,1200]{1,0:T(8,128)(2,1)S(1)}, bf16[320,1200]{1,0:T(8,128)(2,1)S(1)}, u32[]{:S(2)}, u32[]{:S(2)}) collective-permute-start(bf16[320,1200]{1,0:T(8,128)(2,1)S(1)} %collective-permute-done.refs_2_), channel_id=1, source_target_pairs={{0,2},{2,4},{4,6},{6,7},{7,5},{5,3},{3,1},{1,0},{8,10},{10,12},{12... | collective-permute-start | bytes 2304008 | tf_op jit(solution)/shard_map/ppermute | solution.py:160
  70.1 50.6 %collective-permute-start.7 = (bf16[320,1200]{1,0:T(8,128)(2,1)S(1)}, bf16[320,1200]{1,0:T(8,128)(2,1)}, u32[]{:S(2)}, u32[]{:S(2)}) collective-permute-start(bf16[320,1200]{1,0:T(8,128)(2,1)S(1)} %collective-permute-done.3.refs_5_), channel_id=1, source_target_pairs={{2,0},{4,2},{6,4},{7,6},{5,7},{3,5},{1,3},{0,1},{10,8},{12,10},{14... | collective-permute-start | bytes 2304008 | tf_op jit(solution)/shard_map/ppermute | solution.py:161
  85.5 38.2 %collective-permute-start.5 = (bf16[320,1200]{1,0:T(8,128)(2,1)}, bf16[320,1200]{1,0:T(8,128)(2,1)S(1)}, u32[]{:S(2)}, u32[]{:S(2)}) collective-permute-start(bf16[320,1200]{1,0:T(8,128)(2,1)} %collective-permute-done.1.refs_3_), channel_id=1, source_target_pairs={{0,2},{2,4},{4,6},{6,7},{7,5},{5,3},{3,1},{1,0},{8,10},{10,12},{12... | collective-permute-start | bytes 2304008 | tf_op jit(solution)/shard_map/ppermute | solution.py:160
  87.5 52.6 %collective-permute-start.20 = (bf16[320,1200]{1,0:T(8,128)(2,1)S(1)}, bf16[320,1200]{1,0:T(8,128)(2,1)S(1)}, u32[]{:S(2)}, u32[]{:S(2)}) collective-permute-start(bf16[320,1200]{1,0:T(8,128)(2,1)S(1)} %collective-permute-done.16.refs_2_), channel_id=1, source_target_pairs={{0,2},{2,4},{4,6},{6,7},{7,5},{5,3},{3,1},{1,0},{8,10},{10,12},{12... | collective-permute-start | bytes 2304008 | tf_op jit(solution)/shard_map/ppermute | solution.py:160
  103.0 38.1 %collective-permute-start.23 = (bf16[320,1200]{1,0:T(8,128)(2,1)S(1)}, bf16[320,1200]{1,0:T(8,128)(2,1)S(1)}, u32[]{:S(2)}, u32[]{:S(2)}) collective-permute-start(bf16[320,1200]{1,0:T(8,128)(2,1)S(1)} %collective-permute-done.19.refs_5_), channel_id=1, source_target_pairs={{2,0},{4,2},{6,4},{7,6},{5,7},{3,5},{1,3},{0,1},{10,8},{12,10},{14... | collective-permute-start | bytes 2304008 | tf_op jit(solution)/shard_map/ppermute | solution.py:161
  105.9 49.9 %collective-permute-start.22 = (bf16[320,1200]{1,0:T(8,128)(2,1)}, bf16[320,1200]{1,0:T(8,128)(2,1)}, u32[]{:S(2)}, u32[]{:S(2)}) collective-permute-start(bf16[320,1200]{1,0:T(8,128)(2,1)} %collective-permute-done.18.refs_4_), channel_id=1, source_target_pairs={{2,0},{4,2},{6,4},{7,6},{5,7},{3,5},{1,3},{0,1},{10,8},{12,10},{14... | collective-permute-start | bytes 2304008 | tf_op jit(solution)/shard_map/ppermute | solution.py:161
  120.7 37.2 %collective-permute-start.21 = (bf16[320,1200]{1,0:T(8,128)(2,1)S(1)}, bf16[320,1200]{1,0:T(8,128)(2,1)}, u32[]{:S(2)}, u32[]{:S(2)}) collective-permute-start(bf16[320,1200]{1,0:T(8,128)(2,1)S(1)} %collective-permute-done.17.refs_3_), channel_id=1, source_target_pairs={{0,2},{2,4},{4,6},{6,7},{7,5},{5,3},{3,1},{1,0},{8,10},{10,12},{12... | collective-permute-start | bytes 2304008 | tf_op jit(solution)/shard_map/ppermute | solution.py:160
  123.7 51.6 %collective-permute-start.8 = (bf16[320,1200]{1,0:T(8,128)(2,1)S(1)}, bf16[320,1200]{1,0:T(8,128)(2,1)S(1)}, u32[]{:S(2)}, u32[]{:S(2)}) collective-permute-start(bf16[320,1200]{1,0:T(8,128)(2,1)S(1)} %collective-permute-done.4.refs_6_), channel_id=1, source_target_pairs={{0,2},{2,4},{4,6},{6,7},{7,5},{5,3},{3,1},{1,0},{8,10},{10,12},{12... | collective-permute-start | bytes 2304008 | tf_op jit(solution)/shard_map/ppermute | solution.py:160
  140.2 52.8 %collective-permute-start.24 = (bf16[320,1200]{1,0:T(8,128)(2,1)S(1)}, bf16[320,1200]{1,0:T(8,128)(2,1)}, u32[]{:S(2)}, u32[]{:S(2)}) collective-permute-start(bf16[320,1200]{1,0:T(8,128)(2,1)S(1)} %collective-permute-done.20.refs_6_), channel_id=1, source_target_pairs={{0,2},{2,4},{4,6},{6,7},{7,5},{5,3},{3,1},{1,0},{8,10},{10,12},{12... | collective-permute-start | bytes 2304008 | tf_op jit(solution)/shard_map/ppermute | solution.py:160
  141.1 51.9 %collective-permute-start.27 = (bf16[320,1200]{1,0:T(8,128)(2,1)S(1)}, bf16[320,1200]{1,0:T(8,128)(2,1)}, u32[]{:S(2)}, u32[]{:S(2)}) collective-permute-start(bf16[320,1200]{1,0:T(8,128)(2,1)S(1)} %collective-permute-done.23.refs_9_), channel_id=1, source_target_pairs={{2,0},{4,2},{6,4},{7,6},{5,7},{3,5},{1,3},{0,1},{10,8},{12,10},{14... | collective-permute-start | bytes 2304008 | tf_op jit(solution)/shard_map/ppermute | solution.py:161
  155.8 39.3 %collective-permute-start.11 = (bf16[320,1200]{1,0:T(8,128)(2,1)}, bf16[320,1200]{1,0:T(8,128)(2,1)}, u32[]{:S(2)}, u32[]{:S(2)}) collective-permute-start(bf16[320,1200]{1,0:T(8,128)(2,1)} %collective-permute-done.7.refs_9_), channel_id=1, source_target_pairs={{2,0},{4,2},{6,4},{7,6},{5,7},{3,5},{1,3},{0,1},{10,8},{12,10},{14... | collective-permute-start | bytes 2304008 | tf_op jit(solution)/shard_map/ppermute | solution.py:161
  157.8 50.6 %collective-permute-start.26 = (bf16[320,1200]{1,0:T(8,128)(2,1)}, bf16[320,1200]{1,0:T(8,128)(2,1)}, u32[]{:S(2)}, u32[]{:S(2)}) collective-permute-start(bf16[320,1200]{1,0:T(8,128)(2,1)} %collective-permute-done.22.refs_8_), channel_id=1, source_target_pairs={{2,0},{4,2},{6,4},{7,6},{5,7},{3,5},{1,3},{0,1},{10,8},{12,10},{14... | collective-permute-start | bytes 2304008 | tf_op jit(solution)/shard_map/ppermute | solution.py:161
  175.3 35.2 %collective-permute-start.25 = (bf16[320,1200]{1,0:T(8,128)(2,1)}, bf16[320,1200]{1,0:T(8,128)(2,1)}, u32[]{:S(2)}, u32[]{:S(2)}) collective-permute-start(bf16[320,1200]{1,0:T(8,128)(2,1)} %collective-permute-done.21.refs_7_), channel_id=1, source_target_pairs={{0,2},{2,4},{4,6},{6,7},{7,5},{5,3},{3,1},{1,0},{8,10},{10,12},{12... | collective-permute-start | bytes 2304008 | tf_op jit(solution)/shard_map/ppermute | solution.py:160
  192.9 35.1 %collective-permute-start.28 = (bf16[320,1200]{1,0:T(8,128)(2,1)}, bf16[320,1200]{1,0:T(8,128)(2,1)}, u32[]{:S(2)}, u32[]{:S(2)}) collective-permute-start(bf16[320,1200]{1,0:T(8,128)(2,1)} %collective-permute-done.24.refs_10_), channel_id=1, source_target_pairs={{0,2},{2,4},{4,6},{6,7},{7,5},{5,3},{3,1},{1,0},{8,10},{10,12},{12... | collective-permute-start | bytes 2304008 | tf_op jit(solution)/shard_map/ppermute | solution.py:163
  193.0 37.3 %collective-permute-start.29 = (bf16[320,1200]{1,0:T(8,128)(2,1)}, bf16[320,1200]{1,0:T(8,128)(2,1)}, u32[]{:S(2)}, u32[]{:S(2)}) collective-permute-start(bf16[320,1200]{1,0:T(8,128)(2,1)} %collective-permute-done.27.refs_13_), channel_id=1, source_target_pairs={{2,0},{4,2},{6,4},{7,6},{5,7},{3,5},{1,3},{0,1},{10,8},{12,10},{14... | collective-permute-start | bytes 2304008 | tf_op jit(solution)/shard_map/ppermute | solution.py:163
  195.1 68.0 %collective-permute-start.10 = (bf16[320,1200]{1,0:T(8,128)(2,1)}, bf16[320,1200]{1,0:T(8,128)(2,1)S(1)}, u32[]{:S(2)}, u32[]{:S(2)}) collective-permute-start(bf16[320,1200]{1,0:T(8,128)(2,1)} %copy-done.17), channel_id=1, source_target_pairs={{2,0},{4,2},{6,4},{7,6},{5,7},{3,5},{1,3},{0,1},{10,8},{12,10},{14... | collective-permute-start | bytes 2304008 | tf_op jit(solution)/shard_map/ppermute | solution.py:161
  208.5 54.7 %collective-permute-start.9 = (bf16[320,1200]{1,0:T(8,128)(2,1)}, bf16[320,1200]{1,0:T(8,128)(2,1)S(1)}, u32[]{:S(2)}, u32[]{:S(2)}) collective-permute-start(bf16[320,1200]{1,0:T(8,128)(2,1)} %copy-done.18), channel_id=1, source_target_pairs={{0,2},{2,4},{4,6},{6,7},{7,5},{5,3},{3,1},{1,0},{8,10},{10,12},{12... | collective-permute-start | bytes 2304008 | tf_op jit(solution)/shard_map/ppermute | solution.py:160
  210.5 52.6 %collective-permute-start.12 = (bf16[320,1200]{1,0:T(8,128)(2,1)}, bf16[320,1200]{1,0:T(8,128)(2,1)S(1)}, u32[]{:S(2)}, u32[]{:S(2)}) collective-permute-start(bf16[320,1200]{1,0:T(8,128)(2,1)} %copy-done.19), channel_id=1, source_target_pairs={{0,2},{2,4},{4,6},{6,7},{7,5},{5,3},{3,1},{1,0},{8,10},{10,12},{12... | collective-permute-start | bytes 2304008 | tf_op jit(solution)/shard_map/ppermute | solution.py:163
  228.1 35.1 %collective-permute-start.13 = (bf16[320,1200]{1,0:T(8,128)(2,1)}, bf16[320,1200]{1,0:T(8,128)(2,1)S(1)}, u32[]{:S(2)}, u32[]{:S(2)}) collective-permute-start(bf16[320,1200]{1,0:T(8,128)(2,1)} %collective-permute-done.11.refs_13_), channel_id=1, source_target_pairs={{2,0},{4,2},{6,4},{7,6},{5,7},{3,5},{1,3},{0,1},{10,8},{12,10},{14... | collective-permute-start | bytes 2304008 | tf_op jit(solution)/shard_map/ppermute | solution.py:163
  263.0 29.9 %collective-permute-start.30 = (bf16[2,640,1280]{2,1,0:T(8,128)(2,1)}, bf16[2,640,1280]{2,1,0:T(8,128)(2,1)S(1)}, u32[]{:S(2)}, u32[]{:S(2)}) collective-permute-start(bf16[2,640,1280]{2,1,0:T(8,128)(2,1)} %get-tuple-element.12), channel_id=1, source_target_pairs={{0,8},{8,0},{16,24},{24,16},{1,9},{9,1},{17,25},{25,17},{2,10},{10... | collective-permute-start | bytes 9830408 | tf_op jit(solution)/shard_map/ppermute | solution.py:170
  292.3 6.2 %collective-permute-start.14 = (bf16[2,640,1280]{2,1,0:T(8,128)(2,1)}, bf16[2,640,1280]{2,1,0:T(8,128)(2,1)S(1)}, u32[]{:S(2)}, u32[]{:S(2)}) collective-permute-start(bf16[2,640,1280]{2,1,0:T(8,128)(2,1)} %get-tuple-element.10), channel_id=1, source_target_pairs={{0,8},{8,0},{16,24},{24,16},{1,9},{9,1},{17,25},{25,17},{2,10},{10... | collective-permute-start | bytes 9830408 | tf_op jit(solution)/shard_map/ppermute | solution.py:170
  293.2 73.8 %collective-permute-start.31 = (f32[640,1280]{1,0:T(8,128)S(1)}, f32[640,1280]{1,0:T(8,128)S(1)}, u32[]{:S(2)}, u32[]{:S(2)}) collective-permute-start(f32[640,1280]{1,0:T(8,128)S(1)} %add_bitcast_fusion), channel_id=1, source_target_pairs={{0,16},{8,24},{16,0},{24,8},{1,17},{9,25},{17,1},{25,9},{2,18},{10... | collective-permute-start | bytes 9830408 | tf_op jit(solution)/shard_map/ppermute | solution.py:174
  299.0 137.4 %collective-permute-start.15 = (f32[640,1280]{1,0:T(8,128)S(1)}, f32[640,1280]{1,0:T(8,128)S(1)}, u32[]{:S(2)}, u32[]{:S(2)}) collective-permute-start(f32[640,1280]{1,0:T(8,128)S(1)} %add_bitcast_fusion.1), channel_id=1, source_target_pairs={{0,16},{8,24},{16,0},{24,8},{1,17},{9,25},{17,1},{25,9},{2,18},{10... | collective-permute-start | bytes 9830408 | tf_op jit(solution)/shard_map/ppermute | solution.py:174
  (25 other events, 602.8 us)

commit v2 on v1

v2 whole, which is shorter than its diff:
```python
import functools
import math

import jax
import jax.numpy as jnp
import numpy as np
from jax import lax
from jax.experimental import pallas as pl
from jax.experimental.pallas import tpu as pltpu
from jax.sharding import PartitionSpec as P

clip_limit = 0.99
epsilon = 1e-05
SLABS = ("row", "col")
LANES = 128
VMEM = pltpu.CompilerParams(vmem_limit_bytes=56 * 2**20)
ANY = pl.BlockSpec(memory_space=pl.ANY)


def cycle(rows, cols):
    if cols == 1:
        return list(range(rows))
    walk = [(r, 0) for r in range(rows)]
    for i, r in enumerate(reversed(range(rows))):
        back = list(range(1, cols))
        walk += [(r, c) for c in (back if i % 2 == 0 else back[::-1])]
    return [r * cols + c for r, c in walk]


def normalize_kernel(x_ref, first_ref, *other_refs):
    subjects, rows, duration = x_ref.shape
    body = duration // LANES * LANES
    tail = duration - body
    tails = []
    for a in range(subjects):
        values = x_ref[a]
        center = jnp.mean(values, axis=-1, keepdims=True)
        away = values - center
        spread = jnp.mean(away * away, axis=-1, keepdims=True)
        normed = (away * lax.rsqrt(spread + epsilon)).astype(jnp.bfloat16)
        (first_ref if a == 0 else other_refs[a - 1])[:, :body] = normed[:, :body]
        tails.append(normed[:, body:])
    tails.append(jnp.zeros((rows, LANES - subjects * tail), jnp.bfloat16))
    first_ref[:, body:] = jnp.concatenate(tails, axis=1)


def normalize(series, half, half_rows):
    subjects, _, duration = series.shape
    body = duration // LANES * LANES
    step = max(d for d in range(16, 161, 16) if half_rows % d == 0)
    steps = half_rows // step
    widths = [body + LANES] + [body] * (subjects - 1)
    return pl.pallas_call(
        normalize_kernel,
        grid=(steps,),
        in_specs=[pl.BlockSpec((subjects, step, duration), lambda i: (0, half * steps + i, 0))],
        out_specs=[pl.BlockSpec((step, w), lambda i: (i, 0)) for w in widths],
        out_shape=[jax.ShapeDtypeStruct((half_rows, w), jnp.bfloat16) for w in widths],
        compiler_params=VMEM,
    )(series)


def after(piece, *others):
    def nothing(*refs):
        pass

    return pl.pallas_call(
        nothing,
        in_specs=[ANY] * (1 + len(others)),
        out_specs=ANY,
        out_shape=jax.ShapeDtypeStruct(piece.shape, piece.dtype),
        input_output_aliases={0: 0},
    )(piece, *others)


def scores_kernel(
    source_ref, block_start_ref, place_ref, *refs, subject, away, pieces, slab, granule, block_rows, chips, duration
):
    count = source_ref.shape[0]
    bodies, tails = refs[:pieces], refs[pieces : 2 * pieces]
    same_ref, other_ref, ordered, own_rows, products_a, products_b, place_of, sem = refs[-8:]
    half_rows = slab // 2
    body = duration // LANES * LANES
    tail = duration - body
    for a in range(block_start_ref.shape[0]):
        place_of[block_start_ref[a] // block_rows] = a

    for slot in range(count):
        for half in range(2):
            piece = 2 * slot + half
            first = source_ref[slot] * slab + half * half_rows

            def start(g, _, piece=piece, first=first):
                stored = first + g * granule
                block = stored // block_rows
                row = place_of[block] * block_rows + (stored - block * block_rows)
                here = pl.ds(pl.multiple_of(g * granule, granule), granule)
                there = pl.ds(pl.multiple_of(row, granule), granule)
                if subject == 0:
                    pltpu.make_async_copy(tails[piece].at[here], ordered.at[there], sem).start()
                else:
                    pltpu.make_async_copy(bodies[piece].at[here], ordered.at[there, :body], sem).start()
                    pltpu.make_async_copy(tails[piece].at[here, body:], ordered.at[there, body:], sem).start()
                return 0

            lax.fori_loop(0, half_rows // granule, start, 0)
    pltpu.make_async_copy(ordered, ordered, sem).wait()

    position, subj = place_ref[0], place_ref[1]
    chip, core = subj // 2, subj % 2
    rows = pl.ds(pl.multiple_of(position * slab, granule), slab)
    own_rows[:, :body] = ordered[rows, :body]
    lane = lax.broadcasted_iota(jnp.int32, (slab, LANES), 1)
    kept = (lane >= subject * tail) & (lane < (subject + 1) * tail)
    own_rows[:, body:] = jnp.where(kept, ordered[rows, body:].astype(jnp.float32), 0.0).astype(jnp.bfloat16)

    limit = clip_limit * duration
    chunk = same_ref.shape[1]
    width = math.gcd(chunk, 256)
    tiles = []
    for flip, out_ref in ((1, other_ref), (0, same_ref)):
        owner = (chip + away) % chips * 2 + (core + flip) % 2
        tiles += [(owner * chunk + k * width, k * width, out_ref) for k in range(chunk // width)]
    buffers = (products_a, products_b)

    def multiply(i):
        columns = ordered[pl.ds(pl.multiple_of(tiles[i][0], width), width)]
        buffers[i % 2][...] = lax.dot_general(
            own_rows[...], columns, (((1,), (1,)), ((), ())), preferred_element_type=jnp.float32
        )

    def score(i):
        products = jnp.clip(buffers[i % 2][...], -limit, limit)
        fisher = 0.5 * (jnp.log(duration + products) - jnp.log(duration - products))
        tiles[i][2][:, pl.ds(tiles[i][1], width)] = fisher.astype(jnp.bfloat16)

    multiply(0)
    for i in range(1, len(tiles)):
        multiply(i)
        score(i - 1)
    score(len(tiles) - 1)


def scores(source, block_start, place, subject, away, bodies, tails, slab, window, chips, duration, late=()):
    block_rows = window // block_start.shape[0]
    granule = math.gcd(slab // 2, block_rows)
    chunk = window // (2 * chips)
    width = math.gcd(chunk, 256)
    padded = tails[0].shape[1]
    out = jax.ShapeDtypeStruct((slab, chunk), jnp.bfloat16)
    smem = pl.BlockSpec(memory_space=pltpu.SMEM)
    return pl.pallas_call(
        functools.partial(
            scores_kernel,
            subject=subject,
            away=away,
            pieces=len(tails),
            slab=slab,
            granule=granule,
            block_rows=block_rows,
            chips=chips,
            duration=duration,
        ),
        in_specs=[smem, smem, smem] + [ANY] * (2 * len(tails) + len(late)),
        out_shape=[out, out],
        scratch_shapes=[
            pltpu.VMEM((window, padded), jnp.bfloat16),
            pltpu.VMEM((slab, padded), jnp.bfloat16),
            pltpu.VMEM((slab, width), jnp.float32),
            pltpu.VMEM((slab, width), jnp.float32),
            pltpu.SMEM((block_start.shape[0],), jnp.int32),
            pltpu.SemaphoreType.DMA,
        ],
        compiler_params=pltpu.CompilerParams(vmem_limit_bytes=48 * 2**20),
        cost_estimate=pl.CostEstimate(
            flops=4 * slab * chunk * padded,
            bytes_accessed=2 * window * padded + 4 * slab * chunk,
            transcendentals=4 * slab * chunk,
        ),
    )(source, block_start, place, *bodies, *tails, *late)


def on_device(series, block_start):
    local_subjects, slab, duration = series.shape
    rows, cols = lax.axis_size("row"), lax.axis_size("col")
    count = rows * cols
    window = count * slab
    subjs = lax.axis_size("subj")
    chips = subjs // 2
    half_rows = slab // 2
    order = cycle(rows, cols)
    onward = [(order[i], order[(i + 1) % count]) for i in range(count)]
    backward = [(b, a) for a, b in onward]
    reach = count // 2
    offsets = [0]
    for d in range(1, reach):
        offsets += [d, -d]
    offsets.append(reach)
    table = np.zeros((count, count), np.int32)
    for i, device in enumerate(order):
        table[device] = [order[(i - d) % count] for d in offsets]
    position = lax.axis_index(SLABS)
    source = jnp.asarray(table)[position]
    place = jnp.stack([position, lax.axis_index("subj")]).astype(jnp.int32)

    def gather(own):
        got = [own]
        ahead, behind = list(own), list(own)
        for _ in range(1, reach):
            ahead = [lax.ppermute(piece, SLABS, onward) for piece in ahead]
            behind = [lax.ppermute(piece, SLABS, backward) for piece in behind]
            got += [ahead, behind]
        got.append([lax.ppermute(ahead[0], SLABS, onward), lax.ppermute(behind[1], SLABS, backward)])
        return got

    def flat(pairs):
        return [piece for pair in pairs for piece in pair]

    swap = [(s, s ^ 1) for s in range(subjs)]
    normed = [normalize(series, half, half_rows) for half in range(2)]
    gathered = []
    for a in range(local_subjects):
        own = [normed[half][a] for half in range(2)]
        if a:
            before = gathered[-1]
            own = [after(own[half], before[-3][half], before[-2][half]) for half in range(2)]
        gathered.append(gather(own))

    terms = []
    for a in range(local_subjects):
        last = a == local_subjects - 1
        for n, d in enumerate([*range(1, chips), 0]):
            late = () if last else gathered[a + 1][min(2 * n + 1, len(gathered[a + 1]) - 1)][:1]
            same, other = scores(
                source, block_start, place, a, d, flat(gathered[a]), flat(gathered[0]), slab, window, chips, duration, late
            )
            crossed = lax.ppermute(other, "subj", swap)
            part = same.astype(jnp.float32) + crossed.astype(jnp.float32)
            if d:
                part = part.astype(jnp.bfloat16) if last else part
                part = lax.ppermute(part, "subj", [(s, (s + 2 * d) % subjs) for s in range(subjs)])
                part = part.astype(jnp.float32)
            terms.append(part)
    return sum(terms[1:], terms[0]) / (local_subjects * subjs)


def solution(mesh):
    return jax.shard_map(
        on_device,
        mesh=mesh,
        in_specs=(P("subj", SLABS, None), P()),
        out_specs=P(SLABS, "subj"),
        check_vma=False,
    )
```

time: 440 us -> 378 us (0.86)
  waiting for transfers between devices: 303 us -> 256 us
  starting transfers between devices: 46.9 us -> 36.5 us
  local copies, waits for them, and re-layouts: 21.4 us -> 14.1 us
    ppermute x12, waiting for transfers between devices: 47.7 us -> 132 us  [gather(): ahead = [lax.ppermute(piece, SLABS, onward) for piece in ahead]]
    ppermute x4 -> x6, waiting for transfers between devices: 140 us -> 72.6 us  [the longest x2 72.5 us: on_device(): lax.ppermute(part, 'subj', [(s, (s + 2 * d) % subjs) for s in range(subjs)])]
    ppermute x12, waiting for transfers between devices: 100 us -> 38.5 us  [gather(): behind = [lax.ppermute(piece, SLABS, backward) for piece in behind]]
    ppermute x12, starting transfers between devices: 22.2 us -> 3.89 us  [gather(): behind = [lax.ppermute(piece, SLABS, backward) for piece in behind]]
    ppermute x12, starting transfers between devices: 15.7 us -> 24.2 us  [gather(): ahead = [lax.ppermute(piece, SLABS, onward) for piece in ahead]]
    unnamed x51 -> x61, local copies, waits for them, and re-layouts: 20.7 us -> 13.4 us
    ppermute x2, waiting for transfers between devices: 16 us -> 8.76 us  [gather(): lax.ppermute(ahead[0], SLABS, onward)]
    pallas_call x6 -> x8, Pallas kernels: 63.6 us -> 65.9 us  [the longest x4 59.4 us: scores(): pl.pallas_call(functools.partial(scores_kernel, subject=subject, away=awa...]
  transfers between devices with their start and end apart: 32 -> 34, of which waited for: 16 -> 22; matrix products, arithmetic and copies ran while one was open for 0% -> 1% of each run, Pallas kernels for 14% -> 17%
where the time goes in v2:
time: 378 us
  waiting for transfers between devices  256 us (68%)
  Pallas kernels  65.9 us (17%)
  starting transfers between devices  36.5 us (10%)
  local copies, waits for them, and re-layouts  14.1 us (4%)
  other arithmetic  5.51 us (1%)
    ppermute x12, waiting for transfers between devices, gather(): ahead = [lax.ppermute(piece, SLABS, onward) for piece in ahead]  132 us
    ppermute x2, waiting for transfers between devices, on_device(): lax.ppermute(part, 'subj', [(s, (s + 2 * d) % subjs) for s in range(subjs)])  72.5 us
    pallas_call x4, Pallas kernels, scores(): pl.pallas_call(functools.partial(scores_kernel, subject=subject, away=awa...  59.4 us
    ppermute x12, waiting for transfers between devices, gather(): behind = [lax.ppermute(piece, SLABS, backward) for piece in behind]  38.5 us
    ppermute x12, starting transfers between devices, gather(): ahead = [lax.ppermute(piece, SLABS, onward) for piece in ahead]  24.2 us
    unnamed x61, local copies, waits for them, and re-layouts  13.4 us
    ppermute x2, waiting for transfers between devices, gather(): lax.ppermute(ahead[0], SLABS, onward)  8.76 us
  transfers between devices with their start and end apart: 34, of which 22 were waited for; matrix products, arithmetic and copies ran while one was open for 1% of the time, Pallas kernels for 17%

profile of v2, /device:TPU:0, one launch (start us, length us, event | category | flops | bytes accessed | tf_op | source)
XLA Modules:
  0.0 378.0 jit_solution(12398793159512111372)
XLA Ops:
  0.0 8.0 %copy.6.x_ref = f32[2,640,1200]{2,1,0:T(8,128)} copy(f32[2,640,1200]{1,2,0:T(8,128)} %param.3) | data formatting | bytes 12288000 | tf_op args[0]
  8.0 3.2 shard_map.37
  11.2 3.0 collective-permute-start
  14.3 3.2 shard_map.38
  19.6 13.9 %collective-permute-done.refs_2_.refs_18_ = bf16[320,1280]{1,0:T(8,128)(2,1)S(1)} collective-permute-done((bf16[320,1280]{1,0:T(8,128)(2,1)}, bf16[320,1280]{1,0:T(8,128)(2,1)S(1)}, u32[]{:S(2)}, u32[]{:S(2)}) %collective-permute-start) | collective-permute-done | bytes 819232 | tf_op jit(solution)/shard_map/ppermute | solution.py:210
  33.5 2.1 collective-permute-start.4
  35.6 15.4 %collective-permute-done.1.refs_3_.refs_19_ = bf16[320,1280]{1,0:T(8,128)(2,1)S(1)} collective-permute-done((bf16[320,1280]{1,0:T(8,128)(2,1)}, bf16[320,1280]{1,0:T(8,128)(2,1)S(1)}, u32[]{:S(2)}, u32[]{:S(2)}) %collective-permute-start.1) | collective-permute-done | bytes 819232 | tf_op jit(solution)/shard_map/ppermute | solution.py:210
  54.9 13.7 %collective-permute-done.4.refs_6_.refs_22_ = bf16[320,1280]{1,0:T(8,128)(2,1)S(1)} collective-permute-done((bf16[320,1280]{1,0:T(8,128)(2,1)S(1)}, bf16[320,1280]{1,0:T(8,128)(2,1)S(1)}, u32[]{:S(2)}, u32[]{:S(2)}) %collective-permute-start.4) | collective-permute-done | bytes 819232 | tf_op jit(solution)/shard_map/ppermute | solution.py:210
  70.8 15.5 %collective-permute-done.5.refs_7_.refs_23_ = bf16[320,1280]{1,0:T(8,128)(2,1)} collective-permute-done((bf16[320,1280]{1,0:T(8,128)(2,1)S(1)}, bf16[320,1280]{1,0:T(8,128)(2,1)}, u32[]{:S(2)}, u32[]{:S(2)}) %collective-permute-start.5) | collective-permute-done | bytes 819232 | tf_op jit(solution)/shard_map/ppermute | solution.py:210
  86.3 2.1 collective-permute-start.9
  88.4 15.4 %collective-permute-done.8.refs_1_.refs_10_.refs_26_ = bf16[320,1280]{1,0:T(8,128)(2,1)} collective-permute-done((bf16[320,1280]{1,0:T(8,128)(2,1)S(1)}, bf16[320,1280]{1,0:T(8,128)(2,1)}, u32[]{:S(2)}, u32[]{:S(2)}) %collective-permute-start.8) | collective-permute-done | bytes 819232 | tf_op jit(solution)/shard_map/ppermute | solution.py:210
  103.8 2.2 collective-permute-done.10.refs_2_.refs_12_.refs_28_
  107.5 13.8 %collective-permute-done.9.refs_11_.refs_27_.refs_1_ = bf16[320,1280]{1,0:T(8,128)(2,1)} collective-permute-done((bf16[320,1280]{1,0:T(8,128)(2,1)}, bf16[320,1280]{1,0:T(8,128)(2,1)}, u32[]{:S(2)}, u32[]{:S(2)}) %collective-permute-start.9) | collective-permute-done | bytes 819232 | tf_op jit(solution)/shard_map/ppermute | solution.py:210
  126.1 11.1 %collective-permute-done.14.refs_32_.refs_2_ = bf16[320,1152]{1,0:T(8,128)(2,1)} collective-permute-done((bf16[320,1152]{1,0:T(8,128)(2,1)}, bf16[320,1152]{1,0:T(8,128)(2,1)}, u32[]{:S(2)}, u32[]{:S(2)}) %collective-permute-start.14) | collective-permute-done | bytes 737312 | tf_op jit(solution)/shard_map/ppermute | solution.py:210
  139.2 13.7 %collective-permute-done.19.refs_3_ = bf16[320,1152]{1,0:T(8,128)(2,1)} collective-permute-done((bf16[320,1152]{1,0:T(8,128)(2,1)}, bf16[320,1152]{1,0:T(8,128)(2,1)}, u32[]{:S(2)}, u32[]{:S(2)}) %collective-permute-start.19) | collective-permute-done | bytes 737312 | tf_op jit(solution)/shard_map/ppermute | solution.py:210
  155.9 20.9 %collective-permute-done.20.refs_4_ = bf16[320,1152]{1,0:T(8,128)(2,1)} collective-permute-done((bf16[320,1152]{1,0:T(8,128)(2,1)}, bf16[320,1152]{1,0:T(8,128)(2,1)}, u32[]{:S(2)}, u32[]{:S(2)}) %collective-permute-start.20) | collective-permute-done | bytes 737312 | tf_op jit(solution)/shard_map/ppermute | solution.py:211
  178.8 7.6 %collective-permute-done.17.refs_32_.refs_6_ = bf16[320,1152]{1,0:T(8,128)(2,1)} collective-permute-done((bf16[320,1152]{1,0:T(8,128)(2,1)}, bf16[320,1152]{1,0:T(8,128)(2,1)}, u32[]{:S(2)}, u32[]{:S(2)}) %collective-permute-start.17) | collective-permute-done | bytes 737312 | tf_op jit(solution)/shard_map/ppermute | solution.py:210
  186.3 2.1 collective-permute-start.25
  188.4 4.1 %collective-permute-done.24.refs_9_ = bf16[320,1152]{1,0:T(8,128)(2,1)} collective-permute-done((bf16[320,1152]{1,0:T(8,128)(2,1)}, bf16[320,1152]{1,0:T(8,128)(2,1)}, u32[]{:S(2)}, u32[]{:S(2)}) %collective-permute-start.24) | collective-permute-done | bytes 737312 | tf_op jit(solution)/shard_map/ppermute | solution.py:211
  195.3 17.7 %shard_map.40 = (bf16[640,1280]{1,0:T(8,128)(2,1)}, bf16[640,1280]{1,0:T(8,128)(2,1)}) custom-call(s32[8]{0:T(128)S(1)} %dynamic-slice_bitcast_fusion.source_ref, s32[5]{0:T(128)S(1)} %copy-done.16, s32[2]{0:T(128)S(1)} %pad_add_fusion.place_ref, bf16[320,1280]{1,0:T(8,128)(2,1)S(1)} %copy-done, bf16[320,1280]{1,0:T(8,128)(2,1)S(1)} %copy-done.6, ...), custom_call_target="tpu_custom_call" | custom-call | flops 4194304000 | bytes 16384000 | tf_op jit(solution)/shard_map/pallas_call | solution.py:152
  215.2 2.6 collective-permute-done.25.refs_10_
  219.8 4.3 %collective-permute-done.28.refs_13_ = bf16[320,1152]{1,0:T(8,128)(2,1)S(1)} collective-permute-done((bf16[320,1152]{1,0:T(8,128)(2,1)}, bf16[320,1152]{1,0:T(8,128)(2,1)S(1)}, u32[]{:S(2)}, u32[]{:S(2)}) %collective-permute-start.28) | collective-permute-done | bytes 737312 | tf_op jit(solution)/shard_map/ppermute | solution.py:211
  224.5 9.0 %collective-permute-done.26.refs_11_ = bf16[320,1152]{1,0:T(8,128)(2,1)S(1)} collective-permute-done((bf16[320,1152]{1,0:T(8,128)(2,1)S(1)}, bf16[320,1152]{1,0:T(8,128)(2,1)S(1)}, u32[]{:S(2)}, u32[]{:S(2)}) %collective-permute-start.26) | collective-permute-done | bytes 737312 | tf_op jit(solution)/shard_map/ppermute | solution.py:210
  233.5 6.3 %collective-permute-done.27.refs_12_ = bf16[320,1152]{1,0:T(8,128)(2,1)S(1)} collective-permute-done((bf16[320,1152]{1,0:T(8,128)(2,1)S(1)}, bf16[320,1152]{1,0:T(8,128)(2,1)S(1)}, u32[]{:S(2)}, u32[]{:S(2)}) %collective-permute-start.27) | collective-permute-done | bytes 737312 | tf_op jit(solution)/shard_map/ppermute | solution.py:211
  239.8 8.8 %collective-permute-done.29.refs_14_ = bf16[320,1152]{1,0:T(8,128)(2,1)S(1)} collective-permute-done((bf16[320,1152]{1,0:T(8,128)(2,1)S(1)}, bf16[320,1152]{1,0:T(8,128)(2,1)S(1)}, u32[]{:S(2)}, u32[]{:S(2)}) %collective-permute-start.29) | collective-permute-done | bytes 737312 | tf_op jit(solution)/shard_map/ppermute | solution.py:213
  248.6 4.4 %collective-permute-done.30.refs_15_ = bf16[320,1152]{1,0:T(8,128)(2,1)S(1)} collective-permute-done((bf16[320,1152]{1,0:T(8,128)(2,1)S(1)}, bf16[320,1152]{1,0:T(8,128)(2,1)S(1)}, u32[]{:S(2)}, u32[]{:S(2)}) %collective-permute-start.30) | collective-permute-done | bytes 737312 | tf_op jit(solution)/shard_map/ppermute | solution.py:213
  253.9 12.1 %shard_map.43 = (bf16[640,1280]{1,0:T(8,128)(2,1)}, bf16[640,1280]{1,0:T(8,128)(2,1)}) custom-call(s32[8]{0:T(128)S(1)} %dynamic-slice_bitcast_fusion.source_ref, s32[5]{0:T(128)S(1)} %copy-done.16, s32[2]{0:T(128)S(1)} %pad_add_fusion.place_ref, bf16[320,1152]{1,0:T(8,128)(2,1)S(1)} %copy-done.15, bf16[320,1152]{1,0:T(8,128)(2,1)S(1)} %copy-done.14, ...), custom_call_target="tpu_custom_call" | custom-call | flops 4194304000 | bytes 16384000 | tf_op jit(solution)/shard_map/pallas_call | solution.py:152
  268.4 17.7 %shard_map.41 = (bf16[640,1280]{1,0:T(8,128)(2,1)}, bf16[640,1280]{1,0:T(8,128)(2,1)}) custom-call(s32[8]{0:T(128)S(1)} %dynamic-slice_bitcast_fusion.source_ref, s32[5]{0:T(128)S(1)} %copy-done.16, s32[2]{0:T(128)S(1)} %pad_add_fusion.place_ref, bf16[320,1280]{1,0:T(8,128)(2,1)S(1)} %copy-done.1, bf16[320,1280]{1,0:T(8,128)(2,1)S(1)} %copy-done.7, ...), custom_call_target="tpu_custom_call" | custom-call | flops 4194304000 | bytes 16384000 | tf_op jit(solution)/shard_map/pallas_call | solution.py:152
  286.7 12.0 %shard_map.44 = (bf16[640,1280]{1,0:T(8,128)(2,1)}, bf16[640,1280]{1,0:T(8,128)(2,1)}) custom-call(s32[8]{0:T(128)S(1)} %dynamic-slice_bitcast_fusion.source_ref, s32[5]{0:T(128)S(1)} %copy-done.16, s32[2]{0:T(128)S(1)} %pad_add_fusion.place_ref, bf16[320,1152]{1,0:T(8,128)(2,1)S(1)} %copy-done.15, bf16[320,1152]{1,0:T(8,128)(2,1)S(1)} %copy-done.14, ...), custom_call_target="tpu_custom_call" | custom-call | flops 4194304000 | bytes 16384000 | tf_op jit(solution)/shard_map/pallas_call | solution.py:152
  302.5 37.8 %collective-permute-done.16 = f32[640,1280]{1,0:T(8,128)S(1)} collective-permute-done((f32[640,1280]{1,0:T(8,128)S(1)}, f32[640,1280]{1,0:T(8,128)S(1)}, u32[]{:S(2)}, u32[]{:S(2)}) %collective-permute-start.16) | collective-permute-done | bytes 3276832 | tf_op jit(solution)/shard_map/ppermute | solution.py:241
  340.3 34.7 %collective-permute-done.32 = bf16[640,1280]{1,0:T(8,128)(2,1)S(1)} collective-permute-done((bf16[640,1280]{1,0:T(8,128)(2,1)S(1)}, bf16[640,1280]{1,0:T(8,128)(2,1)S(1)}, u32[]{:S(2)}, u32[]{:S(2)}) %collective-permute-start.32) | collective-permute-done | bytes 1638432 | tf_op jit(solution)/shard_map/ppermute | solution.py:241
  375.0 3.0 add_multiply_fusion
  (110 shorter events, 36.6 us)
Async XLA Ops:
  11.2 22.2 %collective-permute-start = (bf16[320,1280]{1,0:T(8,128)(2,1)}, bf16[320,1280]{1,0:T(8,128)(2,1)S(1)}, u32[]{:S(2)}, u32[]{:S(2)}) collective-permute-start(bf16[320,1280]{1,0:T(8,128)(2,1)} %get-tuple-element.17.refs_0_.refs_16_), channel_id=1, source_target_pairs={{0,2},{2,4},{4,6},{6,7},{7,5},{5,3},{3,1},{1,0},{8,10},{10,12},{12... | collective-permute-start | bytes 2457608 | tf_op jit(solution)/shard_map/ppermute | solution.py:210
  14.3 21.4 %collective-permute-start.2 = (bf16[320,1280]{1,0:T(8,128)(2,1)}, bf16[320,1280]{1,0:T(8,128)(2,1)S(1)}, u32[]{:S(2)}, u32[]{:S(2)}) collective-permute-start(bf16[320,1280]{1,0:T(8,128)(2,1)} %get-tuple-element.17.refs_0_.refs_16_), channel_id=1, source_target_pairs={{2,0},{4,2},{6,4},{7,6},{5,7},{3,5},{1,3},{0,1},{10,8},{12,10},{14... | collective-permute-start | bytes 2457608 | tf_op jit(solution)/shard_map/ppermute | solution.py:211
  17.5 33.5 %collective-permute-start.1 = (bf16[320,1280]{1,0:T(8,128)(2,1)}, bf16[320,1280]{1,0:T(8,128)(2,1)S(1)}, u32[]{:S(2)}, u32[]{:S(2)}) collective-permute-start(bf16[320,1280]{1,0:T(8,128)(2,1)} %get-tuple-element.18.refs_1_.refs_17_), channel_id=1, source_target_pairs={{0,2},{2,4},{4,6},{6,7},{7,5},{5,3},{3,1},{1,0},{8,10},{10,12},{12... | collective-permute-start | bytes 2457608 | tf_op jit(solution)/shard_map/ppermute | solution.py:210
  19.6 34.5 %collective-permute-start.3 = (bf16[320,1280]{1,0:T(8,128)(2,1)}, bf16[320,1280]{1,0:T(8,128)(2,1)S(1)}, u32[]{:S(2)}, u32[]{:S(2)}) collective-permute-start(bf16[320,1280]{1,0:T(8,128)(2,1)} %get-tuple-element.18.refs_1_.refs_17_), channel_id=1, source_target_pairs={{2,0},{4,2},{6,4},{7,6},{5,7},{3,5},{1,3},{0,1},{10,8},{12,10},{14... | collective-permute-start | bytes 2457608 | tf_op jit(solution)/shard_map/ppermute | solution.py:211
  33.5 35.1 %collective-permute-start.4 = (bf16[320,1280]{1,0:T(8,128)(2,1)S(1)}, bf16[320,1280]{1,0:T(8,128)(2,1)S(1)}, u32[]{:S(2)}, u32[]{:S(2)}) collective-permute-start(bf16[320,1280]{1,0:T(8,128)(2,1)S(1)} %collective-permute-done.refs_2_.refs_18_), channel_id=1, source_target_pairs={{0,2},{2,4},{4,6},{6,7},{7,5},{5,3},{3,1},{1,0},{8,10},{10,12},{12... | collective-permute-start | bytes 2457608 | tf_op jit(solution)/shard_map/ppermute | solution.py:210
  35.6 35.1 %collective-permute-start.6 = (bf16[320,1280]{1,0:T(8,128)(2,1)S(1)}, bf16[320,1280]{1,0:T(8,128)(2,1)S(1)}, u32[]{:S(2)}, u32[]{:S(2)}) collective-permute-start(bf16[320,1280]{1,0:T(8,128)(2,1)S(1)} %collective-permute-done.2.refs_4_.refs_20_), channel_id=1, source_target_pairs={{2,0},{4,2},{6,4},{7,6},{5,7},{3,5},{1,3},{0,1},{10,8},{12,10},{14... | collective-permute-start | bytes 2457608 | tf_op jit(solution)/shard_map/ppermute | solution.py:211
  51.0 35.2 %collective-permute-start.5 = (bf16[320,1280]{1,0:T(8,128)(2,1)S(1)}, bf16[320,1280]{1,0:T(8,128)(2,1)}, u32[]{:S(2)}, u32[]{:S(2)}) collective-permute-start(bf16[320,1280]{1,0:T(8,128)(2,1)S(1)} %collective-permute-done.1.refs_3_.refs_19_), channel_id=1, source_target_pairs={{0,2},{2,4},{4,6},{6,7},{7,5},{5,3},{3,1},{1,0},{8,10},{10,12},{12... | collective-permute-start | bytes 2457608 | tf_op jit(solution)/shard_map/ppermute | solution.py:210
  54.1 34.4 %collective-permute-start.7 = (bf16[320,1280]{1,0:T(8,128)(2,1)S(1)}, bf16[320,1280]{1,0:T(8,128)(2,1)}, u32[]{:S(2)}, u32[]{:S(2)}) collective-permute-start(bf16[320,1280]{1,0:T(8,128)(2,1)S(1)} %collective-permute-done.3.refs_5_.refs_21_), channel_id=1, source_target_pairs={{2,0},{4,2},{6,4},{7,6},{5,7},{3,5},{1,3},{0,1},{10,8},{12,10},{14... | collective-permute-start | bytes 2457608 | tf_op jit(solution)/shard_map/ppermute | solution.py:211
  68.6 35.2 %collective-permute-start.8 = (bf16[320,1280]{1,0:T(8,128)(2,1)S(1)}, bf16[320,1280]{1,0:T(8,128)(2,1)}, u32[]{:S(2)}, u32[]{:S(2)}) collective-permute-start(bf16[320,1280]{1,0:T(8,128)(2,1)S(1)} %collective-permute-done.4.refs_6_.refs_22_), channel_id=1, source_target_pairs={{0,2},{2,4},{4,6},{6,7},{7,5},{5,3},{3,1},{1,0},{8,10},{10,12},{12... | collective-permute-start | bytes 2457608 | tf_op jit(solution)/shard_map/ppermute | solution.py:210
  70.8 35.2 %collective-permute-start.10 = (bf16[320,1280]{1,0:T(8,128)(2,1)S(1)}, bf16[320,1280]{1,0:T(8,128)(2,1)}, u32[]{:S(2)}, u32[]{:S(2)}) collective-permute-start(bf16[320,1280]{1,0:T(8,128)(2,1)S(1)} %collective-permute-done.6.refs_8_.refs_24_), channel_id=1, source_target_pairs={{2,0},{4,2},{6,4},{7,6},{5,7},{3,5},{1,3},{0,1},{10,8},{12,10},{14... | collective-permute-start | bytes 2457608 | tf_op jit(solution)/shard_map/ppermute | solution.py:211
  86.3 35.1 %collective-permute-start.9 = (bf16[320,1280]{1,0:T(8,128)(2,1)}, bf16[320,1280]{1,0:T(8,128)(2,1)}, u32[]{:S(2)}, u32[]{:S(2)}) collective-permute-start(bf16[320,1280]{1,0:T(8,128)(2,1)} %collective-permute-done.5.refs_7_.refs_23_), channel_id=1, source_target_pairs={{0,2},{2,4},{4,6},{6,7},{7,5},{5,3},{3,1},{1,0},{8,10},{10,12},{12... | collective-permute-start | bytes 2457608 | tf_op jit(solution)/shard_map/ppermute | solution.py:210
  88.4 33.6 %collective-permute-start.11 = (bf16[320,1280]{1,0:T(8,128)(2,1)}, bf16[320,1280]{1,0:T(8,128)(2,1)}, u32[]{:S(2)}, u32[]{:S(2)}) collective-permute-start(bf16[320,1280]{1,0:T(8,128)(2,1)} %collective-permute-done.7.refs_9_.refs_25_), channel_id=1, source_target_pairs={{2,0},{4,2},{6,4},{7,6},{5,7},{3,5},{1,3},{0,1},{10,8},{12,10},{14... | collective-permute-start | bytes 2457608 | tf_op jit(solution)/shard_map/ppermute | solution.py:211
  106.0 31.2 %collective-permute-start.14 = (bf16[320,1152]{1,0:T(8,128)(2,1)}, bf16[320,1152]{1,0:T(8,128)(2,1)}, u32[]{:S(2)}, u32[]{:S(2)}) collective-permute-start(bf16[320,1152]{1,0:T(8,128)(2,1)} %shard_map.39.refs_0_), channel_id=1, source_target_pairs={{0,2},{2,4},{4,6},{6,7},{7,5},{5,3},{3,1},{1,0},{8,10},{10,12},{12... | collective-permute-start | bytes 2211848 | tf_op jit(solution)/shard_map/ppermute | solution.py:210
  122.1 30.9 %collective-permute-start.19 = (bf16[320,1152]{1,0:T(8,128)(2,1)}, bf16[320,1152]{1,0:T(8,128)(2,1)}, u32[]{:S(2)}, u32[]{:S(2)}) collective-permute-start(bf16[320,1152]{1,0:T(8,128)(2,1)} %shard_map.42.refs_1_), channel_id=1, source_target_pairs={{0,2},{2,4},{4,6},{6,7},{7,5},{5,3},{3,1},{1,0},{8,10},{10,12},{12... | collective-permute-start | bytes 2211848 | tf_op jit(solution)/shard_map/ppermute | solution.py:210
  123.6 31.5 %collective-permute-start.21 = (bf16[320,1152]{1,0:T(8,128)(2,1)}, bf16[320,1152]{1,0:T(8,128)(2,1)}, u32[]{:S(2)}, u32[]{:S(2)}) collective-permute-start(bf16[320,1152]{1,0:T(8,128)(2,1)} %shard_map.42.refs_1_), channel_id=1, source_target_pairs={{2,0},{4,2},{6,4},{7,6},{5,7},{3,5},{1,3},{0,1},{10,8},{12,10},{14... | collective-permute-start | bytes 2211848 | tf_op jit(solution)/shard_map/ppermute | solution.py:211
  124.1 54.2 %collective-permute-start.12 = (bf16[320,1280]{1,0:T(8,128)(2,1)}, bf16[320,1280]{1,0:T(8,128)(2,1)}, u32[]{:S(2)}, u32[]{:S(2)}) collective-permute-start(bf16[320,1280]{1,0:T(8,128)(2,1)} %collective-permute-done.8.refs_1_.refs_10_.refs_26_), channel_id=1, source_target_pairs={{0,2},{2,4},{4,6},{6,7},{7,5},{5,3},{3,1},{1,0},{8,10},{10,12},{12... | collective-permute-start | bytes 2457608 | tf_op jit(solution)/shard_map/ppermute | solution.py:213
  125.7 67.3 %collective-permute-start.13 = (bf16[320,1280]{1,0:T(8,128)(2,1)}, bf16[320,1280]{1,0:T(8,128)(2,1)}, u32[]{:S(2)}, u32[]{:S(2)}) collective-permute-start(bf16[320,1280]{1,0:T(8,128)(2,1)} %collective-permute-done.11.refs_13_.refs_29_.refs_2_), channel_id=1, source_target_pairs={{2,0},{4,2},{6,4},{7,6},{5,7},{3,5},{1,3},{0,1},{10,8},{12,10},{14... | collective-permute-start | bytes 2457608 | tf_op jit(solution)/shard_map/ppermute | solution.py:213
  137.2 39.6 %collective-permute-start.20 = (bf16[320,1152]{1,0:T(8,128)(2,1)}, bf16[320,1152]{1,0:T(8,128)(2,1)}, u32[]{:S(2)}, u32[]{:S(2)}) collective-permute-start(bf16[320,1152]{1,0:T(8,128)(2,1)} %shard_map.39.refs_0_), channel_id=1, source_target_pairs={{2,0},{4,2},{6,4},{7,6},{5,7},{3,5},{1,3},{0,1},{10,8},{12,10},{14... | collective-permute-start | bytes 2211848 | tf_op jit(solution)/shard_map/ppermute | solution.py:211
  153.0 33.4 %collective-permute-start.17 = (bf16[320,1152]{1,0:T(8,128)(2,1)}, bf16[320,1152]{1,0:T(8,128)(2,1)}, u32[]{:S(2)}, u32[]{:S(2)}) collective-permute-start(bf16[320,1152]{1,0:T(8,128)(2,1)} %collective-permute-done.14.refs_32_.refs_2_), channel_id=1, source_target_pairs={{0,2},{2,4},{4,6},{6,7},{7,5},{5,3},{3,1},{1,0},{8,10},{10,12},{12... | collective-permute-start | bytes 2211848 | tf_op jit(solution)/shard_map/ppermute | solution.py:210
  155.1 37.4 %collective-permute-start.24 = (bf16[320,1152]{1,0:T(8,128)(2,1)}, bf16[320,1152]{1,0:T(8,128)(2,1)}, u32[]{:S(2)}, u32[]{:S(2)}) collective-permute-start(bf16[320,1152]{1,0:T(8,128)(2,1)} %collective-permute-done.21.refs_5_), channel_id=1, source_target_pairs={{2,0},{4,2},{6,4},{7,6},{5,7},{3,5},{1,3},{0,1},{10,8},{12,10},{14... | collective-permute-start | bytes 2211848 | tf_op jit(solution)/shard_map/ppermute | solution.py:211
  176.7 36.4 %collective-permute-start.22 = (bf16[320,1152]{1,0:T(8,128)(2,1)}, bf16[320,1152]{1,0:T(8,128)(2,1)S(1)}, u32[]{:S(2)}, u32[]{:S(2)}) collective-permute-start(bf16[320,1152]{1,0:T(8,128)(2,1)} %collective-permute-done.19.refs_3_), channel_id=1, source_target_pairs={{0,2},{2,4},{4,6},{6,7},{7,5},{5,3},{3,1},{1,0},{8,10},{10,12},{12... | collective-permute-start | bytes 2211848 | tf_op jit(solution)/shard_map/ppermute | solution.py:210
  178.3 36.4 %collective-permute-start.23 = (bf16[320,1152]{1,0:T(8,128)(2,1)}, bf16[320,1152]{1,0:T(8,128)(2,1)S(1)}, u32[]{:S(2)}, u32[]{:S(2)}) collective-permute-start(bf16[320,1152]{1,0:T(8,128)(2,1)} %collective-permute-done.20.refs_4_), channel_id=1, source_target_pairs={{2,0},{4,2},{6,4},{7,6},{5,7},{3,5},{1,3},{0,1},{10,8},{12,10},{14... | collective-permute-start | bytes 2211848 | tf_op jit(solution)/shard_map/ppermute | solution.py:211
  186.3 31.4 %collective-permute-start.25 = (bf16[320,1152]{1,0:T(8,128)(2,1)}, bf16[320,1152]{1,0:T(8,128)(2,1)S(1)}, u32[]{:S(2)}, u32[]{:S(2)}) collective-permute-start(bf16[320,1152]{1,0:T(8,128)(2,1)} %collective-permute-done.17.refs_32_.refs_6_), channel_id=1, source_target_pairs={{0,2},{2,4},{4,6},{6,7},{7,5},{5,3},{3,1},{1,0},{8,10},{10,12},{12... | collective-permute-start | bytes 2211848 | tf_op jit(solution)/shard_map/ppermute | solution.py:210
  192.5 31.5 %collective-permute-start.28 = (bf16[320,1152]{1,0:T(8,128)(2,1)}, bf16[320,1152]{1,0:T(8,128)(2,1)S(1)}, u32[]{:S(2)}, u32[]{:S(2)}) collective-permute-start(bf16[320,1152]{1,0:T(8,128)(2,1)} %collective-permute-done.24.refs_9_), channel_id=1, source_target_pairs={{2,0},{4,2},{6,4},{7,6},{5,7},{3,5},{1,3},{0,1},{10,8},{12,10},{14... | collective-permute-start | bytes 2211848 | tf_op jit(solution)/shard_map/ppermute | solution.py:211
  213.0 53.0 %collective-permute-start.15 = (bf16[640,1280]{1,0:T(8,128)(2,1)}, bf16[640,1280]{1,0:T(8,128)(2,1)S(1)}, u32[]{:S(2)}, u32[]{:S(2)}) collective-permute-start(bf16[640,1280]{1,0:T(8,128)(2,1)} %get-tuple-element.21), channel_id=1, source_target_pairs={{0,8},{8,0},{16,24},{24,16},{1,9},{9,1},{17,25},{25,17},{2,10},{10... | collective-permute-start | bytes 4915208 | tf_op jit(solution)/shard_map/ppermute | solution.py:237
  213.1 20.4 %collective-permute-start.26 = (bf16[320,1152]{1,0:T(8,128)(2,1)S(1)}, bf16[320,1152]{1,0:T(8,128)(2,1)S(1)}, u32[]{:S(2)}, u32[]{:S(2)}) collective-permute-start(bf16[320,1152]{1,0:T(8,128)(2,1)S(1)} %collective-permute-done.22.refs_7_), channel_id=1, source_target_pairs={{0,2},{2,4},{4,6},{6,7},{7,5},{5,3},{3,1},{1,0},{8,10},{10,12},{12... | collective-permute-start | bytes 2211848 | tf_op jit(solution)/shard_map/ppermute | solution.py:210
  214.7 25.1 %collective-permute-start.27 = (bf16[320,1152]{1,0:T(8,128)(2,1)S(1)}, bf16[320,1152]{1,0:T(8,128)(2,1)S(1)}, u32[]{:S(2)}, u32[]{:S(2)}) collective-permute-start(bf16[320,1152]{1,0:T(8,128)(2,1)S(1)} %collective-permute-done.23.refs_8_), channel_id=1, source_target_pairs={{2,0},{4,2},{6,4},{7,6},{5,7},{3,5},{1,3},{0,1},{10,8},{12,10},{14... | collective-permute-start | bytes 2211848 | tf_op jit(solution)/shard_map/ppermute | solution.py:211
  217.7 30.9 %collective-permute-start.29 = (bf16[320,1152]{1,0:T(8,128)(2,1)S(1)}, bf16[320,1152]{1,0:T(8,128)(2,1)S(1)}, u32[]{:S(2)}, u32[]{:S(2)}) collective-permute-start(bf16[320,1152]{1,0:T(8,128)(2,1)S(1)} %collective-permute-done.25.refs_10_), channel_id=1, source_target_pairs={{0,2},{2,4},{4,6},{6,7},{7,5},{5,3},{3,1},{1,0},{8,10},{10,12},{12... | collective-permute-start | bytes 2211848 | tf_op jit(solution)/shard_map/ppermute | solution.py:213
  224.0 28.9 %collective-permute-start.30 = (bf16[320,1152]{1,0:T(8,128)(2,1)S(1)}, bf16[320,1152]{1,0:T(8,128)(2,1)S(1)}, u32[]{:S(2)}, u32[]{:S(2)}) collective-permute-start(bf16[320,1152]{1,0:T(8,128)(2,1)S(1)} %collective-permute-done.28.refs_13_), channel_id=1, source_target_pairs={{2,0},{4,2},{6,4},{7,6},{5,7},{3,5},{1,3},{0,1},{10,8},{12,10},{14... | collective-permute-start | bytes 2211848 | tf_op jit(solution)/shard_map/ppermute | solution.py:213
  265.9 32.9 %collective-permute-start.31 = (bf16[640,1280]{1,0:T(8,128)(2,1)}, bf16[640,1280]{1,0:T(8,128)(2,1)}, u32[]{:S(2)}, u32[]{:S(2)}) collective-permute-start(bf16[640,1280]{1,0:T(8,128)(2,1)} %get-tuple-element.26), channel_id=1, source_target_pairs={{0,8},{8,0},{16,24},{24,16},{1,9},{9,1},{17,25},{25,17},{2,10},{10... | collective-permute-start | bytes 4915208 | tf_op jit(solution)/shard_map/ppermute | solution.py:237
  266.5 73.8 %collective-permute-start.16 = (f32[640,1280]{1,0:T(8,128)S(1)}, f32[640,1280]{1,0:T(8,128)S(1)}, u32[]{:S(2)}, u32[]{:S(2)}) collective-permute-start(f32[640,1280]{1,0:T(8,128)S(1)} %convert_add_fusion), channel_id=1, source_target_pairs={{0,16},{8,24},{16,0},{24,8},{1,17},{9,25},{17,1},{25,9},{2,18},{10... | collective-permute-start | bytes 9830408 | tf_op jit(solution)/shard_map/ppermute | solution.py:241
  300.9 74.1 %collective-permute-start.32 = (bf16[640,1280]{1,0:T(8,128)(2,1)S(1)}, bf16[640,1280]{1,0:T(8,128)(2,1)S(1)}, u32[]{:S(2)}, u32[]{:S(2)}) collective-permute-start(bf16[640,1280]{1,0:T(8,128)(2,1)S(1)} %add_convert_fusion), channel_id=1, source_target_pairs={{0,16},{8,24},{16,0},{24,8},{1,17},{9,25},{17,1},{25,9},{2,18},{10... | collective-permute-start | bytes 4915208 | tf_op jit(solution)/shard_map/ppermute | solution.py:241
  (32 other events, 1448.7 us)

commit v3 on v2

v3 whole, which is shorter than its diff:
```python
import functools
import math

import jax
import jax.numpy as jnp
import numpy as np
from jax import lax
from jax.experimental import pallas as pl
from jax.experimental.pallas import tpu as pltpu
from jax.sharding import PartitionSpec as P

clip_limit = 0.99
epsilon = 1e-05
SLABS = ("row", "col")
LANES = 128
HINT = pl.CostEstimate(flops=1024, bytes_accessed=1024, transcendentals=0)
ANY = pl.BlockSpec(memory_space=pl.ANY)


def cycle(rows, cols):
    if cols == 1:
        return list(range(rows))
    walk = [(r, 0) for r in range(rows)]
    for i, r in enumerate(reversed(range(rows))):
        back = list(range(1, cols))
        walk += [(r, c) for c in (back if i % 2 == 0 else back[::-1])]
    return [r * cols + c for r, c in walk]


def normalize_kernel(series_ref, first_ref, *refs, begin, lead):
    other_refs, (raw, columns, sems) = refs[:-3], refs[-3:]
    subjects, duration, lanes = raw.shape
    body = duration // LANES * LANES
    tail = duration - body
    rows = first_ref.shape[0]
    width = LANES if lanes % LANES == 0 else lanes
    steps = lanes // width

    def copy(i):
        a, here = i % subjects, pl.ds(i // subjects * width, width)
        there = pl.ds(begin + i // subjects * width, width)
        return pltpu.make_async_copy(series_ref.at[a, :, there], raw.at[a, :, here], sems.at[i])

    for i in range(subjects * steps):
        copy(i).start()
    columns[:, duration + (subjects - 1) * tail :] = jnp.zeros(
        (subjects, LANES - subjects * tail, width), jnp.float32
    )
    for n in range(steps):
        here = pl.ds(n * width, width)
        for a in range(subjects):
            copy(n * subjects + a).wait()
            values = raw[a, :, here]
            center = jnp.mean(values, axis=0, keepdims=True)
            away = values - center
            spread = jnp.mean(away * away, axis=0, keepdims=True)
            normed = away * lax.rsqrt(spread + epsilon)
            columns[a, :duration] = normed
            if a:
                columns[0, duration + (a - 1) * tail : duration + a * tail] = normed[body:]
        kept = min(width, rows - n * width)
        for a, out_ref in enumerate((first_ref, *other_refs)):
            out = columns[a, : out_ref.shape[1]].astype(jnp.bfloat16).T
            out_ref[pl.ds(n * width, kept)] = out[lead : lead + kept]


def normalize(series, begin, end):
    subjects, duration, slab = series.shape
    body = duration // LANES * LANES
    low, high = begin // LANES * LANES, min(-(-end // LANES) * LANES, slab)
    lanes = high - low
    width = LANES if lanes % LANES == 0 else lanes
    widths = [body + LANES] + [body] * (subjects - 1)
    return pl.pallas_call(
        functools.partial(normalize_kernel, begin=low, lead=begin - low),
        in_specs=[pl.BlockSpec(memory_space=pltpu.HBM)],
        out_shape=[jax.ShapeDtypeStruct((end - begin, w), jnp.bfloat16) for w in widths],
        scratch_shapes=[
            pltpu.VMEM((subjects, duration, lanes), jnp.float32),
            pltpu.VMEM((subjects, body + LANES, width), jnp.float32),
            pltpu.SemaphoreType.DMA((subjects * (lanes // width),)),
        ],
        compiler_params=pltpu.CompilerParams(vmem_limit_bytes=48 * 2**20),
        cost_estimate=HINT,
    )(series)


def after(piece, *others):
    def nothing(*refs):
        pass

    return pl.pallas_call(
        nothing,
        in_specs=[ANY] * (1 + len(others)),
        out_specs=ANY,
        out_shape=jax.ShapeDtypeStruct(piece.shape, piece.dtype),
        input_output_aliases={0: 0},
        cost_estimate=HINT,
    )(piece, *others)


def scores_kernel(
    source_ref, block_start_ref, place_ref, *refs, subject, away, cuts, slab, granule, block_rows, chips, duration
):
    count = source_ref.shape[0]
    bodies, tails = refs[: 2 * count], refs[2 * count : 4 * count]
    same_ref, other_ref, ordered, own_rows, products_a, products_b, place_of, sem = refs[-8:]
    body = duration // LANES * LANES
    tail = duration - body
    for a in range(block_start_ref.shape[0]):
        place_of[block_start_ref[a] // block_rows] = a

    for slot in range(count):
        for half in range(2):
            piece = 2 * slot + half
            first = source_ref[slot] * slab + cuts[half]

            def start(g, _, piece=piece, first=first):
                stored = first + g * granule
                block = stored // block_rows
                row = place_of[block] * block_rows + (stored - block * block_rows)
                here = pl.ds(pl.multiple_of(g * granule, granule), granule)
                there = pl.ds(pl.multiple_of(row, granule), granule)
                if subject == 0:
                    pltpu.make_async_copy(tails[piece].at[here], ordered.at[there], sem).start()
                else:
                    pltpu.make_async_copy(bodies[piece].at[here], ordered.at[there, :body], sem).start()
                    pltpu.make_async_copy(tails[piece].at[here, body:], ordered.at[there, body:], sem).start()
                return 0

            lax.fori_loop(0, (cuts[half + 1] - cuts[half]) // granule, start, 0)
    pltpu.make_async_copy(ordered, ordered, sem).wait()

    position, subj = place_ref[0], place_ref[1]
    chip, core = subj // 2, subj % 2
    rows = pl.ds(pl.multiple_of(position * slab, granule), slab)
    own_rows[:, :body] = ordered[rows, :body]
    lane = lax.broadcasted_iota(jnp.int32, (slab, LANES), 1)
    kept = (lane >= subject * tail) & (lane < (subject + 1) * tail)
    own_rows[:, body:] = jnp.where(kept, ordered[rows, body:].astype(jnp.float32), 0.0).astype(jnp.bfloat16)

    limit = clip_limit * duration
    chunk = same_ref.shape[1]
    width = math.gcd(chunk, 256)
    tiles = []
    for flip, out_ref in ((1, other_ref), (0, same_ref)):
        owner = (chip + away) % chips * 2 + (core + flip) % 2
        tiles += [(owner * chunk + k * width, k * width, out_ref) for k in range(chunk // width)]
    buffers = (products_a, products_b)

    def multiply(i):
        columns = ordered[pl.ds(pl.multiple_of(tiles[i][0], width), width)]
        buffers[i % 2][...] = lax.dot_general(
            own_rows[...], columns, (((1,), (1,)), ((), ())), preferred_element_type=jnp.float32
        )

    def score(i):
        products = jnp.clip(buffers[i % 2][...], -limit, limit)
        fisher = 0.5 * (jnp.log(duration + products) - jnp.log(duration - products))
        tiles[i][2][:, pl.ds(tiles[i][1], width)] = fisher.astype(jnp.bfloat16)

    multiply(0)
    for i in range(1, len(tiles)):
        multiply(i)
        score(i - 1)
    score(len(tiles) - 1)


def scores(source, block_start, place, subject, away, bodies, tails, cuts, window, chips, duration, late=()):
    slab = cuts[-1]
    block_rows = window // block_start.shape[0]
    granule = math.gcd(*cuts, block_rows)
    chunk = window // (2 * chips)
    width = math.gcd(chunk, 256)
    padded = tails[0].shape[1]
    out = jax.ShapeDtypeStruct((slab, chunk), jnp.bfloat16)
    smem = pl.BlockSpec(memory_space=pltpu.SMEM)
    return pl.pallas_call(
        functools.partial(
            scores_kernel,
            subject=subject,
            away=away,
            cuts=cuts,
            slab=slab,
            granule=granule,
            block_rows=block_rows,
            chips=chips,
            duration=duration,
        ),
        in_specs=[smem, smem, smem] + [ANY] * (2 * len(tails) + len(late)),
        out_shape=[out, out],
        scratch_shapes=[
            pltpu.VMEM((window, padded), jnp.bfloat16),
            pltpu.VMEM((slab, padded), jnp.bfloat16),
            pltpu.VMEM((slab, width), jnp.float32),
            pltpu.VMEM((slab, width), jnp.float32),
            pltpu.SMEM((block_start.shape[0],), jnp.int32),
            pltpu.SemaphoreType.DMA,
        ],
        compiler_params=pltpu.CompilerParams(vmem_limit_bytes=48 * 2**20),
        cost_estimate=HINT,
    )(source, block_start, place, *bodies, *tails, *late)


def on_device(series, block_start):
    local_subjects, slab, duration = series.shape
    rows, cols = lax.axis_size("row"), lax.axis_size("col")
    count = rows * cols
    window = count * slab
    subjs = lax.axis_size("subj")
    chips = subjs // 2
    half = -(-slab // (2 * LANES)) * LANES if slab % LANES == 0 and slab > LANES else slab // 2
    cuts = (0, half, slab)
    order = cycle(rows, cols)
    onward = [(order[i], order[(i + 1) % count]) for i in range(count)]
    backward = [(b, a) for a, b in onward]
    reach = count // 2
    offsets = [0]
    for d in range(1, reach):
        offsets += [d, -d]
    offsets.append(reach)
    table = np.zeros((count, count), np.int32)
    for i, device in enumerate(order):
        table[device] = [order[(i - d) % count] for d in offsets]
    position = lax.axis_index(SLABS)
    source = jnp.asarray(table)[position]
    place = jnp.stack([position, lax.axis_index("subj")]).astype(jnp.int32)

    def gather(a, gate=None):
        got = [[normed[0][a], normed[1][a]]]
        for d in range(1, reach):
            ahead, behind = got[max(2 * d - 3, 0)], got[max(2 * d - 2, 0)]
            got += [[None, None], [None, None]]
            for half in range(2):
                waits = gate(d, half, got) if gate else ()
                if waits:
                    ahead[half] = after(ahead[half], *waits)
                    if behind is not ahead:
                        behind[half] = after(behind[half], *waits)
                got[-2][half] = lax.ppermute(ahead[half], SLABS, onward)
                got[-1][half] = lax.ppermute(behind[half], SLABS, backward)
        last = [None, None]
        for half in range(2):
            side, way = (-2, onward) if half == a % 2 else (-1, backward)
            last[half] = lax.ppermute(got[side][half], SLABS, way)
        got.append(last)
        return got

    def flat(pairs):
        return [piece for pair in pairs for piece in pair]

    swap = [(s, s ^ 1) for s in range(subjs)]
    columns = jnp.swapaxes(series, 1, 2)
    normed = [normalize(columns, cuts[half], cuts[half + 1]) for half in range(2)]
    everything = [gather(0)]
    terms, sums = [], []
    aways = [*range(1, chips), 0]

    def share(a, d, late=()):
        last = a == local_subjects - 1
        same, other = scores(
            source, block_start, place, a, d, flat(everything[a]), flat(everything[0]), cuts, window, chips, duration, late
        )
        crossed = lax.ppermute(other, "subj", swap)
        part = same.astype(jnp.float32) + crossed.astype(jnp.float32)
        if d:
            part = part.astype(jnp.bfloat16) if last else part
            sums.append(part)
            part = lax.ppermute(part, "subj", [(s, (s + 2 * d) % subjs) for s in range(subjs)])
            part = part.astype(jnp.float32)
        terms.append(part)
        return other

    for a in range(1, local_subjects):

        def gate(d, half, got, a=a, before=everything[-1]):
            if d == 1:
                return [before[-3][half], before[-2][half]]
            if half == 0:
                return sums[-1:] if d == 3 else ()
            if d - 2 < chips:
                return [share(a - 1, aways[d - 2], [got[2 * d - 3][0], got[2 * d - 2][0]])]
            return ()

        everything.append(gather(a, gate))
    for n, d in enumerate(aways):
        share(local_subjects - 1, d, terms[:1] if n == 0 else ())
    return sum(terms[1:], terms[0]) / (local_subjects * subjs)


def solution(mesh):
    return jax.shard_map(
        on_device,
        mesh=mesh,
        in_specs=(P("subj", SLABS, None), P()),
        out_specs=P(SLABS, "subj"),
        check_vma=False,
    )
```

time: 378 us -> 342 us (0.905)
  Pallas kernels: 65.9 us -> 51.6 us
  waiting for transfers between devices: 256 us -> 242 us
  local copies, waits for them, and re-layouts: 14.1 us -> 5.12 us
    pallas_call x4, Pallas kernels: 59.4 us -> 44.9 us  [scores(): pl.pallas_call(functools.partial(scores_kernel, subject=subject, away=awa...]
    ppermute x34, waiting for transfers between devices: 256 us -> 242 us  [the longest x12 122 us: gather(): got[-1][half] = lax.ppermute(behind[half], SLABS, backward)]
    unnamed x61 -> x46, local copies, waits for them, and re-layouts: 13.4 us -> 4.43 us
  transfers between devices with their start and end apart: 34 -> 34, of which waited for: 22 -> 17; matrix products, arithmetic and copies ran while one was open for 1% -> 0% of each run, Pallas kernels for 17% -> 7%
where the time goes in v3:
time: 342 us
  waiting for transfers between devices  242 us (71%)
  Pallas kernels  51.6 us (15%)
  starting transfers between devices  33.4 us (10%)
  other arithmetic  8.81 us (3%)
  local copies, waits for them, and re-layouts  5.12 us (1%)
    ppermute x12, waiting for transfers between devices, gather(): got[-1][half] = lax.ppermute(behind[half], SLABS, backward)  122 us
    ppermute x12, waiting for transfers between devices, gather(): got[-2][half] = lax.ppermute(ahead[half], SLABS, onward)  79.5 us
    pallas_call x4, Pallas kernels, scores(): pl.pallas_call(functools.partial(scores_kernel, subject=subject, away=awa...  44.9 us
    ppermute x2, waiting for transfers between devices, share(): lax.ppermute(part, 'subj', [(s, (s + 2 * d) % subjs) for s in range(subjs)])  35 us
    ppermute x12, starting transfers between devices, gather(): got[-2][half] = lax.ppermute(ahead[half], SLABS, onward)  16 us
    ppermute x12, starting transfers between devices, gather(): got[-1][half] = lax.ppermute(behind[half], SLABS, backward)  10.5 us
  transfers between devices with their start and end apart: 34, of which 17 were waited for; matrix products, arithmetic and copies ran while one was open for 0% of the time, Pallas kernels for 7%

profile of v3, /device:TPU:0, one launch (start us, length us, event | category | flops | bytes accessed | tf_op | source)
XLA Modules:
  0.0 341.6 jit_solution(6896785621004109244)
XLA Ops:
  0.0 3.7 %shard_map.37 = (bf16[384,1280]{1,0:T(8,128)(2,1)S(1)}, bf16[384,1152]{1,0:T(8,128)(2,1)S(1)}) custom-call(f32[2,1200,640]{2,1,0:T(8,128)} %bitcast.5), custom_call_target="tpu_custom_call" | custom-call | flops 1024 | bytes 1024 | tf_op jit(solution)/shard_map/pallas_call | solution.py:74
  4.7 3.0 collective-permute-start
  7.7 21.7 %collective-permute-done.refs_2_.refs_18_ = bf16[384,1280]{1,0:T(8,128)(2,1)S(1)} collective-permute-done((bf16[384,1280]{1,0:T(8,128)(2,1)S(1)}, bf16[384,1280]{1,0:T(8,128)(2,1)S(1)}, u32[]{:S(2)}, u32[]{:S(2)}) %collective-permute-start) | collective-permute-done | bytes 983072 | tf_op jit(solution)/shard_map/ppermute | solution.py:240
  29.4 1.8 collective-permute-start.4
  31.4 3.0 shard_map.38
  35.3 1.6 collective-permute-start.3
  37.3 30.3 %collective-permute-done.3.refs_5_.refs_21_ = bf16[256,1280]{1,0:T(8,128)(2,1)S(1)} collective-permute-done((bf16[256,1280]{1,0:T(8,128)(2,1)S(1)}, bf16[256,1280]{1,0:T(8,128)(2,1)S(1)}, u32[]{:S(2)}, u32[]{:S(2)}) %collective-permute-start.3) | collective-permute-done | bytes 655392 | tf_op jit(solution)/shard_map/ppermute | solution.py:241
  71.7 13.7 %collective-permute-done.7.refs_9_.refs_25_ = bf16[256,1280]{1,0:T(8,128)(2,1)} collective-permute-done((bf16[256,1280]{1,0:T(8,128)(2,1)S(1)}, bf16[256,1280]{1,0:T(8,128)(2,1)}, u32[]{:S(2)}, u32[]{:S(2)}) %collective-permute-start.7) | collective-permute-done | bytes 655392 | tf_op jit(solution)/shard_map/ppermute | solution.py:241
  85.9 7.0 %collective-permute-done.8.refs_1_.refs_10_.refs_26_ = bf16[384,1280]{1,0:T(8,128)(2,1)} collective-permute-done((bf16[384,1280]{1,0:T(8,128)(2,1)S(1)}, bf16[384,1280]{1,0:T(8,128)(2,1)}, u32[]{:S(2)}, u32[]{:S(2)}) %collective-permute-start.8) | collective-permute-done | bytes 983072 | tf_op jit(solution)/shard_map/ppermute | solution.py:240
  94.4 11.9 %collective-permute-done.10.refs_2_.refs_12_.refs_28_ = bf16[384,1280]{1,0:T(8,128)(2,1)S(1)} collective-permute-done((bf16[384,1280]{1,0:T(8,128)(2,1)S(1)}, bf16[384,1280]{1,0:T(8,128)(2,1)S(1)}, u32[]{:S(2)}, u32[]{:S(2)}) %collective-permute-start.10) | collective-permute-done | bytes 983072 | tf_op jit(solution)/shard_map/ppermute | solution.py:241
  107.3 1.6 collective-permute-start.14
  109.4 1.6 collective-permute-start.9
  110.9 9.4 %collective-permute-done.11.refs_13_.refs_29_.refs_2_ = bf16[256,1280]{1,0:T(8,128)(2,1)S(1)} collective-permute-done((bf16[256,1280]{1,0:T(8,128)(2,1)}, bf16[256,1280]{1,0:T(8,128)(2,1)S(1)}, u32[]{:S(2)}, u32[]{:S(2)}) %collective-permute-start.11) | collective-permute-done | bytes 655392 | tf_op jit(solution)/shard_map/ppermute | solution.py:241
  121.7 36.0 %collective-permute-done.9.refs_11_.refs_27_.refs_1_ = bf16[256,1280]{1,0:T(8,128)(2,1)S(1)} collective-permute-done((bf16[256,1280]{1,0:T(8,128)(2,1)}, bf16[256,1280]{1,0:T(8,128)(2,1)S(1)}, u32[]{:S(2)}, u32[]{:S(2)}) %collective-permute-start.9) | collective-permute-done | bytes 655392 | tf_op jit(solution)/shard_map/ppermute | solution.py:240
  157.8 11.2 %shard_map.40 = (bf16[640,1280]{1,0:T(8,128)(2,1)}, bf16[640,1280]{1,0:T(8,128)(2,1)}) custom-call(s32[8]{0:T(128)S(1)} %dynamic-slice_bitcast_fusion.source_ref, s32[5]{0:T(128)S(1)} %copy-done.13, s32[2]{0:T(128)S(1)} %pad_add_fusion.place_ref, bf16[384,1280]{1,0:T(8,128)(2,1)} %copy-done, bf16[256,1280]{1,0:T(8,128)(2,1)S(1)} %get-tuple-element.18.refs_1_.refs_17_, ...), custom_call_target="tpu_custom_call" | custom-call | flops 1024 | bytes 1024 | tf_op jit(solution)/shard_map/pallas_call | solution.py:178
  169.1 3.7 %collective-permute-done.16 = bf16[640,1280]{1,0:T(8,128)(2,1)S(1)} collective-permute-done((bf16[640,1280]{1,0:T(8,128)(2,1)}, bf16[640,1280]{1,0:T(8,128)(2,1)S(1)}, u32[]{:S(2)}, u32[]{:S(2)}) %collective-permute-start.16) | collective-permute-done | bytes 1638432 | tf_op jit(solution)/shard_map/ppermute | solution.py:264
  172.8 3.6 %convert_add_fusion.refs_1_ = f32[640,1280]{1,0:T(8,128)} fusion(bf16[640,1280]{1,0:T(8,128)(2,1)S(1)} %collective-permute-done.16, bf16[640,1280]{1,0:T(8,128)(2,1)} %get-tuple-element.20), kind=kLoop, calls=%fused_computation.2 | loop fusion | flops 2457600 | bytes 6553600 | tf_op jit(solution)/shard_map/add | solution.py:265
  177.4 1.5 collective-permute-start.19
  179.5 1.6 collective-permute-start.18
  181.5 13.9 %collective-permute-done.21.refs_0_ = bf16[256,1152]{1,0:T(8,128)(2,1)S(1)} collective-permute-done((bf16[256,1152]{1,0:T(8,128)(2,1)}, bf16[256,1152]{1,0:T(8,128)(2,1)S(1)}, u32[]{:S(2)}, u32[]{:S(2)}) %collective-permute-start.21) | collective-permute-done | bytes 589856 | tf_op jit(solution)/shard_map/ppermute | solution.py:240
  196.7 3.5 %collective-permute-done.19.refs_0_ = bf16[384,1152]{1,0:T(8,128)(2,1)} collective-permute-done((bf16[384,1152]{1,0:T(8,128)(2,1)}, bf16[384,1152]{1,0:T(8,128)(2,1)}, u32[]{:S(2)}, u32[]{:S(2)}) %collective-permute-start.19) | collective-permute-done | bytes 884768 | tf_op jit(solution)/shard_map/ppermute | solution.py:241
  201.8 11.0 %collective-permute-done.22.refs_0_ = bf16[256,1152]{1,0:T(8,128)(2,1)S(1)} collective-permute-done((bf16[256,1152]{1,0:T(8,128)(2,1)}, bf16[256,1152]{1,0:T(8,128)(2,1)S(1)}, u32[]{:S(2)}, u32[]{:S(2)}) %collective-permute-start.22) | collective-permute-done | bytes 589856 | tf_op jit(solution)/shard_map/ppermute | solution.py:241
  214.5 1.6 collective-permute-start.24
  216.1 11.2 %shard_map.43 = (bf16[640,1280]{1,0:T(8,128)(2,1)}, bf16[640,1280]{1,0:T(8,128)(2,1)}) custom-call(s32[8]{0:T(128)S(1)} %dynamic-slice_bitcast_fusion.source_ref, s32[5]{0:T(128)S(1)} %copy-done.13, s32[2]{0:T(128)S(1)} %pad_add_fusion.place_ref, bf16[384,1280]{1,0:T(8,128)(2,1)} %copy-done, bf16[256,1280]{1,0:T(8,128)(2,1)S(1)} %get-tuple-element.18.refs_1_.refs_17_, ...), custom_call_target="tpu_custom_call" | custom-call | flops 1024 | bytes 1024 | tf_op jit(solution)/shard_map/pallas_call | solution.py:178
  229.3 2.5 collective-permute-done.27.refs_12_
  233.4 11.1 %collective-permute-done.24.refs_0_ = bf16[256,1152]{1,0:T(8,128)(2,1)} collective-permute-done((bf16[256,1152]{1,0:T(8,128)(2,1)}, bf16[256,1152]{1,0:T(8,128)(2,1)}, u32[]{:S(2)}, u32[]{:S(2)}) %collective-permute-start.24) | collective-permute-done | bytes 589856 | tf_op jit(solution)/shard_map/ppermute | solution.py:241
  246.6 28.3 %collective-permute-done.28.refs_13_ = bf16[256,1152]{1,0:T(8,128)(2,1)S(1)} collective-permute-done((bf16[256,1152]{1,0:T(8,128)(2,1)}, bf16[256,1152]{1,0:T(8,128)(2,1)S(1)}, u32[]{:S(2)}, u32[]{:S(2)}) %collective-permute-start.28) | collective-permute-done | bytes 589856 | tf_op jit(solution)/shard_map/ppermute | solution.py:241
  274.9 11.3 %shard_map.49 = (bf16[640,1280]{1,0:T(8,128)(2,1)}, bf16[640,1280]{1,0:T(8,128)(2,1)}) custom-call(s32[8]{0:T(128)S(1)} %dynamic-slice_bitcast_fusion.source_ref, s32[5]{0:T(128)S(1)} %copy-done.13, s32[2]{0:T(128)S(1)} %pad_add_fusion.place_ref, bf16[384,1152]{1,0:T(8,128)(2,1)} %shard_map.39.refs_0_, bf16[256,1152]{1,0:T(8,128)(2,1)S(1)} %copy-done.8, ...), custom_call_target="tpu_custom_call" | custom-call | flops 1024 | bytes 1024 | tf_op jit(solution)/shard_map/pallas_call | solution.py:178
  286.8 11.2 %shard_map.50 = (bf16[640,1280]{1,0:T(8,128)(2,1)}, bf16[640,1280]{1,0:T(8,128)(2,1)}) custom-call(s32[8]{0:T(128)S(1)} %dynamic-slice_bitcast_fusion.source_ref, s32[5]{0:T(128)S(1)} %copy-done.13, s32[2]{0:T(128)S(1)} %pad_add_fusion.place_ref, bf16[384,1152]{1,0:T(8,128)(2,1)} %shard_map.39.refs_0_, bf16[256,1152]{1,0:T(8,128)(2,1)S(1)} %copy-done.8, ...), custom_call_target="tpu_custom_call" | custom-call | flops 1024 | bytes 1024 | tf_op jit(solution)/shard_map/pallas_call | solution.py:178
  299.6 2.2 collective-permute-done.33
  301.8 35.0 %collective-permute-done.32 = bf16[640,1280]{1,0:T(8,128)(2,1)S(1)} collective-permute-done((bf16[640,1280]{1,0:T(8,128)(2,1)S(1)}, bf16[640,1280]{1,0:T(8,128)(2,1)S(1)}, u32[]{:S(2)}, u32[]{:S(2)}) %collective-permute-start.32) | collective-permute-done | bytes 1638432 | tf_op jit(solution)/shard_map/ppermute | solution.py:269
  336.8 4.8 %add_multiply_fusion = f32[640,1280]{1,0:T(8,128)} fusion(bf16[640,1280]{1,0:T(8,128)(2,1)S(1)} %collective-permute-done.33, bf16[640,1280]{1,0:T(8,128)(2,1)S(1)} %copy-done.21, bf16[640,1280]{1,0:T(8,128)(2,1)S(1)} %collective-permute-done.32, f32[640,1280]{1,0:T(8,128)} %collective-permute-done.17.refs_32_, ...), kind=kLoop, calls=%fused_computation | loop fusion | flops 9011200 | bytes 14745600 | tf_op jit(solution)/shard_map/div | solution.py:288
  (101 shorter events, 25.6 us)
Async XLA Ops:
  4.7 24.7 %collective-permute-start = (bf16[384,1280]{1,0:T(8,128)(2,1)S(1)}, bf16[384,1280]{1,0:T(8,128)(2,1)S(1)}, u32[]{:S(2)}, u32[]{:S(2)}) collective-permute-start(bf16[384,1280]{1,0:T(8,128)(2,1)S(1)} %get-tuple-element.17.refs_0_.refs_16_), channel_id=1, source_target_pairs={{0,2},{2,4},{4,6},{6,7},{7,5},{5,3},{3,1},{1,0},{8,10},{10,12},{12... | collective-permute-start | bytes 2949128 | tf_op jit(solution)/shard_map/ppermute | solution.py:240
  7.7 23.5 %collective-permute-start.2 = (bf16[384,1280]{1,0:T(8,128)(2,1)S(1)}, bf16[384,1280]{1,0:T(8,128)(2,1)S(1)}, u32[]{:S(2)}, u32[]{:S(2)}) collective-permute-start(bf16[384,1280]{1,0:T(8,128)(2,1)S(1)} %get-tuple-element.17.refs_0_.refs_16_), channel_id=1, source_target_pairs={{2,0},{4,2},{6,4},{7,6},{5,7},{3,5},{1,3},{0,1},{10,8},{12,10},{14... | collective-permute-start | bytes 2949128 | tf_op jit(solution)/shard_map/ppermute | solution.py:241
  29.4 38.7 %collective-permute-start.4 = (bf16[384,1280]{1,0:T(8,128)(2,1)S(1)}, bf16[384,1280]{1,0:T(8,128)(2,1)S(1)}, u32[]{:S(2)}, u32[]{:S(2)}) collective-permute-start(bf16[384,1280]{1,0:T(8,128)(2,1)S(1)} %collective-permute-done.refs_2_.refs_18_), channel_id=1, source_target_pairs={{0,2},{2,4},{4,6},{6,7},{7,5},{5,3},{3,1},{1,0},{8,10},{10,12},{12... | collective-permute-start | bytes 2949128 | tf_op jit(solution)/shard_map/ppermute | solution.py:240
  31.2 38.4 %collective-permute-start.6 = (bf16[384,1280]{1,0:T(8,128)(2,1)S(1)}, bf16[384,1280]{1,0:T(8,128)(2,1)S(1)}, u32[]{:S(2)}, u32[]{:S(2)}) collective-permute-start(bf16[384,1280]{1,0:T(8,128)(2,1)S(1)} %collective-permute-done.2.refs_4_.refs_20_), channel_id=1, source_target_pairs={{2,0},{4,2},{6,4},{7,6},{5,7},{3,5},{1,3},{0,1},{10,8},{12,10},{14... | collective-permute-start | bytes 2949128 | tf_op jit(solution)/shard_map/ppermute | solution.py:241
  35.3 32.3 %collective-permute-start.3 = (bf16[256,1280]{1,0:T(8,128)(2,1)S(1)}, bf16[256,1280]{1,0:T(8,128)(2,1)S(1)}, u32[]{:S(2)}, u32[]{:S(2)}) collective-permute-start(bf16[256,1280]{1,0:T(8,128)(2,1)S(1)} %get-tuple-element.18.refs_1_.refs_17_), channel_id=1, source_target_pairs={{2,0},{4,2},{6,4},{7,6},{5,7},{3,5},{1,3},{0,1},{10,8},{12,10},{14... | collective-permute-start | bytes 1966088 | tf_op jit(solution)/shard_map/ppermute | solution.py:241
  36.9 33.3 %collective-permute-start.1 = (bf16[256,1280]{1,0:T(8,128)(2,1)S(1)}, bf16[256,1280]{1,0:T(8,128)(2,1)S(1)}, u32[]{:S(2)}, u32[]{:S(2)}) collective-permute-start(bf16[256,1280]{1,0:T(8,128)(2,1)S(1)} %get-tuple-element.18.refs_1_.refs_17_), channel_id=1, source_target_pairs={{0,2},{2,4},{4,6},{6,7},{7,5},{5,3},{3,1},{1,0},{8,10},{10,12},{12... | collective-permute-start | bytes 1966088 | tf_op jit(solution)/shard_map/ppermute | solution.py:240
  67.6 17.8 %collective-permute-start.7 = (bf16[256,1280]{1,0:T(8,128)(2,1)S(1)}, bf16[256,1280]{1,0:T(8,128)(2,1)}, u32[]{:S(2)}, u32[]{:S(2)}) collective-permute-start(bf16[256,1280]{1,0:T(8,128)(2,1)S(1)} %collective-permute-done.3.refs_5_.refs_21_), channel_id=1, source_target_pairs={{2,0},{4,2},{6,4},{7,6},{5,7},{3,5},{1,3},{0,1},{10,8},{12,10},{14... | collective-permute-start | bytes 1966088 | tf_op jit(solution)/shard_map/ppermute | solution.py:241
  68.2 24.8 %collective-permute-start.8 = (bf16[384,1280]{1,0:T(8,128)(2,1)S(1)}, bf16[384,1280]{1,0:T(8,128)(2,1)}, u32[]{:S(2)}, u32[]{:S(2)}) collective-permute-start(bf16[384,1280]{1,0:T(8,128)(2,1)S(1)} %collective-permute-done.4.refs_6_.refs_22_), channel_id=1, source_target_pairs={{0,2},{2,4},{4,6},{6,7},{7,5},{5,3},{3,1},{1,0},{8,10},{10,12},{12... | collective-permute-start | bytes 2949128 | tf_op jit(solution)/shard_map/ppermute | solution.py:240
  69.6 36.7 %collective-permute-start.10 = (bf16[384,1280]{1,0:T(8,128)(2,1)S(1)}, bf16[384,1280]{1,0:T(8,128)(2,1)S(1)}, u32[]{:S(2)}, u32[]{:S(2)}) collective-permute-start(bf16[384,1280]{1,0:T(8,128)(2,1)S(1)} %collective-permute-done.6.refs_8_.refs_24_), channel_id=1, source_target_pairs={{2,0},{4,2},{6,4},{7,6},{5,7},{3,5},{1,3},{0,1},{10,8},{12,10},{14... | collective-permute-start | bytes 2949128 | tf_op jit(solution)/shard_map/ppermute | solution.py:241
  70.2 39.2 %collective-permute-start.5 = (bf16[256,1280]{1,0:T(8,128)(2,1)S(1)}, bf16[256,1280]{1,0:T(8,128)(2,1)}, u32[]{:S(2)}, u32[]{:S(2)}) collective-permute-start(bf16[256,1280]{1,0:T(8,128)(2,1)S(1)} %collective-permute-done.1.refs_3_.refs_19_), channel_id=1, source_target_pairs={{0,2},{2,4},{4,6},{6,7},{7,5},{5,3},{3,1},{1,0},{8,10},{10,12},{12... | collective-permute-start | bytes 1966088 | tf_op jit(solution)/shard_map/ppermute | solution.py:240
  85.4 35.0 %collective-permute-start.11 = (bf16[256,1280]{1,0:T(8,128)(2,1)}, bf16[256,1280]{1,0:T(8,128)(2,1)S(1)}, u32[]{:S(2)}, u32[]{:S(2)}) collective-permute-start(bf16[256,1280]{1,0:T(8,128)(2,1)} %collective-permute-done.7.refs_9_.refs_25_), channel_id=1, source_target_pairs={{2,0},{4,2},{6,4},{7,6},{5,7},{3,5},{1,3},{0,1},{10,8},{12,10},{14... | collective-permute-start | bytes 1966088 | tf_op jit(solution)/shard_map/ppermute | solution.py:241
  93.0 64.8 %collective-permute-start.12 = (bf16[384,1280]{1,0:T(8,128)(2,1)}, bf16[384,1280]{1,0:T(8,128)(2,1)}, u32[]{:S(2)}, u32[]{:S(2)}) collective-permute-start(bf16[384,1280]{1,0:T(8,128)(2,1)} %collective-permute-done.8.refs_1_.refs_10_.refs_26_), channel_id=1, source_target_pairs={{0,2},{2,4},{4,6},{6,7},{7,5},{5,3},{3,1},{1,0},{8,10},{10,12},{12... | collective-permute-start | bytes 2949128 | tf_op jit(solution)/shard_map/ppermute | solution.py:245
  107.3 50.4 %collective-permute-start.14 = (bf16[384,1152]{1,0:T(8,128)(2,1)}, bf16[384,1152]{1,0:T(8,128)(2,1)}, u32[]{:S(2)}, u32[]{:S(2)}) collective-permute-start(bf16[384,1152]{1,0:T(8,128)(2,1)} %shard_map.39.refs_0_), channel_id=1, source_target_pairs={{0,2},{2,4},{4,6},{6,7},{7,5},{5,3},{3,1},{1,0},{8,10},{10,12},{12... | collective-permute-start | bytes 2654216 | tf_op jit(solution)/shard_map/ppermute | solution.py:240
  108.9 48.8 %collective-permute-start.15 = (bf16[384,1152]{1,0:T(8,128)(2,1)}, bf16[384,1152]{1,0:T(8,128)(2,1)}, u32[]{:S(2)}, u32[]{:S(2)}) collective-permute-start(bf16[384,1152]{1,0:T(8,128)(2,1)} %shard_map.39.refs_0_), channel_id=1, source_target_pairs={{2,0},{4,2},{6,4},{7,6},{5,7},{3,5},{1,3},{0,1},{10,8},{12,10},{14... | collective-permute-start | bytes 2654216 | tf_op jit(solution)/shard_map/ppermute | solution.py:241
  109.4 48.4 %collective-permute-start.9 = (bf16[256,1280]{1,0:T(8,128)(2,1)}, bf16[256,1280]{1,0:T(8,128)(2,1)S(1)}, u32[]{:S(2)}, u32[]{:S(2)}) collective-permute-start(bf16[256,1280]{1,0:T(8,128)(2,1)} %collective-permute-done.5.refs_7_.refs_23_), channel_id=1, source_target_pairs={{0,2},{2,4},{4,6},{6,7},{7,5},{5,3},{3,1},{1,0},{8,10},{10,12},{12... | collective-permute-start | bytes 1966088 | tf_op jit(solution)/shard_map/ppermute | solution.py:240
  120.4 37.3 %collective-permute-start.13 = (bf16[256,1280]{1,0:T(8,128)(2,1)S(1)}, bf16[256,1280]{1,0:T(8,128)(2,1)}, u32[]{:S(2)}, u32[]{:S(2)}) collective-permute-start(bf16[256,1280]{1,0:T(8,128)(2,1)S(1)} %collective-permute-done.11.refs_13_.refs_29_.refs_2_), channel_id=1, source_target_pairs={{2,0},{4,2},{6,4},{7,6},{5,7},{3,5},{1,3},{0,1},{10,8},{12,10},{14... | collective-permute-start | bytes 1966088 | tf_op jit(solution)/shard_map/ppermute | solution.py:245
  176.3 98.6 %collective-permute-start.17 = (f32[640,1280]{1,0:T(8,128)}, f32[640,1280]{1,0:T(8,128)}, u32[]{:S(2)}, u32[]{:S(2)}) collective-permute-start(f32[640,1280]{1,0:T(8,128)} %convert_add_fusion.refs_1_), channel_id=1, source_target_pairs={{0,16},{8,24},{16,0},{24,8},{1,17},{9,25},{17,1},{25,9},{2,18},{10... | collective-permute-start | bytes 9830408 | tf_op jit(solution)/shard_map/ppermute | solution.py:269
  177.4 22.9 %collective-permute-start.19 = (bf16[384,1152]{1,0:T(8,128)(2,1)}, bf16[384,1152]{1,0:T(8,128)(2,1)}, u32[]{:S(2)}, u32[]{:S(2)}) collective-permute-start(bf16[384,1152]{1,0:T(8,128)(2,1)} %collective-permute-done.15.refs_33_.refs_4_), channel_id=1, source_target_pairs={{2,0},{4,2},{6,4},{7,6},{5,7},{3,5},{1,3},{0,1},{10,8},{12,10},{14... | collective-permute-start | bytes 2654216 | tf_op jit(solution)/shard_map/ppermute | solution.py:241
  178.9 16.5 %collective-permute-start.21 = (bf16[256,1152]{1,0:T(8,128)(2,1)}, bf16[256,1152]{1,0:T(8,128)(2,1)S(1)}, u32[]{:S(2)}, u32[]{:S(2)}) collective-permute-start(bf16[256,1152]{1,0:T(8,128)(2,1)} %shard_map.44.refs_1_), channel_id=1, source_target_pairs={{0,2},{2,4},{4,6},{6,7},{7,5},{5,3},{3,1},{1,0},{8,10},{10,12},{12... | collective-permute-start | bytes 1769480 | tf_op jit(solution)/shard_map/ppermute | solution.py:240
  179.5 35.0 %collective-permute-start.18 = (bf16[384,1152]{1,0:T(8,128)(2,1)}, bf16[384,1152]{1,0:T(8,128)(2,1)}, u32[]{:S(2)}, u32[]{:S(2)}) collective-permute-start(bf16[384,1152]{1,0:T(8,128)(2,1)} %collective-permute-done.14.refs_32_.refs_2_), channel_id=1, source_target_pairs={{0,2},{2,4},{4,6},{6,7},{7,5},{5,3},{3,1},{1,0},{8,10},{10,12},{12... | collective-permute-start | bytes 2654216 | tf_op jit(solution)/shard_map/ppermute | solution.py:240
  181.0 31.8 %collective-permute-start.22 = (bf16[256,1152]{1,0:T(8,128)(2,1)}, bf16[256,1152]{1,0:T(8,128)(2,1)S(1)}, u32[]{:S(2)}, u32[]{:S(2)}) collective-permute-start(bf16[256,1152]{1,0:T(8,128)(2,1)} %shard_map.44.refs_1_), channel_id=1, source_target_pairs={{2,0},{4,2},{6,4},{7,6},{5,7},{3,5},{1,3},{0,1},{10,8},{12,10},{14... | collective-permute-start | bytes 1769480 | tf_op jit(solution)/shard_map/ppermute | solution.py:241
  196.2 31.0 %collective-permute-start.23 = (bf16[256,1152]{1,0:T(8,128)(2,1)}, bf16[256,1152]{1,0:T(8,128)(2,1)}, u32[]{:S(2)}, u32[]{:S(2)}) collective-permute-start(bf16[256,1152]{1,0:T(8,128)(2,1)} %shard_map.45.refs_3_), channel_id=1, source_target_pairs={{0,2},{2,4},{4,6},{6,7},{7,5},{5,3},{3,1},{1,0},{8,10},{10,12},{12... | collective-permute-start | bytes 1769480 | tf_op jit(solution)/shard_map/ppermute | solution.py:240
  200.3 31.6 %collective-permute-start.27 = (bf16[384,1152]{1,0:T(8,128)(2,1)}, bf16[384,1152]{1,0:T(8,128)(2,1)}, u32[]{:S(2)}, u32[]{:S(2)}) collective-permute-start(bf16[384,1152]{1,0:T(8,128)(2,1)} %shard_map.42.refs_33_.refs_8_), channel_id=1, source_target_pairs={{2,0},{4,2},{6,4},{7,6},{5,7},{3,5},{1,3},{0,1},{10,8},{12,10},{14... | collective-permute-start | bytes 2654216 | tf_op jit(solution)/shard_map/ppermute | solution.py:241
  214.5 30.0 %collective-permute-start.24 = (bf16[256,1152]{1,0:T(8,128)(2,1)}, bf16[256,1152]{1,0:T(8,128)(2,1)}, u32[]{:S(2)}, u32[]{:S(2)}) collective-permute-start(bf16[256,1152]{1,0:T(8,128)(2,1)} %shard_map.46.refs_5_), channel_id=1, source_target_pairs={{2,0},{4,2},{6,4},{7,6},{5,7},{3,5},{1,3},{0,1},{10,8},{12,10},{14... | collective-permute-start | bytes 1769480 | tf_op jit(solution)/shard_map/ppermute | solution.py:241
  227.3 18.7 %collective-permute-start.26 = (bf16[256,1152]{1,0:T(8,128)(2,1)}, bf16[256,1152]{1,0:T(8,128)(2,1)}, u32[]{:S(2)}, u32[]{:S(2)}) collective-permute-start(bf16[256,1152]{1,0:T(8,128)(2,1)} %shard_map.47.refs_7_), channel_id=1, source_target_pairs={{0,2},{2,4},{4,6},{6,7},{7,5},{5,3},{3,1},{1,0},{8,10},{10,12},{12... | collective-permute-start | bytes 1769480 | tf_op jit(solution)/shard_map/ppermute | solution.py:240
  227.8 47.1 %collective-permute-start.25 = (bf16[384,1152]{1,0:T(8,128)(2,1)}, bf16[384,1152]{1,0:T(8,128)(2,1)}, u32[]{:S(2)}, u32[]{:S(2)}) collective-permute-start(bf16[384,1152]{1,0:T(8,128)(2,1)} %shard_map.41.refs_32_.refs_6_), channel_id=1, source_target_pairs={{0,2},{2,4},{4,6},{6,7},{7,5},{5,3},{3,1},{1,0},{8,10},{10,12},{12... | collective-permute-start | bytes 2654216 | tf_op jit(solution)/shard_map/ppermute | solution.py:240
  231.9 43.0 %collective-permute-start.29 = (bf16[384,1152]{1,0:T(8,128)(2,1)}, bf16[384,1152]{1,0:T(8,128)(2,1)}, u32[]{:S(2)}, u32[]{:S(2)}) collective-permute-start(bf16[384,1152]{1,0:T(8,128)(2,1)} %collective-permute-done.27.refs_12_), channel_id=1, source_target_pairs={{2,0},{4,2},{6,4},{7,6},{5,7},{3,5},{1,3},{0,1},{10,8},{12,10},{14... | collective-permute-start | bytes 2654216 | tf_op jit(solution)/shard_map/ppermute | solution.py:245
  244.5 30.4 %collective-permute-start.28 = (bf16[256,1152]{1,0:T(8,128)(2,1)}, bf16[256,1152]{1,0:T(8,128)(2,1)S(1)}, u32[]{:S(2)}, u32[]{:S(2)}) collective-permute-start(bf16[256,1152]{1,0:T(8,128)(2,1)} %shard_map.48.refs_9_), channel_id=1, source_target_pairs={{2,0},{4,2},{6,4},{7,6},{5,7},{3,5},{1,3},{0,1},{10,8},{12,10},{14... | collective-permute-start | bytes 1769480 | tf_op jit(solution)/shard_map/ppermute | solution.py:241
  246.0 28.9 %collective-permute-start.30 = (bf16[256,1152]{1,0:T(8,128)(2,1)}, bf16[256,1152]{1,0:T(8,128)(2,1)S(1)}, u32[]{:S(2)}, u32[]{:S(2)}) collective-permute-start(bf16[256,1152]{1,0:T(8,128)(2,1)} %collective-permute-done.26.refs_11_), channel_id=1, source_target_pairs={{0,2},{2,4},{4,6},{6,7},{7,5},{5,3},{3,1},{1,0},{8,10},{10,12},{12... | collective-permute-start | bytes 1769480 | tf_op jit(solution)/shard_map/ppermute | solution.py:245
  286.2 11.9 %collective-permute-start.31 = (bf16[640,1280]{1,0:T(8,128)(2,1)}, bf16[640,1280]{1,0:T(8,128)(2,1)S(1)}, u32[]{:S(2)}, u32[]{:S(2)}) collective-permute-start(bf16[640,1280]{1,0:T(8,128)(2,1)} %get-tuple-element.26), channel_id=1, source_target_pairs={{0,8},{8,0},{16,24},{24,16},{1,9},{9,1},{17,25},{25,17},{2,10},{10... | collective-permute-start | bytes 4915208 | tf_op jit(solution)/shard_map/ppermute | solution.py:264
  286.3 13.3 %collective-permute-start.20 = (bf16[640,1280]{1,0:T(8,128)(2,1)S(1)}, bf16[640,1280]{1,0:T(8,128)(2,1)S(1)}, u32[]{:S(2)}, u32[]{:S(2)}) collective-permute-start(bf16[640,1280]{1,0:T(8,128)(2,1)S(1)} %copy-done.19), channel_id=1, source_target_pairs={{0,8},{8,0},{16,24},{24,16},{1,9},{9,1},{17,25},{25,17},{2,10},{10... | collective-permute-start | bytes 4915208 | tf_op jit(solution)/shard_map/ppermute | solution.py:264
  298.6 38.2 %collective-permute-start.32 = (bf16[640,1280]{1,0:T(8,128)(2,1)S(1)}, bf16[640,1280]{1,0:T(8,128)(2,1)S(1)}, u32[]{:S(2)}, u32[]{:S(2)}) collective-permute-start(bf16[640,1280]{1,0:T(8,128)(2,1)S(1)} %add_convert_fusion), channel_id=1, source_target_pairs={{0,16},{8,24},{16,0},{24,8},{1,17},{9,25},{17,1},{25,9},{2,18},{10... | collective-permute-start | bytes 4915208 | tf_op jit(solution)/shard_map/ppermute | solution.py:269
  (25 other events, 662.3 us)

commit v4 on v3

--- a/solution.py
+++ b/solution.py
@@ -13,7 +13,7 @@
 epsilon = 1e-05
 SLABS = ("row", "col")
 LANES = 128
-HINT = pl.CostEstimate(flops=1024, bytes_accessed=1024, transcendentals=0)
+AFTER = 36 * 2**20
 ANY = pl.BlockSpec(memory_space=pl.ANY)
 
 
@@ -58,10 +58,10 @@
             columns[a, :duration] = normed
             if a:
                 columns[0, duration + (a - 1) * tail : duration + a * tail] = normed[body:]
-        kept = min(width, rows - n * width)
+        low, high = max(n * width, lead), min((n + 1) * width, lead + rows)
         for a, out_ref in enumerate((first_ref, *other_refs)):
             out = columns[a, : out_ref.shape[1]].astype(jnp.bfloat16).T
-            out_ref[pl.ds(n * width, kept)] = out[lead : lead + kept]
+            out_ref[low - lead : high - lead] = out[low - n * width : high - n * width]
 
 
 def normalize(series, begin, end):
@@ -81,26 +81,49 @@
             pltpu.SemaphoreType.DMA((subjects * (lanes // width),)),
         ],
         compiler_params=pltpu.CompilerParams(vmem_limit_bytes=48 * 2**20),
-        cost_estimate=HINT,
+        cost_estimate=pl.CostEstimate(
+            flops=0, bytes_accessed=6 * subjects * duration * (end - begin), transcendentals=0
+        ),
     )(series)
 
 
-def after(piece, *others):
+def after(pieces, others):
     def nothing(*refs):
         pass
 
     return pl.pallas_call(
         nothing,
-        in_specs=[ANY] * (1 + len(others)),
-        out_specs=ANY,
-        out_shape=jax.ShapeDtypeStruct(piece.shape, piece.dtype),
-        input_output_aliases={0: 0},
-        cost_estimate=HINT,
-    )(piece, *others)
+        in_specs=[ANY] * (len(pieces) + len(others)),
+        out_specs=[ANY] * len(pieces),
+        out_shape=[jax.ShapeDtypeStruct(piece.shape, piece.dtype) for piece in pieces],
+        input_output_aliases={i: i for i in range(len(pieces))},
+        cost_estimate=pl.CostEstimate(flops=0, bytes_accessed=AFTER, transcendentals=0),
+    )(*pieces, *others)
+
+
+def finish_kernel(total_ref, *refs, scale):
+    *last_refs, out_ref = refs
+    first = 0
+    for last_ref in last_refs:
+        here = pl.ds(first, last_ref.shape[1])
+        out_ref[:, here] = (total_ref[:, here] + last_ref[...].astype(jnp.float32)) * scale
+        first += last_ref.shape[1]
+
+
+def finish(total, lasts, scale):
+    slab, chunk = total.shape
+    step = math.gcd(slab, 128)
+    return pl.pallas_call(
+        functools.partial(finish_kernel, scale=scale),
+        grid=(slab // step,),
+        in_specs=[pl.BlockSpec((step, piece.shape[1]), lambda i: (i, 0)) for piece in (total, *lasts)],
+        out_specs=pl.BlockSpec((step, chunk), lambda i: (i, 0)),
+        out_shape=jax.ShapeDtypeStruct(total.shape, jnp.float32),
+    )(total, *lasts)
 
 
 def scores_kernel(
-    source_ref, block_start_ref, place_ref, *refs, subject, away, cuts, slab, granule, block_rows, chips, duration
+    source_ref, block_start_ref, place_ref, *refs, subject, away, part, cuts, slab, granule, block_rows, chips, chunk, duration
 ):
     count = source_ref.shape[0]
     bodies, tails = refs[: 2 * count], refs[2 * count : 4 * count]
@@ -140,12 +163,12 @@
     own_rows[:, body:] = jnp.where(kept, ordered[rows, body:].astype(jnp.float32), 0.0).astype(jnp.bfloat16)
 
     limit = clip_limit * duration
-    chunk = same_ref.shape[1]
     width = math.gcd(chunk, 256)
+    first, columns = part
     tiles = []
     for flip, out_ref in ((1, other_ref), (0, same_ref)):
         owner = (chip + away) % chips * 2 + (core + flip) % 2
-        tiles += [(owner * chunk + k * width, k * width, out_ref) for k in range(chunk // width)]
+        tiles += [(owner * chunk + first + k, k, out_ref) for k in range(0, columns, width)]
     buffers = (products_a, products_b)
 
     def multiply(i):
@@ -166,25 +189,28 @@
     score(len(tiles) - 1)
 
 
-def scores(source, block_start, place, subject, away, bodies, tails, cuts, window, chips, duration, late=()):
+def scores(source, block_start, place, subject, away, part, bodies, tails, cuts, window, chips, duration, late=()):
     slab = cuts[-1]
     block_rows = window // block_start.shape[0]
     granule = math.gcd(*cuts, block_rows)
     chunk = window // (2 * chips)
     width = math.gcd(chunk, 256)
     padded = tails[0].shape[1]
-    out = jax.ShapeDtypeStruct((slab, chunk), jnp.bfloat16)
+    columns = part[1]
+    out = jax.ShapeDtypeStruct((slab, columns), jnp.bfloat16)
     smem = pl.BlockSpec(memory_space=pltpu.SMEM)
     return pl.pallas_call(
         functools.partial(
             scores_kernel,
             subject=subject,
             away=away,
+            part=part,
             cuts=cuts,
             slab=slab,
             granule=granule,
             block_rows=block_rows,
             chips=chips,
+            chunk=chunk,
             duration=duration,
         ),
         in_specs=[smem, smem, smem] + [ANY] * (2 * len(tails) + len(late)),
@@ -198,7 +224,11 @@
             pltpu.SemaphoreType.DMA,
         ],
         compiler_params=pltpu.CompilerParams(vmem_limit_bytes=48 * 2**20),
-        cost_estimate=HINT,
+        cost_estimate=pl.CostEstimate(
+            flops=4 * slab * columns * padded,
+            bytes_accessed=2 * window * padded + 4 * slab * columns,
+            transcendentals=4 * slab * columns,
+        ),
     )(source, block_start, place, *bodies, *tails, *late)
 
 
@@ -209,8 +239,7 @@
     window = count * slab
     subjs = lax.axis_size("subj")
     chips = subjs // 2
-    half = -(-slab // (2 * LANES)) * LANES if slab % LANES == 0 and slab > LANES else slab // 2
-    cuts = (0, half, slab)
+    cuts = (0, slab // 2, slab)
     order = cycle(rows, cols)
     onward = [(order[i], order[(i + 1) % count]) for i in range(count)]
     backward = [(b, a) for a, b in onward]
@@ -233,16 +262,18 @@
             got += [[None, None], [None, None]]
             for half in range(2):
                 waits = gate(d, half, got) if gate else ()
-                if waits:
-                    ahead[half] = after(ahead[half], *waits)
-                    if behind is not ahead:
-                        behind[half] = after(behind[half], *waits)
+                if d > 1:
+                    ahead[half], behind[half] = after([ahead[half], behind[half]], waits)
+                elif waits:
+                    (ahead[half],) = after([ahead[half]], waits)
                 got[-2][half] = lax.ppermute(ahead[half], SLABS, onward)
                 got[-1][half] = lax.ppermute(behind[half], SLABS, backward)
-        last = [None, None]
-        for half in range(2):
-            side, way = (-2, onward) if half == a % 2 else (-1, backward)
-            last[half] = lax.ppermute(got[side][half], SLABS, way)
+        waits = gate(reach, 0, got) if gate else ()
+        last = []
+        for half, side, way in ((0, -2, onward), (1, -1, backward)):
+            if waits:
+                (got[side][half],) = after([got[side][half]], waits)
+            last.append(lax.ppermute(got[side][half], SLABS, way))
         got.append(last)
         return got
 
@@ -253,39 +284,74 @@
     columns = jnp.swapaxes(series, 1, 2)
     normed = [normalize(columns, cuts[half], cuts[half + 1]) for half in range(2)]
     everything = [gather(0)]
-    terms, sums = [], []
+    chunk = window // subjs
+    width = math.gcd(chunk, 256)
+    early = chunk // width // 2 * width
     aways = [*range(1, chips), 0]
 
-    def share(a, d, late=()):
-        last = a == local_subjects - 1
+    def share(a, d, part, late=(), hold=()):
         same, other = scores(
-            source, block_start, place, a, d, flat(everything[a]), flat(everything[0]), cuts, window, chips, duration, late
+            source,
+            block_start,
+            place,
+            a,
+            d,
+            part,
+            flat(everything[a]),
+            flat(everything[0]),
+            cuts,
+            window,
+            chips,
+            duration,
+            late,
         )
+        if hold:
+            (other,) = after([other], hold)
         crossed = lax.ppermute(other, "subj", swap)
-        part = same.astype(jnp.float32) + crossed.astype(jnp.float32)
-        if d:
-            part = part.astype(jnp.bfloat16) if last else part
-            sums.append(part)
-            part = lax.ppermute(part, "subj", [(s, (s + 2 * d) % subjs) for s in range(subjs)])
-            part = part.astype(jnp.float32)
-        terms.append(part)
-        return other
-
+        summed = same.astype(jnp.float32) + crossed.astype(jnp.float32)
+        if not d:
+            return same, summed, d
+        return same, summed.astype(jnp.bfloat16), d
+
+    def send(summed, d):
+        return lax.ppermute(summed, "subj", [(s, (s + 2 * d) % subjs) for s in range(subjs)])
+
+    terms = []
     for a in range(1, local_subjects):
-
-        def gate(d, half, got, a=a, before=everything[-1]):
+        shares = []
+
+        def gate(d, half, got, a=a, before=everything[-1], shares=shares):
             if d == 1:
                 return [before[-3][half], before[-2][half]]
-            if half == 0:
-                return sums[-1:] if d == 3 else ()
-            if d - 2 < chips:
-                return [share(a - 1, aways[d - 2], [got[2 * d - 3][0], got[2 * d - 2][0]])]
-            return ()
+            n = d - 2
+            if half == 0 and n < chips:
+                late = [*got[2 * n - 1], *got[2 * n]] if n else [got[1][0], got[2][0]]
+                hold = () if n else [got[1][1], got[2][1]]
+                shares.append(share(a - 1, aways[n], (0, chunk), late, hold=hold))
+            waits = [shares[n][0]] if n < chips else []
+            if (d, half) == (reach, 0):
+                for _, summed, away in shares[:-1]:
+                    (held,) = after([summed], [*got[3], *got[4]])
+                    terms.append(send(held, away))
+                waits += terms[-len(shares) + 1 :]
+            return waits
 
         everything.append(gather(a, gate))
-    for n, d in enumerate(aways):
-        share(local_subjects - 1, d, terms[:1] if n == 0 else ())
-    return sum(terms[1:], terms[0]) / (local_subjects * subjs)
+        terms.append(shares[-1][1])
+    last = local_subjects - 1
+    received, late = [], ()
+    for d in aways[:-1]:
+        parts = []
+        for part in ((0, early), (early, chunk - early)):
+            _, summed, _ = share(last, d, part, late)
+            parts.append(send(summed, d))
+            late = [summed]
+        received.append(parts)
+    late += [*terms[: chips - 1], received[-1][0]]
+    terms.append(share(last, 0, (0, chunk), late)[1])
+    terms += [jnp.concatenate(parts, axis=1).astype(jnp.float32) for parts in received[:-1]]
+    total = lax.optimization_barrier(sum(term.astype(jnp.float32) for term in terms))
+    return finish(total, received[-1], 1 / (local_subjects * subjs))
 
 
 def solution(mesh):

time: 342 us -> 348 us (1.018)
  waiting for transfers between devices: 242 us -> 215 us
  Pallas kernels: 51.6 us -> 73.4 us
  local copies, waits for them, and re-layouts: 5.12 us -> 12.1 us
    ppermute x12, waiting for transfers between devices: 122 us -> 48.9 us  [gather(): got[-1][half] = lax.ppermute(behind[half], SLABS, backward)]
    ppermute x6 -> x7, waiting for transfers between devices: 35 us -> 60.5 us  [the longest x3 44.9 us: send(): lax.ppermute(summed, 'subj', [(s, (s + 2 * d) % subjs) for s in range(sub...]
    ppermute x12, waiting for transfers between devices: 79.5 us -> 101 us  [gather(): got[-2][half] = lax.ppermute(ahead[half], SLABS, onward)]
    pallas_call x4 -> x5, Pallas kernels: 44.9 us -> 59.4 us  [scores(): pl.pallas_call(functools.partial(scores_kernel, subject=subject, away=awa...]
    ppermute x12, starting transfers between devices: 10.5 us -> 19.6 us  [gather(): got[-1][half] = lax.ppermute(behind[half], SLABS, backward)]
    ppermute x12, starting transfers between devices: 16 us -> 7.38 us  [gather(): got[-2][half] = lax.ppermute(ahead[half], SLABS, onward)]
    unnamed x46 -> x58, local copies, waits for them, and re-layouts: 4.43 us -> 11.4 us
    convert_element_type x1 -> x3, other arithmetic: 0.39 us -> 6.06 us  [share(): return (same, summed.astype(jnp.bfloat16), d)]
  transfers between devices with their start and end apart: 34 -> 36, of which waited for: 17 -> 23; matrix products, arithmetic and copies ran while one was open for 0% -> 2% of each run, Pallas kernels for 7% -> 13%
where the time goes in v4:
time: 348 us
  waiting for transfers between devices  215 us (62%)
  Pallas kernels  73.4 us (21%)
  starting transfers between devices  36.2 us (10%)
  local copies, waits for them, and re-layouts  12.1 us (3%)
  other arithmetic  10.4 us (3%)
    ppermute x12, waiting for transfers between devices, gather(): got[-2][half] = lax.ppermute(ahead[half], SLABS, onward)  101 us
    pallas_call x5, Pallas kernels, scores(): pl.pallas_call(functools.partial(scores_kernel, subject=subject, away=awa...  59.4 us
    ppermute x12, waiting for transfers between devices, gather(): got[-1][half] = lax.ppermute(behind[half], SLABS, backward)  48.9 us
    ppermute x3, waiting for transfers between devices, send(): lax.ppermute(summed, 'subj', [(s, (s + 2 * d) % subjs) for s in range(sub...  44.9 us
    ppermute x12, starting transfers between devices, gather(): got[-1][half] = lax.ppermute(behind[half], SLABS, backward)  19.6 us
    ppermute x4, waiting for transfers between devices, gather(): last.append(lax.ppermute(got[side][half], SLABS, way))  15.5 us
    unnamed x58, local copies, waits for them, and re-layouts  11.4 us
    pallas_call x2, Pallas kernels, normalize(): pl.pallas_call(functools.partial(normalize_kernel, begin=low, lead=begin...  8.29 us
  transfers between devices with their start and end apart: 36, of which 23 were waited for; matrix products, arithmetic and copies ran while one was open for 2% of the time, Pallas kernels for 13%

profile of v4, /device:TPU:0, one launch (start us, length us, event | category | flops | bytes accessed | tf_op | source)
XLA Modules:
  0.0 347.6 jit_solution(3328707364806710140)
XLA Ops:
  0.0 3.7 %shard_map.37 = (bf16[320,1280]{1,0:T(8,128)(2,1)S(1)}, bf16[320,1152]{1,0:T(8,128)(2,1)S(1)}) custom-call(f32[2,1200,640]{2,1,0:T(8,128)} %bitcast.5), custom_call_target="tpu_custom_call" | custom-call | bytes 4608000 | tf_op jit(solution)/shard_map/pallas_call | solution.py:74
  4.7 3.0 collective-permute-start.1
  7.7 4.6 %shard_map.38 = (bf16[320,1280]{1,0:T(8,128)(2,1)}, bf16[320,1152]{1,0:T(8,128)(2,1)S(1)}) custom-call(f32[2,1200,640]{2,1,0:T(8,128)} %bitcast.6), custom_call_target="tpu_custom_call" | custom-call | bytes 4608000 | tf_op jit(solution)/shard_map/pallas_call | solution.py:74
  15.2 11.6 %collective-permute-done.1.refs_1_ = bf16[320,1280]{1,0:T(8,128)(2,1)S(1)} collective-permute-done((bf16[320,1280]{1,0:T(8,128)(2,1)S(1)}, bf16[320,1280]{1,0:T(8,128)(2,1)S(1)}, u32[]{:S(2)}, u32[]{:S(2)}) %collective-permute-start.1) | collective-permute-done | bytes 819232 | tf_op jit(solution)/shard_map/ppermute | solution.py:270
  26.8 2.0 collective-permute-done.refs_0_
  31.7 12.7 %collective-permute-done.3.refs_1_ = bf16[320,1280]{1,0:T(8,128)(2,1)} collective-permute-done((bf16[320,1280]{1,0:T(8,128)(2,1)}, bf16[320,1280]{1,0:T(8,128)(2,1)}, u32[]{:S(2)}, u32[]{:S(2)}) %collective-permute-start.3) | collective-permute-done | bytes 819232 | tf_op jit(solution)/shard_map/ppermute | solution.py:270
  49.3 14.6 %collective-permute-done.4.refs_0_ = bf16[320,1280]{1,0:T(8,128)(2,1)S(1)} collective-permute-done((bf16[320,1280]{1,0:T(8,128)(2,1)}, bf16[320,1280]{1,0:T(8,128)(2,1)S(1)}, u32[]{:S(2)}, u32[]{:S(2)}) %collective-permute-start.4) | collective-permute-done | bytes 819232 | tf_op jit(solution)/shard_map/ppermute | solution.py:269
  65.8 2.0 collective-permute-start.10
  67.8 13.7 %collective-permute-done.6.refs_0_ = bf16[320,1280]{1,0:T(8,128)(2,1)} collective-permute-done((bf16[320,1280]{1,0:T(8,128)(2,1)}, bf16[320,1280]{1,0:T(8,128)(2,1)}, u32[]{:S(2)}, u32[]{:S(2)}) %collective-permute-start.6) | collective-permute-done | bytes 819232 | tf_op jit(solution)/shard_map/ppermute | solution.py:269
  83.6 15.4 %collective-permute-done.8.refs_1_.refs_10_.refs_26_ = bf16[320,1280]{1,0:T(8,128)(2,1)S(1)} collective-permute-done((bf16[320,1280]{1,0:T(8,128)(2,1)}, bf16[320,1280]{1,0:T(8,128)(2,1)S(1)}, u32[]{:S(2)}, u32[]{:S(2)}) %collective-permute-start.8) | collective-permute-done | bytes 819232 | tf_op jit(solution)/shard_map/ppermute | solution.py:269
  101.9 12.7 %collective-permute-done.11.refs_13_.refs_29_.refs_2_ = bf16[320,1280]{1,0:T(8,128)(2,1)} collective-permute-done((bf16[320,1280]{1,0:T(8,128)(2,1)}, bf16[320,1280]{1,0:T(8,128)(2,1)}, u32[]{:S(2)}, u32[]{:S(2)}) %collective-permute-start.11) | collective-permute-done | bytes 819232 | tf_op jit(solution)/shard_map/ppermute | solution.py:270
  116.7 2.0 collective-permute-start.14
  118.7 11.7 %collective-permute-done.15.refs_33_.refs_1_ = bf16[320,1152]{1,0:T(8,128)(2,1)} collective-permute-done((bf16[320,1152]{1,0:T(8,128)(2,1)}, bf16[320,1152]{1,0:T(8,128)(2,1)}, u32[]{:S(2)}, u32[]{:S(2)}) %collective-permute-start.15) | collective-permute-done | bytes 737312 | tf_op jit(solution)/shard_map/ppermute | solution.py:270
  130.4 2.1 collective-permute-start.16
  133.3 20.7 %collective-permute-done.14.refs_32_.refs_0_ = bf16[320,1152]{1,0:T(8,128)(2,1)} collective-permute-done((bf16[320,1152]{1,0:T(8,128)(2,1)}, bf16[320,1152]{1,0:T(8,128)(2,1)}, u32[]{:S(2)}, u32[]{:S(2)}) %collective-permute-start.14) | collective-permute-done | bytes 737312 | tf_op jit(solution)/shard_map/ppermute | solution.py:269
  154.0 15.7 %shard_map.44 = (bf16[640,1280]{1,0:T(8,128)(2,1)}, bf16[640,1280]{1,0:T(8,128)(2,1)}) custom-call(s32[8]{0:T(128)S(1)} %dynamic-slice_bitcast_fusion.source_ref, s32[5]{0:T(128)S(1)} %copy-done.15, s32[2]{0:T(128)S(1)} %pad_add_fusion.place_ref, bf16[320,1280]{1,0:T(8,128)(2,1)S(1)} %get-tuple-element.35.refs_0_.refs_16_, ...), custom_call_target="tpu_custom_call" | custom-call | flops 4194304000 | bytes 16384000 | tf_op jit(solution)/shard_map/pallas_call | solution.py:202
  173.9 13.9 %shard_map.49 = (bf16[640,1280]{1,0:T(8,128)(2,1)}, bf16[640,1280]{1,0:T(8,128)(2,1)}) custom-call(s32[8]{0:T(128)S(1)} %dynamic-slice_bitcast_fusion.source_ref, s32[5]{0:T(128)S(1)} %copy-done.15, s32[2]{0:T(128)S(1)} %pad_add_fusion.place_ref, bf16[320,1280]{1,0:T(8,128)(2,1)S(1)} %get-tuple-element.35.refs_0_.refs_16_, ...), custom_call_target="tpu_custom_call" | custom-call | flops 4194304000 | bytes 16384000 | tf_op jit(solution)/shard_map/pallas_call | solution.py:202
  189.6 15.2 %collective-permute-done.19.refs_0_ = bf16[320,1152]{1,0:T(8,128)(2,1)S(1)} collective-permute-done((bf16[320,1152]{1,0:T(8,128)(2,1)}, bf16[320,1152]{1,0:T(8,128)(2,1)S(1)}, u32[]{:S(2)}, u32[]{:S(2)}) %collective-permute-start.19) | collective-permute-done | bytes 737312 | tf_op jit(solution)/shard_map/ppermute | solution.py:269
  205.6 3.5 add_convert_fusion.refs_0_
  214.7 15.4 %collective-permute-done.25.refs_0_ = bf16[320,1152]{1,0:T(8,128)(2,1)S(1)} collective-permute-done((bf16[320,1152]{1,0:T(8,128)(2,1)S(1)}, bf16[320,1152]{1,0:T(8,128)(2,1)S(1)}, u32[]{:S(2)}, u32[]{:S(2)}) %collective-permute-start.25) | collective-permute-done | bytes 737312 | tf_op jit(solution)/shard_map/ppermute | solution.py:269
  230.0 16.8 %collective-permute-done.23.refs_1_.refs_33_ = bf16[640,1280]{1,0:T(8,128)(2,1)S(1)} collective-permute-done((bf16[640,1280]{1,0:T(8,128)(2,1)}, bf16[640,1280]{1,0:T(8,128)(2,1)S(1)}, u32[]{:S(2)}, u32[]{:S(2)}) %collective-permute-start.23) | collective-permute-done | bytes 1638432 | tf_op jit(solution)/shard_map/ppermute | solution.py:317
  250.0 15.4 %collective-permute-done.29.refs_14_ = bf16[320,1152]{1,0:T(8,128)(2,1)S(1)} collective-permute-done((bf16[320,1152]{1,0:T(8,128)(2,1)}, bf16[320,1152]{1,0:T(8,128)(2,1)S(1)}, u32[]{:S(2)}, u32[]{:S(2)}) %collective-permute-start.29) | collective-permute-done | bytes 737312 | tf_op jit(solution)/shard_map/ppermute | solution.py:276
  267.3 8.0 %shard_map.55 = (bf16[640,512]{1,0:T(8,128)(2,1)S(1)}, bf16[640,512]{1,0:T(8,128)(2,1)S(1)}) custom-call(s32[8]{0:T(128)S(1)} %dynamic-slice_bitcast_fusion.source_ref, s32[5]{0:T(128)S(1)} %copy-done.15, s32[2]{0:T(128)S(1)} %pad_add_fusion.place_ref, bf16[320,1152]{1,0:T(8,128)(2,1)S(1)} %copy-done.13, bf16[320,1152]{1,0:T(8,128)(2,1)S(1)} %copy-done.11, ...), custom_call_target="tpu_custom_call" | custom-call | flops 1677721600 | bytes 14417920 | tf_op jit(solution)/shard_map/pallas_call | solution.py:202
  275.3 2.1 collective-permute-done.31
  277.6 9.8 %shard_map.56 = (bf16[640,768]{1,0:T(8,128)(2,1)}, bf16[640,768]{1,0:T(8,128)(2,1)}) custom-call(s32[8]{0:T(128)S(1)} %dynamic-slice_bitcast_fusion.source_ref, s32[5]{0:T(128)S(1)} %copy-done.15, s32[2]{0:T(128)S(1)} %pad_add_fusion.place_ref, bf16[320,1152]{1,0:T(8,128)(2,1)S(1)} %copy-done.13, bf16[320,1152]{1,0:T(8,128)(2,1)S(1)} %copy-done.11, ...), custom_call_target="tpu_custom_call" | custom-call | flops 2516582400 | bytes 15073280 | tf_op jit(solution)/shard_map/pallas_call | solution.py:202
  290.3 2.4 add_convert_fusion.1.refs_32_
  292.7 12.0 %collective-permute-done.33.refs_34_.refs_0_ = bf16[640,512]{1,0:T(8,128)(2,1)S(1)} collective-permute-done((bf16[640,512]{1,0:T(8,128)(2,1)S(1)}, bf16[640,512]{1,0:T(8,128)(2,1)S(1)}, u32[]{:S(2)}, u32[]{:S(2)}) %collective-permute-start.33) | collective-permute-done | bytes 655392 | tf_op jit(solution)/shard_map/ppermute | solution.py:317
  304.7 12.0 %shard_map.57 = (bf16[640,1280]{1,0:T(8,128)(2,1)}, bf16[640,1280]{1,0:T(8,128)(2,1)}) custom-call(s32[8]{0:T(128)S(1)} %dynamic-slice_bitcast_fusion.source_ref, s32[5]{0:T(128)S(1)} %copy-done.15, s32[2]{0:T(128)S(1)} %pad_add_fusion.place_ref, bf16[320,1152]{1,0:T(8,128)(2,1)S(1)} %copy-done.13, bf16[320,1152]{1,0:T(8,128)(2,1)S(1)} %copy-done.11, ...), custom_call_target="tpu_custom_call" | custom-call | flops 4194304000 | bytes 16384000 | tf_op jit(solution)/shard_map/pallas_call | solution.py:202
  318.4 2.1 collective-permute-done.34
  320.5 4.2 %add_add_fusion.total_ref = f32[640,1280]{1,0:T(8,128)} fusion(bf16[640,1280]{1,0:T(8,128)(2,1)S(1)} %collective-permute-done.34, bf16[640,1280]{1,0:T(8,128)(2,1)} %get-tuple-element.63, bf16[640,1280]{1,0:T(8,128)(2,1)S(1)} %collective-permute-done.24, bf16[640,1280]{1,0:T(8,128)(2,1)S(1)} %copy-done.22, bf16[640,1280]{1,0:T(8,128)(2,1)S(1)} %copy-done.21), kind=kLoop, calls=%fused_computation | loop fusion | flops 7372800 | bytes 11468800 | tf_op jit(solution)/shard_map/add | solution.py:353
  324.7 16.2 %collective-permute-done.35.refs_1_ = bf16[640,768]{1,0:T(8,128)(2,1)S(1)} collective-permute-done((bf16[640,768]{1,0:T(8,128)(2,1)S(1)}, bf16[640,768]{1,0:T(8,128)(2,1)S(1)}, u32[]{:S(2)}, u32[]{:S(2)}) %collective-permute-start.35) | collective-permute-done | bytes 983072 | tf_op jit(solution)/shard_map/ppermute | solution.py:317
  341.9 5.7 %shard_map.58 = f32[640,1280]{1,0:T(8,128)} custom-call(f32[640,1280]{1,0:T(8,128)} %add_add_fusion.total_ref, bf16[640,512]{1,0:T(8,128)(2,1)} %copy-done.14, bf16[640,768]{1,0:T(8,128)(2,1)} %copy-done.27), custom_call_target="tpu_custom_call" | custom-call | tf_op jit(solution)/shard_map/pallas_call | solution.py:116
  (126 shorter events, 44.5 us)
Async XLA Ops:
  4.7 22.1 %collective-permute-start.1 = (bf16[320,1280]{1,0:T(8,128)(2,1)S(1)}, bf16[320,1280]{1,0:T(8,128)(2,1)S(1)}, u32[]{:S(2)}, u32[]{:S(2)}) collective-permute-start(bf16[320,1280]{1,0:T(8,128)(2,1)S(1)} %get-tuple-element.35.refs_0_.refs_16_), channel_id=1, source_target_pairs={{2,0},{4,2},{6,4},{7,6},{5,7},{3,5},{1,3},{0,1},{10,8},{12,10},{14... | collective-permute-start | bytes 2457608 | tf_op jit(solution)/shard_map/ppermute | solution.py:270
  7.6 21.2 %collective-permute-start = (bf16[320,1280]{1,0:T(8,128)(2,1)S(1)}, bf16[320,1280]{1,0:T(8,128)(2,1)S(1)}, u32[]{:S(2)}, u32[]{:S(2)}) collective-permute-start(bf16[320,1280]{1,0:T(8,128)(2,1)S(1)} %get-tuple-element.35.refs_0_.refs_16_), channel_id=1, source_target_pairs={{0,2},{2,4},{4,6},{6,7},{7,5},{5,3},{3,1},{1,0},{8,10},{10,12},{12... | collective-permute-start | bytes 2457608 | tf_op jit(solution)/shard_map/ppermute | solution.py:269
  13.2 31.3 %collective-permute-start.3 = (bf16[320,1280]{1,0:T(8,128)(2,1)}, bf16[320,1280]{1,0:T(8,128)(2,1)}, u32[]{:S(2)}, u32[]{:S(2)}) collective-permute-start(bf16[320,1280]{1,0:T(8,128)(2,1)} %get-tuple-element.36.refs_1_.refs_17_), channel_id=1, source_target_pairs={{2,0},{4,2},{6,4},{7,6},{5,7},{3,5},{1,3},{0,1},{10,8},{12,10},{14... | collective-permute-start | bytes 2457608 | tf_op jit(solution)/shard_map/ppermute | solution.py:270
  15.1 31.2 %collective-permute-start.2 = (bf16[320,1280]{1,0:T(8,128)(2,1)}, bf16[320,1280]{1,0:T(8,128)(2,1)S(1)}, u32[]{:S(2)}, u32[]{:S(2)}) collective-permute-start(bf16[320,1280]{1,0:T(8,128)(2,1)} %get-tuple-element.36.refs_1_.refs_17_), channel_id=1, source_target_pairs={{0,2},{2,4},{4,6},{6,7},{7,5},{5,3},{3,1},{1,0},{8,10},{10,12},{12... | collective-permute-start | bytes 2457608 | tf_op jit(solution)/shard_map/ppermute | solution.py:269
  29.7 34.2 %collective-permute-start.4 = (bf16[320,1280]{1,0:T(8,128)(2,1)}, bf16[320,1280]{1,0:T(8,128)(2,1)S(1)}, u32[]{:S(2)}, u32[]{:S(2)}) collective-permute-start(bf16[320,1280]{1,0:T(8,128)(2,1)} %get-tuple-element.37.refs_2_.refs_18_), channel_id=1, source_target_pairs={{0,2},{2,4},{4,6},{6,7},{7,5},{5,3},{3,1},{1,0},{8,10},{10,12},{12... | collective-permute-start | bytes 2457608 | tf_op jit(solution)/shard_map/ppermute | solution.py:269
  30.6 33.3 %collective-permute-start.5 = (bf16[320,1280]{1,0:T(8,128)(2,1)}, bf16[320,1280]{1,0:T(8,128)(2,1)S(1)}, u32[]{:S(2)}, u32[]{:S(2)}) collective-permute-start(bf16[320,1280]{1,0:T(8,128)(2,1)} %get-tuple-element.39.refs_4_.refs_20_), channel_id=1, source_target_pairs={{2,0},{4,2},{6,4},{7,6},{5,7},{3,5},{1,3},{0,1},{10,8},{12,10},{14... | collective-permute-start | bytes 2457608 | tf_op jit(solution)/shard_map/ppermute | solution.py:270
  47.3 34.3 %collective-permute-start.6 = (bf16[320,1280]{1,0:T(8,128)(2,1)}, bf16[320,1280]{1,0:T(8,128)(2,1)}, u32[]{:S(2)}, u32[]{:S(2)}) collective-permute-start(bf16[320,1280]{1,0:T(8,128)(2,1)} %get-tuple-element.38.refs_3_.refs_19_), channel_id=1, source_target_pairs={{0,2},{2,4},{4,6},{6,7},{7,5},{5,3},{3,1},{1,0},{8,10},{10,12},{12... | collective-permute-start | bytes 2457608 | tf_op jit(solution)/shard_map/ppermute | solution.py:269
  47.4 34.2 %collective-permute-start.7 = (bf16[320,1280]{1,0:T(8,128)(2,1)}, bf16[320,1280]{1,0:T(8,128)(2,1)}, u32[]{:S(2)}, u32[]{:S(2)}) collective-permute-start(bf16[320,1280]{1,0:T(8,128)(2,1)} %get-tuple-element.40.refs_5_.refs_21_), channel_id=1, source_target_pairs={{2,0},{4,2},{6,4},{7,6},{5,7},{3,5},{1,3},{0,1},{10,8},{12,10},{14... | collective-permute-start | bytes 2457608 | tf_op jit(solution)/shard_map/ppermute | solution.py:270
  65.8 33.2 %collective-permute-start.8 = (bf16[320,1280]{1,0:T(8,128)(2,1)}, bf16[320,1280]{1,0:T(8,128)(2,1)S(1)}, u32[]{:S(2)}, u32[]{:S(2)}) collective-permute-start(bf16[320,1280]{1,0:T(8,128)(2,1)} %get-tuple-element.41.refs_6_.refs_22_), channel_id=1, source_target_pairs={{0,2},{2,4},{4,6},{6,7},{7,5},{5,3},{3,1},{1,0},{8,10},{10,12},{12... | collective-permute-start | bytes 2457608 | tf_op jit(solution)/shard_map/ppermute | solution.py:269
  65.8 33.2 %collective-permute-start.10 = (bf16[320,1280]{1,0:T(8,128)(2,1)}, bf16[320,1280]{1,0:T(8,128)(2,1)S(1)}, u32[]{:S(2)}, u32[]{:S(2)}) collective-permute-start(bf16[320,1280]{1,0:T(8,128)(2,1)} %get-tuple-element.43.refs_8_.refs_24_), channel_id=1, source_target_pairs={{2,0},{4,2},{6,4},{7,6},{5,7},{3,5},{1,3},{0,1},{10,8},{12,10},{14... | collective-permute-start | bytes 2457608 | tf_op jit(solution)/shard_map/ppermute | solution.py:270
  81.6 33.1 %collective-permute-start.11 = (bf16[320,1280]{1,0:T(8,128)(2,1)}, bf16[320,1280]{1,0:T(8,128)(2,1)}, u32[]{:S(2)}, u32[]{:S(2)}) collective-permute-start(bf16[320,1280]{1,0:T(8,128)(2,1)} %get-tuple-element.44.refs_9_.refs_25_), channel_id=1, source_target_pairs={{2,0},{4,2},{6,4},{7,6},{5,7},{3,5},{1,3},{0,1},{10,8},{12,10},{14... | collective-permute-start | bytes 2457608 | tf_op jit(solution)/shard_map/ppermute | solution.py:270
  83.1 35.6 %collective-permute-start.9 = (bf16[320,1280]{1,0:T(8,128)(2,1)}, bf16[320,1280]{1,0:T(8,128)(2,1)}, u32[]{:S(2)}, u32[]{:S(2)}) collective-permute-start(bf16[320,1280]{1,0:T(8,128)(2,1)} %get-tuple-element.42.refs_7_.refs_23_), channel_id=1, source_target_pairs={{0,2},{2,4},{4,6},{6,7},{7,5},{5,3},{3,1},{1,0},{8,10},{10,12},{12... | collective-permute-start | bytes 2457608 | tf_op jit(solution)/shard_map/ppermute | solution.py:269
  100.3 30.1 %collective-permute-start.15 = (bf16[320,1152]{1,0:T(8,128)(2,1)}, bf16[320,1152]{1,0:T(8,128)(2,1)}, u32[]{:S(2)}, u32[]{:S(2)}) collective-permute-start(bf16[320,1152]{1,0:T(8,128)(2,1)} %shard_map.43.refs_0_), channel_id=1, source_target_pairs={{2,0},{4,2},{6,4},{7,6},{5,7},{3,5},{1,3},{0,1},{10,8},{12,10},{14... | collective-permute-start | bytes 2211848 | tf_op jit(solution)/shard_map/ppermute | solution.py:270
  114.6 39.3 %collective-permute-start.13 = (bf16[320,1280]{1,0:T(8,128)(2,1)}, bf16[320,1280]{1,0:T(8,128)(2,1)}, u32[]{:S(2)}, u32[]{:S(2)}) collective-permute-start(bf16[320,1280]{1,0:T(8,128)(2,1)} %collective-permute-done.11.refs_13_.refs_29_.refs_2_), channel_id=1, source_target_pairs={{2,0},{4,2},{6,4},{7,6},{5,7},{3,5},{1,3},{0,1},{10,8},{12,10},{14... | collective-permute-start | bytes 2457608 | tf_op jit(solution)/shard_map/ppermute | solution.py:276
  116.6 37.3 %collective-permute-start.12 = (bf16[320,1280]{1,0:T(8,128)(2,1)}, bf16[320,1280]{1,0:T(8,128)(2,1)}, u32[]{:S(2)}, u32[]{:S(2)}) collective-permute-start(bf16[320,1280]{1,0:T(8,128)(2,1)} %copy-done.16), channel_id=1, source_target_pairs={{0,2},{2,4},{4,6},{6,7},{7,5},{5,3},{3,1},{1,0},{8,10},{10,12},{12... | collective-permute-start | bytes 2457608 | tf_op jit(solution)/shard_map/ppermute | solution.py:276
  116.7 37.2 %collective-permute-start.14 = (bf16[320,1152]{1,0:T(8,128)(2,1)}, bf16[320,1152]{1,0:T(8,128)(2,1)}, u32[]{:S(2)}, u32[]{:S(2)}) collective-permute-start(bf16[320,1152]{1,0:T(8,128)(2,1)} %shard_map.43.refs_0_), channel_id=1, source_target_pairs={{0,2},{2,4},{4,6},{6,7},{7,5},{5,3},{3,1},{1,0},{8,10},{10,12},{12... | collective-permute-start | bytes 2211848 | tf_op jit(solution)/shard_map/ppermute | solution.py:269
  118.7 51.0 %collective-permute-start.17 = (bf16[320,1152]{1,0:T(8,128)(2,1)}, bf16[320,1152]{1,0:T(8,128)(2,1)}, u32[]{:S(2)}, u32[]{:S(2)}) collective-permute-start(bf16[320,1152]{1,0:T(8,128)(2,1)} %shard_map.45.refs_1_), channel_id=1, source_target_pairs={{2,0},{4,2},{6,4},{7,6},{5,7},{3,5},{1,3},{0,1},{10,8},{12,10},{14... | collective-permute-start | bytes 2211848 | tf_op jit(solution)/shard_map/ppermute | solution.py:270
  130.4 39.3 %collective-permute-start.16 = (bf16[320,1152]{1,0:T(8,128)(2,1)}, bf16[320,1152]{1,0:T(8,128)(2,1)}, u32[]{:S(2)}, u32[]{:S(2)}) collective-permute-start(bf16[320,1152]{1,0:T(8,128)(2,1)} %shard_map.45.refs_1_), channel_id=1, source_target_pairs={{0,2},{2,4},{4,6},{6,7},{7,5},{5,3},{3,1},{1,0},{8,10},{10,12},{12... | collective-permute-start | bytes 2211848 | tf_op jit(solution)/shard_map/ppermute | solution.py:269
  169.7 35.9 %collective-permute-start.18 = (bf16[640,1280]{1,0:T(8,128)(2,1)}, bf16[640,1280]{1,0:T(8,128)(2,1)}, u32[]{:S(2)}, u32[]{:S(2)}) collective-permute-start(bf16[640,1280]{1,0:T(8,128)(2,1)} %shard_map.46), channel_id=1, source_target_pairs={{0,8},{8,0},{16,24},{24,16},{1,9},{9,1},{17,25},{25,17},{2,10},{10... | collective-permute-start | bytes 4915208 | tf_op jit(solution)/shard_map/ppermute | solution.py:310
  169.8 19.7 %collective-permute-start.21 = (bf16[320,1152]{1,0:T(8,128)(2,1)}, bf16[320,1152]{1,0:T(8,128)(2,1)}, u32[]{:S(2)}, u32[]{:S(2)}) collective-permute-start(bf16[320,1152]{1,0:T(8,128)(2,1)} %get-tuple-element.51.refs_33_.refs_3_), channel_id=1, source_target_pairs={{0,2},{2,4},{4,6},{6,7},{7,5},{5,3},{3,1},{1,0},{8,10},{10,12},{12... | collective-permute-start | bytes 2211848 | tf_op jit(solution)/shard_map/ppermute | solution.py:269
  169.9 19.6 %collective-permute-start.22 = (bf16[320,1152]{1,0:T(8,128)(2,1)}, bf16[320,1152]{1,0:T(8,128)(2,1)}, u32[]{:S(2)}, u32[]{:S(2)}) collective-permute-start(bf16[320,1152]{1,0:T(8,128)(2,1)} %get-tuple-element.52.refs_35_.refs_5_), channel_id=1, source_target_pairs={{2,0},{4,2},{6,4},{7,6},{5,7},{3,5},{1,3},{0,1},{10,8},{12,10},{14... | collective-permute-start | bytes 2211848 | tf_op jit(solution)/shard_map/ppermute | solution.py:270
  171.9 32.8 %collective-permute-start.19 = (bf16[320,1152]{1,0:T(8,128)(2,1)}, bf16[320,1152]{1,0:T(8,128)(2,1)S(1)}, u32[]{:S(2)}, u32[]{:S(2)}) collective-permute-start(bf16[320,1152]{1,0:T(8,128)(2,1)} %get-tuple-element.49.refs_32_.refs_2_), channel_id=1, source_target_pairs={{0,2},{2,4},{4,6},{6,7},{7,5},{5,3},{3,1},{1,0},{8,10},{10,12},{12... | collective-permute-start | bytes 2211848 | tf_op jit(solution)/shard_map/ppermute | solution.py:269
  172.0 32.9 %collective-permute-start.20 = (bf16[320,1152]{1,0:T(8,128)(2,1)}, bf16[320,1152]{1,0:T(8,128)(2,1)}, u32[]{:S(2)}, u32[]{:S(2)}) collective-permute-start(bf16[320,1152]{1,0:T(8,128)(2,1)} %get-tuple-element.50.refs_34_.refs_4_), channel_id=1, source_target_pairs={{2,0},{4,2},{6,4},{7,6},{5,7},{3,5},{1,3},{0,1},{10,8},{12,10},{14... | collective-permute-start | bytes 2211848 | tf_op jit(solution)/shard_map/ppermute | solution.py:270
  209.1 37.7 %collective-permute-start.23 = (bf16[640,1280]{1,0:T(8,128)(2,1)}, bf16[640,1280]{1,0:T(8,128)(2,1)S(1)}, u32[]{:S(2)}, u32[]{:S(2)}) collective-permute-start(bf16[640,1280]{1,0:T(8,128)(2,1)} %shard_map.52), channel_id=1, source_target_pairs={{0,16},{8,24},{16,0},{24,8},{1,17},{9,25},{17,1},{25,9},{2,18},{10... | collective-permute-start | bytes 4915208 | tf_op jit(solution)/shard_map/ppermute | solution.py:317
  210.6 19.4 %collective-permute-start.25 = (bf16[320,1152]{1,0:T(8,128)(2,1)S(1)}, bf16[320,1152]{1,0:T(8,128)(2,1)S(1)}, u32[]{:S(2)}, u32[]{:S(2)}) collective-permute-start(bf16[320,1152]{1,0:T(8,128)(2,1)S(1)} %copy-done.8), channel_id=1, source_target_pairs={{0,2},{2,4},{4,6},{6,7},{7,5},{5,3},{3,1},{1,0},{8,10},{10,12},{12... | collective-permute-start | bytes 2211848 | tf_op jit(solution)/shard_map/ppermute | solution.py:269
  211.6 36.9 %collective-permute-start.28 = (bf16[320,1152]{1,0:T(8,128)(2,1)}, bf16[320,1152]{1,0:T(8,128)(2,1)}, u32[]{:S(2)}, u32[]{:S(2)}) collective-permute-start(bf16[320,1152]{1,0:T(8,128)(2,1)} %get-tuple-element.57.refs_4_.refs_9_), channel_id=1, source_target_pairs={{2,0},{4,2},{6,4},{7,6},{5,7},{3,5},{1,3},{0,1},{10,8},{12,10},{14... | collective-permute-start | bytes 2211848 | tf_op jit(solution)/shard_map/ppermute | solution.py:270
  212.6 37.4 %collective-permute-start.27 = (bf16[320,1152]{1,0:T(8,128)(2,1)}, bf16[320,1152]{1,0:T(8,128)(2,1)}, u32[]{:S(2)}, u32[]{:S(2)}) collective-permute-start(bf16[320,1152]{1,0:T(8,128)(2,1)} %get-tuple-element.56.refs_3_.refs_8_), channel_id=1, source_target_pairs={{2,0},{4,2},{6,4},{7,6},{5,7},{3,5},{1,3},{0,1},{10,8},{12,10},{14... | collective-permute-start | bytes 2211848 | tf_op jit(solution)/shard_map/ppermute | solution.py:270
  214.2 35.8 %collective-permute-start.26 = (bf16[320,1152]{1,0:T(8,128)(2,1)}, bf16[320,1152]{1,0:T(8,128)(2,1)}, u32[]{:S(2)}, u32[]{:S(2)}) collective-permute-start(bf16[320,1152]{1,0:T(8,128)(2,1)} %get-tuple-element.55.refs_2_.refs_7_), channel_id=1, source_target_pairs={{0,2},{2,4},{4,6},{6,7},{7,5},{5,3},{3,1},{1,0},{8,10},{10,12},{12... | collective-permute-start | bytes 2211848 | tf_op jit(solution)/shard_map/ppermute | solution.py:269
  248.0 17.5 %collective-permute-start.29 = (bf16[320,1152]{1,0:T(8,128)(2,1)}, bf16[320,1152]{1,0:T(8,128)(2,1)S(1)}, u32[]{:S(2)}, u32[]{:S(2)}) collective-permute-start(bf16[320,1152]{1,0:T(8,128)(2,1)} %shard_map.53.refs_10_), channel_id=1, source_target_pairs={{0,2},{2,4},{4,6},{6,7},{7,5},{5,3},{3,1},{1,0},{8,10},{10,12},{12... | collective-permute-start | bytes 2211848 | tf_op jit(solution)/shard_map/ppermute | solution.py:276
  287.7 17.0 %collective-permute-start.33 = (bf16[640,512]{1,0:T(8,128)(2,1)S(1)}, bf16[640,512]{1,0:T(8,128)(2,1)S(1)}, u32[]{:S(2)}, u32[]{:S(2)}) collective-permute-start(bf16[640,512]{1,0:T(8,128)(2,1)S(1)} %add_convert_fusion.2.refs_32_), channel_id=1, source_target_pairs={{0,16},{8,24},{16,0},{24,8},{1,17},{9,25},{17,1},{25,9},{2,18},{10... | collective-permute-start | bytes 1966088 | tf_op jit(solution)/shard_map/ppermute | solution.py:317
  289.2 29.2 %collective-permute-start.24 = (bf16[640,1280]{1,0:T(8,128)(2,1)S(1)}, bf16[640,1280]{1,0:T(8,128)(2,1)S(1)}, u32[]{:S(2)}, u32[]{:S(2)}) collective-permute-start(bf16[640,1280]{1,0:T(8,128)(2,1)S(1)} %copy-done.28), channel_id=1, source_target_pairs={{0,8},{8,0},{16,24},{24,16},{1,9},{9,1},{17,25},{25,17},{2,10},{10... | collective-permute-start | bytes 4915208 | tf_op jit(solution)/shard_map/ppermute | solution.py:310
  316.8 24.2 %collective-permute-start.35 = (bf16[640,768]{1,0:T(8,128)(2,1)S(1)}, bf16[640,768]{1,0:T(8,128)(2,1)S(1)}, u32[]{:S(2)}, u32[]{:S(2)}) collective-permute-start(bf16[640,768]{1,0:T(8,128)(2,1)S(1)} %copy-done.26), channel_id=1, source_target_pairs={{0,16},{8,24},{16,0},{24,8},{1,17},{9,25},{17,1},{25,9},{2,18},{10... | collective-permute-start | bytes 2949128 | tf_op jit(solution)/shard_map/ppermute | solution.py:317
  (33 other events, 586.8 us)

commit v5 on v4

--- a/solution.py
+++ b/solution.py
@@ -13,7 +13,9 @@
 epsilon = 1e-05
 SLABS = ("row", "col")
 LANES = 128
-AFTER = 36 * 2**20
+HINT = pl.CostEstimate(flops=0, bytes_accessed=1024, transcendentals=0)
+SHORT = pl.CostEstimate(flops=0, bytes_accessed=2**25, transcendentals=0)
+LONG = pl.CostEstimate(flops=0, bytes_accessed=2**27, transcendentals=0)
 ANY = pl.BlockSpec(memory_space=pl.ANY)
 
 
@@ -81,13 +83,11 @@
             pltpu.SemaphoreType.DMA((subjects * (lanes // width),)),
         ],
         compiler_params=pltpu.CompilerParams(vmem_limit_bytes=48 * 2**20),
-        cost_estimate=pl.CostEstimate(
-            flops=0, bytes_accessed=6 * subjects * duration * (end - begin), transcendentals=0
-        ),
+        cost_estimate=HINT,
     )(series)
 
 
-def after(pieces, others):
+def after(pieces, others, cost=HINT):
     def nothing(*refs):
         pass
 
@@ -97,7 +97,7 @@
         out_specs=[ANY] * len(pieces),
         out_shape=[jax.ShapeDtypeStruct(piece.shape, piece.dtype) for piece in pieces],
         input_output_aliases={i: i for i in range(len(pieces))},
-        cost_estimate=pl.CostEstimate(flops=0, bytes_accessed=AFTER, transcendentals=0),
+        cost_estimate=cost,
     )(*pieces, *others)
 
 
@@ -224,11 +224,7 @@
             pltpu.SemaphoreType.DMA,
         ],
         compiler_params=pltpu.CompilerParams(vmem_limit_bytes=48 * 2**20),
-        cost_estimate=pl.CostEstimate(
-            flops=4 * slab * columns * padded,
-            bytes_accessed=2 * window * padded + 4 * slab * columns,
-            transcendentals=4 * slab * columns,
-        ),
+        cost_estimate=HINT,
     )(source, block_start, place, *bodies, *tails, *late)
 
 
@@ -286,7 +282,7 @@
     everything = [gather(0)]
     chunk = window // subjs
     width = math.gcd(chunk, 256)
-    early = chunk // width // 2 * width
+    early = -(-chunk // width // 2) * width
     aways = [*range(1, chips), 0]
 
     def share(a, d, part, late=(), hold=()):
@@ -311,10 +307,11 @@
         summed = same.astype(jnp.float32) + crossed.astype(jnp.float32)
         if not d:
             return same, summed, d
-        return same, summed.astype(jnp.bfloat16), d
-
-    def send(summed, d):
-        return lax.ppermute(summed, "subj", [(s, (s + 2 * d) % subjs) for s in range(subjs)])
+        return same, summed.astype(jnp.bfloat16) if a == local_subjects - 1 else summed, d
+
+    def send(summed, d, cost):
+        there = lax.ppermute(summed, "subj", [(s, (s + 2 * d) % subjs) for s in range(subjs)])
+        return after([there], (), cost)[0]
 
     terms = []
     for a in range(1, local_subjects):
@@ -325,30 +322,23 @@
                 return [before[-3][half], before[-2][half]]
             n = d - 2
             if half == 0 and n < chips:
-                late = [*got[2 * n - 1], *got[2 * n]] if n else [got[1][0], got[2][0]]
-                hold = () if n else [got[1][1], got[2][1]]
-                shares.append(share(a - 1, aways[n], (0, chunk), late, hold=hold))
-            waits = [shares[n][0]] if n < chips else []
-            if (d, half) == (reach, 0):
-                for _, summed, away in shares[:-1]:
-                    (held,) = after([summed], [*got[3], *got[4]])
-                    terms.append(send(held, away))
-                waits += terms[-len(shares) + 1 :]
-            return waits
+                late = [*got[2 * n - 1], *got[2 * n]] if n else ()
+                hold = () if n else [*got[1], *got[2]]
+                shares.append(share(a - 1, aways[n], (0, chunk), late, hold))
+            return [shares[n][0]] if n < chips else ()
 
         everything.append(gather(a, gate))
-        terms.append(shares[-1][1])
+        terms += [send(summed, d, SHORT) if d else summed for _, summed, d in shares]
     last = local_subjects - 1
-    received, late = [], ()
+    received, late = [], terms[: chips - 1]
     for d in aways[:-1]:
         parts = []
         for part in ((0, early), (early, chunk - early)):
             _, summed, _ = share(last, d, part, late)
-            parts.append(send(summed, d))
+            parts.append(send(summed, d, LONG))
             late = [summed]
         received.append(parts)
-    late += [*terms[: chips - 1], received[-1][0]]
-    terms.append(share(last, 0, (0, chunk), late)[1])
+    terms.append(share(last, 0, (0, chunk), late, received[-1][:1])[1])
     terms += [jnp.concatenate(parts, axis=1).astype(jnp.float32) for parts in received[:-1]]
     total = lax.optimization_barrier(sum(term.astype(jnp.float32) for term in terms))
     return finish(total, received[-1], 1 / (local_subjects * subjs))

time: 348 us -> 329 us (0.945)
  waiting for transfers between devices: 215 us -> 192 us
    ppermute x12, waiting for transfers between devices: 101 us -> 83.7 us  [gather(): got[-2][half] = lax.ppermute(ahead[half], SLABS, onward)]
    ppermute x3, waiting for transfers between devices: 44.9 us -> 31 us  [send(): lax.ppermute(summed, 'subj', [(s, (s + 2 * d) % subjs) for s in range(sub...]
    ppermute x4, waiting for transfers between devices: 15.5 us -> 23 us  [gather(): last.append(lax.ppermute(got[side][half], SLABS, way))]
    convert_element_type x3 -> x2, other arithmetic: 6.06 us -> 1.6 us  [share(): summed.astype(jnp.bfloat16)]
    unnamed x58 -> x62, local copies, waits for them, and re-layouts: 11.4 us -> 13.7 us
  transfers between devices with their start and end apart: 36 -> 36, of which waited for: 23 -> 26; matrix products, arithmetic and copies ran while one was open for 2% -> 0% of each run, Pallas kernels for 13% -> 17%
where the time goes in v5:
time: 329 us; the launch traced here: 328 us
  waiting for transfers between devices  192 us (58%)
  Pallas kernels  74.9 us (23%)
  starting transfers between devices  36.3 us (11%)
  local copies, waits for them, and re-layouts  14.4 us (4%)
  other arithmetic  10.2 us (3%)
    ppermute x12, waiting for transfers between devices, gather(): got[-2][half] = lax.ppermute(ahead[half], SLABS, onward)  83.7 us
    pallas_call x5, Pallas kernels, scores(): pl.pallas_call(functools.partial(scores_kernel, subject=subject, away=awa...  60.9 us
    ppermute x12, waiting for transfers between devices, gather(): got[-1][half] = lax.ppermute(behind[half], SLABS, backward)  46.4 us
    ppermute x3, waiting for transfers between devices, send(): lax.ppermute(summed, 'subj', [(s, (s + 2 * d) % subjs) for s in range(sub...  31 us
    ppermute x4, waiting for transfers between devices, gather(): last.append(lax.ppermute(got[side][half], SLABS, way))  23 us
    ppermute x12, starting transfers between devices, gather(): got[-1][half] = lax.ppermute(behind[half], SLABS, backward)  18.6 us
    unnamed x62, local copies, waits for them, and re-layouts  13.7 us
    ppermute x12, starting transfers between devices, gather(): got[-2][half] = lax.ppermute(ahead[half], SLABS, onward)  9.45 us
  transfers between devices with their start and end apart: 36, of which 26 were waited for; matrix products, arithmetic and copies ran while one was open for 0% of the time, Pallas kernels for 17%

profile of v5, /device:TPU:0, one launch (start us, length us, event | category | flops | bytes accessed | tf_op | source)
XLA Modules:
  0.0 328.3 jit_solution(5393642887680505581)
XLA Ops:
  0.0 3.7 %shard_map.38 = (bf16[320,1280]{1,0:T(8,128)(2,1)S(1)}, bf16[320,1152]{1,0:T(8,128)(2,1)S(1)}) custom-call(f32[2,1200,640]{2,1,0:T(8,128)} %bitcast.5), custom_call_target="tpu_custom_call" | custom-call | bytes 1024 | tf_op jit(solution)/shard_map/pallas_call | solution.py:76
  4.6 3.0 collective-permute-start.3
  7.6 4.5 %shard_map.37 = (bf16[320,1280]{1,0:T(8,128)(2,1)}, bf16[320,1152]{1,0:T(8,128)(2,1)S(1)}) custom-call(f32[2,1200,640]{2,1,0:T(8,128)} %bitcast.6), custom_call_target="tpu_custom_call" | custom-call | bytes 1024 | tf_op jit(solution)/shard_map/pallas_call | solution.py:76
  15.1 11.6 %collective-permute-done.3.refs_1_ = bf16[320,1280]{1,0:T(8,128)(2,1)S(1)} collective-permute-done((bf16[320,1280]{1,0:T(8,128)(2,1)S(1)}, bf16[320,1280]{1,0:T(8,128)(2,1)S(1)}, u32[]{:S(2)}, u32[]{:S(2)}) %collective-permute-start.3) | collective-permute-done | bytes 819232 | tf_op jit(solution)/shard_map/ppermute | solution.py:266
  31.7 12.6 %collective-permute-done.1.refs_1_ = bf16[320,1280]{1,0:T(8,128)(2,1)S(1)} collective-permute-done((bf16[320,1280]{1,0:T(8,128)(2,1)}, bf16[320,1280]{1,0:T(8,128)(2,1)S(1)}, u32[]{:S(2)}, u32[]{:S(2)}) %collective-permute-start.1) | collective-permute-done | bytes 819232 | tf_op jit(solution)/shard_map/ppermute | solution.py:266
  49.3 14.6 %collective-permute-done.6.refs_0_ = bf16[320,1280]{1,0:T(8,128)(2,1)S(1)} collective-permute-done((bf16[320,1280]{1,0:T(8,128)(2,1)}, bf16[320,1280]{1,0:T(8,128)(2,1)S(1)}, u32[]{:S(2)}, u32[]{:S(2)}) %collective-permute-start.6) | collective-permute-done | bytes 819232 | tf_op jit(solution)/shard_map/ppermute | solution.py:265
  67.3 12.7 %collective-permute-done.4.refs_0_ = bf16[320,1280]{1,0:T(8,128)(2,1)S(1)} collective-permute-done((bf16[320,1280]{1,0:T(8,128)(2,1)}, bf16[320,1280]{1,0:T(8,128)(2,1)S(1)}, u32[]{:S(2)}, u32[]{:S(2)}) %collective-permute-start.4) | collective-permute-done | bytes 819232 | tf_op jit(solution)/shard_map/ppermute | solution.py:265
  84.4 12.7 %collective-permute-done.11.refs_13_.refs_29_.refs_2_ = bf16[320,1280]{1,0:T(8,128)(2,1)} collective-permute-done((bf16[320,1280]{1,0:T(8,128)(2,1)}, bf16[320,1280]{1,0:T(8,128)(2,1)}, u32[]{:S(2)}, u32[]{:S(2)}) %collective-permute-start.11) | collective-permute-done | bytes 819232 | tf_op jit(solution)/shard_map/ppermute | solution.py:266
  99.0 4.2 %collective-permute-done.8.refs_10_.refs_26_.refs_1_ = bf16[320,1280]{1,0:T(8,128)(2,1)} collective-permute-done((bf16[320,1280]{1,0:T(8,128)(2,1)}, bf16[320,1280]{1,0:T(8,128)(2,1)}, u32[]{:S(2)}, u32[]{:S(2)}) %collective-permute-start.8) | collective-permute-done | bytes 819232 | tf_op jit(solution)/shard_map/ppermute | solution.py:265
  103.8 16.9 %collective-permute-done.9.refs_11_.refs_27_.refs_1_ = bf16[320,1280]{1,0:T(8,128)(2,1)S(1)} collective-permute-done((bf16[320,1280]{1,0:T(8,128)(2,1)}, bf16[320,1280]{1,0:T(8,128)(2,1)S(1)}, u32[]{:S(2)}, u32[]{:S(2)}) %collective-permute-start.9) | collective-permute-done | bytes 819232 | tf_op jit(solution)/shard_map/ppermute | solution.py:265
  125.3 6.8 %collective-permute-done.13.refs_15_.refs_31_ = bf16[320,1280]{1,0:T(8,128)(2,1)} collective-permute-done((bf16[320,1280]{1,0:T(8,128)(2,1)}, bf16[320,1280]{1,0:T(8,128)(2,1)}, u32[]{:S(2)}, u32[]{:S(2)}) %collective-permute-start.13) | collective-permute-done | bytes 819232 | tf_op jit(solution)/shard_map/ppermute | solution.py:272
  132.1 2.1 collective-permute-start.14
  135.0 3.4 %collective-permute-done.12.refs_14_.refs_30_ = bf16[320,1280]{1,0:T(8,128)(2,1)} collective-permute-done((bf16[320,1280]{1,0:T(8,128)(2,1)}, bf16[320,1280]{1,0:T(8,128)(2,1)}, u32[]{:S(2)}, u32[]{:S(2)}) %collective-permute-start.12) | collective-permute-done | bytes 819232 | tf_op jit(solution)/shard_map/ppermute | solution.py:272
  140.7 17.5 %shard_map.43 = (bf16[640,1280]{1,0:T(8,128)(2,1)}, bf16[640,1280]{1,0:T(8,128)(2,1)}) custom-call(s32[8]{0:T(128)S(1)} %dynamic-slice_bitcast_fusion.source_ref, s32[5]{0:T(128)S(1)} %copy-done.22, s32[2]{0:T(128)S(1)} %pad_add_fusion.place_ref, bf16[320,1280]{1,0:T(8,128)(2,1)} %get-tuple-element.35.refs_0_.refs_16_, bf16[320,1280]{1,0:T(8,128)(2,1)S(1)} %copy-done.11, ...), custom_call_target="tpu_custom_call" | custom-call | bytes 1024 | tf_op jit(solution)/shard_map/pallas_call | solution.py:202
  158.2 4.7 %collective-permute-done.16.refs_3_.refs_1_ = bf16[320,1152]{1,0:T(8,128)(2,1)} collective-permute-done((bf16[320,1152]{1,0:T(8,128)(2,1)}, bf16[320,1152]{1,0:T(8,128)(2,1)}, u32[]{:S(2)}, u32[]{:S(2)}) %collective-permute-start.16) | collective-permute-done | bytes 737312 | tf_op jit(solution)/shard_map/ppermute | solution.py:266
  162.9 4.7 %collective-permute-done.14.refs_1_.refs_0_ = bf16[320,1152]{1,0:T(8,128)(2,1)} collective-permute-done((bf16[320,1152]{1,0:T(8,128)(2,1)}, bf16[320,1152]{1,0:T(8,128)(2,1)}, u32[]{:S(2)}, u32[]{:S(2)}) %collective-permute-start.14) | collective-permute-done | bytes 737312 | tf_op jit(solution)/shard_map/ppermute | solution.py:265
  167.6 3.7 %collective-permute-done.18 = bf16[640,1280]{1,0:T(8,128)(2,1)S(1)} collective-permute-done((bf16[640,1280]{1,0:T(8,128)(2,1)}, bf16[640,1280]{1,0:T(8,128)(2,1)S(1)}, u32[]{:S(2)}, u32[]{:S(2)}) %collective-permute-start.18) | collective-permute-done | bytes 1638432 | tf_op jit(solution)/shard_map/ppermute | solution.py:306
  171.3 2.1 convert_add_fusion
  179.0 13.9 %shard_map.50 = (bf16[640,1280]{1,0:T(8,128)(2,1)}, bf16[640,1280]{1,0:T(8,128)(2,1)}) custom-call(s32[8]{0:T(128)S(1)} %dynamic-slice_bitcast_fusion.source_ref, s32[5]{0:T(128)S(1)} %copy-done.22, s32[2]{0:T(128)S(1)} %pad_add_fusion.place_ref, bf16[320,1280]{1,0:T(8,128)(2,1)} %get-tuple-element.35.refs_0_.refs_16_, bf16[320,1280]{1,0:T(8,128)(2,1)S(1)} %copy-done.12, ...), custom_call_target="tpu_custom_call" | custom-call | bytes 1024 | tf_op jit(solution)/shard_map/pallas_call | solution.py:202
  196.7 13.6 %collective-permute-done.23.refs_0_ = bf16[320,1152]{1,0:T(8,128)(2,1)S(1)} collective-permute-done((bf16[320,1152]{1,0:T(8,128)(2,1)}, bf16[320,1152]{1,0:T(8,128)(2,1)S(1)}, u32[]{:S(2)}, u32[]{:S(2)}) %collective-permute-start.23) | collective-permute-done | bytes 737312 | tf_op jit(solution)/shard_map/ppermute | solution.py:265
  214.8 11.4 %collective-permute-done.25.refs_10_ = bf16[320,1152]{1,0:T(8,128)(2,1)} collective-permute-done((bf16[320,1152]{1,0:T(8,128)(2,1)}, bf16[320,1152]{1,0:T(8,128)(2,1)}, u32[]{:S(2)}, u32[]{:S(2)}) %collective-permute-start.25) | collective-permute-done | bytes 737312 | tf_op jit(solution)/shard_map/ppermute | solution.py:265
  226.7 4.2 %collective-permute-done.28.refs_13_ = bf16[320,1152]{1,0:T(8,128)(2,1)} collective-permute-done((bf16[320,1152]{1,0:T(8,128)(2,1)}, bf16[320,1152]{1,0:T(8,128)(2,1)}, u32[]{:S(2)}, u32[]{:S(2)}) %collective-permute-start.28) | collective-permute-done | bytes 737312 | tf_op jit(solution)/shard_map/ppermute | solution.py:266
  232.5 14.2 %collective-permute-done.19.refs_0_ = f32[640,1280]{1,0:T(8,128)} collective-permute-done((f32[640,1280]{1,0:T(8,128)}, f32[640,1280]{1,0:T(8,128)}, u32[]{:S(2)}, u32[]{:S(2)}) %collective-permute-start.19) | collective-permute-done | bytes 3276832 | tf_op jit(solution)/shard_map/ppermute | solution.py:313
  246.7 10.0 %collective-permute-done.29.refs_14_ = bf16[320,1152]{1,0:T(8,128)(2,1)} collective-permute-done((bf16[320,1152]{1,0:T(8,128)(2,1)}, bf16[320,1152]{1,0:T(8,128)(2,1)}, u32[]{:S(2)}, u32[]{:S(2)}) %collective-permute-start.29) | collective-permute-done | bytes 737312 | tf_op jit(solution)/shard_map/ppermute | solution.py:272
  256.7 2.8 collective-permute-done.30.refs_15_
  259.5 9.5 %shard_map.53 = (bf16[640,768]{1,0:T(8,128)(2,1)}, bf16[640,768]{1,0:T(8,128)(2,1)}) custom-call(s32[8]{0:T(128)S(1)} %dynamic-slice_bitcast_fusion.source_ref, s32[5]{0:T(128)S(1)} %copy-done.22, s32[2]{0:T(128)S(1)} %pad_add_fusion.place_ref, bf16[320,1152]{1,0:T(8,128)(2,1)S(1)} %copy-done.14, bf16[320,1152]{1,0:T(8,128)(2,1)S(1)} %copy-done.16, ...), custom_call_target="tpu_custom_call" | custom-call | bytes 1024 | tf_op jit(solution)/shard_map/pallas_call | solution.py:202
  269.1 2.8 collective-permute-done.31
  274.3 7.9 %shard_map.54 = (bf16[640,512]{1,0:T(8,128)(2,1)S(1)}, bf16[640,512]{1,0:T(8,128)(2,1)S(1)}) custom-call(s32[8]{0:T(128)S(1)} %dynamic-slice_bitcast_fusion.source_ref, s32[5]{0:T(128)S(1)} %copy-done.22, s32[2]{0:T(128)S(1)} %pad_add_fusion.place_ref, bf16[320,1152]{1,0:T(8,128)(2,1)S(1)} %copy-done.14, bf16[320,1152]{1,0:T(8,128)(2,1)S(1)} %copy-done.16, ...), custom_call_target="tpu_custom_call" | custom-call | bytes 1024 | tf_op jit(solution)/shard_map/pallas_call | solution.py:202
  284.6 12.0 %shard_map.55 = (bf16[640,1280]{1,0:T(8,128)(2,1)}, bf16[640,1280]{1,0:T(8,128)(2,1)}) custom-call(s32[8]{0:T(128)S(1)} %dynamic-slice_bitcast_fusion.source_ref, s32[5]{0:T(128)S(1)} %copy-done.22, s32[2]{0:T(128)S(1)} %pad_add_fusion.place_ref, bf16[320,1152]{1,0:T(8,128)(2,1)S(1)} %copy-done.14, bf16[320,1152]{1,0:T(8,128)(2,1)S(1)} %copy-done.16, ...), custom_call_target="tpu_custom_call" | custom-call | bytes 1024 | tf_op jit(solution)/shard_map/pallas_call | solution.py:202
  299.1 16.3 %collective-permute-done.35.refs_0_ = bf16[640,512]{1,0:T(8,128)(2,1)S(1)} collective-permute-done((bf16[640,512]{1,0:T(8,128)(2,1)S(1)}, bf16[640,512]{1,0:T(8,128)(2,1)S(1)}, u32[]{:S(2)}, u32[]{:S(2)}) %collective-permute-start.35) | collective-permute-done | bytes 655392 | tf_op jit(solution)/shard_map/ppermute | solution.py:313
  316.2 6.4 %add_add_fusion.total_ref = f32[640,1280]{1,0:T(8,128)} fusion(bf16[640,1280]{1,0:T(8,128)(2,1)} %collective-permute-done.34, bf16[640,1280]{1,0:T(8,128)(2,1)} %get-tuple-element.63, f32[640,1280]{1,0:T(8,128)} %shard_map.47.refs_32_, bf16[640,1280]{1,0:T(8,128)(2,1)} %collective-permute-done.20, bf16[640,1280]{1,0:T(8,128)(2,1)} %get-tuple-element.53.refs_2_), kind=kLoop, calls=%fused_computation | loop fusion | flops 6553600 | bytes 13107200 | tf_op jit(solution)/shard_map/add | solution.py:343
  322.6 5.7 %shard_map.59 = f32[640,1280]{1,0:T(8,128)} custom-call(f32[640,1280]{1,0:T(8,128)} %add_add_fusion.total_ref, bf16[640,768]{1,0:T(8,128)(2,1)} %shard_map.56.refs_1_.refs_0_, bf16[640,512]{1,0:T(8,128)(2,1)} %shard_map.58.refs_1_), custom_call_target="tpu_custom_call" | custom-call | tf_op jit(solution)/shard_map/pallas_call | solution.py:116
  (131 shorter events, 56.0 us)
Async XLA Ops:
  4.6 22.1 %collective-permute-start.3 = (bf16[320,1280]{1,0:T(8,128)(2,1)S(1)}, bf16[320,1280]{1,0:T(8,128)(2,1)S(1)}, u32[]{:S(2)}, u32[]{:S(2)}) collective-permute-start(bf16[320,1280]{1,0:T(8,128)(2,1)S(1)} %get-tuple-element.36.refs_1_.refs_17_), channel_id=1, source_target_pairs={{2,0},{4,2},{6,4},{7,6},{5,7},{3,5},{1,3},{0,1},{10,8},{12,10},{14... | collective-permute-start | bytes 2457608 | tf_op jit(solution)/shard_map/ppermute | solution.py:266
  7.6 21.2 %collective-permute-start.2 = (bf16[320,1280]{1,0:T(8,128)(2,1)S(1)}, bf16[320,1280]{1,0:T(8,128)(2,1)S(1)}, u32[]{:S(2)}, u32[]{:S(2)}) collective-permute-start(bf16[320,1280]{1,0:T(8,128)(2,1)S(1)} %get-tuple-element.36.refs_1_.refs_17_), channel_id=1, source_target_pairs={{0,2},{2,4},{4,6},{6,7},{7,5},{5,3},{3,1},{1,0},{8,10},{10,12},{12... | collective-permute-start | bytes 2457608 | tf_op jit(solution)/shard_map/ppermute | solution.py:265
  13.1 31.2 %collective-permute-start.1 = (bf16[320,1280]{1,0:T(8,128)(2,1)}, bf16[320,1280]{1,0:T(8,128)(2,1)S(1)}, u32[]{:S(2)}, u32[]{:S(2)}) collective-permute-start(bf16[320,1280]{1,0:T(8,128)(2,1)} %get-tuple-element.35.refs_0_.refs_16_), channel_id=1, source_target_pairs={{2,0},{4,2},{6,4},{7,6},{5,7},{3,5},{1,3},{0,1},{10,8},{12,10},{14... | collective-permute-start | bytes 2457608 | tf_op jit(solution)/shard_map/ppermute | solution.py:266
  15.0 31.3 %collective-permute-start = (bf16[320,1280]{1,0:T(8,128)(2,1)}, bf16[320,1280]{1,0:T(8,128)(2,1)S(1)}, u32[]{:S(2)}, u32[]{:S(2)}) collective-permute-start(bf16[320,1280]{1,0:T(8,128)(2,1)} %get-tuple-element.35.refs_0_.refs_16_), channel_id=1, source_target_pairs={{0,2},{2,4},{4,6},{6,7},{7,5},{5,3},{3,1},{1,0},{8,10},{10,12},{12... | collective-permute-start | bytes 2457608 | tf_op jit(solution)/shard_map/ppermute | solution.py:265
  29.6 34.2 %collective-permute-start.6 = (bf16[320,1280]{1,0:T(8,128)(2,1)}, bf16[320,1280]{1,0:T(8,128)(2,1)S(1)}, u32[]{:S(2)}, u32[]{:S(2)}) collective-permute-start(bf16[320,1280]{1,0:T(8,128)(2,1)} %get-tuple-element.38.refs_3_.refs_19_), channel_id=1, source_target_pairs={{0,2},{2,4},{4,6},{6,7},{7,5},{5,3},{3,1},{1,0},{8,10},{10,12},{12... | collective-permute-start | bytes 2457608 | tf_op jit(solution)/shard_map/ppermute | solution.py:265
  30.6 33.3 %collective-permute-start.7 = (bf16[320,1280]{1,0:T(8,128)(2,1)}, bf16[320,1280]{1,0:T(8,128)(2,1)S(1)}, u32[]{:S(2)}, u32[]{:S(2)}) collective-permute-start(bf16[320,1280]{1,0:T(8,128)(2,1)} %get-tuple-element.40.refs_5_.refs_21_), channel_id=1, source_target_pairs={{2,0},{4,2},{6,4},{7,6},{5,7},{3,5},{1,3},{0,1},{10,8},{12,10},{14... | collective-permute-start | bytes 2457608 | tf_op jit(solution)/shard_map/ppermute | solution.py:266
  47.2 32.7 %collective-permute-start.4 = (bf16[320,1280]{1,0:T(8,128)(2,1)}, bf16[320,1280]{1,0:T(8,128)(2,1)S(1)}, u32[]{:S(2)}, u32[]{:S(2)}) collective-permute-start(bf16[320,1280]{1,0:T(8,128)(2,1)} %get-tuple-element.37.refs_2_.refs_18_), channel_id=1, source_target_pairs={{0,2},{2,4},{4,6},{6,7},{7,5},{5,3},{3,1},{1,0},{8,10},{10,12},{12... | collective-permute-start | bytes 2457608 | tf_op jit(solution)/shard_map/ppermute | solution.py:265
  48.1 31.8 %collective-permute-start.5 = (bf16[320,1280]{1,0:T(8,128)(2,1)}, bf16[320,1280]{1,0:T(8,128)(2,1)S(1)}, u32[]{:S(2)}, u32[]{:S(2)}) collective-permute-start(bf16[320,1280]{1,0:T(8,128)(2,1)} %get-tuple-element.39.refs_4_.refs_20_), channel_id=1, source_target_pairs={{2,0},{4,2},{6,4},{7,6},{5,7},{3,5},{1,3},{0,1},{10,8},{12,10},{14... | collective-permute-start | bytes 2457608 | tf_op jit(solution)/shard_map/ppermute | solution.py:266
  65.7 31.4 %collective-permute-start.11 = (bf16[320,1280]{1,0:T(8,128)(2,1)}, bf16[320,1280]{1,0:T(8,128)(2,1)}, u32[]{:S(2)}, u32[]{:S(2)}) collective-permute-start(bf16[320,1280]{1,0:T(8,128)(2,1)} %get-tuple-element.44.refs_9_.refs_25_), channel_id=1, source_target_pairs={{2,0},{4,2},{6,4},{7,6},{5,7},{3,5},{1,3},{0,1},{10,8},{12,10},{14... | collective-permute-start | bytes 2457608 | tf_op jit(solution)/shard_map/ppermute | solution.py:266
  81.8 21.5 %collective-permute-start.8 = (bf16[320,1280]{1,0:T(8,128)(2,1)}, bf16[320,1280]{1,0:T(8,128)(2,1)}, u32[]{:S(2)}, u32[]{:S(2)}) collective-permute-start(bf16[320,1280]{1,0:T(8,128)(2,1)} %get-tuple-element.41.refs_6_.refs_22_), channel_id=1, source_target_pairs={{0,2},{2,4},{4,6},{6,7},{7,5},{5,3},{3,1},{1,0},{8,10},{10,12},{12... | collective-permute-start | bytes 2457608 | tf_op jit(solution)/shard_map/ppermute | solution.py:265
  82.3 38.4 %collective-permute-start.9 = (bf16[320,1280]{1,0:T(8,128)(2,1)}, bf16[320,1280]{1,0:T(8,128)(2,1)S(1)}, u32[]{:S(2)}, u32[]{:S(2)}) collective-permute-start(bf16[320,1280]{1,0:T(8,128)(2,1)} %get-tuple-element.42.refs_7_.refs_23_), channel_id=1, source_target_pairs={{0,2},{2,4},{4,6},{6,7},{7,5},{5,3},{3,1},{1,0},{8,10},{10,12},{12... | collective-permute-start | bytes 2457608 | tf_op jit(solution)/shard_map/ppermute | solution.py:265
  83.9 39.8 %collective-permute-start.10 = (bf16[320,1280]{1,0:T(8,128)(2,1)}, bf16[320,1280]{1,0:T(8,128)(2,1)}, u32[]{:S(2)}, u32[]{:S(2)}) collective-permute-start(bf16[320,1280]{1,0:T(8,128)(2,1)} %get-tuple-element.43.refs_8_.refs_24_), channel_id=1, source_target_pairs={{2,0},{4,2},{6,4},{7,6},{5,7},{3,5},{1,3},{0,1},{10,8},{12,10},{14... | collective-permute-start | bytes 2457608 | tf_op jit(solution)/shard_map/ppermute | solution.py:266
  97.0 35.1 %collective-permute-start.13 = (bf16[320,1280]{1,0:T(8,128)(2,1)}, bf16[320,1280]{1,0:T(8,128)(2,1)}, u32[]{:S(2)}, u32[]{:S(2)}) collective-permute-start(bf16[320,1280]{1,0:T(8,128)(2,1)} %collective-permute-done.11.refs_13_.refs_29_.refs_2_), channel_id=1, source_target_pairs={{2,0},{4,2},{6,4},{7,6},{5,7},{3,5},{1,3},{0,1},{10,8},{12,10},{14... | collective-permute-start | bytes 2457608 | tf_op jit(solution)/shard_map/ppermute | solution.py:272
  103.3 35.1 %collective-permute-start.12 = (bf16[320,1280]{1,0:T(8,128)(2,1)}, bf16[320,1280]{1,0:T(8,128)(2,1)}, u32[]{:S(2)}, u32[]{:S(2)}) collective-permute-start(bf16[320,1280]{1,0:T(8,128)(2,1)} %collective-permute-done.8.refs_10_.refs_26_.refs_1_), channel_id=1, source_target_pairs={{0,2},{2,4},{4,6},{6,7},{7,5},{5,3},{3,1},{1,0},{8,10},{10,12},{12... | collective-permute-start | bytes 2457608 | tf_op jit(solution)/shard_map/ppermute | solution.py:272
  121.6 36.5 %collective-permute-start.17 = (bf16[320,1152]{1,0:T(8,128)(2,1)}, bf16[320,1152]{1,0:T(8,128)(2,1)}, u32[]{:S(2)}, u32[]{:S(2)}) collective-permute-start(bf16[320,1152]{1,0:T(8,128)(2,1)} %shard_map.45.refs_1_), channel_id=1, source_target_pairs={{2,0},{4,2},{6,4},{7,6},{5,7},{3,5},{1,3},{0,1},{10,8},{12,10},{14... | collective-permute-start | bytes 2211848 | tf_op jit(solution)/shard_map/ppermute | solution.py:266
  123.3 34.9 %collective-permute-start.15 = (bf16[320,1152]{1,0:T(8,128)(2,1)}, bf16[320,1152]{1,0:T(8,128)(2,1)}, u32[]{:S(2)}, u32[]{:S(2)}) collective-permute-start(bf16[320,1152]{1,0:T(8,128)(2,1)} %shard_map.45.refs_1_), channel_id=1, source_target_pairs={{0,2},{2,4},{4,6},{6,7},{7,5},{5,3},{3,1},{1,0},{8,10},{10,12},{12... | collective-permute-start | bytes 2211848 | tf_op jit(solution)/shard_map/ppermute | solution.py:265
  123.7 39.2 %collective-permute-start.16 = (bf16[320,1152]{1,0:T(8,128)(2,1)}, bf16[320,1152]{1,0:T(8,128)(2,1)}, u32[]{:S(2)}, u32[]{:S(2)}) collective-permute-start(bf16[320,1152]{1,0:T(8,128)(2,1)} %shard_map.44.refs_0_), channel_id=1, source_target_pairs={{2,0},{4,2},{6,4},{7,6},{5,7},{3,5},{1,3},{0,1},{10,8},{12,10},{14... | collective-permute-start | bytes 2211848 | tf_op jit(solution)/shard_map/ppermute | solution.py:266
  132.1 35.4 %collective-permute-start.14 = (bf16[320,1152]{1,0:T(8,128)(2,1)}, bf16[320,1152]{1,0:T(8,128)(2,1)}, u32[]{:S(2)}, u32[]{:S(2)}) collective-permute-start(bf16[320,1152]{1,0:T(8,128)(2,1)} %shard_map.44.refs_0_), channel_id=1, source_target_pairs={{0,2},{2,4},{4,6},{6,7},{7,5},{5,3},{3,1},{1,0},{8,10},{10,12},{12... | collective-permute-start | bytes 2211848 | tf_op jit(solution)/shard_map/ppermute | solution.py:265
  173.4 73.3 %collective-permute-start.19 = (f32[640,1280]{1,0:T(8,128)}, f32[640,1280]{1,0:T(8,128)}, u32[]{:S(2)}, u32[]{:S(2)}) collective-permute-start(f32[640,1280]{1,0:T(8,128)} %convert_add_fusion), channel_id=1, source_target_pairs={{0,16},{8,24},{16,0},{24,8},{1,17},{9,25},{17,1},{25,9},{2,18},{10... | collective-permute-start | bytes 9830408 | tf_op jit(solution)/shard_map/ppermute | solution.py:313
  174.9 19.6 %collective-permute-start.21 = (bf16[320,1152]{1,0:T(8,128)(2,1)}, bf16[320,1152]{1,0:T(8,128)(2,1)S(1)}, u32[]{:S(2)}, u32[]{:S(2)}) collective-permute-start(bf16[320,1152]{1,0:T(8,128)(2,1)} %get-tuple-element.49.refs_32_.refs_2_), channel_id=1, source_target_pairs={{0,2},{2,4},{4,6},{6,7},{7,5},{5,3},{3,1},{1,0},{8,10},{10,12},{12... | collective-permute-start | bytes 2211848 | tf_op jit(solution)/shard_map/ppermute | solution.py:265
  175.4 19.7 %collective-permute-start.22 = (bf16[320,1152]{1,0:T(8,128)(2,1)}, bf16[320,1152]{1,0:T(8,128)(2,1)}, u32[]{:S(2)}, u32[]{:S(2)}) collective-permute-start(bf16[320,1152]{1,0:T(8,128)(2,1)} %get-tuple-element.51.refs_34_.refs_4_), channel_id=1, source_target_pairs={{2,0},{4,2},{6,4},{7,6},{5,7},{3,5},{1,3},{0,1},{10,8},{12,10},{14... | collective-permute-start | bytes 2211848 | tf_op jit(solution)/shard_map/ppermute | solution.py:266
  177.0 33.4 %collective-permute-start.23 = (bf16[320,1152]{1,0:T(8,128)(2,1)}, bf16[320,1152]{1,0:T(8,128)(2,1)S(1)}, u32[]{:S(2)}, u32[]{:S(2)}) collective-permute-start(bf16[320,1152]{1,0:T(8,128)(2,1)} %get-tuple-element.50.refs_33_.refs_3_), channel_id=1, source_target_pairs={{0,2},{2,4},{4,6},{6,7},{7,5},{5,3},{3,1},{1,0},{8,10},{10,12},{12... | collective-permute-start | bytes 2211848 | tf_op jit(solution)/shard_map/ppermute | solution.py:265
  177.5 32.9 %collective-permute-start.24 = (bf16[320,1152]{1,0:T(8,128)(2,1)}, bf16[320,1152]{1,0:T(8,128)(2,1)}, u32[]{:S(2)}, u32[]{:S(2)}) collective-permute-start(bf16[320,1152]{1,0:T(8,128)(2,1)} %get-tuple-element.52.refs_35_.refs_5_), channel_id=1, source_target_pairs={{2,0},{4,2},{6,4},{7,6},{5,7},{3,5},{1,3},{0,1},{10,8},{12,10},{14... | collective-permute-start | bytes 2211848 | tf_op jit(solution)/shard_map/ppermute | solution.py:266
  195.4 30.8 %collective-permute-start.25 = (bf16[320,1152]{1,0:T(8,128)(2,1)}, bf16[320,1152]{1,0:T(8,128)(2,1)}, u32[]{:S(2)}, u32[]{:S(2)}) collective-permute-start(bf16[320,1152]{1,0:T(8,128)(2,1)} %get-tuple-element.55.refs_6_), channel_id=1, source_target_pairs={{0,2},{2,4},{4,6},{6,7},{7,5},{5,3},{3,1},{1,0},{8,10},{10,12},{12... | collective-permute-start | bytes 2211848 | tf_op jit(solution)/shard_map/ppermute | solution.py:265
  211.2 19.7 %collective-permute-start.28 = (bf16[320,1152]{1,0:T(8,128)(2,1)}, bf16[320,1152]{1,0:T(8,128)(2,1)}, u32[]{:S(2)}, u32[]{:S(2)}) collective-permute-start(bf16[320,1152]{1,0:T(8,128)(2,1)} %get-tuple-element.58.refs_9_), channel_id=1, source_target_pairs={{2,0},{4,2},{6,4},{7,6},{5,7},{3,5},{1,3},{0,1},{10,8},{12,10},{14... | collective-permute-start | bytes 2211848 | tf_op jit(solution)/shard_map/ppermute | solution.py:266
  212.8 34.0 %collective-permute-start.27 = (bf16[320,1152]{1,0:T(8,128)(2,1)}, bf16[320,1152]{1,0:T(8,128)(2,1)}, u32[]{:S(2)}, u32[]{:S(2)}) collective-permute-start(bf16[320,1152]{1,0:T(8,128)(2,1)} %get-tuple-element.57.refs_8_), channel_id=1, source_target_pairs={{2,0},{4,2},{6,4},{7,6},{5,7},{3,5},{1,3},{0,1},{10,8},{12,10},{14... | collective-permute-start | bytes 2211848 | tf_op jit(solution)/shard_map/ppermute | solution.py:266
  214.3 32.4 %collective-permute-start.26 = (bf16[320,1152]{1,0:T(8,128)(2,1)}, bf16[320,1152]{1,0:T(8,128)(2,1)}, u32[]{:S(2)}, u32[]{:S(2)}) collective-permute-start(bf16[320,1152]{1,0:T(8,128)(2,1)} %get-tuple-element.56.refs_7_), channel_id=1, source_target_pairs={{0,2},{2,4},{4,6},{6,7},{7,5},{5,3},{3,1},{1,0},{8,10},{10,12},{12... | collective-permute-start | bytes 2211848 | tf_op jit(solution)/shard_map/ppermute | solution.py:265
  226.2 30.5 %collective-permute-start.29 = (bf16[320,1152]{1,0:T(8,128)(2,1)}, bf16[320,1152]{1,0:T(8,128)(2,1)}, u32[]{:S(2)}, u32[]{:S(2)}) collective-permute-start(bf16[320,1152]{1,0:T(8,128)(2,1)} %collective-permute-done.25.refs_10_), channel_id=1, source_target_pairs={{0,2},{2,4},{4,6},{6,7},{7,5},{5,3},{3,1},{1,0},{8,10},{10,12},{12... | collective-permute-start | bytes 2211848 | tf_op jit(solution)/shard_map/ppermute | solution.py:272
  230.9 28.5 %collective-permute-start.30 = (bf16[320,1152]{1,0:T(8,128)(2,1)}, bf16[320,1152]{1,0:T(8,128)(2,1)}, u32[]{:S(2)}, u32[]{:S(2)}) collective-permute-start(bf16[320,1152]{1,0:T(8,128)(2,1)} %collective-permute-done.28.refs_13_), channel_id=1, source_target_pairs={{2,0},{4,2},{6,4},{7,6},{5,7},{3,5},{1,3},{0,1},{10,8},{12,10},{14... | collective-permute-start | bytes 2211848 | tf_op jit(solution)/shard_map/ppermute | solution.py:272
  273.3 23.9 %collective-permute-start.33 = (bf16[640,768]{1,0:T(8,128)(2,1)S(1)}, bf16[640,768]{1,0:T(8,128)(2,1)S(1)}, u32[]{:S(2)}, u32[]{:S(2)}) collective-permute-start(bf16[640,768]{1,0:T(8,128)(2,1)S(1)} %add_convert_fusion.refs_32_), channel_id=1, source_target_pairs={{0,16},{8,24},{16,0},{24,8},{1,17},{9,25},{17,1},{25,9},{2,18},{10... | collective-permute-start | bytes 2949128 | tf_op jit(solution)/shard_map/ppermute | solution.py:313
  282.4 33.8 %collective-permute-start.20 = (bf16[640,1280]{1,0:T(8,128)(2,1)}, bf16[640,1280]{1,0:T(8,128)(2,1)}, u32[]{:S(2)}, u32[]{:S(2)}) collective-permute-start(bf16[640,1280]{1,0:T(8,128)(2,1)} %get-tuple-element.54), channel_id=1, source_target_pairs={{0,8},{8,0},{16,24},{24,16},{1,9},{9,1},{17,25},{25,17},{2,10},{10... | collective-permute-start | bytes 4915208 | tf_op jit(solution)/shard_map/ppermute | solution.py:306
  298.2 18.0 %collective-permute-start.34 = (bf16[640,1280]{1,0:T(8,128)(2,1)}, bf16[640,1280]{1,0:T(8,128)(2,1)}, u32[]{:S(2)}, u32[]{:S(2)}) collective-permute-start(bf16[640,1280]{1,0:T(8,128)(2,1)} %shard_map.57), channel_id=1, source_target_pairs={{0,8},{8,0},{16,24},{24,16},{1,9},{9,1},{17,25},{25,17},{2,10},{10... | collective-permute-start | bytes 4915208 | tf_op jit(solution)/shard_map/ppermute | solution.py:306
  (35 other events, 326.9 us)

commit v6 on v5

--- a/solution.py
+++ b/solution.py
@@ -14,7 +14,7 @@
 SLABS = ("row", "col")
 LANES = 128
 HINT = pl.CostEstimate(flops=0, bytes_accessed=1024, transcendentals=0)
-SHORT = pl.CostEstimate(flops=0, bytes_accessed=2**25, transcendentals=0)
+SHORT = pl.CostEstimate(flops=0, bytes_accessed=1024, transcendentals=0)
 LONG = pl.CostEstimate(flops=0, bytes_accessed=2**27, transcendentals=0)
 ANY = pl.BlockSpec(memory_space=pl.ANY)
 
@@ -101,25 +101,50 @@
     )(*pieces, *others)
 
 
-def finish_kernel(total_ref, *refs, scale):
-    *last_refs, out_ref = refs
-    first = 0
-    for last_ref in last_refs:
-        here = pl.ds(first, last_ref.shape[1])
-        out_ref[:, here] = (total_ref[:, here] + last_ref[...].astype(jnp.float32)) * scale
-        first += last_ref.shape[1]
-
-
-def finish(total, lasts, scale):
-    slab, chunk = total.shape
-    step = math.gcd(slab, 128)
+def combine_kernel(*refs, starts, scale):
+    *in_refs, out_ref = refs
+    total = jnp.zeros(out_ref.shape, jnp.float32)
+    for ref, start in zip(in_refs, starts):
+        if start is None:
+            total = total + ref[...].astype(jnp.float32)
+    out_ref[...] = total * scale
+    for ref, start in zip(in_refs, starts):
+        if start is not None:
+            here = pl.ds(start, ref.shape[1])
+            out_ref[:, here] = out_ref[:, here] + ref[...].astype(jnp.float32) * scale
+
+
+def combine(terms, starts, slab, columns, scale):
+    step = max(d for d in range(16, 161, 16) if slab % d == 0)
+    return pl.pallas_call(
+        functools.partial(combine_kernel, starts=starts, scale=scale),
+        grid=(slab // step,),
+        in_specs=[pl.BlockSpec((step, term.shape[1]), lambda i: (i, 0)) for term in terms],
+        out_specs=pl.BlockSpec((step, columns), lambda i: (i, 0)),
+        out_shape=jax.ShapeDtypeStruct((slab, columns), jnp.float32),
+        compiler_params=pltpu.CompilerParams(vmem_limit_bytes=48 * 2**20),
+        cost_estimate=HINT,
+    )(*terms)
+
+
+def finish_kernel(part_ref, before_ref, out_ref, *, scale):
+    out_ref[...] = before_ref[...] + part_ref[...].astype(jnp.float32) * scale
+
+
+def finish(part, before, first, scale):
+    slab = before.shape[0]
+    width = math.gcd(part.shape[1], first)
+    block = (slab // 2 if slab % 32 == 0 else slab, width)
+    there = pl.BlockSpec(block, lambda i, j: (i, first // width + j))
     return pl.pallas_call(
         functools.partial(finish_kernel, scale=scale),
-        grid=(slab // step,),
-        in_specs=[pl.BlockSpec((step, piece.shape[1]), lambda i: (i, 0)) for piece in (total, *lasts)],
-        out_specs=pl.BlockSpec((step, chunk), lambda i: (i, 0)),
-        out_shape=jax.ShapeDtypeStruct(total.shape, jnp.float32),
-    )(total, *lasts)
+        grid=(slab // block[0], part.shape[1] // width),
+        in_specs=[pl.BlockSpec(block, lambda i, j: (i, j)), there],
+        out_specs=there,
+        out_shape=jax.ShapeDtypeStruct(before.shape, jnp.float32),
+        input_output_aliases={1: 0},
+        cost_estimate=HINT,
+    )(part, before)
 
 
 def scores_kernel(
@@ -127,54 +152,71 @@
 ):
     count = source_ref.shape[0]
     bodies, tails = refs[: 2 * count], refs[2 * count : 4 * count]
-    same_ref, other_ref, ordered, own_rows, products_a, products_b, place_of, sem = refs[-8:]
+    same_ref, other_ref, own_rows, other_columns, same_columns, products_a, products_b, place_of, sems = refs[-9:]
     body = duration // LANES * LANES
     tail = duration - body
     for a in range(block_start_ref.shape[0]):
         place_of[block_start_ref[a] // block_rows] = a
 
+    position, subj = place_ref[0], place_ref[1]
+    chip, core = subj // 2, subj % 2
+    first, columns = part
+    wanted = [(position * slab, own_rows)]
+    for flip, columns_ref in ((1, other_columns), (0, same_columns)):
+        owner = (chip + away) % chips * 2 + (core + flip) % 2
+        wanted.append((owner * chunk + first, columns_ref))
+
     for slot in range(count):
         for half in range(2):
             piece = 2 * slot + half
-            first = source_ref[slot] * slab + cuts[half]
-
-            def start(g, _, piece=piece, first=first):
-                stored = first + g * granule
+            low = source_ref[slot] * slab + cuts[half]
+
+            def start(g, _, piece=piece, low=low):
+                stored = low + g * granule
                 block = stored // block_rows
                 row = place_of[block] * block_rows + (stored - block * block_rows)
                 here = pl.ds(pl.multiple_of(g * granule, granule), granule)
-                there = pl.ds(pl.multiple_of(row, granule), granule)
-                if subject == 0:
-                    pltpu.make_async_copy(tails[piece].at[here], ordered.at[there], sem).start()
-                else:
-                    pltpu.make_async_copy(bodies[piece].at[here], ordered.at[there, :body], sem).start()
-                    pltpu.make_async_copy(tails[piece].at[here, body:], ordered.at[there, body:], sem).start()
+                for n, (begin, to_ref) in enumerate(wanted):
+
+                    @pl.when((row >= begin) & (row < begin + to_ref.shape[0]))
+                    def _():
+                        there = pl.ds(pl.multiple_of(row - begin, granule), granule)
+                        if subject == 0:
+                            pltpu.make_async_copy(tails[piece].at[here], to_ref.at[there], sems.at[n]).start()
+                        else:
+                            pltpu.make_async_copy(
+                                bodies[piece].at[here], to_ref.at[there, :body], sems.at[n]
+                            ).start()
+                            pltpu.make_async_copy(
+                                tails[piece].at[here, body:], to_ref.at[there, body:], sems.at[n]
+                            ).start()
+
                 return 0
 
             lax.fori_loop(0, (cuts[half + 1] - cuts[half]) // granule, start, 0)
-    pltpu.make_async_copy(ordered, ordered, sem).wait()
-
-    position, subj = place_ref[0], place_ref[1]
-    chip, core = subj // 2, subj % 2
-    rows = pl.ds(pl.multiple_of(position * slab, granule), slab)
-    own_rows[:, :body] = ordered[rows, :body]
+
+    def arrived(n):
+        to_ref = wanted[n][1]
+        pltpu.make_async_copy(to_ref, to_ref, sems.at[n]).wait()
+
+    arrived(0)
     lane = lax.broadcasted_iota(jnp.int32, (slab, LANES), 1)
     kept = (lane >= subject * tail) & (lane < (subject + 1) * tail)
-    own_rows[:, body:] = jnp.where(kept, ordered[rows, body:].astype(jnp.float32), 0.0).astype(jnp.bfloat16)
+    own_rows[:, body:] = jnp.where(kept, own_rows[:, body:].astype(jnp.float32), 0.0).astype(jnp.bfloat16)
 
     limit = clip_limit * duration
-    width = math.gcd(chunk, 256)
-    first, columns = part
+    width = math.gcd(columns, 256)
     tiles = []
-    for flip, out_ref in ((1, other_ref), (0, same_ref)):
-        owner = (chip + away) % chips * 2 + (core + flip) % 2
-        tiles += [(owner * chunk + first + k, k, out_ref) for k in range(0, columns, width)]
+    for n, out_ref in ((1, other_ref), (2, same_ref)):
+        tiles += [(n, k, out_ref) for k in range(0, columns, width)]
     buffers = (products_a, products_b)
 
     def multiply(i):
-        columns = ordered[pl.ds(pl.multiple_of(tiles[i][0], width), width)]
+        n, k, _ = tiles[i]
+        if k == 0:
+            arrived(n)
         buffers[i % 2][...] = lax.dot_general(
-            own_rows[...], columns, (((1,), (1,)), ((), ())), preferred_element_type=jnp.float32
+            own_rows[...], wanted[n][1][pl.ds(k, width)], (((1,), (1,)), ((), ())), preferred_element_type=jnp.float32
         )
 
     def score(i):
@@ -192,11 +234,11 @@
 def scores(source, block_start, place, subject, away, part, bodies, tails, cuts, window, chips, duration, late=()):
     slab = cuts[-1]
     block_rows = window // block_start.shape[0]
-    granule = math.gcd(*cuts, block_rows)
+    granule = math.gcd(*cuts, *part, block_rows)
     chunk = window // (2 * chips)
-    width = math.gcd(chunk, 256)
     padded = tails[0].shape[1]
     columns = part[1]
+    width = math.gcd(columns, 256)
     out = jax.ShapeDtypeStruct((slab, columns), jnp.bfloat16)
     smem = pl.BlockSpec(memory_space=pltpu.SMEM)
     return pl.pallas_call(
@@ -216,12 +258,13 @@
         in_specs=[smem, smem, smem] + [ANY] * (2 * len(tails) + len(late)),
         out_shape=[out, out],
         scratch_shapes=[
-            pltpu.VMEM((window, padded), jnp.bfloat16),
             pltpu.VMEM((slab, padded), jnp.bfloat16),
+            pltpu.VMEM((columns, padded), jnp.bfloat16),
+            pltpu.VMEM((columns, padded), jnp.bfloat16),
             pltpu.VMEM((slab, width), jnp.float32),
             pltpu.VMEM((slab, width), jnp.float32),
             pltpu.SMEM((block_start.shape[0],), jnp.int32),
-            pltpu.SemaphoreType.DMA,
+            pltpu.SemaphoreType.DMA((3,)),
         ],
         compiler_params=pltpu.CompilerParams(vmem_limit_bytes=48 * 2**20),
         cost_estimate=HINT,
@@ -304,16 +347,16 @@
         if hold:
             (other,) = after([other], hold)
         crossed = lax.ppermute(other, "subj", swap)
-        summed = same.astype(jnp.float32) + crossed.astype(jnp.float32)
-        if not d:
-            return same, summed, d
-        return same, summed.astype(jnp.bfloat16) if a == local_subjects - 1 else summed, d
-
-    def send(summed, d, cost):
+        return same, crossed
+
+    def send(summed, d, cost, before=()):
         there = lax.ppermute(summed, "subj", [(s, (s + 2 * d) % subjs) for s in range(subjs)])
-        return after([there], (), cost)[0]
-
-    terms = []
+        return after([there], before, cost)[0]
+
+    def added(same, crossed):
+        return (same.astype(jnp.float32) + crossed.astype(jnp.float32)).astype(jnp.bfloat16)
+
+    terms, starts = [], []
     for a in range(1, local_subjects):
         shares = []
 
@@ -328,20 +371,30 @@
             return [shares[n][0]] if n < chips else ()
 
         everything.append(gather(a, gate))
-        terms += [send(summed, d, SHORT) if d else summed for _, summed, d in shares]
+        for d, (same, crossed) in zip(aways[:-1], shares):
+            terms.append(send(added(same, crossed), d, SHORT))
+            starts.append(None)
+        terms += shares[-1]
+        starts += [None, None]
     last = local_subjects - 1
-    received, late = [], terms[: chips - 1]
+    scale = 1 / (local_subjects * subjs)
+    cut = ((0, early), (early, chunk - early))
+    late, received = terms[: chips - 1], []
     for d in aways[:-1]:
-        parts = []
-        for part in ((0, early), (early, chunk - early)):
-            _, summed, _ = share(last, d, part, late)
-            parts.append(send(summed, d, LONG))
-            late = [summed]
-        received.append(parts)
-    terms.append(share(last, 0, (0, chunk), late, received[-1][:1])[1])
-    terms += [jnp.concatenate(parts, axis=1).astype(jnp.float32) for parts in received[:-1]]
-    total = lax.optimization_barrier(sum(term.astype(jnp.float32) for term in terms))
-    return finish(total, received[-1], 1 / (local_subjects * subjs))
+        shares = []
+        for part in cut:
+            shares.append(added(*share(last, d, part, late)))
+            late = [shares[-1]]
+        received.append(shares)
+    for d, shares in zip(aways[:-2], received[:-1]):
+        terms += [send(summed, d, LONG) for summed in shares]
+        starts += [0, early]
+    d = aways[-2]
+    there = send(received[-1][0], d, LONG)
+    terms += [*share(last, 0, (0, chunk), late, [there]), there]
+    starts += [None, None, 0]
+    out = combine(terms, starts, slab, chunk, scale)
+    return finish(send(received[-1][1], d, LONG, [out]), out, early, scale)
 
 
 def solution(mesh):

time: 329 us -> 312 us (0.948)
  waiting for transfers between devices: 192 us -> 181 us
  other arithmetic: 10.2 us -> 4.66 us
  Pallas kernels: 74.9 us -> 70.7 us
    ppermute x3, waiting for transfers between devices: 31 us -> 6.93 us  [send(): lax.ppermute(summed, 'subj', [(s, (s + 2 * d) % subjs) for s in range(sub...]
    ppermute x12, waiting for transfers between devices: 46.4 us -> 62.9 us  [gather(): got[-1][half] = lax.ppermute(behind[half], SLABS, backward)]
    add x2 -> x0, other arithmetic: 8.53 us -> none  [the longest x1 6.41 us: on_device(): sum((term.astype(jnp.float32) for term in terms))]
    pallas_call x5, Pallas kernels: 60.9 us -> 53.2 us  [scores(): pl.pallas_call(functools.partial(scores_kernel, subject=subject, away=awa...]
    pallas_call x0 -> x1, Pallas kernels: none -> 5.61 us  [combine(): pl.pallas_call(functools.partial(combine_kernel, starts=starts, scale=sca...]
  transfers between devices with their start and end apart: 36 -> 36, of which waited for: 26 -> 24; matrix products, arithmetic and copies ran while one was open for 0% -> 1% of each run, Pallas kernels for 17% -> 18%
where the time goes in v6:
time: 312 us; the launch traced here: 311 us
  waiting for transfers between devices  181 us (58%)
  Pallas kernels  70.7 us (23%)
  starting transfers between devices  39.4 us (13%)
  local copies, waits for them, and re-layouts  14.7 us (5%)
  other arithmetic  4.66 us (1%)
    ppermute x12, waiting for transfers between devices, gather(): got[-2][half] = lax.ppermute(ahead[half], SLABS, onward)  80.6 us
    ppermute x12, waiting for transfers between devices, gather(): got[-1][half] = lax.ppermute(behind[half], SLABS, backward)  62.9 us
    pallas_call x5, Pallas kernels, scores(): pl.pallas_call(functools.partial(scores_kernel, subject=subject, away=awa...  53.2 us
    ppermute x4, waiting for transfers between devices, gather(): last.append(lax.ppermute(got[side][half], SLABS, way))  24.3 us
    ppermute x12, starting transfers between devices, gather(): got[-1][half] = lax.ppermute(behind[half], SLABS, backward)  18.2 us
    unnamed x62, local copies, waits for them, and re-layouts  14 us
    ppermute x12, starting transfers between devices, gather(): got[-2][half] = lax.ppermute(ahead[half], SLABS, onward)  10.4 us
    pallas_call x2, Pallas kernels, normalize(): pl.pallas_call(functools.partial(normalize_kernel, begin=low, lead=begin...  8.27 us
  transfers between devices with their start and end apart: 36, of which 24 were waited for; matrix products, arithmetic and copies ran while one was open for 1% of the time, Pallas kernels for 18%

profile of v6, /device:TPU:0, one launch (start us, length us, event | category | flops | bytes accessed | tf_op | source)
XLA Modules:
  0.0 310.9 jit_solution(12840978478193370854)
XLA Ops:
  0.0 3.7 %shard_map.41 = (bf16[320,1280]{1,0:T(8,128)(2,1)S(1)}, bf16[320,1152]{1,0:T(8,128)(2,1)S(1)}) custom-call(f32[2,1200,640]{2,1,0:T(8,128)} %bitcast.5), custom_call_target="tpu_custom_call" | custom-call | bytes 1024 | tf_op jit(solution)/shard_map/pallas_call | solution.py:76
  4.7 3.0 collective-permute-start.7
  7.7 4.5 %shard_map.37 = (bf16[320,1280]{1,0:T(8,128)(2,1)}, bf16[320,1152]{1,0:T(8,128)(2,1)S(1)}) custom-call(f32[2,1200,640]{2,1,0:T(8,128)} %bitcast.6), custom_call_target="tpu_custom_call" | custom-call | bytes 1024 | tf_op jit(solution)/shard_map/pallas_call | solution.py:76
  15.1 11.6 %collective-permute-done.7.refs_1_ = bf16[320,1280]{1,0:T(8,128)(2,1)S(1)} collective-permute-done((bf16[320,1280]{1,0:T(8,128)(2,1)S(1)}, bf16[320,1280]{1,0:T(8,128)(2,1)S(1)}, u32[]{:S(2)}, u32[]{:S(2)}) %collective-permute-start.7) | collective-permute-done | bytes 819232 | tf_op jit(solution)/shard_map/ppermute | solution.py:309
  26.8 2.0 collective-permute-done.6.refs_0_
  31.7 12.6 %collective-permute-done.1.refs_1_ = bf16[320,1280]{1,0:T(8,128)(2,1)S(1)} collective-permute-done((bf16[320,1280]{1,0:T(8,128)(2,1)}, bf16[320,1280]{1,0:T(8,128)(2,1)S(1)}, u32[]{:S(2)}, u32[]{:S(2)}) %collective-permute-start.1) | collective-permute-done | bytes 819232 | tf_op jit(solution)/shard_map/ppermute | solution.py:309
  49.3 14.6 %collective-permute-done.8.refs_0_ = bf16[320,1280]{1,0:T(8,128)(2,1)S(1)} collective-permute-done((bf16[320,1280]{1,0:T(8,128)(2,1)}, bf16[320,1280]{1,0:T(8,128)(2,1)S(1)}, u32[]{:S(2)}, u32[]{:S(2)}) %collective-permute-start.8) | collective-permute-done | bytes 819232 | tf_op jit(solution)/shard_map/ppermute | solution.py:308
  67.3 12.7 %collective-permute-done.2.refs_0_ = bf16[320,1280]{1,0:T(8,128)(2,1)S(1)} collective-permute-done((bf16[320,1280]{1,0:T(8,128)(2,1)}, bf16[320,1280]{1,0:T(8,128)(2,1)S(1)}, u32[]{:S(2)}, u32[]{:S(2)}) %collective-permute-start.2) | collective-permute-done | bytes 819232 | tf_op jit(solution)/shard_map/ppermute | solution.py:308
  83.6 13.5 %collective-permute-done.11.refs_2_.refs_13_.refs_29_ = bf16[320,1280]{1,0:T(8,128)(2,1)} collective-permute-done((bf16[320,1280]{1,0:T(8,128)(2,1)}, bf16[320,1280]{1,0:T(8,128)(2,1)}, u32[]{:S(2)}, u32[]{:S(2)}) %collective-permute-start.11) | collective-permute-done | bytes 819232 | tf_op jit(solution)/shard_map/ppermute | solution.py:309
  99.1 3.3 %collective-permute-done.4.refs_1_.refs_10_.refs_26_ = bf16[320,1280]{1,0:T(8,128)(2,1)} collective-permute-done((bf16[320,1280]{1,0:T(8,128)(2,1)}, bf16[320,1280]{1,0:T(8,128)(2,1)}, u32[]{:S(2)}, u32[]{:S(2)}) %collective-permute-start.4) | collective-permute-done | bytes 819232 | tf_op jit(solution)/shard_map/ppermute | solution.py:308
  103.1 16.7 %collective-permute-done.10.refs_1_.refs_11_.refs_27_ = bf16[320,1280]{1,0:T(8,128)(2,1)S(1)} collective-permute-done((bf16[320,1280]{1,0:T(8,128)(2,1)S(1)}, bf16[320,1280]{1,0:T(8,128)(2,1)S(1)}, u32[]{:S(2)}, u32[]{:S(2)}) %collective-permute-start.10) | collective-permute-done | bytes 819232 | tf_op jit(solution)/shard_map/ppermute | solution.py:308
  124.4 7.8 %collective-permute-done.15.refs_15_.refs_31_ = bf16[320,1280]{1,0:T(8,128)(2,1)} collective-permute-done((bf16[320,1280]{1,0:T(8,128)(2,1)}, bf16[320,1280]{1,0:T(8,128)(2,1)}, u32[]{:S(2)}, u32[]{:S(2)}) %collective-permute-start.15) | collective-permute-done | bytes 819232 | tf_op jit(solution)/shard_map/ppermute | solution.py:315
  132.2 2.1 collective-permute-start.12
  135.0 2.5 collective-permute-done.14.refs_14_.refs_30_
  139.8 14.2 %shard_map.45 = (bf16[640,1280]{1,0:T(8,128)(2,1)}, bf16[640,1280]{1,0:T(8,128)(2,1)}) custom-call(s32[8]{0:T(128)S(1)} %dynamic-slice_bitcast_fusion.source_ref, s32[5]{0:T(128)S(1)} %copy-done.23, s32[2]{0:T(128)S(1)} %pad_add_fusion.place_ref, bf16[320,1280]{1,0:T(8,128)(2,1)} %get-tuple-element.36.refs_0_.refs_16_, bf16[320,1280]{1,0:T(8,128)(2,1)S(1)} %copy-done.11, ...), custom_call_target="tpu_custom_call" | custom-call | bytes 1024 | tf_op jit(solution)/shard_map/pallas_call | solution.py:244
  154.0 8.9 %collective-permute-done.13.refs_1_.refs_3_ = bf16[320,1152]{1,0:T(8,128)(2,1)} collective-permute-done((bf16[320,1152]{1,0:T(8,128)(2,1)}, bf16[320,1152]{1,0:T(8,128)(2,1)}, u32[]{:S(2)}, u32[]{:S(2)}) %collective-permute-start.13) | collective-permute-done | bytes 737312 | tf_op jit(solution)/shard_map/ppermute | solution.py:309
  163.0 3.8 %collective-permute-done.12.refs_0_.refs_1_ = bf16[320,1152]{1,0:T(8,128)(2,1)} collective-permute-done((bf16[320,1152]{1,0:T(8,128)(2,1)}, bf16[320,1152]{1,0:T(8,128)(2,1)}, u32[]{:S(2)}, u32[]{:S(2)}) %collective-permute-start.12) | collective-permute-done | bytes 737312 | tf_op jit(solution)/shard_map/ppermute | solution.py:308
  170.9 3.0 add_convert_fusion
  175.4 11.9 %shard_map.48 = (bf16[640,1280]{1,0:T(8,128)(2,1)}, bf16[640,1280]{1,0:T(8,128)(2,1)}) custom-call(s32[8]{0:T(128)S(1)} %dynamic-slice_bitcast_fusion.source_ref, s32[5]{0:T(128)S(1)} %copy-done.23, s32[2]{0:T(128)S(1)} %pad_add_fusion.place_ref, bf16[320,1280]{1,0:T(8,128)(2,1)} %get-tuple-element.36.refs_0_.refs_16_, bf16[320,1280]{1,0:T(8,128)(2,1)S(1)} %copy-done.12, ...), custom_call_target="tpu_custom_call" | custom-call | bytes 1024 | tf_op jit(solution)/shard_map/pallas_call | solution.py:244
  189.2 13.1 %collective-permute-done.20.refs_0_ = bf16[320,1152]{1,0:T(8,128)(2,1)} collective-permute-done((bf16[320,1152]{1,0:T(8,128)(2,1)}, bf16[320,1152]{1,0:T(8,128)(2,1)}, u32[]{:S(2)}, u32[]{:S(2)}) %collective-permute-start.20) | collective-permute-done | bytes 737312 | tf_op jit(solution)/shard_map/ppermute | solution.py:308
  205.9 12.2 %collective-permute-done.22.refs_10_ = bf16[320,1152]{1,0:T(8,128)(2,1)} collective-permute-done((bf16[320,1152]{1,0:T(8,128)(2,1)}, bf16[320,1152]{1,0:T(8,128)(2,1)}, u32[]{:S(2)}, u32[]{:S(2)}) %collective-permute-start.22) | collective-permute-done | bytes 737312 | tf_op jit(solution)/shard_map/ppermute | solution.py:308
  218.7 3.3 %collective-permute-done.25.refs_13_ = bf16[320,1152]{1,0:T(8,128)(2,1)} collective-permute-done((bf16[320,1152]{1,0:T(8,128)(2,1)}, bf16[320,1152]{1,0:T(8,128)(2,1)}, u32[]{:S(2)}, u32[]{:S(2)}) %collective-permute-start.25) | collective-permute-done | bytes 737312 | tf_op jit(solution)/shard_map/ppermute | solution.py:309
  224.8 13.0 %collective-permute-done.24.refs_12_ = bf16[320,1152]{1,0:T(8,128)(2,1)} collective-permute-done((bf16[320,1152]{1,0:T(8,128)(2,1)}, bf16[320,1152]{1,0:T(8,128)(2,1)}, u32[]{:S(2)}, u32[]{:S(2)}) %collective-permute-start.24) | collective-permute-done | bytes 737312 | tf_op jit(solution)/shard_map/ppermute | solution.py:309
  237.8 11.4 %collective-permute-done.26.refs_14_ = bf16[320,1152]{1,0:T(8,128)(2,1)} collective-permute-done((bf16[320,1152]{1,0:T(8,128)(2,1)}, bf16[320,1152]{1,0:T(8,128)(2,1)}, u32[]{:S(2)}, u32[]{:S(2)}) %collective-permute-start.26) | collective-permute-done | bytes 737312 | tf_op jit(solution)/shard_map/ppermute | solution.py:315
  249.2 2.6 collective-permute-done.27.refs_15_
  251.9 8.7 %shard_map.53 = (bf16[640,768]{1,0:T(8,128)(2,1)}, bf16[640,768]{1,0:T(8,128)(2,1)}) custom-call(s32[8]{0:T(128)S(1)} %dynamic-slice_bitcast_fusion.source_ref, s32[5]{0:T(128)S(1)} %copy-done.23, s32[2]{0:T(128)S(1)} %pad_add_fusion.place_ref, bf16[320,1152]{1,0:T(8,128)(2,1)S(1)} %copy-done.17, bf16[320,1152]{1,0:T(8,128)(2,1)S(1)} %copy-done.19, ...), custom_call_target="tpu_custom_call" | custom-call | bytes 1024 | tf_op jit(solution)/shard_map/pallas_call | solution.py:244
  260.7 2.8 collective-permute-done.30
  266.7 6.3 %shard_map.54 = (bf16[640,512]{1,0:T(8,128)(2,1)S(1)}, bf16[640,512]{1,0:T(8,128)(2,1)S(1)}) custom-call(s32[8]{0:T(128)S(1)} %dynamic-slice_bitcast_fusion.source_ref, s32[5]{0:T(128)S(1)} %copy-done.23, s32[2]{0:T(128)S(1)} %pad_add_fusion.place_ref, bf16[320,1152]{1,0:T(8,128)(2,1)S(1)} %copy-done.17, bf16[320,1152]{1,0:T(8,128)(2,1)S(1)} %copy-done.19, ...), custom_call_target="tpu_custom_call" | custom-call | bytes 1024 | tf_op jit(solution)/shard_map/pallas_call | solution.py:244
  275.5 12.1 %shard_map.55 = (bf16[640,1280]{1,0:T(8,128)(2,1)}, bf16[640,1280]{1,0:T(8,128)(2,1)}) custom-call(s32[8]{0:T(128)S(1)} %dynamic-slice_bitcast_fusion.source_ref, s32[5]{0:T(128)S(1)} %copy-done.23, s32[2]{0:T(128)S(1)} %pad_add_fusion.place_ref, bf16[320,1152]{1,0:T(8,128)(2,1)S(1)} %copy-done.17, bf16[320,1152]{1,0:T(8,128)(2,1)S(1)} %copy-done.19, ...), custom_call_target="tpu_custom_call" | custom-call | bytes 1024 | tf_op jit(solution)/shard_map/pallas_call | solution.py:244
  295.8 5.6 %shard_map.58.refs_1_.before_ref = f32[640,1280]{1,0:T(8,128)} custom-call(bf16[640,1280]{1,0:T(8,128)(2,1)S(1)} %copy-done.14, bf16[640,1280]{1,0:T(8,128)(2,1)S(1)} %copy-done.15, bf16[640,1280]{1,0:T(8,128)(2,1)} %collective-permute-done.33.refs_2_, bf16[640,1280]{1,0:T(8,128)(2,1)} %get-tuple-element.63.refs_3_, bf16[640,1280]{1,0:T(8,128)(2,1)} %copy-done.30, ...), custom_call_target="tpu_custom_call" | custom-call | bytes 1024 | tf_op jit(solution)/shard_map/pallas_call | solution.py:119
  301.4 5.8 %collective-permute-done.32.refs_0_ = bf16[640,512]{1,0:T(8,128)(2,1)} collective-permute-done((bf16[640,512]{1,0:T(8,128)(2,1)}, bf16[640,512]{1,0:T(8,128)(2,1)}, u32[]{:S(2)}, u32[]{:S(2)}) %collective-permute-start.32) | collective-permute-done | bytes 655392 | tf_op jit(solution)/shard_map/ppermute | solution.py:353
  307.2 3.7 %shard_map.60 = f32[640,1280]{1,0:T(8,128)} custom-call(bf16[640,512]{1,0:T(8,128)(2,1)} %shard_map.59.part_ref, f32[640,1280]{1,0:T(8,128)} %shard_map.58.refs_1_.before_ref), custom_call_target="tpu_custom_call", output_to_operand_aliasing={{}: (1, {})} | custom-call | bytes 1024 | tf_op jit(solution)/shard_map/pallas_call | solution.py:139
  (131 shorter events, 57.6 us)
Async XLA Ops:
  4.7 22.1 %collective-permute-start.7 = (bf16[320,1280]{1,0:T(8,128)(2,1)S(1)}, bf16[320,1280]{1,0:T(8,128)(2,1)S(1)}, u32[]{:S(2)}, u32[]{:S(2)}) collective-permute-start(bf16[320,1280]{1,0:T(8,128)(2,1)S(1)} %get-tuple-element.42.refs_1_.refs_17_), channel_id=1, source_target_pairs={{2,0},{4,2},{6,4},{7,6},{5,7},{3,5},{1,3},{0,1},{10,8},{12,10},{14... | collective-permute-start | bytes 2457608 | tf_op jit(solution)/shard_map/ppermute | solution.py:309
  7.6 21.2 %collective-permute-start.6 = (bf16[320,1280]{1,0:T(8,128)(2,1)S(1)}, bf16[320,1280]{1,0:T(8,128)(2,1)S(1)}, u32[]{:S(2)}, u32[]{:S(2)}) collective-permute-start(bf16[320,1280]{1,0:T(8,128)(2,1)S(1)} %get-tuple-element.42.refs_1_.refs_17_), channel_id=1, source_target_pairs={{0,2},{2,4},{4,6},{6,7},{7,5},{5,3},{3,1},{1,0},{8,10},{10,12},{12... | collective-permute-start | bytes 2457608 | tf_op jit(solution)/shard_map/ppermute | solution.py:308
  13.1 31.2 %collective-permute-start.1 = (bf16[320,1280]{1,0:T(8,128)(2,1)}, bf16[320,1280]{1,0:T(8,128)(2,1)S(1)}, u32[]{:S(2)}, u32[]{:S(2)}) collective-permute-start(bf16[320,1280]{1,0:T(8,128)(2,1)} %get-tuple-element.36.refs_0_.refs_16_), channel_id=1, source_target_pairs={{2,0},{4,2},{6,4},{7,6},{5,7},{3,5},{1,3},{0,1},{10,8},{12,10},{14... | collective-permute-start | bytes 2457608 | tf_op jit(solution)/shard_map/ppermute | solution.py:309
  15.1 31.3 %collective-permute-start = (bf16[320,1280]{1,0:T(8,128)(2,1)}, bf16[320,1280]{1,0:T(8,128)(2,1)S(1)}, u32[]{:S(2)}, u32[]{:S(2)}) collective-permute-start(bf16[320,1280]{1,0:T(8,128)(2,1)} %get-tuple-element.36.refs_0_.refs_16_), channel_id=1, source_target_pairs={{0,2},{2,4},{4,6},{6,7},{7,5},{5,3},{3,1},{1,0},{8,10},{10,12},{12... | collective-permute-start | bytes 2457608 | tf_op jit(solution)/shard_map/ppermute | solution.py:308
  29.7 34.2 %collective-permute-start.8 = (bf16[320,1280]{1,0:T(8,128)(2,1)}, bf16[320,1280]{1,0:T(8,128)(2,1)S(1)}, u32[]{:S(2)}, u32[]{:S(2)}) collective-permute-start(bf16[320,1280]{1,0:T(8,128)(2,1)} %get-tuple-element.43.refs_3_.refs_19_), channel_id=1, source_target_pairs={{0,2},{2,4},{4,6},{6,7},{7,5},{5,3},{3,1},{1,0},{8,10},{10,12},{12... | collective-permute-start | bytes 2457608 | tf_op jit(solution)/shard_map/ppermute | solution.py:308
  30.6 33.3 %collective-permute-start.9 = (bf16[320,1280]{1,0:T(8,128)(2,1)}, bf16[320,1280]{1,0:T(8,128)(2,1)S(1)}, u32[]{:S(2)}, u32[]{:S(2)}) collective-permute-start(bf16[320,1280]{1,0:T(8,128)(2,1)} %get-tuple-element.44.refs_5_.refs_21_), channel_id=1, source_target_pairs={{2,0},{4,2},{6,4},{7,6},{5,7},{3,5},{1,3},{0,1},{10,8},{12,10},{14... | collective-permute-start | bytes 2457608 | tf_op jit(solution)/shard_map/ppermute | solution.py:309
  47.3 32.8 %collective-permute-start.2 = (bf16[320,1280]{1,0:T(8,128)(2,1)}, bf16[320,1280]{1,0:T(8,128)(2,1)S(1)}, u32[]{:S(2)}, u32[]{:S(2)}) collective-permute-start(bf16[320,1280]{1,0:T(8,128)(2,1)} %get-tuple-element.37.refs_2_.refs_18_), channel_id=1, source_target_pairs={{0,2},{2,4},{4,6},{6,7},{7,5},{5,3},{3,1},{1,0},{8,10},{10,12},{12... | collective-permute-start | bytes 2457608 | tf_op jit(solution)/shard_map/ppermute | solution.py:308
  48.2 31.8 %collective-permute-start.3 = (bf16[320,1280]{1,0:T(8,128)(2,1)}, bf16[320,1280]{1,0:T(8,128)(2,1)}, u32[]{:S(2)}, u32[]{:S(2)}) collective-permute-start(bf16[320,1280]{1,0:T(8,128)(2,1)} %get-tuple-element.38.refs_4_.refs_20_), channel_id=1, source_target_pairs={{2,0},{4,2},{6,4},{7,6},{5,7},{3,5},{1,3},{0,1},{10,8},{12,10},{14... | collective-permute-start | bytes 2457608 | tf_op jit(solution)/shard_map/ppermute | solution.py:309
  65.7 31.4 %collective-permute-start.11 = (bf16[320,1280]{1,0:T(8,128)(2,1)}, bf16[320,1280]{1,0:T(8,128)(2,1)}, u32[]{:S(2)}, u32[]{:S(2)}) collective-permute-start(bf16[320,1280]{1,0:T(8,128)(2,1)} %get-tuple-element.46.refs_9_.refs_25_), channel_id=1, source_target_pairs={{2,0},{4,2},{6,4},{7,6},{5,7},{3,5},{1,3},{0,1},{10,8},{12,10},{14... | collective-permute-start | bytes 2457608 | tf_op jit(solution)/shard_map/ppermute | solution.py:309
  80.9 21.5 %collective-permute-start.4 = (bf16[320,1280]{1,0:T(8,128)(2,1)}, bf16[320,1280]{1,0:T(8,128)(2,1)}, u32[]{:S(2)}, u32[]{:S(2)}) collective-permute-start(bf16[320,1280]{1,0:T(8,128)(2,1)} %get-tuple-element.39.refs_6_.refs_22_), channel_id=1, source_target_pairs={{0,2},{2,4},{4,6},{6,7},{7,5},{5,3},{3,1},{1,0},{8,10},{10,12},{12... | collective-permute-start | bytes 2457608 | tf_op jit(solution)/shard_map/ppermute | solution.py:308
  81.6 38.2 %collective-permute-start.10 = (bf16[320,1280]{1,0:T(8,128)(2,1)S(1)}, bf16[320,1280]{1,0:T(8,128)(2,1)S(1)}, u32[]{:S(2)}, u32[]{:S(2)}) collective-permute-start(bf16[320,1280]{1,0:T(8,128)(2,1)S(1)} %copy-done.26), channel_id=1, source_target_pairs={{0,2},{2,4},{4,6},{6,7},{7,5},{5,3},{3,1},{1,0},{8,10},{10,12},{12... | collective-permute-start | bytes 2457608 | tf_op jit(solution)/shard_map/ppermute | solution.py:308
  83.2 39.7 %collective-permute-start.5 = (bf16[320,1280]{1,0:T(8,128)(2,1)}, bf16[320,1280]{1,0:T(8,128)(2,1)}, u32[]{:S(2)}, u32[]{:S(2)}) collective-permute-start(bf16[320,1280]{1,0:T(8,128)(2,1)} %get-tuple-element.40.refs_8_.refs_24_), channel_id=1, source_target_pairs={{2,0},{4,2},{6,4},{7,6},{5,7},{3,5},{1,3},{0,1},{10,8},{12,10},{14... | collective-permute-start | bytes 2457608 | tf_op jit(solution)/shard_map/ppermute | solution.py:309
  97.1 35.1 %collective-permute-start.15 = (bf16[320,1280]{1,0:T(8,128)(2,1)}, bf16[320,1280]{1,0:T(8,128)(2,1)}, u32[]{:S(2)}, u32[]{:S(2)}) collective-permute-start(bf16[320,1280]{1,0:T(8,128)(2,1)} %collective-permute-done.11.refs_2_.refs_13_.refs_29_), channel_id=1, source_target_pairs={{2,0},{4,2},{6,4},{7,6},{5,7},{3,5},{1,3},{0,1},{10,8},{12,10},{14... | collective-permute-start | bytes 2457608 | tf_op jit(solution)/shard_map/ppermute | solution.py:315
  102.4 35.1 %collective-permute-start.14 = (bf16[320,1280]{1,0:T(8,128)(2,1)}, bf16[320,1280]{1,0:T(8,128)(2,1)}, u32[]{:S(2)}, u32[]{:S(2)}) collective-permute-start(bf16[320,1280]{1,0:T(8,128)(2,1)} %collective-permute-done.4.refs_1_.refs_10_.refs_26_), channel_id=1, source_target_pairs={{0,2},{2,4},{4,6},{6,7},{7,5},{5,3},{3,1},{1,0},{8,10},{10,12},{12... | collective-permute-start | bytes 2457608 | tf_op jit(solution)/shard_map/ppermute | solution.py:315
  120.8 33.3 %collective-permute-start.17 = (bf16[320,1152]{1,0:T(8,128)(2,1)}, bf16[320,1152]{1,0:T(8,128)(2,1)}, u32[]{:S(2)}, u32[]{:S(2)}) collective-permute-start(bf16[320,1152]{1,0:T(8,128)(2,1)} %shard_map.44.refs_1_), channel_id=1, source_target_pairs={{2,0},{4,2},{6,4},{7,6},{5,7},{3,5},{1,3},{0,1},{10,8},{12,10},{14... | collective-permute-start | bytes 2211848 | tf_op jit(solution)/shard_map/ppermute | solution.py:309
  122.4 31.6 %collective-permute-start.16 = (bf16[320,1152]{1,0:T(8,128)(2,1)}, bf16[320,1152]{1,0:T(8,128)(2,1)}, u32[]{:S(2)}, u32[]{:S(2)}) collective-permute-start(bf16[320,1152]{1,0:T(8,128)(2,1)} %shard_map.44.refs_1_), channel_id=1, source_target_pairs={{0,2},{2,4},{4,6},{6,7},{7,5},{5,3},{3,1},{1,0},{8,10},{10,12},{12... | collective-permute-start | bytes 2211848 | tf_op jit(solution)/shard_map/ppermute | solution.py:308
  122.8 40.1 %collective-permute-start.13 = (bf16[320,1152]{1,0:T(8,128)(2,1)}, bf16[320,1152]{1,0:T(8,128)(2,1)}, u32[]{:S(2)}, u32[]{:S(2)}) collective-permute-start(bf16[320,1152]{1,0:T(8,128)(2,1)} %shard_map.40.refs_0_), channel_id=1, source_target_pairs={{2,0},{4,2},{6,4},{7,6},{5,7},{3,5},{1,3},{0,1},{10,8},{12,10},{14... | collective-permute-start | bytes 2211848 | tf_op jit(solution)/shard_map/ppermute | solution.py:309
  132.2 34.6 %collective-permute-start.12 = (bf16[320,1152]{1,0:T(8,128)(2,1)}, bf16[320,1152]{1,0:T(8,128)(2,1)}, u32[]{:S(2)}, u32[]{:S(2)}) collective-permute-start(bf16[320,1152]{1,0:T(8,128)(2,1)} %shard_map.40.refs_0_), channel_id=1, source_target_pairs={{0,2},{2,4},{4,6},{6,7},{7,5},{5,3},{3,1},{1,0},{8,10},{10,12},{12... | collective-permute-start | bytes 2211848 | tf_op jit(solution)/shard_map/ppermute | solution.py:308
  166.8 20.5 %collective-permute-start.18 = (bf16[320,1152]{1,0:T(8,128)(2,1)}, bf16[320,1152]{1,0:T(8,128)(2,1)}, u32[]{:S(2)}, u32[]{:S(2)}) collective-permute-start(bf16[320,1152]{1,0:T(8,128)(2,1)} %get-tuple-element.48.refs_32_.refs_2_), channel_id=1, source_target_pairs={{0,2},{2,4},{4,6},{6,7},{7,5},{5,3},{3,1},{1,0},{8,10},{10,12},{12... | collective-permute-start | bytes 2211848 | tf_op jit(solution)/shard_map/ppermute | solution.py:308
  167.5 19.8 %collective-permute-start.19 = (bf16[320,1152]{1,0:T(8,128)(2,1)}, bf16[320,1152]{1,0:T(8,128)(2,1)}, u32[]{:S(2)}, u32[]{:S(2)}) collective-permute-start(bf16[320,1152]{1,0:T(8,128)(2,1)} %get-tuple-element.50.refs_34_.refs_4_), channel_id=1, source_target_pairs={{2,0},{4,2},{6,4},{7,6},{5,7},{3,5},{1,3},{0,1},{10,8},{12,10},{14... | collective-permute-start | bytes 2211848 | tf_op jit(solution)/shard_map/ppermute | solution.py:309
  168.9 33.4 %collective-permute-start.20 = (bf16[320,1152]{1,0:T(8,128)(2,1)}, bf16[320,1152]{1,0:T(8,128)(2,1)}, u32[]{:S(2)}, u32[]{:S(2)}) collective-permute-start(bf16[320,1152]{1,0:T(8,128)(2,1)} %get-tuple-element.49.refs_33_.refs_3_), channel_id=1, source_target_pairs={{0,2},{2,4},{4,6},{6,7},{7,5},{5,3},{3,1},{1,0},{8,10},{10,12},{12... | collective-permute-start | bytes 2211848 | tf_op jit(solution)/shard_map/ppermute | solution.py:308
  169.6 32.7 %collective-permute-start.21 = (bf16[320,1152]{1,0:T(8,128)(2,1)}, bf16[320,1152]{1,0:T(8,128)(2,1)}, u32[]{:S(2)}, u32[]{:S(2)}) collective-permute-start(bf16[320,1152]{1,0:T(8,128)(2,1)} %get-tuple-element.51.refs_35_.refs_5_), channel_id=1, source_target_pairs={{2,0},{4,2},{6,4},{7,6},{5,7},{3,5},{1,3},{0,1},{10,8},{12,10},{14... | collective-permute-start | bytes 2211848 | tf_op jit(solution)/shard_map/ppermute | solution.py:309
  173.9 49.7 %collective-permute-start.29 = (bf16[640,1280]{1,0:T(8,128)(2,1)}, bf16[640,1280]{1,0:T(8,128)(2,1)S(1)}, u32[]{:S(2)}, u32[]{:S(2)}) collective-permute-start(bf16[640,1280]{1,0:T(8,128)(2,1)} %add_convert_fusion), channel_id=1, source_target_pairs={{0,16},{8,24},{16,0},{24,8},{1,17},{9,25},{17,1},{25,9},{2,18},{10... | collective-permute-start | bytes 4915208 | tf_op jit(solution)/shard_map/ppermute | solution.py:353
  187.4 30.7 %collective-permute-start.22 = (bf16[320,1152]{1,0:T(8,128)(2,1)}, bf16[320,1152]{1,0:T(8,128)(2,1)}, u32[]{:S(2)}, u32[]{:S(2)}) collective-permute-start(bf16[320,1152]{1,0:T(8,128)(2,1)} %get-tuple-element.53.refs_6_), channel_id=1, source_target_pairs={{0,2},{2,4},{4,6},{6,7},{7,5},{5,3},{3,1},{1,0},{8,10},{10,12},{12... | collective-permute-start | bytes 2211848 | tf_op jit(solution)/shard_map/ppermute | solution.py:308
  202.3 19.7 %collective-permute-start.25 = (bf16[320,1152]{1,0:T(8,128)(2,1)}, bf16[320,1152]{1,0:T(8,128)(2,1)}, u32[]{:S(2)}, u32[]{:S(2)}) collective-permute-start(bf16[320,1152]{1,0:T(8,128)(2,1)} %get-tuple-element.56.refs_9_), channel_id=1, source_target_pairs={{2,0},{4,2},{6,4},{7,6},{5,7},{3,5},{1,3},{0,1},{10,8},{12,10},{14... | collective-permute-start | bytes 2211848 | tf_op jit(solution)/shard_map/ppermute | solution.py:309
  203.8 34.0 %collective-permute-start.24 = (bf16[320,1152]{1,0:T(8,128)(2,1)}, bf16[320,1152]{1,0:T(8,128)(2,1)}, u32[]{:S(2)}, u32[]{:S(2)}) collective-permute-start(bf16[320,1152]{1,0:T(8,128)(2,1)} %get-tuple-element.55.refs_8_), channel_id=1, source_target_pairs={{2,0},{4,2},{6,4},{7,6},{5,7},{3,5},{1,3},{0,1},{10,8},{12,10},{14... | collective-permute-start | bytes 2211848 | tf_op jit(solution)/shard_map/ppermute | solution.py:309
  205.4 32.4 %collective-permute-start.23 = (bf16[320,1152]{1,0:T(8,128)(2,1)}, bf16[320,1152]{1,0:T(8,128)(2,1)}, u32[]{:S(2)}, u32[]{:S(2)}) collective-permute-start(bf16[320,1152]{1,0:T(8,128)(2,1)} %get-tuple-element.54.refs_7_), channel_id=1, source_target_pairs={{0,2},{2,4},{4,6},{6,7},{7,5},{5,3},{3,1},{1,0},{8,10},{10,12},{12... | collective-permute-start | bytes 2211848 | tf_op jit(solution)/shard_map/ppermute | solution.py:308
  218.1 31.2 %collective-permute-start.26 = (bf16[320,1152]{1,0:T(8,128)(2,1)}, bf16[320,1152]{1,0:T(8,128)(2,1)}, u32[]{:S(2)}, u32[]{:S(2)}) collective-permute-start(bf16[320,1152]{1,0:T(8,128)(2,1)} %collective-permute-done.22.refs_10_), channel_id=1, source_target_pairs={{0,2},{2,4},{4,6},{6,7},{7,5},{5,3},{3,1},{1,0},{8,10},{10,12},{12... | collective-permute-start | bytes 2211848 | tf_op jit(solution)/shard_map/ppermute | solution.py:315
  222.0 29.9 %collective-permute-start.27 = (bf16[320,1152]{1,0:T(8,128)(2,1)}, bf16[320,1152]{1,0:T(8,128)(2,1)}, u32[]{:S(2)}, u32[]{:S(2)}) collective-permute-start(bf16[320,1152]{1,0:T(8,128)(2,1)} %collective-permute-done.25.refs_13_), channel_id=1, source_target_pairs={{2,0},{4,2},{6,4},{7,6},{5,7},{3,5},{1,3},{0,1},{10,8},{12,10},{14... | collective-permute-start | bytes 2211848 | tf_op jit(solution)/shard_map/ppermute | solution.py:315
  264.9 23.9 %collective-permute-start.34 = (bf16[640,768]{1,0:T(8,128)(2,1)S(1)}, bf16[640,768]{1,0:T(8,128)(2,1)S(1)}, u32[]{:S(2)}, u32[]{:S(2)}) collective-permute-start(bf16[640,768]{1,0:T(8,128)(2,1)S(1)} %add_convert_fusion.1.refs_32_), channel_id=1, source_target_pairs={{0,16},{8,24},{16,0},{24,8},{1,17},{9,25},{17,1},{25,9},{2,18},{10... | collective-permute-start | bytes 2949128 | tf_op jit(solution)/shard_map/ppermute | solution.py:353
  273.1 18.5 %collective-permute-start.33 = (bf16[640,1280]{1,0:T(8,128)(2,1)}, bf16[640,1280]{1,0:T(8,128)(2,1)}, u32[]{:S(2)}, u32[]{:S(2)}) collective-permute-start(bf16[640,1280]{1,0:T(8,128)(2,1)} %get-tuple-element.62), channel_id=1, source_target_pairs={{0,8},{8,0},{16,24},{24,16},{1,9},{9,1},{17,25},{25,17},{2,10},{10... | collective-permute-start | bytes 4915208 | tf_op jit(solution)/shard_map/ppermute | solution.py:349
  289.8 17.5 %collective-permute-start.32 = (bf16[640,512]{1,0:T(8,128)(2,1)}, bf16[640,512]{1,0:T(8,128)(2,1)}, u32[]{:S(2)}, u32[]{:S(2)}) collective-permute-start(bf16[640,512]{1,0:T(8,128)(2,1)} %copy-done.22), channel_id=1, source_target_pairs={{0,16},{8,24},{16,0},{24,8},{1,17},{9,25},{17,1},{25,9},{2,18},{10... | collective-permute-start | bytes 1966088 | tf_op jit(solution)/shard_map/ppermute | solution.py:353
  (35 other events, 265.0 us)

commit v7 on v6

--- a/solution.py
+++ b/solution.py
@@ -134,7 +134,7 @@
 def finish(part, before, first, scale):
     slab = before.shape[0]
     width = math.gcd(part.shape[1], first)
-    block = (slab // 2 if slab % 32 == 0 else slab, width)
+    block = (slab, width)
     there = pl.BlockSpec(block, lambda i, j: (i, first // width + j))
     return pl.pallas_call(
         functools.partial(finish_kernel, scale=scale),
@@ -148,11 +148,13 @@
 
 
 def scores_kernel(
-    source_ref, block_start_ref, place_ref, *refs, subject, away, part, cuts, slab, granule, block_rows, chips, chunk, duration
+    source_ref, block_start_ref, place_ref, *refs, subject, targets, cuts, slab, granule, block_rows, chips, chunk, duration
 ):
     count = source_ref.shape[0]
     bodies, tails = refs[: 2 * count], refs[2 * count : 4 * count]
-    same_ref, other_ref, own_rows, other_columns, same_columns, products_a, products_b, place_of, sems = refs[-9:]
+    own_rows, products_a, products_b, place_of, sems = refs[-5:]
+    refs = refs[-5 - 2 * len(targets) : -5]
+    out_refs, columns_refs = refs[: len(targets)], refs[len(targets) :]
     body = duration // LANES * LANES
     tail = duration - body
     for a in range(block_start_ref.shape[0]):
@@ -160,9 +162,8 @@
 
     position, subj = place_ref[0], place_ref[1]
     chip, core = subj // 2, subj % 2
-    first, columns = part
     wanted = [(position * slab, own_rows)]
-    for flip, columns_ref in ((1, other_columns), (0, same_columns)):
+    for (away, flip, first, _), columns_ref in zip(targets, columns_refs):
         owner = (chip + away) % chips * 2 + (core + flip) % 2
         wanted.append((owner * chunk + first, columns_ref))
 
@@ -205,10 +206,10 @@
     own_rows[:, body:] = jnp.where(kept, own_rows[:, body:].astype(jnp.float32), 0.0).astype(jnp.bfloat16)
 
     limit = clip_limit * duration
-    width = math.gcd(columns, 256)
+    width = products_a.shape[1]
     tiles = []
-    for n, out_ref in ((1, other_ref), (2, same_ref)):
-        tiles += [(n, k, out_ref) for k in range(0, columns, width)]
+    for n, out_ref in enumerate(out_refs):
+        tiles += [(n + 1, k, out_ref) for k in range(0, out_ref.shape[1], width)]
     buffers = (products_a, products_b)
 
     def multiply(i):
@@ -231,22 +232,20 @@
     score(len(tiles) - 1)
 
 
-def scores(source, block_start, place, subject, away, part, bodies, tails, cuts, window, chips, duration, late=()):
+def scores(source, block_start, place, subject, targets, bodies, tails, cuts, window, chips, duration, late=()):
     slab = cuts[-1]
     block_rows = window // block_start.shape[0]
-    granule = math.gcd(*cuts, *part, block_rows)
     chunk = window // (2 * chips)
+    sizes = [columns for _, _, _, columns in targets]
+    granule = math.gcd(*cuts, *sizes, *(first for _, _, first, _ in targets), block_rows)
+    width = math.gcd(*sizes, 256)
     padded = tails[0].shape[1]
-    columns = part[1]
-    width = math.gcd(columns, 256)
-    out = jax.ShapeDtypeStruct((slab, columns), jnp.bfloat16)
     smem = pl.BlockSpec(memory_space=pltpu.SMEM)
     return pl.pallas_call(
         functools.partial(
             scores_kernel,
             subject=subject,
-            away=away,
-            part=part,
+            targets=targets,
             cuts=cuts,
             slab=slab,
             granule=granule,
@@ -256,15 +255,14 @@
             duration=duration,
         ),
         in_specs=[smem, smem, smem] + [ANY] * (2 * len(tails) + len(late)),
-        out_shape=[out, out],
-        scratch_shapes=[
+        out_shape=[jax.ShapeDtypeStruct((slab, columns), jnp.bfloat16) for columns in sizes],
+        scratch_shapes=[pltpu.VMEM((columns, padded), jnp.bfloat16) for columns in sizes]
+        + [
             pltpu.VMEM((slab, padded), jnp.bfloat16),
-            pltpu.VMEM((columns, padded), jnp.bfloat16),
-            pltpu.VMEM((columns, padded), jnp.bfloat16),
             pltpu.VMEM((slab, width), jnp.float32),
             pltpu.VMEM((slab, width), jnp.float32),
             pltpu.SMEM((block_start.shape[0],), jnp.int32),
-            pltpu.SemaphoreType.DMA((3,)),
+            pltpu.SemaphoreType.DMA((1 + len(targets),)),
         ],
         compiler_params=pltpu.CompilerParams(vmem_limit_bytes=48 * 2**20),
         cost_estimate=HINT,
@@ -326,28 +324,17 @@
     chunk = window // subjs
     width = math.gcd(chunk, 256)
     early = -(-chunk // width // 2) * width
+    cut = ((0, early), (early, chunk - early))
     aways = [*range(1, chips), 0]
 
-    def share(a, d, part, late=(), hold=()):
-        same, other = scores(
-            source,
-            block_start,
-            place,
-            a,
-            d,
-            part,
-            flat(everything[a]),
-            flat(everything[0]),
-            cuts,
-            window,
-            chips,
-            duration,
-            late,
-        )
+    def share(a, targets, late=()):
+        bodies, tails = flat(everything[a]), flat(everything[0])
+        return scores(source, block_start, place, a, targets, bodies, tails, cuts, window, chips, duration, late)
+
+    def cross(other, hold=()):
         if hold:
             (other,) = after([other], hold)
-        crossed = lax.ppermute(other, "subj", swap)
-        return same, crossed
+        return lax.ppermute(other, "subj", swap)
 
     def send(summed, d, cost, before=()):
         there = lax.ppermute(summed, "subj", [(s, (s + 2 * d) % subjs) for s in range(subjs)])
@@ -358,43 +345,54 @@
 
     terms, starts = [], []
     for a in range(1, local_subjects):
-        shares = []
-
-        def gate(d, half, got, a=a, before=everything[-1], shares=shares):
+        shares, sums = [], []
+
+        def gate(d, half, got, a=a, before=everything[-1], shares=shares, sums=sums):
             if d == 1:
                 return [before[-3][half], before[-2][half]]
             n = d - 2
             if half == 0 and n < chips:
                 late = [*got[2 * n - 1], *got[2 * n]] if n else ()
-                hold = () if n else [*got[1], *got[2]]
-                shares.append(share(a - 1, aways[n], (0, chunk), late, hold))
-            return [shares[n][0]] if n < chips else ()
+                parts = cut if aways[n] else ((0, chunk),)
+                shares.append(share(a - 1, [(aways[n], flip, *part) for part in parts for flip in (0, 1)], late))
+            waits = [shares[n][0]] if n < chips else []
+            if (d, half) == (reach, 0):
+                for m, (away, arrays) in enumerate(zip(aways[:-1], shares)):
+                    hold = [*got[2 * m + 1], *got[2 * m + 2]]
+                    for (start, _), same, other in zip(cut, arrays[::2], arrays[1::2]):
+                        sums.append((added(same, cross(other, hold)), away, start))
+            if d >= reach:
+                waits += [summed for summed, _, _ in sums]
+            return waits
 
         everything.append(gather(a, gate))
-        for d, (same, crossed) in zip(aways[:-1], shares):
-            terms.append(send(added(same, crossed), d, SHORT))
-            starts.append(None)
-        terms += shares[-1]
+        for summed, d, start in sums:
+            terms.append(send(summed, d, SHORT))
+            starts.append(start)
+        same, other = shares[-1]
+        gone = list(terms)
+        terms += [same, cross(other)]
         starts += [None, None]
     last = local_subjects - 1
     scale = 1 / (local_subjects * subjs)
-    cut = ((0, early), (early, chunk - early))
-    late, received = terms[: chips - 1], []
-    for d in aways[:-1]:
-        shares = []
-        for part in cut:
-            shares.append(added(*share(last, d, part, late)))
-            late = [shares[-1]]
-        received.append(shares)
-    for d, shares in zip(aways[:-2], received[:-1]):
-        terms += [send(summed, d, LONG) for summed in shares]
-        starts += [0, early]
+    late = gone
+    for d in aways[:-2]:
+        same, other = share(last, [(d, 0, 0, chunk), (d, 1, 0, chunk)], late)
+        late = [added(same, cross(other))]
+        terms.append(send(late[0], d, LONG))
+        starts.append(None)
     d = aways[-2]
-    there = send(received[-1][0], d, LONG)
-    terms += [*share(last, 0, (0, chunk), late, [there]), there]
+    same, other = share(last, [(d, 0, 0, early), (d, 1, 0, early)], late)
+    summed = added(same, cross(other))
+    there = send(summed, d, LONG)
+    rest = chunk - early
+    other, same, others = share(last, [(d, 1, early, rest), (d, 0, early, rest), (0, 1, 0, chunk)], [summed])
+    summed = added(same, cross(other))
+    (same,) = share(last, [(0, 0, 0, chunk)], [summed, there])
+    terms += [same, cross(others), there]
     starts += [None, None, 0]
     out = combine(terms, starts, slab, chunk, scale)
-    return finish(send(received[-1][1], d, LONG, [out]), out, early, scale)
+    return finish(send(summed, d, LONG, [out]), out, early, scale)
 
 
 def solution(mesh):

time: 312 us -> 323 us (1.035)
  waiting for transfers between devices: 181 us -> 190 us
  other arithmetic: 4.66 us -> 8.16 us
    ppermute x3 -> x4, waiting for transfers between devices: 6.93 us -> 38.5 us  [send(): lax.ppermute(summed, 'subj', [(s, (s + 2 * d) % subjs) for s in range(sub...]
    ppermute x12, waiting for transfers between devices: 80.6 us -> 66.6 us  [gather(): got[-2][half] = lax.ppermute(ahead[half], SLABS, onward)]
    ppermute x12, waiting for transfers between devices: 62.9 us -> 54.5 us  [gather(): got[-1][half] = lax.ppermute(behind[half], SLABS, backward)]
    convert_element_type x3 -> x4, other arithmetic: 4.59 us -> 8.09 us  [added(): (same.astype(jnp.float32) + crossed.astype(jnp.float32)).astype(jnp.bfloa...]
    unnamed x62 -> x66, local copies, waits for them, and re-layouts: 14 us -> 13.4 us
    ppermute x5 -> x6, waiting for transfers between devices: 6.4 us -> 6.64 us  [cross(): return lax.ppermute(other, 'subj', swap)]
  transfers between devices with their start and end apart: 36 -> 38, of which waited for: 24 -> 22; matrix products, arithmetic and copies ran while one was open for 1% -> 3% of each run, Pallas kernels for 18% -> 17%
where the time goes in v7:
time: 323 us; the launch traced here: 322 us
  waiting for transfers between devices  190 us (59%)
  Pallas kernels  70.1 us (22%)
  starting transfers between devices  39.7 us (12%)
  local copies, waits for them, and re-layouts  14.1 us (4%)
  other arithmetic  8.16 us (3%)
    ppermute x12, waiting for transfers between devices, gather(): got[-2][half] = lax.ppermute(ahead[half], SLABS, onward)  66.6 us
    ppermute x12, waiting for transfers between devices, gather(): got[-1][half] = lax.ppermute(behind[half], SLABS, backward)  54.5 us
    pallas_call x5, Pallas kernels, scores(): pl.pallas_call(functools.partial(scores_kernel, subject=subject, targets=...  53.3 us
    ppermute x4, waiting for transfers between devices, send(): lax.ppermute(summed, 'subj', [(s, (s + 2 * d) % subjs) for s in range(sub...  38.5 us
    ppermute x4, waiting for transfers between devices, gather(): last.append(lax.ppermute(got[side][half], SLABS, way))  23.7 us
    ppermute x12, starting transfers between devices, gather(): got[-1][half] = lax.ppermute(behind[half], SLABS, backward)  20.7 us
    unnamed x66, local copies, waits for them, and re-layouts  13.4 us
    ppermute x12, starting transfers between devices, gather(): got[-2][half] = lax.ppermute(ahead[half], SLABS, onward)  8.45 us
  transfers between devices with their start and end apart: 38, of which 22 were waited for; matrix products, arithmetic and copies ran while one was open for 3% of the time, Pallas kernels for 17%

profile of v7, /device:TPU:0, one launch (start us, length us, event | category | flops | bytes accessed | tf_op | source)
XLA Modules:
  0.0 322.2 jit_solution(525098944426547437)
XLA Ops:
  0.0 3.7 %shard_map.41 = (bf16[320,1280]{1,0:T(8,128)(2,1)S(1)}, bf16[320,1152]{1,0:T(8,128)(2,1)S(1)}) custom-call(f32[2,1200,640]{2,1,0:T(8,128)} %bitcast.5), custom_call_target="tpu_custom_call" | custom-call | bytes 1024 | tf_op jit(solution)/shard_map/pallas_call | solution.py:76
  4.6 3.0 collective-permute-start.7
  7.6 4.5 %shard_map.37 = (bf16[320,1280]{1,0:T(8,128)(2,1)}, bf16[320,1152]{1,0:T(8,128)(2,1)S(1)}) custom-call(f32[2,1200,640]{2,1,0:T(8,128)} %bitcast.6), custom_call_target="tpu_custom_call" | custom-call | bytes 1024 | tf_op jit(solution)/shard_map/pallas_call | solution.py:76
  15.1 11.6 %collective-permute-done.7.refs_1_ = bf16[320,1280]{1,0:T(8,128)(2,1)S(1)} collective-permute-done((bf16[320,1280]{1,0:T(8,128)(2,1)S(1)}, bf16[320,1280]{1,0:T(8,128)(2,1)S(1)}, u32[]{:S(2)}, u32[]{:S(2)}) %collective-permute-start.7) | collective-permute-done | bytes 819232 | tf_op jit(solution)/shard_map/ppermute | solution.py:307
  31.7 12.5 %collective-permute-done.1.refs_1_ = bf16[320,1280]{1,0:T(8,128)(2,1)S(1)} collective-permute-done((bf16[320,1280]{1,0:T(8,128)(2,1)}, bf16[320,1280]{1,0:T(8,128)(2,1)S(1)}, u32[]{:S(2)}, u32[]{:S(2)}) %collective-permute-start.1) | collective-permute-done | bytes 819232 | tf_op jit(solution)/shard_map/ppermute | solution.py:307
  49.3 14.7 %collective-permute-done.8.refs_0_ = bf16[320,1280]{1,0:T(8,128)(2,1)} collective-permute-done((bf16[320,1280]{1,0:T(8,128)(2,1)}, bf16[320,1280]{1,0:T(8,128)(2,1)}, u32[]{:S(2)}, u32[]{:S(2)}) %collective-permute-start.8) | collective-permute-done | bytes 819232 | tf_op jit(solution)/shard_map/ppermute | solution.py:306
  66.4 13.5 %collective-permute-done.2.refs_0_ = bf16[320,1280]{1,0:T(8,128)(2,1)S(1)} collective-permute-done((bf16[320,1280]{1,0:T(8,128)(2,1)}, bf16[320,1280]{1,0:T(8,128)(2,1)S(1)}, u32[]{:S(2)}, u32[]{:S(2)}) %collective-permute-start.2) | collective-permute-done | bytes 819232 | tf_op jit(solution)/shard_map/ppermute | solution.py:306
  84.4 12.7 %collective-permute-done.11.refs_2_.refs_13_.refs_29_ = bf16[320,1280]{1,0:T(8,128)(2,1)} collective-permute-done((bf16[320,1280]{1,0:T(8,128)(2,1)}, bf16[320,1280]{1,0:T(8,128)(2,1)}, u32[]{:S(2)}, u32[]{:S(2)}) %collective-permute-start.11) | collective-permute-done | bytes 819232 | tf_op jit(solution)/shard_map/ppermute | solution.py:307
  99.0 4.2 %collective-permute-done.4.refs_1_.refs_10_.refs_26_ = bf16[320,1280]{1,0:T(8,128)(2,1)} collective-permute-done((bf16[320,1280]{1,0:T(8,128)(2,1)}, bf16[320,1280]{1,0:T(8,128)(2,1)}, u32[]{:S(2)}, u32[]{:S(2)}) %collective-permute-start.4) | collective-permute-done | bytes 819232 | tf_op jit(solution)/shard_map/ppermute | solution.py:306
  103.8 10.7 %collective-permute-done.5.refs_2_.refs_12_.refs_28_ = bf16[320,1280]{1,0:T(8,128)(2,1)S(1)} collective-permute-done((bf16[320,1280]{1,0:T(8,128)(2,1)}, bf16[320,1280]{1,0:T(8,128)(2,1)S(1)}, u32[]{:S(2)}, u32[]{:S(2)}) %collective-permute-start.5) | collective-permute-done | bytes 819232 | tf_op jit(solution)/shard_map/ppermute | solution.py:307
  117.6 3.2 collective-permute-done.10.refs_1_.refs_11_.refs_27_
  122.4 9.8 %collective-permute-done.15.refs_15_.refs_31_ = bf16[320,1280]{1,0:T(8,128)(2,1)} collective-permute-done((bf16[320,1280]{1,0:T(8,128)(2,1)}, bf16[320,1280]{1,0:T(8,128)(2,1)}, u32[]{:S(2)}, u32[]{:S(2)}) %collective-permute-start.15) | collective-permute-done | bytes 819232 | tf_op jit(solution)/shard_map/ppermute | solution.py:313
  135.0 3.4 %collective-permute-done.14.refs_14_.refs_30_ = bf16[320,1280]{1,0:T(8,128)(2,1)} collective-permute-done((bf16[320,1280]{1,0:T(8,128)(2,1)}, bf16[320,1280]{1,0:T(8,128)(2,1)}, u32[]{:S(2)}, u32[]{:S(2)}) %collective-permute-start.14) | collective-permute-done | bytes 819232 | tf_op jit(solution)/shard_map/ppermute | solution.py:313
  138.4 15.3 %shard_map.45 = (bf16[640,768]{1,0:T(8,128)(2,1)}, bf16[640,768]{1,0:T(8,128)(2,1)}, bf16[640,512]{1,0:T(8,128)(2,1)S(1)}, bf16[640,512]{1,0:T(8,128)(2,1)S(1)}) custom-call(s32[8]{0:T(128)S(1)} %dynamic-slice_bitcast_fusion.source_ref, s32[5]{0:T(128)S(1)} %copy-done.21, s32[2]{0:T(128)S(1)} %pad_add_fusion.place_ref, ...), custom_call_target="tpu_custom_call" | custom-call | bytes 1024 | tf_op jit(solution)/shard_map/pallas_call | solution.py:244
  157.4 6.3 %collective-permute-done.17.refs_1_ = bf16[320,1152]{1,0:T(8,128)(2,1)} collective-permute-done((bf16[320,1152]{1,0:T(8,128)(2,1)}, bf16[320,1152]{1,0:T(8,128)(2,1)}, u32[]{:S(2)}, u32[]{:S(2)}) %collective-permute-start.17) | collective-permute-done | bytes 737312 | tf_op jit(solution)/shard_map/ppermute | solution.py:307
  163.7 6.2 %collective-permute-done.16.refs_0_ = bf16[320,1152]{1,0:T(8,128)(2,1)} collective-permute-done((bf16[320,1152]{1,0:T(8,128)(2,1)}, bf16[320,1152]{1,0:T(8,128)(2,1)}, u32[]{:S(2)}, u32[]{:S(2)}) %collective-permute-start.16) | collective-permute-done | bytes 737312 | tf_op jit(solution)/shard_map/ppermute | solution.py:306
  172.0 13.7 %collective-permute-done.18.refs_0_ = bf16[320,1152]{1,0:T(8,128)(2,1)S(1)} collective-permute-done((bf16[320,1152]{1,0:T(8,128)(2,1)}, bf16[320,1152]{1,0:T(8,128)(2,1)S(1)}, u32[]{:S(2)}, u32[]{:S(2)}) %collective-permute-start.18) | collective-permute-done | bytes 737312 | tf_op jit(solution)/shard_map/ppermute | solution.py:306
  185.6 11.2 %shard_map.48 = (bf16[640,1280]{1,0:T(8,128)(2,1)}, bf16[640,1280]{1,0:T(8,128)(2,1)}) custom-call(s32[8]{0:T(128)S(1)} %dynamic-slice_bitcast_fusion.source_ref, s32[5]{0:T(128)S(1)} %copy-done.21, s32[2]{0:T(128)S(1)} %pad_add_fusion.place_ref, bf16[320,1280]{1,0:T(8,128)(2,1)} %get-tuple-element.37.refs_0_.refs_16_, ...), custom_call_target="tpu_custom_call" | custom-call | bytes 1024 | tf_op jit(solution)/shard_map/pallas_call | solution.py:244
  196.9 2.3 collective-permute-start.22
  205.7 2.4 add_convert_fusion.1.refs_1_
  210.2 7.9 %collective-permute-done.22.refs_0_ = bf16[320,1152]{1,0:T(8,128)(2,1)S(1)} collective-permute-done((bf16[320,1152]{1,0:T(8,128)(2,1)}, bf16[320,1152]{1,0:T(8,128)(2,1)S(1)}, u32[]{:S(2)}, u32[]{:S(2)}) %collective-permute-start.22) | collective-permute-done | bytes 737312 | tf_op jit(solution)/shard_map/ppermute | solution.py:306
  223.5 18.7 %collective-permute-done.30.refs_0_ = bf16[640,768]{1,0:T(8,128)(2,1)} collective-permute-done((bf16[640,768]{1,0:T(8,128)(2,1)}, bf16[640,768]{1,0:T(8,128)(2,1)}, u32[]{:S(2)}, u32[]{:S(2)}) %collective-permute-start.30) | collective-permute-done | bytes 983072 | tf_op jit(solution)/shard_map/ppermute | solution.py:340
  242.3 10.5 %collective-permute-done.28.refs_14_ = bf16[320,1152]{1,0:T(8,128)(2,1)} collective-permute-done((bf16[320,1152]{1,0:T(8,128)(2,1)}, bf16[320,1152]{1,0:T(8,128)(2,1)}, u32[]{:S(2)}, u32[]{:S(2)}) %collective-permute-start.28) | collective-permute-done | bytes 737312 | tf_op jit(solution)/shard_map/ppermute | solution.py:313
  253.9 9.3 %shard_map.57 = (bf16[640,768]{1,0:T(8,128)(2,1)}, bf16[640,768]{1,0:T(8,128)(2,1)}) custom-call(s32[8]{0:T(128)S(1)} %dynamic-slice_bitcast_fusion.source_ref, s32[5]{0:T(128)S(1)} %copy-done.21, s32[2]{0:T(128)S(1)} %pad_add_fusion.place_ref, bf16[320,1152]{1,0:T(8,128)(2,1)S(1)} %copy-done.11, bf16[320,1152]{1,0:T(8,128)(2,1)S(1)} %copy-done.9, ...), custom_call_target="tpu_custom_call" | custom-call | bytes 1024 | tf_op jit(solution)/shard_map/pallas_call | solution.py:244
  263.8 2.9 collective-permute-done.32
  266.7 2.5 add_convert_fusion.refs_32_
  269.2 9.9 %shard_map.58 = (bf16[640,512]{1,0:T(8,128)(2,1)S(1)}, bf16[640,512]{1,0:T(8,128)(2,1)S(1)}, bf16[640,1280]{1,0:T(8,128)(2,1)}) custom-call(s32[8]{0:T(128)S(1)} %dynamic-slice_bitcast_fusion.source_ref, s32[5]{0:T(128)S(1)} %copy-done.21, s32[2]{0:T(128)S(1)} %pad_add_fusion.place_ref, bf16[320,1152]{1,0:T(8,128)(2,1)S(1)} %copy-done.11, ...), custom_call_target="tpu_custom_call" | custom-call | bytes 1024 | tf_op jit(solution)/shard_map/pallas_call | solution.py:244
  280.6 3.7 %collective-permute-done.33 = bf16[640,512]{1,0:T(8,128)(2,1)S(1)} collective-permute-done((bf16[640,512]{1,0:T(8,128)(2,1)S(1)}, bf16[640,512]{1,0:T(8,128)(2,1)S(1)}, u32[]{:S(2)}, u32[]{:S(2)}) %collective-permute-start.33) | collective-permute-done | bytes 655392 | tf_op jit(solution)/shard_map/ppermute | solution.py:337
  285.4 19.8 %collective-permute-done.36.refs_0_ = bf16[640,768]{1,0:T(8,128)(2,1)} collective-permute-done((bf16[640,768]{1,0:T(8,128)(2,1)S(1)}, bf16[640,768]{1,0:T(8,128)(2,1)}, u32[]{:S(2)}, u32[]{:S(2)}) %collective-permute-start.36) | collective-permute-done | bytes 983072 | tf_op jit(solution)/shard_map/ppermute | solution.py:340
  305.2 7.6 %shard_map.60.refs_4_ = bf16[640,1280]{1,0:T(8,128)(2,1)} custom-call(s32[8]{0:T(128)S(1)} %dynamic-slice_bitcast_fusion.source_ref, s32[5]{0:T(128)S(1)} %copy-done.21, s32[2]{0:T(128)S(1)} %pad_add_fusion.place_ref, bf16[320,1152]{1,0:T(8,128)(2,1)S(1)} %copy-done.11, bf16[320,1152]{1,0:T(8,128)(2,1)S(1)} %copy-done.9, ...), custom_call_target="tpu_custom_call" | custom-call | bytes 1024 | tf_op jit(solution)/shard_map/pallas_call | solution.py:244
  312.9 6.1 %shard_map.61.refs_1_.before_ref = f32[640,1280]{1,0:T(8,128)} custom-call(bf16[640,768]{1,0:T(8,128)(2,1)} %shard_map.55.refs_32_.refs_0_, bf16[640,512]{1,0:T(8,128)(2,1)S(1)} %copy-done.17, bf16[640,1280]{1,0:T(8,128)(2,1)S(1)} %copy-done.7, bf16[640,1280]{1,0:T(8,128)(2,1)} %collective-permute-done.35.refs_3_, bf16[640,1280]{1,0:T(8,128)(2,1)} %shard_map.60.refs_4_, ...), custom_call_target="tpu_custom_call" | custom-call | bytes 1024 | tf_op jit(solution)/shard_map/pallas_call | solution.py:119
  319.8 2.4 shard_map.63
  (143 shorter events, 55.7 us)
Async XLA Ops:
  4.6 22.1 %collective-permute-start.7 = (bf16[320,1280]{1,0:T(8,128)(2,1)S(1)}, bf16[320,1280]{1,0:T(8,128)(2,1)S(1)}, u32[]{:S(2)}, u32[]{:S(2)}) collective-permute-start(bf16[320,1280]{1,0:T(8,128)(2,1)S(1)} %get-tuple-element.43.refs_1_.refs_17_), channel_id=1, source_target_pairs={{2,0},{4,2},{6,4},{7,6},{5,7},{3,5},{1,3},{0,1},{10,8},{12,10},{14... | collective-permute-start | bytes 2457608 | tf_op jit(solution)/shard_map/ppermute | solution.py:307
  13.1 31.2 %collective-permute-start.1 = (bf16[320,1280]{1,0:T(8,128)(2,1)}, bf16[320,1280]{1,0:T(8,128)(2,1)S(1)}, u32[]{:S(2)}, u32[]{:S(2)}) collective-permute-start(bf16[320,1280]{1,0:T(8,128)(2,1)} %get-tuple-element.37.refs_0_.refs_16_), channel_id=1, source_target_pairs={{2,0},{4,2},{6,4},{7,6},{5,7},{3,5},{1,3},{0,1},{10,8},{12,10},{14... | collective-permute-start | bytes 2457608 | tf_op jit(solution)/shard_map/ppermute | solution.py:307
  15.0 31.3 %collective-permute-start = (bf16[320,1280]{1,0:T(8,128)(2,1)}, bf16[320,1280]{1,0:T(8,128)(2,1)S(1)}, u32[]{:S(2)}, u32[]{:S(2)}) collective-permute-start(bf16[320,1280]{1,0:T(8,128)(2,1)} %get-tuple-element.37.refs_0_.refs_16_), channel_id=1, source_target_pairs={{0,2},{2,4},{4,6},{6,7},{7,5},{5,3},{3,1},{1,0},{8,10},{10,12},{12... | collective-permute-start | bytes 2457608 | tf_op jit(solution)/shard_map/ppermute | solution.py:306
  29.7 34.3 %collective-permute-start.8 = (bf16[320,1280]{1,0:T(8,128)(2,1)}, bf16[320,1280]{1,0:T(8,128)(2,1)}, u32[]{:S(2)}, u32[]{:S(2)}) collective-permute-start(bf16[320,1280]{1,0:T(8,128)(2,1)} %get-tuple-element.44.refs_3_.refs_19_), channel_id=1, source_target_pairs={{0,2},{2,4},{4,6},{6,7},{7,5},{5,3},{3,1},{1,0},{8,10},{10,12},{12... | collective-permute-start | bytes 2457608 | tf_op jit(solution)/shard_map/ppermute | solution.py:306
  30.6 33.4 %collective-permute-start.9 = (bf16[320,1280]{1,0:T(8,128)(2,1)}, bf16[320,1280]{1,0:T(8,128)(2,1)S(1)}, u32[]{:S(2)}, u32[]{:S(2)}) collective-permute-start(bf16[320,1280]{1,0:T(8,128)(2,1)} %get-tuple-element.45.refs_5_.refs_21_), channel_id=1, source_target_pairs={{2,0},{4,2},{6,4},{7,6},{5,7},{3,5},{1,3},{0,1},{10,8},{12,10},{14... | collective-permute-start | bytes 2457608 | tf_op jit(solution)/shard_map/ppermute | solution.py:307
  47.2 32.7 %collective-permute-start.2 = (bf16[320,1280]{1,0:T(8,128)(2,1)}, bf16[320,1280]{1,0:T(8,128)(2,1)S(1)}, u32[]{:S(2)}, u32[]{:S(2)}) collective-permute-start(bf16[320,1280]{1,0:T(8,128)(2,1)} %get-tuple-element.38.refs_2_.refs_18_), channel_id=1, source_target_pairs={{0,2},{2,4},{4,6},{6,7},{7,5},{5,3},{3,1},{1,0},{8,10},{10,12},{12... | collective-permute-start | bytes 2457608 | tf_op jit(solution)/shard_map/ppermute | solution.py:306
  48.1 31.8 %collective-permute-start.3 = (bf16[320,1280]{1,0:T(8,128)(2,1)}, bf16[320,1280]{1,0:T(8,128)(2,1)S(1)}, u32[]{:S(2)}, u32[]{:S(2)}) collective-permute-start(bf16[320,1280]{1,0:T(8,128)(2,1)} %get-tuple-element.39.refs_4_.refs_20_), channel_id=1, source_target_pairs={{2,0},{4,2},{6,4},{7,6},{5,7},{3,5},{1,3},{0,1},{10,8},{12,10},{14... | collective-permute-start | bytes 2457608 | tf_op jit(solution)/shard_map/ppermute | solution.py:307
  64.9 32.2 %collective-permute-start.11 = (bf16[320,1280]{1,0:T(8,128)(2,1)}, bf16[320,1280]{1,0:T(8,128)(2,1)}, u32[]{:S(2)}, u32[]{:S(2)}) collective-permute-start(bf16[320,1280]{1,0:T(8,128)(2,1)} %get-tuple-element.47.refs_9_.refs_25_), channel_id=1, source_target_pairs={{2,0},{4,2},{6,4},{7,6},{5,7},{3,5},{1,3},{0,1},{10,8},{12,10},{14... | collective-permute-start | bytes 2457608 | tf_op jit(solution)/shard_map/ppermute | solution.py:307
  81.7 21.5 %collective-permute-start.4 = (bf16[320,1280]{1,0:T(8,128)(2,1)}, bf16[320,1280]{1,0:T(8,128)(2,1)}, u32[]{:S(2)}, u32[]{:S(2)}) collective-permute-start(bf16[320,1280]{1,0:T(8,128)(2,1)} %get-tuple-element.40.refs_6_.refs_22_), channel_id=1, source_target_pairs={{0,2},{2,4},{4,6},{6,7},{7,5},{5,3},{3,1},{1,0},{8,10},{10,12},{12... | collective-permute-start | bytes 2457608 | tf_op jit(solution)/shard_map/ppermute | solution.py:306
  82.3 32.2 %collective-permute-start.5 = (bf16[320,1280]{1,0:T(8,128)(2,1)}, bf16[320,1280]{1,0:T(8,128)(2,1)S(1)}, u32[]{:S(2)}, u32[]{:S(2)}) collective-permute-start(bf16[320,1280]{1,0:T(8,128)(2,1)} %get-tuple-element.41.refs_8_.refs_24_), channel_id=1, source_target_pairs={{2,0},{4,2},{6,4},{7,6},{5,7},{3,5},{1,3},{0,1},{10,8},{12,10},{14... | collective-permute-start | bytes 2457608 | tf_op jit(solution)/shard_map/ppermute | solution.py:307
  83.8 37.0 %collective-permute-start.10 = (bf16[320,1280]{1,0:T(8,128)(2,1)}, bf16[320,1280]{1,0:T(8,128)(2,1)}, u32[]{:S(2)}, u32[]{:S(2)}) collective-permute-start(bf16[320,1280]{1,0:T(8,128)(2,1)} %get-tuple-element.46.refs_7_.refs_23_), channel_id=1, source_target_pairs={{0,2},{2,4},{4,6},{6,7},{7,5},{5,3},{3,1},{1,0},{8,10},{10,12},{12... | collective-permute-start | bytes 2457608 | tf_op jit(solution)/shard_map/ppermute | solution.py:306
  97.0 35.1 %collective-permute-start.15 = (bf16[320,1280]{1,0:T(8,128)(2,1)}, bf16[320,1280]{1,0:T(8,128)(2,1)}, u32[]{:S(2)}, u32[]{:S(2)}) collective-permute-start(bf16[320,1280]{1,0:T(8,128)(2,1)} %collective-permute-done.11.refs_2_.refs_13_.refs_29_), channel_id=1, source_target_pairs={{2,0},{4,2},{6,4},{7,6},{5,7},{3,5},{1,3},{0,1},{10,8},{12,10},{14... | collective-permute-start | bytes 2457608 | tf_op jit(solution)/shard_map/ppermute | solution.py:313
  103.2 35.1 %collective-permute-start.14 = (bf16[320,1280]{1,0:T(8,128)(2,1)}, bf16[320,1280]{1,0:T(8,128)(2,1)}, u32[]{:S(2)}, u32[]{:S(2)}) collective-permute-start(bf16[320,1280]{1,0:T(8,128)(2,1)} %collective-permute-done.4.refs_1_.refs_10_.refs_26_), channel_id=1, source_target_pairs={{0,2},{2,4},{4,6},{6,7},{7,5},{5,3},{3,1},{1,0},{8,10},{10,12},{12... | collective-permute-start | bytes 2457608 | tf_op jit(solution)/shard_map/ppermute | solution.py:313
  115.4 40.0 %collective-permute-start.13 = (bf16[320,1152]{1,0:T(8,128)(2,1)}, bf16[320,1152]{1,0:T(8,128)(2,1)}, u32[]{:S(2)}, u32[]{:S(2)}) collective-permute-start(bf16[320,1152]{1,0:T(8,128)(2,1)} %shard_map.40.refs_0_), channel_id=1, source_target_pairs={{2,0},{4,2},{6,4},{7,6},{5,7},{3,5},{1,3},{0,1},{10,8},{12,10},{14... | collective-permute-start | bytes 2211848 | tf_op jit(solution)/shard_map/ppermute | solution.py:307
  117.5 37.9 %collective-permute-start.12 = (bf16[320,1152]{1,0:T(8,128)(2,1)}, bf16[320,1152]{1,0:T(8,128)(2,1)}, u32[]{:S(2)}, u32[]{:S(2)}) collective-permute-start(bf16[320,1152]{1,0:T(8,128)(2,1)} %shard_map.40.refs_0_), channel_id=1, source_target_pairs={{0,2},{2,4},{4,6},{6,7},{7,5},{5,3},{3,1},{1,0},{8,10},{10,12},{12... | collective-permute-start | bytes 2211848 | tf_op jit(solution)/shard_map/ppermute | solution.py:306
  120.8 43.0 %collective-permute-start.17 = (bf16[320,1152]{1,0:T(8,128)(2,1)}, bf16[320,1152]{1,0:T(8,128)(2,1)}, u32[]{:S(2)}, u32[]{:S(2)}) collective-permute-start(bf16[320,1152]{1,0:T(8,128)(2,1)} %shard_map.44.refs_1_), channel_id=1, source_target_pairs={{2,0},{4,2},{6,4},{7,6},{5,7},{3,5},{1,3},{0,1},{10,8},{12,10},{14... | collective-permute-start | bytes 2211848 | tf_op jit(solution)/shard_map/ppermute | solution.py:307
  132.1 37.8 %collective-permute-start.16 = (bf16[320,1152]{1,0:T(8,128)(2,1)}, bf16[320,1152]{1,0:T(8,128)(2,1)}, u32[]{:S(2)}, u32[]{:S(2)}) collective-permute-start(bf16[320,1152]{1,0:T(8,128)(2,1)} %shard_map.44.refs_1_), channel_id=1, source_target_pairs={{0,2},{2,4},{4,6},{6,7},{7,5},{5,3},{3,1},{1,0},{8,10},{10,12},{12... | collective-permute-start | bytes 2211848 | tf_op jit(solution)/shard_map/ppermute | solution.py:306
  155.4 30.3 %collective-permute-start.18 = (bf16[320,1152]{1,0:T(8,128)(2,1)}, bf16[320,1152]{1,0:T(8,128)(2,1)S(1)}, u32[]{:S(2)}, u32[]{:S(2)}) collective-permute-start(bf16[320,1152]{1,0:T(8,128)(2,1)} %get-tuple-element.49.refs_32_.refs_1_.refs_2_), channel_id=1, source_target_pairs={{0,2},{2,4},{4,6},{6,7},{7,5},{5,3},{3,1},{1,0},{8,10},{10,12},{12... | collective-permute-start | bytes 2211848 | tf_op jit(solution)/shard_map/ppermute | solution.py:306
  155.4 41.5 %collective-permute-start.19 = (bf16[320,1152]{1,0:T(8,128)(2,1)}, bf16[320,1152]{1,0:T(8,128)(2,1)}, u32[]{:S(2)}, u32[]{:S(2)}) collective-permute-start(bf16[320,1152]{1,0:T(8,128)(2,1)} %get-tuple-element.51.refs_34_.refs_3_.refs_4_), channel_id=1, source_target_pairs={{2,0},{4,2},{6,4},{7,6},{5,7},{3,5},{1,3},{0,1},{10,8},{12,10},{14... | collective-permute-start | bytes 2211848 | tf_op jit(solution)/shard_map/ppermute | solution.py:307
  169.9 29.3 %collective-permute-start.20 = (bf16[320,1152]{1,0:T(8,128)(2,1)}, bf16[320,1152]{1,0:T(8,128)(2,1)}, u32[]{:S(2)}, u32[]{:S(2)}) collective-permute-start(bf16[320,1152]{1,0:T(8,128)(2,1)} %get-tuple-element.50.refs_33_.refs_2_.refs_3_), channel_id=1, source_target_pairs={{0,2},{2,4},{4,6},{6,7},{7,5},{5,3},{3,1},{1,0},{8,10},{10,12},{12... | collective-permute-start | bytes 2211848 | tf_op jit(solution)/shard_map/ppermute | solution.py:306
  170.5 28.7 %collective-permute-start.21 = (bf16[320,1152]{1,0:T(8,128)(2,1)}, bf16[320,1152]{1,0:T(8,128)(2,1)S(1)}, u32[]{:S(2)}, u32[]{:S(2)}) collective-permute-start(bf16[320,1152]{1,0:T(8,128)(2,1)} %get-tuple-element.52.refs_35_.refs_4_.refs_5_), channel_id=1, source_target_pairs={{2,0},{4,2},{6,4},{7,6},{5,7},{3,5},{1,3},{0,1},{10,8},{12,10},{14... | collective-permute-start | bytes 2211848 | tf_op jit(solution)/shard_map/ppermute | solution.py:307
  172.0 29.7 %collective-permute-start.24 = (bf16[640,512]{1,0:T(8,128)(2,1)}, bf16[640,512]{1,0:T(8,128)(2,1)}, u32[]{:S(2)}, u32[]{:S(2)}) collective-permute-start(bf16[640,512]{1,0:T(8,128)(2,1)} %shard_map.52), channel_id=1, source_target_pairs={{0,8},{8,0},{16,24},{24,16},{1,9},{9,1},{17,25},{25,17},{2,10},{10... | collective-permute-start | bytes 1966088 | tf_op jit(solution)/shard_map/ppermute | solution.py:337
  196.9 21.2 %collective-permute-start.22 = (bf16[320,1152]{1,0:T(8,128)(2,1)}, bf16[320,1152]{1,0:T(8,128)(2,1)S(1)}, u32[]{:S(2)}, u32[]{:S(2)}) collective-permute-start(bf16[320,1152]{1,0:T(8,128)(2,1)} %get-tuple-element.54.refs_6_), channel_id=1, source_target_pairs={{0,2},{2,4},{4,6},{6,7},{7,5},{5,3},{3,1},{1,0},{8,10},{10,12},{12... | collective-permute-start | bytes 2211848 | tf_op jit(solution)/shard_map/ppermute | solution.py:306
  208.1 34.1 %collective-permute-start.30 = (bf16[640,768]{1,0:T(8,128)(2,1)}, bf16[640,768]{1,0:T(8,128)(2,1)}, u32[]{:S(2)}, u32[]{:S(2)}) collective-permute-start(bf16[640,768]{1,0:T(8,128)(2,1)} %add_convert_fusion.1.refs_1_), channel_id=1, source_target_pairs={{0,16},{8,24},{16,0},{24,8},{1,17},{9,25},{17,1},{25,9},{2,18},{10... | collective-permute-start | bytes 2949128 | tf_op jit(solution)/shard_map/ppermute | solution.py:340
  208.2 34.0 %collective-permute-start.26 = (bf16[320,1152]{1,0:T(8,128)(2,1)}, bf16[320,1152]{1,0:T(8,128)(2,1)}, u32[]{:S(2)}, u32[]{:S(2)}) collective-permute-start(bf16[320,1152]{1,0:T(8,128)(2,1)} %get-tuple-element.56.refs_8_), channel_id=1, source_target_pairs={{2,0},{4,2},{6,4},{7,6},{5,7},{3,5},{1,3},{0,1},{10,8},{12,10},{14... | collective-permute-start | bytes 2211848 | tf_op jit(solution)/shard_map/ppermute | solution.py:307
  218.1 24.2 %collective-permute-start.25 = (bf16[320,1152]{1,0:T(8,128)(2,1)}, bf16[320,1152]{1,0:T(8,128)(2,1)}, u32[]{:S(2)}, u32[]{:S(2)}) collective-permute-start(bf16[320,1152]{1,0:T(8,128)(2,1)} %get-tuple-element.55.refs_7_), channel_id=1, source_target_pairs={{0,2},{2,4},{4,6},{6,7},{7,5},{5,3},{3,1},{1,0},{8,10},{10,12},{12... | collective-permute-start | bytes 2211848 | tf_op jit(solution)/shard_map/ppermute | solution.py:306
  219.7 33.1 %collective-permute-start.28 = (bf16[320,1152]{1,0:T(8,128)(2,1)}, bf16[320,1152]{1,0:T(8,128)(2,1)}, u32[]{:S(2)}, u32[]{:S(2)}) collective-permute-start(bf16[320,1152]{1,0:T(8,128)(2,1)} %shard_map.53.refs_10_), channel_id=1, source_target_pairs={{0,2},{2,4},{4,6},{6,7},{7,5},{5,3},{3,1},{1,0},{8,10},{10,12},{12... | collective-permute-start | bytes 2211848 | tf_op jit(solution)/shard_map/ppermute | solution.py:313
  221.6 31.2 %collective-permute-start.29 = (bf16[320,1152]{1,0:T(8,128)(2,1)}, bf16[320,1152]{1,0:T(8,128)(2,1)}, u32[]{:S(2)}, u32[]{:S(2)}) collective-permute-start(bf16[320,1152]{1,0:T(8,128)(2,1)} %shard_map.54.refs_13_), channel_id=1, source_target_pairs={{2,0},{4,2},{6,4},{7,6},{5,7},{3,5},{1,3},{0,1},{10,8},{12,10},{14... | collective-permute-start | bytes 2211848 | tf_op jit(solution)/shard_map/ppermute | solution.py:313
  263.3 49.5 %collective-permute-start.35 = (bf16[640,1280]{1,0:T(8,128)(2,1)}, bf16[640,1280]{1,0:T(8,128)(2,1)}, u32[]{:S(2)}, u32[]{:S(2)}) collective-permute-start(bf16[640,1280]{1,0:T(8,128)(2,1)} %get-tuple-element.65), channel_id=1, source_target_pairs={{0,8},{8,0},{16,24},{24,16},{1,9},{9,1},{17,25},{25,17},{2,10},{10... | collective-permute-start | bytes 4915208 | tf_op jit(solution)/shard_map/ppermute | solution.py:337
  279.1 33.8 %collective-permute-start.37 = (bf16[640,1280]{1,0:T(8,128)(2,1)}, bf16[640,1280]{1,0:T(8,128)(2,1)}, u32[]{:S(2)}, u32[]{:S(2)}) collective-permute-start(bf16[640,1280]{1,0:T(8,128)(2,1)} %get-tuple-element.66), channel_id=1, source_target_pairs={{0,8},{8,0},{16,24},{24,16},{1,9},{9,1},{17,25},{25,17},{2,10},{10... | collective-permute-start | bytes 4915208 | tf_op jit(solution)/shard_map/ppermute | solution.py:337
  280.5 24.7 %collective-permute-start.36 = (bf16[640,768]{1,0:T(8,128)(2,1)S(1)}, bf16[640,768]{1,0:T(8,128)(2,1)}, u32[]{:S(2)}, u32[]{:S(2)}) collective-permute-start(bf16[640,768]{1,0:T(8,128)(2,1)S(1)} %copy-done.31), channel_id=1, source_target_pairs={{0,16},{8,24},{16,0},{24,8},{1,17},{9,25},{17,1},{25,9},{2,18},{10... | collective-permute-start | bytes 2949128 | tf_op jit(solution)/shard_map/ppermute | solution.py:340
  285.4 33.5 %collective-permute-start.34 = (bf16[640,512]{1,0:T(8,128)(2,1)}, bf16[640,512]{1,0:T(8,128)(2,1)S(1)}, u32[]{:S(2)}, u32[]{:S(2)}) collective-permute-start(bf16[640,512]{1,0:T(8,128)(2,1)} %add_convert_fusion.2.refs_32_), channel_id=1, source_target_pairs={{0,16},{8,24},{16,0},{24,8},{1,17},{9,25},{17,1},{25,9},{2,18},{10... | collective-permute-start | bytes 1966088 | tf_op jit(solution)/shard_map/ppermute | solution.py:340
  (39 other events, 541.1 us)

commit v8 on v7

--- a/solution.py
+++ b/solution.py
@@ -351,11 +351,10 @@
             if d == 1:
                 return [before[-3][half], before[-2][half]]
             n = d - 2
-            if half == 0 and n < chips:
+            if half == 0 and n < chips - 1:
                 late = [*got[2 * n - 1], *got[2 * n]] if n else ()
-                parts = cut if aways[n] else ((0, chunk),)
-                shares.append(share(a - 1, [(aways[n], flip, *part) for part in parts for flip in (0, 1)], late))
-            waits = [shares[n][0]] if n < chips else []
+                shares.append(share(a - 1, [(aways[n], flip, *part) for part in cut for flip in (0, 1)], late))
+            waits = [shares[n][0]] if n < chips - 1 else []
             if (d, half) == (reach, 0):
                 for m, (away, arrays) in enumerate(zip(aways[:-1], shares)):
                     hold = [*got[2 * m + 1], *got[2 * m + 2]]
@@ -369,8 +368,8 @@
         for summed, d, start in sums:
             terms.append(send(summed, d, SHORT))
             starts.append(start)
-        same, other = shares[-1]
-        gone = list(terms)
+        same, other = share(a - 1, [(0, flip, 0, chunk) for flip in (0, 1)], [*everything[a][-3], *everything[a][-2]])
+        gone = [*terms, same]
         terms += [same, cross(other)]
         starts += [None, None]
     last = local_subjects - 1
@@ -383,13 +382,13 @@
         starts.append(None)
     d = aways[-2]
     same, other = share(last, [(d, 0, 0, early), (d, 1, 0, early)], late)
+    leading = added(same, cross(other))
+    rest = chunk - early
+    other, same, others = share(last, [(d, 1, early, rest), (d, 0, early, rest), (0, 1, 0, chunk)], [leading])
     summed = added(same, cross(other))
-    there = send(summed, d, LONG)
-    rest = chunk - early
-    other, same, others = share(last, [(d, 1, early, rest), (d, 0, early, rest), (0, 1, 0, chunk)], [summed])
-    summed = added(same, cross(other))
-    (same,) = share(last, [(0, 0, 0, chunk)], [summed, there])
-    terms += [same, cross(others), there]
+    (same,) = share(last, [(0, 0, 0, chunk)], [summed])
+    there = send(leading, d, LONG, [same])
+    terms += [same, cross(others, [there]), there]
     starts += [None, None, 0]
     out = combine(terms, starts, slab, chunk, scale)
     return finish(send(summed, d, LONG, [out]), out, early, scale)

time: 323 us -> 313 us (0.969)
  waiting for transfers between devices: 190 us -> 177 us
    ppermute x4, waiting for transfers between devices: 38.5 us -> 7.79 us  [send(): lax.ppermute(summed, 'subj', [(s, (s + 2 * d) % subjs) for s in range(sub...]
    ppermute x12, waiting for transfers between devices: 54.5 us -> 72.5 us  [gather(): got[-1][half] = lax.ppermute(behind[half], SLABS, backward)]
    ppermute x4, waiting for transfers between devices: 23.7 us -> 13.2 us  [gather(): last.append(lax.ppermute(got[side][half], SLABS, way))]
    ppermute x12, waiting for transfers between devices: 66.6 us -> 76.4 us  [gather(): got[-2][half] = lax.ppermute(ahead[half], SLABS, onward)]
    unnamed x66 -> x62, local copies, waits for them, and re-layouts: 13.4 us -> 15.9 us
  transfers between devices with their start and end apart: 38 -> 38, of which waited for: 22 -> 24; matrix products, arithmetic and copies ran while one was open for 3% -> 2% of each run, Pallas kernels for 17% -> 18%
where the time goes in v8:
time: 313 us; the launch traced here: 311 us
  waiting for transfers between devices  177 us (57%)
  Pallas kernels  71.8 us (23%)
  starting transfers between devices  38.1 us (12%)
  local copies, waits for them, and re-layouts  16.5 us (5%)
  other arithmetic  7.49 us (2%)
    ppermute x12, waiting for transfers between devices, gather(): got[-2][half] = lax.ppermute(ahead[half], SLABS, onward)  76.4 us
    ppermute x12, waiting for transfers between devices, gather(): got[-1][half] = lax.ppermute(behind[half], SLABS, backward)  72.5 us
    pallas_call x5, Pallas kernels, scores(): pl.pallas_call(functools.partial(scores_kernel, subject=subject, targets=...  54.9 us
    ppermute x12, starting transfers between devices, gather(): got[-1][half] = lax.ppermute(behind[half], SLABS, backward)  19.9 us
    unnamed x62, local copies, waits for them, and re-layouts  15.9 us
    ppermute x4, waiting for transfers between devices, gather(): last.append(lax.ppermute(got[side][half], SLABS, way))  13.2 us
    pallas_call x2, Pallas kernels, normalize(): pl.pallas_call(functools.partial(normalize_kernel, begin=low, lead=begin...  8.36 us
    ppermute x4, waiting for transfers between devices, send(): lax.ppermute(summed, 'subj', [(s, (s + 2 * d) % subjs) for s in range(sub...  7.79 us
  transfers between devices with their start and end apart: 38, of which 24 were waited for; matrix products, arithmetic and copies ran while one was open for 2% of the time, Pallas kernels for 18%

profile of v8, /device:TPU:0, one launch (start us, length us, event | category | flops | bytes accessed | tf_op | source)
XLA Modules:
  0.0 311.3 jit_solution(453494655770935977)
XLA Ops:
  0.0 3.7 %shard_map.41 = (bf16[320,1280]{1,0:T(8,128)(2,1)S(1)}, bf16[320,1152]{1,0:T(8,128)(2,1)S(1)}) custom-call(f32[2,1200,640]{2,1,0:T(8,128)} %bitcast.5), custom_call_target="tpu_custom_call" | custom-call | bytes 1024 | tf_op jit(solution)/shard_map/pallas_call | solution.py:76
  4.6 3.0 collective-permute-start.7
  7.7 4.6 %shard_map.37 = (bf16[320,1280]{1,0:T(8,128)(2,1)}, bf16[320,1152]{1,0:T(8,128)(2,1)S(1)}) custom-call(f32[2,1200,640]{2,1,0:T(8,128)} %bitcast.6), custom_call_target="tpu_custom_call" | custom-call | bytes 1024 | tf_op jit(solution)/shard_map/pallas_call | solution.py:76
  15.2 11.5 %collective-permute-done.7.refs_1_ = bf16[320,1280]{1,0:T(8,128)(2,1)S(1)} collective-permute-done((bf16[320,1280]{1,0:T(8,128)(2,1)S(1)}, bf16[320,1280]{1,0:T(8,128)(2,1)S(1)}, u32[]{:S(2)}, u32[]{:S(2)}) %collective-permute-start.7) | collective-permute-done | bytes 819232 | tf_op jit(solution)/shard_map/ppermute | solution.py:307
  31.7 12.6 %collective-permute-done.1.refs_1_ = bf16[320,1280]{1,0:T(8,128)(2,1)S(1)} collective-permute-done((bf16[320,1280]{1,0:T(8,128)(2,1)}, bf16[320,1280]{1,0:T(8,128)(2,1)S(1)}, u32[]{:S(2)}, u32[]{:S(2)}) %collective-permute-start.1) | collective-permute-done | bytes 819232 | tf_op jit(solution)/shard_map/ppermute | solution.py:307
  49.3 14.7 %collective-permute-done.8.refs_0_ = bf16[320,1280]{1,0:T(8,128)(2,1)} collective-permute-done((bf16[320,1280]{1,0:T(8,128)(2,1)}, bf16[320,1280]{1,0:T(8,128)(2,1)}, u32[]{:S(2)}, u32[]{:S(2)}) %collective-permute-start.8) | collective-permute-done | bytes 819232 | tf_op jit(solution)/shard_map/ppermute | solution.py:306
  66.5 13.5 %collective-permute-done.2.refs_0_ = bf16[320,1280]{1,0:T(8,128)(2,1)S(1)} collective-permute-done((bf16[320,1280]{1,0:T(8,128)(2,1)}, bf16[320,1280]{1,0:T(8,128)(2,1)S(1)}, u32[]{:S(2)}, u32[]{:S(2)}) %collective-permute-start.2) | collective-permute-done | bytes 819232 | tf_op jit(solution)/shard_map/ppermute | solution.py:306
  84.4 12.7 %collective-permute-done.11.refs_2_.refs_13_.refs_29_ = bf16[320,1280]{1,0:T(8,128)(2,1)} collective-permute-done((bf16[320,1280]{1,0:T(8,128)(2,1)}, bf16[320,1280]{1,0:T(8,128)(2,1)}, u32[]{:S(2)}, u32[]{:S(2)}) %collective-permute-start.11) | collective-permute-done | bytes 819232 | tf_op jit(solution)/shard_map/ppermute | solution.py:307
  99.1 4.2 %collective-permute-done.4.refs_1_.refs_10_.refs_26_ = bf16[320,1280]{1,0:T(8,128)(2,1)} collective-permute-done((bf16[320,1280]{1,0:T(8,128)(2,1)}, bf16[320,1280]{1,0:T(8,128)(2,1)}, u32[]{:S(2)}, u32[]{:S(2)}) %collective-permute-start.4) | collective-permute-done | bytes 819232 | tf_op jit(solution)/shard_map/ppermute | solution.py:306
  103.9 10.6 %collective-permute-done.5.refs_2_.refs_12_.refs_28_ = bf16[320,1280]{1,0:T(8,128)(2,1)S(1)} collective-permute-done((bf16[320,1280]{1,0:T(8,128)(2,1)}, bf16[320,1280]{1,0:T(8,128)(2,1)S(1)}, u32[]{:S(2)}, u32[]{:S(2)}) %collective-permute-start.5) | collective-permute-done | bytes 819232 | tf_op jit(solution)/shard_map/ppermute | solution.py:307
  117.6 3.2 %collective-permute-done.10.refs_1_.refs_11_.refs_27_ = bf16[320,1280]{1,0:T(8,128)(2,1)} collective-permute-done((bf16[320,1280]{1,0:T(8,128)(2,1)}, bf16[320,1280]{1,0:T(8,128)(2,1)}, u32[]{:S(2)}, u32[]{:S(2)}) %collective-permute-start.10) | collective-permute-done | bytes 819232 | tf_op jit(solution)/shard_map/ppermute | solution.py:306
  122.4 9.7 %collective-permute-done.15.refs_15_.refs_31_ = bf16[320,1280]{1,0:T(8,128)(2,1)} collective-permute-done((bf16[320,1280]{1,0:T(8,128)(2,1)}, bf16[320,1280]{1,0:T(8,128)(2,1)}, u32[]{:S(2)}, u32[]{:S(2)}) %collective-permute-start.15) | collective-permute-done | bytes 819232 | tf_op jit(solution)/shard_map/ppermute | solution.py:313
  135.0 3.4 %collective-permute-done.14.refs_14_.refs_30_ = bf16[320,1280]{1,0:T(8,128)(2,1)} collective-permute-done((bf16[320,1280]{1,0:T(8,128)(2,1)}, bf16[320,1280]{1,0:T(8,128)(2,1)}, u32[]{:S(2)}, u32[]{:S(2)}) %collective-permute-start.14) | collective-permute-done | bytes 819232 | tf_op jit(solution)/shard_map/ppermute | solution.py:313
  138.4 14.1 %shard_map.45 = (bf16[640,768]{1,0:T(8,128)(2,1)}, bf16[640,768]{1,0:T(8,128)(2,1)}, bf16[640,512]{1,0:T(8,128)(2,1)S(1)}, bf16[640,512]{1,0:T(8,128)(2,1)S(1)}) custom-call(s32[8]{0:T(128)S(1)} %dynamic-slice_bitcast_fusion.source_ref, s32[5]{0:T(128)S(1)} %copy-done.23, s32[2]{0:T(128)S(1)} %pad_add_fusion.place_ref, ...), custom_call_target="tpu_custom_call" | custom-call | bytes 1024 | tf_op jit(solution)/shard_map/pallas_call | solution.py:244
  156.2 7.5 %collective-permute-done.17.refs_1_ = bf16[320,1152]{1,0:T(8,128)(2,1)} collective-permute-done((bf16[320,1152]{1,0:T(8,128)(2,1)}, bf16[320,1152]{1,0:T(8,128)(2,1)}, u32[]{:S(2)}, u32[]{:S(2)}) %collective-permute-start.17) | collective-permute-done | bytes 737312 | tf_op jit(solution)/shard_map/ppermute | solution.py:307
  163.8 6.2 %collective-permute-done.16.refs_0_ = bf16[320,1152]{1,0:T(8,128)(2,1)} collective-permute-done((bf16[320,1152]{1,0:T(8,128)(2,1)}, bf16[320,1152]{1,0:T(8,128)(2,1)}, u32[]{:S(2)}, u32[]{:S(2)}) %collective-permute-start.16) | collective-permute-done | bytes 737312 | tf_op jit(solution)/shard_map/ppermute | solution.py:306
  172.0 13.7 %collective-permute-done.18.refs_0_ = bf16[320,1152]{1,0:T(8,128)(2,1)S(1)} collective-permute-done((bf16[320,1152]{1,0:T(8,128)(2,1)}, bf16[320,1152]{1,0:T(8,128)(2,1)S(1)}, u32[]{:S(2)}, u32[]{:S(2)}) %collective-permute-start.18) | collective-permute-done | bytes 737312 | tf_op jit(solution)/shard_map/ppermute | solution.py:306
  187.1 14.5 %collective-permute-done.20.refs_0_ = bf16[320,1152]{1,0:T(8,128)(2,1)} collective-permute-done((bf16[320,1152]{1,0:T(8,128)(2,1)}, bf16[320,1152]{1,0:T(8,128)(2,1)}, u32[]{:S(2)}, u32[]{:S(2)}) %collective-permute-start.20) | collective-permute-done | bytes 737312 | tf_op jit(solution)/shard_map/ppermute | solution.py:306
  203.2 2.3 add_convert_fusion.3.refs_2_
  207.0 2.7 add_convert_fusion.1.refs_1_
  211.8 3.2 %collective-permute-done.22.refs_0_ = bf16[320,1152]{1,0:T(8,128)(2,1)S(1)} collective-permute-done((bf16[320,1152]{1,0:T(8,128)(2,1)}, bf16[320,1152]{1,0:T(8,128)(2,1)S(1)}, u32[]{:S(2)}, u32[]{:S(2)}) %collective-permute-start.22) | collective-permute-done | bytes 737312 | tf_op jit(solution)/shard_map/ppermute | solution.py:306
  215.8 5.4 %collective-permute-done.27.refs_0_ = bf16[320,1152]{1,0:T(8,128)(2,1)S(1)} collective-permute-done((bf16[320,1152]{1,0:T(8,128)(2,1)}, bf16[320,1152]{1,0:T(8,128)(2,1)S(1)}, u32[]{:S(2)}, u32[]{:S(2)}) %collective-permute-start.27) | collective-permute-done | bytes 737312 | tf_op jit(solution)/shard_map/ppermute | solution.py:307
  225.0 12.1 %collective-permute-done.26.refs_34_.refs_12_ = bf16[320,1152]{1,0:T(8,128)(2,1)} collective-permute-done((bf16[320,1152]{1,0:T(8,128)(2,1)}, bf16[320,1152]{1,0:T(8,128)(2,1)}, u32[]{:S(2)}, u32[]{:S(2)}) %collective-permute-start.26) | collective-permute-done | bytes 737312 | tf_op jit(solution)/shard_map/ppermute | solution.py:307
  237.2 12.6 %shard_map.56 = (bf16[640,1280]{1,0:T(8,128)(2,1)}, bf16[640,1280]{1,0:T(8,128)(2,1)}) custom-call(s32[8]{0:T(128)S(1)} %dynamic-slice_bitcast_fusion.source_ref, s32[5]{0:T(128)S(1)} %copy-done.23, s32[2]{0:T(128)S(1)} %pad_add_fusion.place_ref, bf16[320,1280]{1,0:T(8,128)(2,1)} %get-tuple-element.37.refs_0_.refs_16_, ...), custom_call_target="tpu_custom_call" | custom-call | bytes 1024 | tf_op jit(solution)/shard_map/pallas_call | solution.py:244
  252.2 8.7 %shard_map.57 = (bf16[640,768]{1,0:T(8,128)(2,1)}, bf16[640,768]{1,0:T(8,128)(2,1)}) custom-call(s32[8]{0:T(128)S(1)} %dynamic-slice_bitcast_fusion.source_ref, s32[5]{0:T(128)S(1)} %copy-done.23, s32[2]{0:T(128)S(1)} %pad_add_fusion.place_ref, bf16[320,1152]{1,0:T(8,128)(2,1)S(1)} %copy-done.14, bf16[320,1152]{1,0:T(8,128)(2,1)S(1)} %copy-done.12, ...), custom_call_target="tpu_custom_call" | custom-call | bytes 1024 | tf_op jit(solution)/shard_map/pallas_call | solution.py:244
  261.0 2.8 collective-permute-done.32
  267.5 11.5 %shard_map.58 = (bf16[640,512]{1,0:T(8,128)(2,1)S(1)}, bf16[640,512]{1,0:T(8,128)(2,1)S(1)}, bf16[640,1280]{1,0:T(8,128)(2,1)}) custom-call(s32[8]{0:T(128)S(1)} %dynamic-slice_bitcast_fusion.source_ref, s32[5]{0:T(128)S(1)} %copy-done.23, s32[2]{0:T(128)S(1)} %pad_add_fusion.place_ref, bf16[320,1152]{1,0:T(8,128)(2,1)S(1)} %copy-done.14, ...), custom_call_target="tpu_custom_call" | custom-call | bytes 1024 | tf_op jit(solution)/shard_map/pallas_call | solution.py:244
  282.3 8.1 %shard_map.59.refs_1_.refs_4_ = bf16[640,1280]{1,0:T(8,128)(2,1)} custom-call(s32[8]{0:T(128)S(1)} %dynamic-slice_bitcast_fusion.source_ref, s32[5]{0:T(128)S(1)} %copy-done.23, s32[2]{0:T(128)S(1)} %pad_add_fusion.place_ref, bf16[320,1152]{1,0:T(8,128)(2,1)S(1)} %copy-done.14, bf16[320,1152]{1,0:T(8,128)(2,1)S(1)} %copy-done.12, ...), custom_call_target="tpu_custom_call" | custom-call | bytes 1024 | tf_op jit(solution)/shard_map/pallas_call | solution.py:244
  292.4 2.8 collective-permute-done.37.refs_5_
  296.4 6.1 %shard_map.62.refs_1_.before_ref = f32[640,1280]{1,0:T(8,128)} custom-call(bf16[640,768]{1,0:T(8,128)(2,1)} %shard_map.54.refs_32_.refs_0_, bf16[640,512]{1,0:T(8,128)(2,1)} %shard_map.55.refs_33_.refs_1_, bf16[640,1280]{1,0:T(8,128)(2,1)S(1)} %copy-done.20, bf16[640,1280]{1,0:T(8,128)(2,1)} %collective-permute-done.35.refs_3_, ...), custom_call_target="tpu_custom_call" | custom-call | bytes 1024 | tf_op jit(solution)/shard_map/pallas_call | solution.py:119
  302.5 6.4 %collective-permute-done.34.refs_0_ = bf16[640,512]{1,0:T(8,128)(2,1)} collective-permute-done((bf16[640,512]{1,0:T(8,128)(2,1)}, bf16[640,512]{1,0:T(8,128)(2,1)}, u32[]{:S(2)}, u32[]{:S(2)}) %collective-permute-start.34) | collective-permute-done | bytes 655392 | tf_op jit(solution)/shard_map/ppermute | solution.py:340
  308.9 2.4 shard_map.64
  (140 shorter events, 60.5 us)
Async XLA Ops:
  4.6 22.1 %collective-permute-start.7 = (bf16[320,1280]{1,0:T(8,128)(2,1)S(1)}, bf16[320,1280]{1,0:T(8,128)(2,1)S(1)}, u32[]{:S(2)}, u32[]{:S(2)}) collective-permute-start(bf16[320,1280]{1,0:T(8,128)(2,1)S(1)} %get-tuple-element.43.refs_1_.refs_17_), channel_id=1, source_target_pairs={{2,0},{4,2},{6,4},{7,6},{5,7},{3,5},{1,3},{0,1},{10,8},{12,10},{14... | collective-permute-start | bytes 2457608 | tf_op jit(solution)/shard_map/ppermute | solution.py:307
  7.6 21.2 %collective-permute-start.6 = (bf16[320,1280]{1,0:T(8,128)(2,1)S(1)}, bf16[320,1280]{1,0:T(8,128)(2,1)S(1)}, u32[]{:S(2)}, u32[]{:S(2)}) collective-permute-start(bf16[320,1280]{1,0:T(8,128)(2,1)S(1)} %get-tuple-element.43.refs_1_.refs_17_), channel_id=1, source_target_pairs={{0,2},{2,4},{4,6},{6,7},{7,5},{5,3},{3,1},{1,0},{8,10},{10,12},{12... | collective-permute-start | bytes 2457608 | tf_op jit(solution)/shard_map/ppermute | solution.py:306
  13.2 31.1 %collective-permute-start.1 = (bf16[320,1280]{1,0:T(8,128)(2,1)}, bf16[320,1280]{1,0:T(8,128)(2,1)S(1)}, u32[]{:S(2)}, u32[]{:S(2)}) collective-permute-start(bf16[320,1280]{1,0:T(8,128)(2,1)} %get-tuple-element.37.refs_0_.refs_16_), channel_id=1, source_target_pairs={{2,0},{4,2},{6,4},{7,6},{5,7},{3,5},{1,3},{0,1},{10,8},{12,10},{14... | collective-permute-start | bytes 2457608 | tf_op jit(solution)/shard_map/ppermute | solution.py:307
  15.1 31.2 %collective-permute-start = (bf16[320,1280]{1,0:T(8,128)(2,1)}, bf16[320,1280]{1,0:T(8,128)(2,1)S(1)}, u32[]{:S(2)}, u32[]{:S(2)}) collective-permute-start(bf16[320,1280]{1,0:T(8,128)(2,1)} %get-tuple-element.37.refs_0_.refs_16_), channel_id=1, source_target_pairs={{0,2},{2,4},{4,6},{6,7},{7,5},{5,3},{3,1},{1,0},{8,10},{10,12},{12... | collective-permute-start | bytes 2457608 | tf_op jit(solution)/shard_map/ppermute | solution.py:306
  29.7 34.3 %collective-permute-start.8 = (bf16[320,1280]{1,0:T(8,128)(2,1)}, bf16[320,1280]{1,0:T(8,128)(2,1)}, u32[]{:S(2)}, u32[]{:S(2)}) collective-permute-start(bf16[320,1280]{1,0:T(8,128)(2,1)} %get-tuple-element.44.refs_3_.refs_19_), channel_id=1, source_target_pairs={{0,2},{2,4},{4,6},{6,7},{7,5},{5,3},{3,1},{1,0},{8,10},{10,12},{12... | collective-permute-start | bytes 2457608 | tf_op jit(solution)/shard_map/ppermute | solution.py:306
  30.6 33.4 %collective-permute-start.9 = (bf16[320,1280]{1,0:T(8,128)(2,1)}, bf16[320,1280]{1,0:T(8,128)(2,1)S(1)}, u32[]{:S(2)}, u32[]{:S(2)}) collective-permute-start(bf16[320,1280]{1,0:T(8,128)(2,1)} %get-tuple-element.45.refs_5_.refs_21_), channel_id=1, source_target_pairs={{2,0},{4,2},{6,4},{7,6},{5,7},{3,5},{1,3},{0,1},{10,8},{12,10},{14... | collective-permute-start | bytes 2457608 | tf_op jit(solution)/shard_map/ppermute | solution.py:307
  47.2 32.7 %collective-permute-start.2 = (bf16[320,1280]{1,0:T(8,128)(2,1)}, bf16[320,1280]{1,0:T(8,128)(2,1)S(1)}, u32[]{:S(2)}, u32[]{:S(2)}) collective-permute-start(bf16[320,1280]{1,0:T(8,128)(2,1)} %get-tuple-element.38.refs_2_.refs_18_), channel_id=1, source_target_pairs={{0,2},{2,4},{4,6},{6,7},{7,5},{5,3},{3,1},{1,0},{8,10},{10,12},{12... | collective-permute-start | bytes 2457608 | tf_op jit(solution)/shard_map/ppermute | solution.py:306
  48.2 31.8 %collective-permute-start.3 = (bf16[320,1280]{1,0:T(8,128)(2,1)}, bf16[320,1280]{1,0:T(8,128)(2,1)S(1)}, u32[]{:S(2)}, u32[]{:S(2)}) collective-permute-start(bf16[320,1280]{1,0:T(8,128)(2,1)} %get-tuple-element.39.refs_4_.refs_20_), channel_id=1, source_target_pairs={{2,0},{4,2},{6,4},{7,6},{5,7},{3,5},{1,3},{0,1},{10,8},{12,10},{14... | collective-permute-start | bytes 2457608 | tf_op jit(solution)/shard_map/ppermute | solution.py:307
  64.9 32.1 %collective-permute-start.11 = (bf16[320,1280]{1,0:T(8,128)(2,1)}, bf16[320,1280]{1,0:T(8,128)(2,1)}, u32[]{:S(2)}, u32[]{:S(2)}) collective-permute-start(bf16[320,1280]{1,0:T(8,128)(2,1)} %get-tuple-element.47.refs_9_.refs_25_), channel_id=1, source_target_pairs={{2,0},{4,2},{6,4},{7,6},{5,7},{3,5},{1,3},{0,1},{10,8},{12,10},{14... | collective-permute-start | bytes 2457608 | tf_op jit(solution)/shard_map/ppermute | solution.py:307
  81.8 21.5 %collective-permute-start.4 = (bf16[320,1280]{1,0:T(8,128)(2,1)}, bf16[320,1280]{1,0:T(8,128)(2,1)}, u32[]{:S(2)}, u32[]{:S(2)}) collective-permute-start(bf16[320,1280]{1,0:T(8,128)(2,1)} %get-tuple-element.40.refs_6_.refs_22_), channel_id=1, source_target_pairs={{0,2},{2,4},{4,6},{6,7},{7,5},{5,3},{3,1},{1,0},{8,10},{10,12},{12... | collective-permute-start | bytes 2457608 | tf_op jit(solution)/shard_map/ppermute | solution.py:306
  82.4 32.1 %collective-permute-start.5 = (bf16[320,1280]{1,0:T(8,128)(2,1)}, bf16[320,1280]{1,0:T(8,128)(2,1)S(1)}, u32[]{:S(2)}, u32[]{:S(2)}) collective-permute-start(bf16[320,1280]{1,0:T(8,128)(2,1)} %get-tuple-element.41.refs_8_.refs_24_), channel_id=1, source_target_pairs={{2,0},{4,2},{6,4},{7,6},{5,7},{3,5},{1,3},{0,1},{10,8},{12,10},{14... | collective-permute-start | bytes 2457608 | tf_op jit(solution)/shard_map/ppermute | solution.py:307
  83.8 37.0 %collective-permute-start.10 = (bf16[320,1280]{1,0:T(8,128)(2,1)}, bf16[320,1280]{1,0:T(8,128)(2,1)}, u32[]{:S(2)}, u32[]{:S(2)}) collective-permute-start(bf16[320,1280]{1,0:T(8,128)(2,1)} %get-tuple-element.46.refs_7_.refs_23_), channel_id=1, source_target_pairs={{0,2},{2,4},{4,6},{6,7},{7,5},{5,3},{3,1},{1,0},{8,10},{10,12},{12... | collective-permute-start | bytes 2457608 | tf_op jit(solution)/shard_map/ppermute | solution.py:306
  97.1 35.1 %collective-permute-start.15 = (bf16[320,1280]{1,0:T(8,128)(2,1)}, bf16[320,1280]{1,0:T(8,128)(2,1)}, u32[]{:S(2)}, u32[]{:S(2)}) collective-permute-start(bf16[320,1280]{1,0:T(8,128)(2,1)} %collective-permute-done.11.refs_2_.refs_13_.refs_29_), channel_id=1, source_target_pairs={{2,0},{4,2},{6,4},{7,6},{5,7},{3,5},{1,3},{0,1},{10,8},{12,10},{14... | collective-permute-start | bytes 2457608 | tf_op jit(solution)/shard_map/ppermute | solution.py:313
  103.3 35.1 %collective-permute-start.14 = (bf16[320,1280]{1,0:T(8,128)(2,1)}, bf16[320,1280]{1,0:T(8,128)(2,1)}, u32[]{:S(2)}, u32[]{:S(2)}) collective-permute-start(bf16[320,1280]{1,0:T(8,128)(2,1)} %collective-permute-done.4.refs_1_.refs_10_.refs_26_), channel_id=1, source_target_pairs={{0,2},{2,4},{4,6},{6,7},{7,5},{5,3},{3,1},{1,0},{8,10},{10,12},{12... | collective-permute-start | bytes 2457608 | tf_op jit(solution)/shard_map/ppermute | solution.py:313
  115.4 38.7 %collective-permute-start.13 = (bf16[320,1152]{1,0:T(8,128)(2,1)}, bf16[320,1152]{1,0:T(8,128)(2,1)}, u32[]{:S(2)}, u32[]{:S(2)}) collective-permute-start(bf16[320,1152]{1,0:T(8,128)(2,1)} %shard_map.40.refs_0_), channel_id=1, source_target_pairs={{2,0},{4,2},{6,4},{7,6},{5,7},{3,5},{1,3},{0,1},{10,8},{12,10},{14... | collective-permute-start | bytes 2211848 | tf_op jit(solution)/shard_map/ppermute | solution.py:307
  117.5 36.7 %collective-permute-start.12 = (bf16[320,1152]{1,0:T(8,128)(2,1)}, bf16[320,1152]{1,0:T(8,128)(2,1)}, u32[]{:S(2)}, u32[]{:S(2)}) collective-permute-start(bf16[320,1152]{1,0:T(8,128)(2,1)} %shard_map.40.refs_0_), channel_id=1, source_target_pairs={{0,2},{2,4},{4,6},{6,7},{7,5},{5,3},{3,1},{1,0},{8,10},{10,12},{12... | collective-permute-start | bytes 2211848 | tf_op jit(solution)/shard_map/ppermute | solution.py:306
  120.9 42.9 %collective-permute-start.17 = (bf16[320,1152]{1,0:T(8,128)(2,1)}, bf16[320,1152]{1,0:T(8,128)(2,1)}, u32[]{:S(2)}, u32[]{:S(2)}) collective-permute-start(bf16[320,1152]{1,0:T(8,128)(2,1)} %shard_map.44.refs_1_), channel_id=1, source_target_pairs={{2,0},{4,2},{6,4},{7,6},{5,7},{3,5},{1,3},{0,1},{10,8},{12,10},{14... | collective-permute-start | bytes 2211848 | tf_op jit(solution)/shard_map/ppermute | solution.py:307
  132.2 37.8 %collective-permute-start.16 = (bf16[320,1152]{1,0:T(8,128)(2,1)}, bf16[320,1152]{1,0:T(8,128)(2,1)}, u32[]{:S(2)}, u32[]{:S(2)}) collective-permute-start(bf16[320,1152]{1,0:T(8,128)(2,1)} %shard_map.44.refs_1_), channel_id=1, source_target_pairs={{0,2},{2,4},{4,6},{6,7},{7,5},{5,3},{3,1},{1,0},{8,10},{10,12},{12... | collective-permute-start | bytes 2211848 | tf_op jit(solution)/shard_map/ppermute | solution.py:306
  154.2 31.5 %collective-permute-start.18 = (bf16[320,1152]{1,0:T(8,128)(2,1)}, bf16[320,1152]{1,0:T(8,128)(2,1)S(1)}, u32[]{:S(2)}, u32[]{:S(2)}) collective-permute-start(bf16[320,1152]{1,0:T(8,128)(2,1)} %get-tuple-element.49.refs_1_.refs_2_), channel_id=1, source_target_pairs={{0,2},{2,4},{4,6},{6,7},{7,5},{5,3},{3,1},{1,0},{8,10},{10,12},{12... | collective-permute-start | bytes 2211848 | tf_op jit(solution)/shard_map/ppermute | solution.py:306
  154.8 30.9 %collective-permute-start.19 = (bf16[320,1152]{1,0:T(8,128)(2,1)}, bf16[320,1152]{1,0:T(8,128)(2,1)}, u32[]{:S(2)}, u32[]{:S(2)}) collective-permute-start(bf16[320,1152]{1,0:T(8,128)(2,1)} %get-tuple-element.51.refs_3_.refs_4_), channel_id=1, source_target_pairs={{2,0},{4,2},{6,4},{7,6},{5,7},{3,5},{1,3},{0,1},{10,8},{12,10},{14... | collective-permute-start | bytes 2211848 | tf_op jit(solution)/shard_map/ppermute | solution.py:307
  170.0 31.6 %collective-permute-start.20 = (bf16[320,1152]{1,0:T(8,128)(2,1)}, bf16[320,1152]{1,0:T(8,128)(2,1)}, u32[]{:S(2)}, u32[]{:S(2)}) collective-permute-start(bf16[320,1152]{1,0:T(8,128)(2,1)} %get-tuple-element.50.refs_2_.refs_3_), channel_id=1, source_target_pairs={{0,2},{2,4},{4,6},{6,7},{7,5},{5,3},{3,1},{1,0},{8,10},{10,12},{12... | collective-permute-start | bytes 2211848 | tf_op jit(solution)/shard_map/ppermute | solution.py:306
  170.6 31.0 %collective-permute-start.21 = (bf16[320,1152]{1,0:T(8,128)(2,1)}, bf16[320,1152]{1,0:T(8,128)(2,1)}, u32[]{:S(2)}, u32[]{:S(2)}) collective-permute-start(bf16[320,1152]{1,0:T(8,128)(2,1)} %get-tuple-element.52.refs_4_.refs_5_), channel_id=1, source_target_pairs={{2,0},{4,2},{6,4},{7,6},{5,7},{3,5},{1,3},{0,1},{10,8},{12,10},{14... | collective-permute-start | bytes 2211848 | tf_op jit(solution)/shard_map/ppermute | solution.py:307
  172.0 31.2 %collective-permute-start.24 = (bf16[640,512]{1,0:T(8,128)(2,1)}, bf16[640,512]{1,0:T(8,128)(2,1)}, u32[]{:S(2)}, u32[]{:S(2)}) collective-permute-start(bf16[640,512]{1,0:T(8,128)(2,1)} %shard_map.51), channel_id=1, source_target_pairs={{0,8},{8,0},{16,24},{24,16},{1,9},{9,1},{17,25},{25,17},{2,10},{10... | collective-permute-start | bytes 1966088 | tf_op jit(solution)/shard_map/ppermute | solution.py:337
  185.7 21.3 %collective-permute-start.23 = (bf16[640,768]{1,0:T(8,128)(2,1)}, bf16[640,768]{1,0:T(8,128)(2,1)}, u32[]{:S(2)}, u32[]{:S(2)}) collective-permute-start(bf16[640,768]{1,0:T(8,128)(2,1)} %shard_map.50), channel_id=1, source_target_pairs={{0,8},{8,0},{16,24},{24,16},{1,9},{9,1},{17,25},{25,17},{2,10},{10... | collective-permute-start | bytes 2949128 | tf_op jit(solution)/shard_map/ppermute | solution.py:337
  186.6 28.3 %collective-permute-start.22 = (bf16[320,1152]{1,0:T(8,128)(2,1)}, bf16[320,1152]{1,0:T(8,128)(2,1)S(1)}, u32[]{:S(2)}, u32[]{:S(2)}) collective-permute-start(bf16[320,1152]{1,0:T(8,128)(2,1)} %get-tuple-element.53.refs_6_), channel_id=1, source_target_pairs={{0,2},{2,4},{4,6},{6,7},{7,5},{5,3},{3,1},{1,0},{8,10},{10,12},{12... | collective-permute-start | bytes 2211848 | tf_op jit(solution)/shard_map/ppermute | solution.py:306
  201.6 19.6 %collective-permute-start.27 = (bf16[320,1152]{1,0:T(8,128)(2,1)}, bf16[320,1152]{1,0:T(8,128)(2,1)S(1)}, u32[]{:S(2)}, u32[]{:S(2)}) collective-permute-start(bf16[320,1152]{1,0:T(8,128)(2,1)} %get-tuple-element.56.refs_9_), channel_id=1, source_target_pairs={{2,0},{4,2},{6,4},{7,6},{5,7},{3,5},{1,3},{0,1},{10,8},{12,10},{14... | collective-permute-start | bytes 2211848 | tf_op jit(solution)/shard_map/ppermute | solution.py:307
  209.6 40.1 %collective-permute-start.30 = (bf16[640,768]{1,0:T(8,128)(2,1)}, bf16[640,768]{1,0:T(8,128)(2,1)}, u32[]{:S(2)}, u32[]{:S(2)}) collective-permute-start(bf16[640,768]{1,0:T(8,128)(2,1)} %add_convert_fusion.1.refs_1_), channel_id=1, source_target_pairs={{0,16},{8,24},{16,0},{24,8},{1,17},{9,25},{17,1},{25,9},{2,18},{10... | collective-permute-start | bytes 2949128 | tf_op jit(solution)/shard_map/ppermute | solution.py:340
  210.2 27.0 %collective-permute-start.26 = (bf16[320,1152]{1,0:T(8,128)(2,1)}, bf16[320,1152]{1,0:T(8,128)(2,1)}, u32[]{:S(2)}, u32[]{:S(2)}) collective-permute-start(bf16[320,1152]{1,0:T(8,128)(2,1)} %get-tuple-element.55.refs_8_), channel_id=1, source_target_pairs={{2,0},{4,2},{6,4},{7,6},{5,7},{3,5},{1,3},{0,1},{10,8},{12,10},{14... | collective-permute-start | bytes 2211848 | tf_op jit(solution)/shard_map/ppermute | solution.py:307
  214.9 22.2 %collective-permute-start.25 = (bf16[320,1152]{1,0:T(8,128)(2,1)}, bf16[320,1152]{1,0:T(8,128)(2,1)}, u32[]{:S(2)}, u32[]{:S(2)}) collective-permute-start(bf16[320,1152]{1,0:T(8,128)(2,1)} %get-tuple-element.54.refs_7_), channel_id=1, source_target_pairs={{0,2},{2,4},{4,6},{6,7},{7,5},{5,3},{3,1},{1,0},{8,10},{10,12},{12... | collective-permute-start | bytes 2211848 | tf_op jit(solution)/shard_map/ppermute | solution.py:306
  221.3 28.5 %collective-permute-start.28 = (bf16[320,1152]{1,0:T(8,128)(2,1)}, bf16[320,1152]{1,0:T(8,128)(2,1)}, u32[]{:S(2)}, u32[]{:S(2)}) collective-permute-start(bf16[320,1152]{1,0:T(8,128)(2,1)} %shard_map.52.refs_32_.refs_10_), channel_id=1, source_target_pairs={{0,2},{2,4},{4,6},{6,7},{7,5},{5,3},{3,1},{1,0},{8,10},{10,12},{12... | collective-permute-start | bytes 2211848 | tf_op jit(solution)/shard_map/ppermute | solution.py:313
  223.5 26.3 %collective-permute-start.29 = (bf16[320,1152]{1,0:T(8,128)(2,1)}, bf16[320,1152]{1,0:T(8,128)(2,1)}, u32[]{:S(2)}, u32[]{:S(2)}) collective-permute-start(bf16[320,1152]{1,0:T(8,128)(2,1)} %shard_map.53.refs_35_.refs_13_), channel_id=1, source_target_pairs={{2,0},{4,2},{6,4},{7,6},{5,7},{3,5},{1,3},{0,1},{10,8},{12,10},{14... | collective-permute-start | bytes 2211848 | tf_op jit(solution)/shard_map/ppermute | solution.py:313
  265.2 25.1 %collective-permute-start.36 = (bf16[640,768]{1,0:T(8,128)(2,1)S(1)}, bf16[640,768]{1,0:T(8,128)(2,1)S(1)}, u32[]{:S(2)}, u32[]{:S(2)}) collective-permute-start(bf16[640,768]{1,0:T(8,128)(2,1)S(1)} %add_convert_fusion.refs_32_), channel_id=1, source_target_pairs={{0,16},{8,24},{16,0},{24,8},{1,17},{9,25},{17,1},{25,9},{2,18},{10... | collective-permute-start | bytes 2949128 | tf_op jit(solution)/shard_map/ppermute | solution.py:340
  (37 other events, 454.2 us)

commit v9 on v8

--- a/solution.py
+++ b/solution.py
@@ -368,7 +368,7 @@
         for summed, d, start in sums:
             terms.append(send(summed, d, SHORT))
             starts.append(start)
-        same, other = share(a - 1, [(0, flip, 0, chunk) for flip in (0, 1)], [*everything[a][-3], *everything[a][-2]])
+        same, other = share(a - 1, [(0, flip, 0, chunk) for flip in (0, 1)], [everything[a][-3][0], everything[a][-2][1]])
         gone = [*terms, same]
         terms += [same, cross(other)]
         starts += [None, None]
@@ -387,8 +387,8 @@
     other, same, others = share(last, [(d, 1, early, rest), (d, 0, early, rest), (0, 1, 0, chunk)], [leading])
     summed = added(same, cross(other))
     (same,) = share(last, [(0, 0, 0, chunk)], [summed])
-    there = send(leading, d, LONG, [same])
-    terms += [same, cross(others, [there]), there]
+    there = send(leading, d, LONG)
+    terms += [same, cross(others, [there, summed]), there]
     starts += [None, None, 0]
     out = combine(terms, starts, slab, chunk, scale)
     return finish(send(summed, d, LONG, [out]), out, early, scale)

time: 313 us -> 306 us (0.978)
  waiting for transfers between devices: 177 us -> 173 us
    ppermute x12, waiting for transfers between devices: 72.5 us -> 59.8 us  [gather(): got[-1][half] = lax.ppermute(behind[half], SLABS, backward)]
    ppermute x4, waiting for transfers between devices: 13.2 us -> 21.2 us  [gather(): last.append(lax.ppermute(got[side][half], SLABS, way))]
    unnamed x62 -> x54, local copies, waits for them, and re-layouts: 15.9 us -> 14 us
  transfers between devices with their start and end apart: 38 -> 38, of which waited for: 24 -> 23; matrix products, arithmetic and copies ran while one was open for 2% -> 2% of each run, Pallas kernels for 18% -> 19%
where the time goes in v9:
time: 306 us
  waiting for transfers between devices  173 us (57%)
  Pallas kernels  72.7 us (24%)
  starting transfers between devices  38.1 us (12%)
  local copies, waits for them, and re-layouts  14.7 us (5%)
  other arithmetic  7.31 us (2%)
    ppermute x12, waiting for transfers between devices, gather(): got[-2][half] = lax.ppermute(ahead[half], SLABS, onward)  77.3 us
    ppermute x12, waiting for transfers between devices, gather(): got[-1][half] = lax.ppermute(behind[half], SLABS, backward)  59.8 us
    pallas_call x5, Pallas kernels, scores(): pl.pallas_call(functools.partial(scores_kernel, subject=subject, targets=...  55.9 us
    ppermute x4, waiting for transfers between devices, gather(): last.append(lax.ppermute(got[side][half], SLABS, way))  21.2 us
    ppermute x12, starting transfers between devices, gather(): got[-1][half] = lax.ppermute(behind[half], SLABS, backward)  20.4 us
    unnamed x54, local copies, waits for them, and re-layouts  14 us
    ppermute x4, waiting for transfers between devices, send(): lax.ppermute(summed, 'subj', [(s, (s + 2 * d) % subjs) for s in range(sub...  10.1 us
    pallas_call x2, Pallas kernels, normalize(): pl.pallas_call(functools.partial(normalize_kernel, begin=low, lead=begin...  8.27 us
  transfers between devices with their start and end apart: 38, of which 23 were waited for; matrix products, arithmetic and copies ran while one was open for 2% of the time, Pallas kernels for 19%

profile of v9, /device:TPU:0, one launch (start us, length us, event | category | flops | bytes accessed | tf_op | source)
XLA Modules:
  0.0 306.1 jit_solution(9122026166032934959)
XLA Ops:
  0.0 3.7 %shard_map.41 = (bf16[320,1280]{1,0:T(8,128)(2,1)S(1)}, bf16[320,1152]{1,0:T(8,128)(2,1)S(1)}) custom-call(f32[2,1200,640]{2,1,0:T(8,128)} %bitcast.5), custom_call_target="tpu_custom_call" | custom-call | bytes 1024 | tf_op jit(solution)/shard_map/pallas_call | solution.py:76
  4.7 3.0 collective-permute-start.7
  7.7 4.5 %shard_map.37 = (bf16[320,1280]{1,0:T(8,128)(2,1)}, bf16[320,1152]{1,0:T(8,128)(2,1)S(1)}) custom-call(f32[2,1200,640]{2,1,0:T(8,128)} %bitcast.6), custom_call_target="tpu_custom_call" | custom-call | bytes 1024 | tf_op jit(solution)/shard_map/pallas_call | solution.py:76
  15.2 11.6 %collective-permute-done.7.refs_1_ = bf16[320,1280]{1,0:T(8,128)(2,1)S(1)} collective-permute-done((bf16[320,1280]{1,0:T(8,128)(2,1)S(1)}, bf16[320,1280]{1,0:T(8,128)(2,1)S(1)}, u32[]{:S(2)}, u32[]{:S(2)}) %collective-permute-start.7) | collective-permute-done | bytes 819232 | tf_op jit(solution)/shard_map/ppermute | solution.py:307
  31.8 12.6 %collective-permute-done.1.refs_1_ = bf16[320,1280]{1,0:T(8,128)(2,1)S(1)} collective-permute-done((bf16[320,1280]{1,0:T(8,128)(2,1)}, bf16[320,1280]{1,0:T(8,128)(2,1)S(1)}, u32[]{:S(2)}, u32[]{:S(2)}) %collective-permute-start.1) | collective-permute-done | bytes 819232 | tf_op jit(solution)/shard_map/ppermute | solution.py:307
  49.3 14.7 %collective-permute-done.8.refs_0_ = bf16[320,1280]{1,0:T(8,128)(2,1)} collective-permute-done((bf16[320,1280]{1,0:T(8,128)(2,1)}, bf16[320,1280]{1,0:T(8,128)(2,1)}, u32[]{:S(2)}, u32[]{:S(2)}) %collective-permute-start.8) | collective-permute-done | bytes 819232 | tf_op jit(solution)/shard_map/ppermute | solution.py:306
  66.6 13.5 %collective-permute-done.2.refs_0_ = bf16[320,1280]{1,0:T(8,128)(2,1)S(1)} collective-permute-done((bf16[320,1280]{1,0:T(8,128)(2,1)}, bf16[320,1280]{1,0:T(8,128)(2,1)S(1)}, u32[]{:S(2)}, u32[]{:S(2)}) %collective-permute-start.2) | collective-permute-done | bytes 819232 | tf_op jit(solution)/shard_map/ppermute | solution.py:306
  84.4 12.7 %collective-permute-done.11.refs_2_.refs_13_.refs_29_ = bf16[320,1280]{1,0:T(8,128)(2,1)} collective-permute-done((bf16[320,1280]{1,0:T(8,128)(2,1)}, bf16[320,1280]{1,0:T(8,128)(2,1)}, u32[]{:S(2)}, u32[]{:S(2)}) %collective-permute-start.11) | collective-permute-done | bytes 819232 | tf_op jit(solution)/shard_map/ppermute | solution.py:307
  99.1 4.2 %collective-permute-done.4.refs_1_.refs_10_.refs_26_ = bf16[320,1280]{1,0:T(8,128)(2,1)} collective-permute-done((bf16[320,1280]{1,0:T(8,128)(2,1)}, bf16[320,1280]{1,0:T(8,128)(2,1)}, u32[]{:S(2)}, u32[]{:S(2)}) %collective-permute-start.4) | collective-permute-done | bytes 819232 | tf_op jit(solution)/shard_map/ppermute | solution.py:306
  103.9 10.7 %collective-permute-done.5.refs_2_.refs_12_.refs_28_ = bf16[320,1280]{1,0:T(8,128)(2,1)S(1)} collective-permute-done((bf16[320,1280]{1,0:T(8,128)(2,1)}, bf16[320,1280]{1,0:T(8,128)(2,1)S(1)}, u32[]{:S(2)}, u32[]{:S(2)}) %collective-permute-start.5) | collective-permute-done | bytes 819232 | tf_op jit(solution)/shard_map/ppermute | solution.py:307
  117.7 3.2 %collective-permute-done.10.refs_1_.refs_11_.refs_27_ = bf16[320,1280]{1,0:T(8,128)(2,1)} collective-permute-done((bf16[320,1280]{1,0:T(8,128)(2,1)}, bf16[320,1280]{1,0:T(8,128)(2,1)}, u32[]{:S(2)}, u32[]{:S(2)}) %collective-permute-start.10) | collective-permute-done | bytes 819232 | tf_op jit(solution)/shard_map/ppermute | solution.py:306
  122.5 9.8 %collective-permute-done.15.refs_15_.refs_31_ = bf16[320,1280]{1,0:T(8,128)(2,1)} collective-permute-done((bf16[320,1280]{1,0:T(8,128)(2,1)}, bf16[320,1280]{1,0:T(8,128)(2,1)}, u32[]{:S(2)}, u32[]{:S(2)}) %collective-permute-start.15) | collective-permute-done | bytes 819232 | tf_op jit(solution)/shard_map/ppermute | solution.py:313
  132.2 2.1 collective-permute-start.16
  135.1 3.4 %collective-permute-done.14.refs_14_.refs_30_ = bf16[320,1280]{1,0:T(8,128)(2,1)} collective-permute-done((bf16[320,1280]{1,0:T(8,128)(2,1)}, bf16[320,1280]{1,0:T(8,128)(2,1)}, u32[]{:S(2)}, u32[]{:S(2)}) %collective-permute-start.14) | collective-permute-done | bytes 819232 | tf_op jit(solution)/shard_map/ppermute | solution.py:313
  138.5 15.1 %shard_map.45 = (bf16[640,768]{1,0:T(8,128)(2,1)}, bf16[640,768]{1,0:T(8,128)(2,1)}, bf16[640,512]{1,0:T(8,128)(2,1)S(1)}, bf16[640,512]{1,0:T(8,128)(2,1)S(1)}) custom-call(s32[8]{0:T(128)S(1)} %dynamic-slice_bitcast_fusion.source_ref, s32[5]{0:T(128)S(1)} %copy-done.17, s32[2]{0:T(128)S(1)} %pad_add_fusion.place_ref, ...), custom_call_target="tpu_custom_call" | custom-call | bytes 1024 | tf_op jit(solution)/shard_map/pallas_call | solution.py:244
  157.3 6.6 %collective-permute-done.17.refs_1_ = bf16[320,1152]{1,0:T(8,128)(2,1)} collective-permute-done((bf16[320,1152]{1,0:T(8,128)(2,1)}, bf16[320,1152]{1,0:T(8,128)(2,1)}, u32[]{:S(2)}, u32[]{:S(2)}) %collective-permute-start.17) | collective-permute-done | bytes 737312 | tf_op jit(solution)/shard_map/ppermute | solution.py:307
  163.8 6.2 %collective-permute-done.16.refs_0_ = bf16[320,1152]{1,0:T(8,128)(2,1)} collective-permute-done((bf16[320,1152]{1,0:T(8,128)(2,1)}, bf16[320,1152]{1,0:T(8,128)(2,1)}, u32[]{:S(2)}, u32[]{:S(2)}) %collective-permute-start.16) | collective-permute-done | bytes 737312 | tf_op jit(solution)/shard_map/ppermute | solution.py:306
  172.1 13.8 %collective-permute-done.18.refs_0_ = bf16[320,1152]{1,0:T(8,128)(2,1)} collective-permute-done((bf16[320,1152]{1,0:T(8,128)(2,1)}, bf16[320,1152]{1,0:T(8,128)(2,1)}, u32[]{:S(2)}, u32[]{:S(2)}) %collective-permute-start.18) | collective-permute-done | bytes 737312 | tf_op jit(solution)/shard_map/ppermute | solution.py:306
  186.5 15.2 %collective-permute-done.20.refs_0_ = bf16[320,1152]{1,0:T(8,128)(2,1)} collective-permute-done((bf16[320,1152]{1,0:T(8,128)(2,1)}, bf16[320,1152]{1,0:T(8,128)(2,1)}, u32[]{:S(2)}, u32[]{:S(2)}) %collective-permute-start.20) | collective-permute-done | bytes 737312 | tf_op jit(solution)/shard_map/ppermute | solution.py:306
  203.2 2.3 add_convert_fusion.3.refs_2_
  207.1 2.4 add_convert_fusion.1.refs_1_
  211.6 3.4 %collective-permute-done.22.refs_0_ = bf16[320,1152]{1,0:T(8,128)(2,1)} collective-permute-done((bf16[320,1152]{1,0:T(8,128)(2,1)}, bf16[320,1152]{1,0:T(8,128)(2,1)}, u32[]{:S(2)}, u32[]{:S(2)}) %collective-permute-start.22) | collective-permute-done | bytes 737312 | tf_op jit(solution)/shard_map/ppermute | solution.py:306
  215.7 5.7 %collective-permute-done.27.refs_0_ = bf16[320,1152]{1,0:T(8,128)(2,1)} collective-permute-done((bf16[320,1152]{1,0:T(8,128)(2,1)}, bf16[320,1152]{1,0:T(8,128)(2,1)}, u32[]{:S(2)}, u32[]{:S(2)}) %collective-permute-start.27) | collective-permute-done | bytes 737312 | tf_op jit(solution)/shard_map/ppermute | solution.py:307
  225.1 14.1 %shard_map.56 = (bf16[640,1280]{1,0:T(8,128)(2,1)}, bf16[640,1280]{1,0:T(8,128)(2,1)}) custom-call(s32[8]{0:T(128)S(1)} %dynamic-slice_bitcast_fusion.source_ref, s32[5]{0:T(128)S(1)} %copy-done.17, s32[2]{0:T(128)S(1)} %pad_add_fusion.place_ref, bf16[320,1280]{1,0:T(8,128)(2,1)} %get-tuple-element.37.refs_0_.refs_16_, ...), custom_call_target="tpu_custom_call" | custom-call | bytes 1024 | tf_op jit(solution)/shard_map/pallas_call | solution.py:244
  239.3 8.0 %collective-permute-done.28.refs_14_ = bf16[320,1152]{1,0:T(8,128)(2,1)} collective-permute-done((bf16[320,1152]{1,0:T(8,128)(2,1)}, bf16[320,1152]{1,0:T(8,128)(2,1)}, u32[]{:S(2)}, u32[]{:S(2)}) %collective-permute-start.28) | collective-permute-done | bytes 737312 | tf_op jit(solution)/shard_map/ppermute | solution.py:313
  247.3 9.1 %shard_map.57 = (bf16[640,768]{1,0:T(8,128)(2,1)}, bf16[640,768]{1,0:T(8,128)(2,1)}) custom-call(s32[8]{0:T(128)S(1)} %dynamic-slice_bitcast_fusion.source_ref, s32[5]{0:T(128)S(1)} %copy-done.17, s32[2]{0:T(128)S(1)} %pad_add_fusion.place_ref, bf16[320,1152]{1,0:T(8,128)(2,1)S(1)} %copy-done.10, bf16[320,1152]{1,0:T(8,128)(2,1)S(1)} %copy-done.8, ...), custom_call_target="tpu_custom_call" | custom-call | bytes 1024 | tf_op jit(solution)/shard_map/pallas_call | solution.py:244
  256.5 2.8 collective-permute-done.32
  262.0 10.1 %shard_map.58 = (bf16[640,512]{1,0:T(8,128)(2,1)S(1)}, bf16[640,512]{1,0:T(8,128)(2,1)S(1)}, bf16[640,1280]{1,0:T(8,128)(2,1)}) custom-call(s32[8]{0:T(128)S(1)} %dynamic-slice_bitcast_fusion.source_ref, s32[5]{0:T(128)S(1)} %copy-done.17, s32[2]{0:T(128)S(1)} %pad_add_fusion.place_ref, bf16[320,1152]{1,0:T(8,128)(2,1)S(1)} %copy-done.10, ...), custom_call_target="tpu_custom_call" | custom-call | bytes 1024 | tf_op jit(solution)/shard_map/pallas_call | solution.py:244
  276.1 8.5 %collective-permute-done.36.refs_0_ = bf16[640,768]{1,0:T(8,128)(2,1)S(1)} collective-permute-done((bf16[640,768]{1,0:T(8,128)(2,1)S(1)}, bf16[640,768]{1,0:T(8,128)(2,1)S(1)}, u32[]{:S(2)}, u32[]{:S(2)}) %collective-permute-start.36) | collective-permute-done | bytes 983072 | tf_op jit(solution)/shard_map/ppermute | solution.py:340
  287.9 7.6 %shard_map.59.refs_4_ = bf16[640,1280]{1,0:T(8,128)(2,1)} custom-call(s32[8]{0:T(128)S(1)} %dynamic-slice_bitcast_fusion.source_ref, s32[5]{0:T(128)S(1)} %copy-done.17, s32[2]{0:T(128)S(1)} %pad_add_fusion.place_ref, bf16[320,1152]{1,0:T(8,128)(2,1)S(1)} %copy-done.10, bf16[320,1152]{1,0:T(8,128)(2,1)S(1)} %copy-done.8, ...), custom_call_target="tpu_custom_call" | custom-call | bytes 1024 | tf_op jit(solution)/shard_map/pallas_call | solution.py:244
  296.7 6.1 %shard_map.62.refs_1_.before_ref = f32[640,1280]{1,0:T(8,128)} custom-call(bf16[640,768]{1,0:T(8,128)(2,1)} %shard_map.54.refs_32_.refs_0_, bf16[640,512]{1,0:T(8,128)(2,1)} %shard_map.55.refs_33_.refs_1_, bf16[640,1280]{1,0:T(8,128)(2,1)S(1)} %copy-done.13, bf16[640,1280]{1,0:T(8,128)(2,1)} %collective-permute-done.35.refs_3_, ...), custom_call_target="tpu_custom_call" | custom-call | bytes 1024 | tf_op jit(solution)/shard_map/pallas_call | solution.py:119
  303.7 2.4 shard_map.64
  (132 shorter events, 57.0 us)
Async XLA Ops:
  4.7 22.1 %collective-permute-start.7 = (bf16[320,1280]{1,0:T(8,128)(2,1)S(1)}, bf16[320,1280]{1,0:T(8,128)(2,1)S(1)}, u32[]{:S(2)}, u32[]{:S(2)}) collective-permute-start(bf16[320,1280]{1,0:T(8,128)(2,1)S(1)} %get-tuple-element.43.refs_1_.refs_17_), channel_id=1, source_target_pairs={{2,0},{4,2},{6,4},{7,6},{5,7},{3,5},{1,3},{0,1},{10,8},{12,10},{14... | collective-permute-start | bytes 2457608 | tf_op jit(solution)/shard_map/ppermute | solution.py:307
  7.7 21.2 %collective-permute-start.6 = (bf16[320,1280]{1,0:T(8,128)(2,1)S(1)}, bf16[320,1280]{1,0:T(8,128)(2,1)S(1)}, u32[]{:S(2)}, u32[]{:S(2)}) collective-permute-start(bf16[320,1280]{1,0:T(8,128)(2,1)S(1)} %get-tuple-element.43.refs_1_.refs_17_), channel_id=1, source_target_pairs={{0,2},{2,4},{4,6},{6,7},{7,5},{5,3},{3,1},{1,0},{8,10},{10,12},{12... | collective-permute-start | bytes 2457608 | tf_op jit(solution)/shard_map/ppermute | solution.py:306
  13.1 31.2 %collective-permute-start.1 = (bf16[320,1280]{1,0:T(8,128)(2,1)}, bf16[320,1280]{1,0:T(8,128)(2,1)S(1)}, u32[]{:S(2)}, u32[]{:S(2)}) collective-permute-start(bf16[320,1280]{1,0:T(8,128)(2,1)} %get-tuple-element.37.refs_0_.refs_16_), channel_id=1, source_target_pairs={{2,0},{4,2},{6,4},{7,6},{5,7},{3,5},{1,3},{0,1},{10,8},{12,10},{14... | collective-permute-start | bytes 2457608 | tf_op jit(solution)/shard_map/ppermute | solution.py:307
  15.1 31.3 %collective-permute-start = (bf16[320,1280]{1,0:T(8,128)(2,1)}, bf16[320,1280]{1,0:T(8,128)(2,1)S(1)}, u32[]{:S(2)}, u32[]{:S(2)}) collective-permute-start(bf16[320,1280]{1,0:T(8,128)(2,1)} %get-tuple-element.37.refs_0_.refs_16_), channel_id=1, source_target_pairs={{0,2},{2,4},{4,6},{6,7},{7,5},{5,3},{3,1},{1,0},{8,10},{10,12},{12... | collective-permute-start | bytes 2457608 | tf_op jit(solution)/shard_map/ppermute | solution.py:306
  29.7 34.3 %collective-permute-start.8 = (bf16[320,1280]{1,0:T(8,128)(2,1)}, bf16[320,1280]{1,0:T(8,128)(2,1)}, u32[]{:S(2)}, u32[]{:S(2)}) collective-permute-start(bf16[320,1280]{1,0:T(8,128)(2,1)} %get-tuple-element.44.refs_3_.refs_19_), channel_id=1, source_target_pairs={{0,2},{2,4},{4,6},{6,7},{7,5},{5,3},{3,1},{1,0},{8,10},{10,12},{12... | collective-permute-start | bytes 2457608 | tf_op jit(solution)/shard_map/ppermute | solution.py:306
  30.7 33.4 %collective-permute-start.9 = (bf16[320,1280]{1,0:T(8,128)(2,1)}, bf16[320,1280]{1,0:T(8,128)(2,1)S(1)}, u32[]{:S(2)}, u32[]{:S(2)}) collective-permute-start(bf16[320,1280]{1,0:T(8,128)(2,1)} %get-tuple-element.45.refs_5_.refs_21_), channel_id=1, source_target_pairs={{2,0},{4,2},{6,4},{7,6},{5,7},{3,5},{1,3},{0,1},{10,8},{12,10},{14... | collective-permute-start | bytes 2457608 | tf_op jit(solution)/shard_map/ppermute | solution.py:307
  47.3 32.7 %collective-permute-start.2 = (bf16[320,1280]{1,0:T(8,128)(2,1)}, bf16[320,1280]{1,0:T(8,128)(2,1)S(1)}, u32[]{:S(2)}, u32[]{:S(2)}) collective-permute-start(bf16[320,1280]{1,0:T(8,128)(2,1)} %get-tuple-element.38.refs_2_.refs_18_), channel_id=1, source_target_pairs={{0,2},{2,4},{4,6},{6,7},{7,5},{5,3},{3,1},{1,0},{8,10},{10,12},{12... | collective-permute-start | bytes 2457608 | tf_op jit(solution)/shard_map/ppermute | solution.py:306
  48.3 31.8 %collective-permute-start.3 = (bf16[320,1280]{1,0:T(8,128)(2,1)}, bf16[320,1280]{1,0:T(8,128)(2,1)S(1)}, u32[]{:S(2)}, u32[]{:S(2)}) collective-permute-start(bf16[320,1280]{1,0:T(8,128)(2,1)} %get-tuple-element.39.refs_4_.refs_20_), channel_id=1, source_target_pairs={{2,0},{4,2},{6,4},{7,6},{5,7},{3,5},{1,3},{0,1},{10,8},{12,10},{14... | collective-permute-start | bytes 2457608 | tf_op jit(solution)/shard_map/ppermute | solution.py:307
  65.0 32.1 %collective-permute-start.11 = (bf16[320,1280]{1,0:T(8,128)(2,1)}, bf16[320,1280]{1,0:T(8,128)(2,1)}, u32[]{:S(2)}, u32[]{:S(2)}) collective-permute-start(bf16[320,1280]{1,0:T(8,128)(2,1)} %get-tuple-element.47.refs_9_.refs_25_), channel_id=1, source_target_pairs={{2,0},{4,2},{6,4},{7,6},{5,7},{3,5},{1,3},{0,1},{10,8},{12,10},{14... | collective-permute-start | bytes 2457608 | tf_op jit(solution)/shard_map/ppermute | solution.py:307
  81.8 21.5 %collective-permute-start.4 = (bf16[320,1280]{1,0:T(8,128)(2,1)}, bf16[320,1280]{1,0:T(8,128)(2,1)}, u32[]{:S(2)}, u32[]{:S(2)}) collective-permute-start(bf16[320,1280]{1,0:T(8,128)(2,1)} %get-tuple-element.40.refs_6_.refs_22_), channel_id=1, source_target_pairs={{0,2},{2,4},{4,6},{6,7},{7,5},{5,3},{3,1},{1,0},{8,10},{10,12},{12... | collective-permute-start | bytes 2457608 | tf_op jit(solution)/shard_map/ppermute | solution.py:306
  82.4 32.2 %collective-permute-start.5 = (bf16[320,1280]{1,0:T(8,128)(2,1)}, bf16[320,1280]{1,0:T(8,128)(2,1)S(1)}, u32[]{:S(2)}, u32[]{:S(2)}) collective-permute-start(bf16[320,1280]{1,0:T(8,128)(2,1)} %get-tuple-element.41.refs_8_.refs_24_), channel_id=1, source_target_pairs={{2,0},{4,2},{6,4},{7,6},{5,7},{3,5},{1,3},{0,1},{10,8},{12,10},{14... | collective-permute-start | bytes 2457608 | tf_op jit(solution)/shard_map/ppermute | solution.py:307
  83.9 37.0 %collective-permute-start.10 = (bf16[320,1280]{1,0:T(8,128)(2,1)}, bf16[320,1280]{1,0:T(8,128)(2,1)}, u32[]{:S(2)}, u32[]{:S(2)}) collective-permute-start(bf16[320,1280]{1,0:T(8,128)(2,1)} %get-tuple-element.46.refs_7_.refs_23_), channel_id=1, source_target_pairs={{0,2},{2,4},{4,6},{6,7},{7,5},{5,3},{3,1},{1,0},{8,10},{10,12},{12... | collective-permute-start | bytes 2457608 | tf_op jit(solution)/shard_map/ppermute | solution.py:306
  97.1 35.1 %collective-permute-start.15 = (bf16[320,1280]{1,0:T(8,128)(2,1)}, bf16[320,1280]{1,0:T(8,128)(2,1)}, u32[]{:S(2)}, u32[]{:S(2)}) collective-permute-start(bf16[320,1280]{1,0:T(8,128)(2,1)} %collective-permute-done.11.refs_2_.refs_13_.refs_29_), channel_id=1, source_target_pairs={{2,0},{4,2},{6,4},{7,6},{5,7},{3,5},{1,3},{0,1},{10,8},{12,10},{14... | collective-permute-start | bytes 2457608 | tf_op jit(solution)/shard_map/ppermute | solution.py:313
  103.3 35.1 %collective-permute-start.14 = (bf16[320,1280]{1,0:T(8,128)(2,1)}, bf16[320,1280]{1,0:T(8,128)(2,1)}, u32[]{:S(2)}, u32[]{:S(2)}) collective-permute-start(bf16[320,1280]{1,0:T(8,128)(2,1)} %collective-permute-done.4.refs_1_.refs_10_.refs_26_), channel_id=1, source_target_pairs={{0,2},{2,4},{4,6},{6,7},{7,5},{5,3},{3,1},{1,0},{8,10},{10,12},{12... | collective-permute-start | bytes 2457608 | tf_op jit(solution)/shard_map/ppermute | solution.py:313
  115.5 39.7 %collective-permute-start.13 = (bf16[320,1152]{1,0:T(8,128)(2,1)}, bf16[320,1152]{1,0:T(8,128)(2,1)}, u32[]{:S(2)}, u32[]{:S(2)}) collective-permute-start(bf16[320,1152]{1,0:T(8,128)(2,1)} %shard_map.40.refs_0_), channel_id=1, source_target_pairs={{2,0},{4,2},{6,4},{7,6},{5,7},{3,5},{1,3},{0,1},{10,8},{12,10},{14... | collective-permute-start | bytes 2211848 | tf_op jit(solution)/shard_map/ppermute | solution.py:307
  117.6 37.6 %collective-permute-start.12 = (bf16[320,1152]{1,0:T(8,128)(2,1)}, bf16[320,1152]{1,0:T(8,128)(2,1)}, u32[]{:S(2)}, u32[]{:S(2)}) collective-permute-start(bf16[320,1152]{1,0:T(8,128)(2,1)} %shard_map.40.refs_0_), channel_id=1, source_target_pairs={{0,2},{2,4},{4,6},{6,7},{7,5},{5,3},{3,1},{1,0},{8,10},{10,12},{12... | collective-permute-start | bytes 2211848 | tf_op jit(solution)/shard_map/ppermute | solution.py:306
  120.9 42.9 %collective-permute-start.17 = (bf16[320,1152]{1,0:T(8,128)(2,1)}, bf16[320,1152]{1,0:T(8,128)(2,1)}, u32[]{:S(2)}, u32[]{:S(2)}) collective-permute-start(bf16[320,1152]{1,0:T(8,128)(2,1)} %shard_map.44.refs_1_), channel_id=1, source_target_pairs={{2,0},{4,2},{6,4},{7,6},{5,7},{3,5},{1,3},{0,1},{10,8},{12,10},{14... | collective-permute-start | bytes 2211848 | tf_op jit(solution)/shard_map/ppermute | solution.py:307
  132.2 37.8 %collective-permute-start.16 = (bf16[320,1152]{1,0:T(8,128)(2,1)}, bf16[320,1152]{1,0:T(8,128)(2,1)}, u32[]{:S(2)}, u32[]{:S(2)}) collective-permute-start(bf16[320,1152]{1,0:T(8,128)(2,1)} %shard_map.44.refs_1_), channel_id=1, source_target_pairs={{0,2},{2,4},{4,6},{6,7},{7,5},{5,3},{3,1},{1,0},{8,10},{10,12},{12... | collective-permute-start | bytes 2211848 | tf_op jit(solution)/shard_map/ppermute | solution.py:306
  155.2 30.6 %collective-permute-start.18 = (bf16[320,1152]{1,0:T(8,128)(2,1)}, bf16[320,1152]{1,0:T(8,128)(2,1)}, u32[]{:S(2)}, u32[]{:S(2)}) collective-permute-start(bf16[320,1152]{1,0:T(8,128)(2,1)} %get-tuple-element.49.refs_1_.refs_2_), channel_id=1, source_target_pairs={{0,2},{2,4},{4,6},{6,7},{7,5},{5,3},{3,1},{1,0},{8,10},{10,12},{12... | collective-permute-start | bytes 2211848 | tf_op jit(solution)/shard_map/ppermute | solution.py:306
  155.2 30.6 %collective-permute-start.19 = (bf16[320,1152]{1,0:T(8,128)(2,1)}, bf16[320,1152]{1,0:T(8,128)(2,1)}, u32[]{:S(2)}, u32[]{:S(2)}) collective-permute-start(bf16[320,1152]{1,0:T(8,128)(2,1)} %get-tuple-element.51.refs_3_.refs_4_), channel_id=1, source_target_pairs={{2,0},{4,2},{6,4},{7,6},{5,7},{3,5},{1,3},{0,1},{10,8},{12,10},{14... | collective-permute-start | bytes 2211848 | tf_op jit(solution)/shard_map/ppermute | solution.py:307
  170.0 31.6 %collective-permute-start.20 = (bf16[320,1152]{1,0:T(8,128)(2,1)}, bf16[320,1152]{1,0:T(8,128)(2,1)}, u32[]{:S(2)}, u32[]{:S(2)}) collective-permute-start(bf16[320,1152]{1,0:T(8,128)(2,1)} %get-tuple-element.50.refs_2_.refs_3_), channel_id=1, source_target_pairs={{0,2},{2,4},{4,6},{6,7},{7,5},{5,3},{3,1},{1,0},{8,10},{10,12},{12... | collective-permute-start | bytes 2211848 | tf_op jit(solution)/shard_map/ppermute | solution.py:306
  170.6 31.0 %collective-permute-start.21 = (bf16[320,1152]{1,0:T(8,128)(2,1)}, bf16[320,1152]{1,0:T(8,128)(2,1)}, u32[]{:S(2)}, u32[]{:S(2)}) collective-permute-start(bf16[320,1152]{1,0:T(8,128)(2,1)} %get-tuple-element.52.refs_4_.refs_5_), channel_id=1, source_target_pairs={{2,0},{4,2},{6,4},{7,6},{5,7},{3,5},{1,3},{0,1},{10,8},{12,10},{14... | collective-permute-start | bytes 2211848 | tf_op jit(solution)/shard_map/ppermute | solution.py:307
  172.1 31.2 %collective-permute-start.24 = (bf16[640,512]{1,0:T(8,128)(2,1)}, bf16[640,512]{1,0:T(8,128)(2,1)}, u32[]{:S(2)}, u32[]{:S(2)}) collective-permute-start(bf16[640,512]{1,0:T(8,128)(2,1)} %shard_map.51), channel_id=1, source_target_pairs={{0,8},{8,0},{16,24},{24,16},{1,9},{9,1},{17,25},{25,17},{2,10},{10... | collective-permute-start | bytes 1966088 | tf_op jit(solution)/shard_map/ppermute | solution.py:337
  185.8 21.2 %collective-permute-start.23 = (bf16[640,768]{1,0:T(8,128)(2,1)}, bf16[640,768]{1,0:T(8,128)(2,1)}, u32[]{:S(2)}, u32[]{:S(2)}) collective-permute-start(bf16[640,768]{1,0:T(8,128)(2,1)} %shard_map.50), channel_id=1, source_target_pairs={{0,8},{8,0},{16,24},{24,16},{1,9},{9,1},{17,25},{25,17},{2,10},{10... | collective-permute-start | bytes 2949128 | tf_op jit(solution)/shard_map/ppermute | solution.py:337
  185.9 29.2 %collective-permute-start.22 = (bf16[320,1152]{1,0:T(8,128)(2,1)}, bf16[320,1152]{1,0:T(8,128)(2,1)}, u32[]{:S(2)}, u32[]{:S(2)}) collective-permute-start(bf16[320,1152]{1,0:T(8,128)(2,1)} %get-tuple-element.53.refs_6_), channel_id=1, source_target_pairs={{0,2},{2,4},{4,6},{6,7},{7,5},{5,3},{3,1},{1,0},{8,10},{10,12},{12... | collective-permute-start | bytes 2211848 | tf_op jit(solution)/shard_map/ppermute | solution.py:306
  209.5 29.8 %collective-permute-start.30 = (bf16[640,768]{1,0:T(8,128)(2,1)}, bf16[640,768]{1,0:T(8,128)(2,1)}, u32[]{:S(2)}, u32[]{:S(2)}) collective-permute-start(bf16[640,768]{1,0:T(8,128)(2,1)} %add_convert_fusion.1.refs_1_), channel_id=1, source_target_pairs={{0,16},{8,24},{16,0},{24,8},{1,17},{9,25},{17,1},{25,9},{2,18},{10... | collective-permute-start | bytes 2949128 | tf_op jit(solution)/shard_map/ppermute | solution.py:340
  210.0 29.2 %collective-permute-start.26 = (bf16[320,1152]{1,0:T(8,128)(2,1)}, bf16[320,1152]{1,0:T(8,128)(2,1)}, u32[]{:S(2)}, u32[]{:S(2)}) collective-permute-start(bf16[320,1152]{1,0:T(8,128)(2,1)} %get-tuple-element.55.refs_8_), channel_id=1, source_target_pairs={{2,0},{4,2},{6,4},{7,6},{5,7},{3,5},{1,3},{0,1},{10,8},{12,10},{14... | collective-permute-start | bytes 2211848 | tf_op jit(solution)/shard_map/ppermute | solution.py:307
  215.1 24.2 %collective-permute-start.25 = (bf16[320,1152]{1,0:T(8,128)(2,1)}, bf16[320,1152]{1,0:T(8,128)(2,1)}, u32[]{:S(2)}, u32[]{:S(2)}) collective-permute-start(bf16[320,1152]{1,0:T(8,128)(2,1)} %get-tuple-element.54.refs_7_), channel_id=1, source_target_pairs={{0,2},{2,4},{4,6},{6,7},{7,5},{5,3},{3,1},{1,0},{8,10},{10,12},{12... | collective-permute-start | bytes 2211848 | tf_op jit(solution)/shard_map/ppermute | solution.py:306
  221.4 25.9 %collective-permute-start.28 = (bf16[320,1152]{1,0:T(8,128)(2,1)}, bf16[320,1152]{1,0:T(8,128)(2,1)}, u32[]{:S(2)}, u32[]{:S(2)}) collective-permute-start(bf16[320,1152]{1,0:T(8,128)(2,1)} %shard_map.52.refs_32_.refs_10_), channel_id=1, source_target_pairs={{0,2},{2,4},{4,6},{6,7},{7,5},{5,3},{3,1},{1,0},{8,10},{10,12},{12... | collective-permute-start | bytes 2211848 | tf_op jit(solution)/shard_map/ppermute | solution.py:313
  223.6 23.7 %collective-permute-start.29 = (bf16[320,1152]{1,0:T(8,128)(2,1)}, bf16[320,1152]{1,0:T(8,128)(2,1)}, u32[]{:S(2)}, u32[]{:S(2)}) collective-permute-start(bf16[320,1152]{1,0:T(8,128)(2,1)} %shard_map.53.refs_33_.refs_13_), channel_id=1, source_target_pairs={{2,0},{4,2},{6,4},{7,6},{5,7},{3,5},{1,3},{0,1},{10,8},{12,10},{14... | collective-permute-start | bytes 2211848 | tf_op jit(solution)/shard_map/ppermute | solution.py:313
  260.7 23.9 %collective-permute-start.36 = (bf16[640,768]{1,0:T(8,128)(2,1)S(1)}, bf16[640,768]{1,0:T(8,128)(2,1)S(1)}, u32[]{:S(2)}, u32[]{:S(2)}) collective-permute-start(bf16[640,768]{1,0:T(8,128)(2,1)S(1)} %add_convert_fusion.refs_32_), channel_id=1, source_target_pairs={{0,16},{8,24},{16,0},{24,8},{1,17},{9,25},{17,1},{25,9},{2,18},{10... | collective-permute-start | bytes 2949128 | tf_op jit(solution)/shard_map/ppermute | solution.py:340
  273.2 22.3 %collective-permute-start.35 = (bf16[640,1280]{1,0:T(8,128)(2,1)}, bf16[640,1280]{1,0:T(8,128)(2,1)}, u32[]{:S(2)}, u32[]{:S(2)}) collective-permute-start(bf16[640,1280]{1,0:T(8,128)(2,1)} %get-tuple-element.65), channel_id=1, source_target_pairs={{0,8},{8,0},{16,24},{24,16},{1,9},{9,1},{17,25},{25,17},{2,10},{10... | collective-permute-start | bytes 4915208 | tf_op jit(solution)/shard_map/ppermute | solution.py:337
  (33 other events, 442.8 us)

commit v10 on v9

--- a/solution.py
+++ b/solution.py
@@ -305,11 +305,10 @@
                     (ahead[half],) = after([ahead[half]], waits)
                 got[-2][half] = lax.ppermute(ahead[half], SLABS, onward)
                 got[-1][half] = lax.ppermute(behind[half], SLABS, backward)
-        waits = gate(reach, 0, got) if gate else ()
         last = []
         for half, side, way in ((0, -2, onward), (1, -1, backward)):
-            if waits:
-                (got[side][half],) = after([got[side][half]], waits)
+            waits = gate(reach, half, got) if gate else ()
+            (got[side][half],) = after([got[side][half]], [got[-3 - side][half], *waits])
             last.append(lax.ppermute(got[side][half], SLABS, way))
         got.append(last)
         return got
@@ -345,9 +344,9 @@
 
     terms, starts = [], []
     for a in range(1, local_subjects):
-        shares, sums = [], []
-
-        def gate(d, half, got, a=a, before=everything[-1], shares=shares, sums=sums):
+        shares, sums, gone = [], [], []
+
+        def gate(d, half, got, a=a, before=everything[-1], shares=shares, sums=sums, gone=gone):
             if d == 1:
                 return [before[-3][half], before[-2][half]]
             n = d - 2
@@ -355,21 +354,22 @@
                 late = [*got[2 * n - 1], *got[2 * n]] if n else ()
                 shares.append(share(a - 1, [(aways[n], flip, *part) for part in cut for flip in (0, 1)], late))
             waits = [shares[n][0]] if n < chips - 1 else []
-            if (d, half) == (reach, 0):
+            if d < reach:
+                return waits
+            if half == 0:
                 for m, (away, arrays) in enumerate(zip(aways[:-1], shares)):
-                    hold = [*got[2 * m + 1], *got[2 * m + 2]]
+                    hold = [got[2 * m + 1][0], got[2 * m + 2][0]]
                     for (start, _), same, other in zip(cut, arrays[::2], arrays[1::2]):
-                        sums.append((added(same, cross(other, hold)), away, start))
-            if d >= reach:
-                waits += [summed for summed, _, _ in sums]
-            return waits
+                        sums.append(added(same, cross(other, hold)))
+                        gone.append(send(sums[-1], away, SHORT))
+                        starts.append(start)
+                return sums
+            return [*sums, *gone[1::2]]
 
         everything.append(gather(a, gate))
-        for summed, d, start in sums:
-            terms.append(send(summed, d, SHORT))
-            starts.append(start)
+        terms += gone
         same, other = share(a - 1, [(0, flip, 0, chunk) for flip in (0, 1)], [everything[a][-3][0], everything[a][-2][1]])
-        gone = [*terms, same]
+        gone.append(same)
         terms += [same, cross(other)]
         starts += [None, None]
     last = local_subjects - 1

time: 306 us -> 309 us (level)
  starting transfers between devices: 38.1 us -> 44.3 us
    ppermute x12, waiting for transfers between devices: 77.3 us -> 107 us  [gather(): got[-2][half] = lax.ppermute(ahead[half], SLABS, onward)]
    ppermute x12, waiting for transfers between devices: 59.8 us -> 35.8 us  [gather(): got[-1][half] = lax.ppermute(behind[half], SLABS, backward)]
    ppermute x4, waiting for transfers between devices: 21.2 us -> 14.6 us  [gather(): last.append(lax.ppermute(got[side][half], SLABS, way))]
    ppermute x4, starting transfers between devices: 4.53 us -> 9.66 us  [send(): lax.ppermute(summed, 'subj', [(s, (s + 2 * d) % subjs) for s in range(sub...]
  transfers between devices with their start and end apart: 38 -> 38, of which waited for: 23 -> 20; matrix products, arithmetic and copies ran while one was open for 2% -> 2% of each run, Pallas kernels for 19% -> 18%
where the time goes in v10:
time: 309 us; the launch traced here: 310 us
  waiting for transfers between devices  170 us (55%)
  Pallas kernels  72 us (23%)
  starting transfers between devices  44.3 us (14%)
  local copies, waits for them, and re-layouts  15.9 us (5%)
  other arithmetic  7.57 us (2%)
    ppermute x12, waiting for transfers between devices, gather(): got[-2][half] = lax.ppermute(ahead[half], SLABS, onward)  107 us
    pallas_call x5, Pallas kernels, scores(): pl.pallas_call(functools.partial(scores_kernel, subject=subject, targets=...  55.2 us
    ppermute x12, waiting for transfers between devices, gather(): got[-1][half] = lax.ppermute(behind[half], SLABS, backward)  35.8 us
    ppermute x12, starting transfers between devices, gather(): got[-1][half] = lax.ppermute(behind[half], SLABS, backward)  17.8 us
    unnamed x54, local copies, waits for them, and re-layouts  15.2 us
    ppermute x4, waiting for transfers between devices, gather(): last.append(lax.ppermute(got[side][half], SLABS, way))  14.6 us
    ppermute x4, starting transfers between devices, send(): lax.ppermute(summed, 'subj', [(s, (s + 2 * d) % subjs) for s in range(sub...  9.66 us
    ppermute x12, starting transfers between devices, gather(): got[-2][half] = lax.ppermute(ahead[half], SLABS, onward)  9.58 us
  transfers between devices with their start and end apart: 38, of which 20 were waited for; matrix products, arithmetic and copies ran while one was open for 2% of the time, Pallas kernels for 18%

profile of v10, /device:TPU:0, one launch (start us, length us, event | category | flops | bytes accessed | tf_op | source)
XLA Modules:
  0.0 309.9 jit_solution(7091680999757005095)
XLA Ops:
  0.0 3.7 %shard_map.42 = (bf16[320,1280]{1,0:T(8,128)(2,1)S(1)}, bf16[320,1152]{1,0:T(8,128)(2,1)S(1)}) custom-call(f32[2,1200,640]{2,1,0:T(8,128)} %bitcast.5), custom_call_target="tpu_custom_call" | custom-call | bytes 1024 | tf_op jit(solution)/shard_map/pallas_call | solution.py:76
  3.8 3.0 collective-permute-start.7
  6.9 4.5 %shard_map.37 = (bf16[320,1280]{1,0:T(8,128)(2,1)}, bf16[320,1152]{1,0:T(8,128)(2,1)S(1)}) custom-call(f32[2,1200,640]{2,1,0:T(8,128)} %bitcast.6), custom_call_target="tpu_custom_call" | custom-call | bytes 1024 | tf_op jit(solution)/shard_map/pallas_call | solution.py:76
  14.3 11.6 %collective-permute-done.7.refs_1_ = bf16[320,1280]{1,0:T(8,128)(2,1)S(1)} collective-permute-done((bf16[320,1280]{1,0:T(8,128)(2,1)S(1)}, bf16[320,1280]{1,0:T(8,128)(2,1)S(1)}, u32[]{:S(2)}, u32[]{:S(2)}) %collective-permute-start.7) | collective-permute-done | bytes 819232 | tf_op jit(solution)/shard_map/ppermute | solution.py:307
  30.9 12.6 %collective-permute-done.1.refs_1_ = bf16[320,1280]{1,0:T(8,128)(2,1)S(1)} collective-permute-done((bf16[320,1280]{1,0:T(8,128)(2,1)}, bf16[320,1280]{1,0:T(8,128)(2,1)S(1)}, u32[]{:S(2)}, u32[]{:S(2)}) %collective-permute-start.1) | collective-permute-done | bytes 819232 | tf_op jit(solution)/shard_map/ppermute | solution.py:307
  43.5 2.0 collective-permute-done.refs_0_
  48.5 14.6 %collective-permute-done.8.refs_0_ = bf16[320,1280]{1,0:T(8,128)(2,1)S(1)} collective-permute-done((bf16[320,1280]{1,0:T(8,128)(2,1)}, bf16[320,1280]{1,0:T(8,128)(2,1)S(1)}, u32[]{:S(2)}, u32[]{:S(2)}) %collective-permute-start.8) | collective-permute-done | bytes 819232 | tf_op jit(solution)/shard_map/ppermute | solution.py:306
  66.0 14.6 %collective-permute-done.2.refs_0_ = bf16[320,1280]{1,0:T(8,128)(2,1)S(1)} collective-permute-done((bf16[320,1280]{1,0:T(8,128)(2,1)}, bf16[320,1280]{1,0:T(8,128)(2,1)S(1)}, u32[]{:S(2)}, u32[]{:S(2)}) %collective-permute-start.2) | collective-permute-done | bytes 819232 | tf_op jit(solution)/shard_map/ppermute | solution.py:306
  83.6 14.6 %collective-permute-done.10.refs_1_.refs_11_.refs_27_ = bf16[320,1280]{1,0:T(8,128)(2,1)S(1)} collective-permute-done((bf16[320,1280]{1,0:T(8,128)(2,1)}, bf16[320,1280]{1,0:T(8,128)(2,1)S(1)}, u32[]{:S(2)}, u32[]{:S(2)}) %collective-permute-start.10) | collective-permute-done | bytes 819232 | tf_op jit(solution)/shard_map/ppermute | solution.py:306
  101.6 12.8 %collective-permute-done.4.refs_0_ = bf16[320,1280]{1,0:T(8,128)(2,1)} collective-permute-done((bf16[320,1280]{1,0:T(8,128)(2,1)}, bf16[320,1280]{1,0:T(8,128)(2,1)}, u32[]{:S(2)}, u32[]{:S(2)}) %collective-permute-start.4) | collective-permute-done | bytes 819232 | tf_op jit(solution)/shard_map/ppermute | solution.py:306
  119.5 11.9 %collective-permute-done.15.refs_15_.refs_31_ = bf16[320,1280]{1,0:T(8,128)(2,1)} collective-permute-done((bf16[320,1280]{1,0:T(8,128)(2,1)}, bf16[320,1280]{1,0:T(8,128)(2,1)}, u32[]{:S(2)}, u32[]{:S(2)}) %collective-permute-start.15) | collective-permute-done | bytes 819232 | tf_op jit(solution)/shard_map/ppermute | solution.py:312
  131.4 2.1 collective-permute-start.16
  134.1 2.7 collective-permute-done.14.refs_14_.refs_30_
  136.8 14.7 %shard_map.47 = (bf16[640,768]{1,0:T(8,128)(2,1)}, bf16[640,768]{1,0:T(8,128)(2,1)}, bf16[640,512]{1,0:T(8,128)(2,1)S(1)}, bf16[640,512]{1,0:T(8,128)(2,1)S(1)}) custom-call(s32[8]{0:T(128)S(1)} %dynamic-slice_bitcast_fusion.source_ref, s32[5]{0:T(128)S(1)} %copy-done.17, s32[2]{0:T(128)S(1)} %pad_add_fusion.place_ref, ...), custom_call_target="tpu_custom_call" | custom-call | bytes 1024 | tf_op jit(solution)/shard_map/pallas_call | solution.py:244
  154.5 7.6 %collective-permute-done.17.refs_1_ = bf16[320,1152]{1,0:T(8,128)(2,1)} collective-permute-done((bf16[320,1152]{1,0:T(8,128)(2,1)}, bf16[320,1152]{1,0:T(8,128)(2,1)}, u32[]{:S(2)}, u32[]{:S(2)}) %collective-permute-start.17) | collective-permute-done | bytes 737312 | tf_op jit(solution)/shard_map/ppermute | solution.py:307
  163.8 4.6 %collective-permute-done.16.refs_0_ = bf16[320,1152]{1,0:T(8,128)(2,1)} collective-permute-done((bf16[320,1152]{1,0:T(8,128)(2,1)}, bf16[320,1152]{1,0:T(8,128)(2,1)}, u32[]{:S(2)}, u32[]{:S(2)}) %collective-permute-start.16) | collective-permute-done | bytes 737312 | tf_op jit(solution)/shard_map/ppermute | solution.py:306
  170.4 2.3 add_convert_fusion.3.refs_3_
  172.8 11.4 %collective-permute-done.18.refs_0_ = bf16[320,1152]{1,0:T(8,128)(2,1)} collective-permute-done((bf16[320,1152]{1,0:T(8,128)(2,1)}, bf16[320,1152]{1,0:T(8,128)(2,1)}, u32[]{:S(2)}, u32[]{:S(2)}) %collective-permute-start.18) | collective-permute-done | bytes 737312 | tf_op jit(solution)/shard_map/ppermute | solution.py:306
  187.1 12.9 %collective-permute-done.20.refs_0_ = bf16[320,1152]{1,0:T(8,128)(2,1)} collective-permute-done((bf16[320,1152]{1,0:T(8,128)(2,1)}, bf16[320,1152]{1,0:T(8,128)(2,1)}, u32[]{:S(2)}, u32[]{:S(2)}) %collective-permute-start.20) | collective-permute-done | bytes 737312 | tf_op jit(solution)/shard_map/ppermute | solution.py:306
  203.6 2.7 add_convert_fusion.1.refs_2_
  207.8 8.0 %collective-permute-done.22.refs_0_ = bf16[320,1152]{1,0:T(8,128)(2,1)} collective-permute-done((bf16[320,1152]{1,0:T(8,128)(2,1)}, bf16[320,1152]{1,0:T(8,128)(2,1)}, u32[]{:S(2)}, u32[]{:S(2)}) %collective-permute-start.22) | collective-permute-done | bytes 737312 | tf_op jit(solution)/shard_map/ppermute | solution.py:306
  215.8 3.9 %collective-permute-done.23.refs_1_.refs_12_ = bf16[320,1152]{1,0:T(8,128)(2,1)} collective-permute-done((bf16[320,1152]{1,0:T(8,128)(2,1)}, bf16[320,1152]{1,0:T(8,128)(2,1)}, u32[]{:S(2)}, u32[]{:S(2)}) %collective-permute-start.23) | collective-permute-done | bytes 737312 | tf_op jit(solution)/shard_map/ppermute | solution.py:307
  221.1 10.5 %collective-permute-done.26.refs_1_.refs_11_ = bf16[320,1152]{1,0:T(8,128)(2,1)} collective-permute-done((bf16[320,1152]{1,0:T(8,128)(2,1)}, bf16[320,1152]{1,0:T(8,128)(2,1)}, u32[]{:S(2)}, u32[]{:S(2)}) %collective-permute-start.26) | collective-permute-done | bytes 737312 | tf_op jit(solution)/shard_map/ppermute | solution.py:306
  233.2 12.4 %shard_map.58 = (bf16[640,1280]{1,0:T(8,128)(2,1)}, bf16[640,1280]{1,0:T(8,128)(2,1)}) custom-call(s32[8]{0:T(128)S(1)} %dynamic-slice_bitcast_fusion.source_ref, s32[5]{0:T(128)S(1)} %copy-done.17, s32[2]{0:T(128)S(1)} %pad_add_fusion.place_ref, bf16[320,1280]{1,0:T(8,128)(2,1)} %get-tuple-element.37.refs_0_.refs_16_, ...), custom_call_target="tpu_custom_call" | custom-call | bytes 1024 | tf_op jit(solution)/shard_map/pallas_call | solution.py:244
  247.0 8.9 %shard_map.59 = (bf16[640,768]{1,0:T(8,128)(2,1)}, bf16[640,768]{1,0:T(8,128)(2,1)}) custom-call(s32[8]{0:T(128)S(1)} %dynamic-slice_bitcast_fusion.source_ref, s32[5]{0:T(128)S(1)} %copy-done.17, s32[2]{0:T(128)S(1)} %pad_add_fusion.place_ref, bf16[320,1152]{1,0:T(8,128)(2,1)S(1)} %copy-done.10, bf16[320,1152]{1,0:T(8,128)(2,1)S(1)} %copy-done.8, ...), custom_call_target="tpu_custom_call" | custom-call | bytes 1024 | tf_op jit(solution)/shard_map/pallas_call | solution.py:244
  256.0 2.8 collective-permute-done.32
  260.2 4.9 %collective-permute-start.36 = (bf16[640,768]{1,0:T(8,128)(2,1)S(1)}, bf16[640,768]{1,0:T(8,128)(2,1)S(1)}, u32[]{:S(2)}, u32[]{:S(2)}) collective-permute-start(bf16[640,768]{1,0:T(8,128)(2,1)S(1)} %add_convert_fusion.refs_32_), channel_id=1, source_target_pairs={{0,16},{8,24},{16,0},{24,8},{1,17},{9,25},{17,1},{25,9},{2,18},{10... | collective-permute-start | bytes 2949128 | tf_op jit(solution)/shard_map/ppermute | solution.py:339
  265.1 10.9 %shard_map.60 = (bf16[640,512]{1,0:T(8,128)(2,1)S(1)}, bf16[640,512]{1,0:T(8,128)(2,1)S(1)}, bf16[640,1280]{1,0:T(8,128)(2,1)}) custom-call(s32[8]{0:T(128)S(1)} %dynamic-slice_bitcast_fusion.source_ref, s32[5]{0:T(128)S(1)} %copy-done.17, s32[2]{0:T(128)S(1)} %pad_add_fusion.place_ref, bf16[320,1152]{1,0:T(8,128)(2,1)S(1)} %copy-done.10, ...), custom_call_target="tpu_custom_call" | custom-call | bytes 1024 | tf_op jit(solution)/shard_map/pallas_call | solution.py:244
  279.5 7.7 %collective-permute-done.36.refs_0_ = bf16[640,768]{1,0:T(8,128)(2,1)S(1)} collective-permute-done((bf16[640,768]{1,0:T(8,128)(2,1)S(1)}, bf16[640,768]{1,0:T(8,128)(2,1)S(1)}, u32[]{:S(2)}, u32[]{:S(2)}) %collective-permute-start.36) | collective-permute-done | bytes 983072 | tf_op jit(solution)/shard_map/ppermute | solution.py:339
  291.0 8.3 %shard_map.61.refs_4_ = bf16[640,1280]{1,0:T(8,128)(2,1)} custom-call(s32[8]{0:T(128)S(1)} %dynamic-slice_bitcast_fusion.source_ref, s32[5]{0:T(128)S(1)} %copy-done.17, s32[2]{0:T(128)S(1)} %pad_add_fusion.place_ref, bf16[320,1152]{1,0:T(8,128)(2,1)S(1)} %copy-done.10, bf16[320,1152]{1,0:T(8,128)(2,1)S(1)} %copy-done.8, ...), custom_call_target="tpu_custom_call" | custom-call | bytes 1024 | tf_op jit(solution)/shard_map/pallas_call | solution.py:244
  300.5 6.1 %shard_map.64.refs_1_.before_ref = f32[640,1280]{1,0:T(8,128)} custom-call(bf16[640,768]{1,0:T(8,128)(2,1)} %shard_map.57.refs_32_.refs_0_, bf16[640,512]{1,0:T(8,128)(2,1)} %shard_map.55.refs_4_.refs_33_.refs_1_, bf16[640,1280]{1,0:T(8,128)(2,1)S(1)} %copy-done.13, bf16[640,1280]{1,0:T(8,128)(2,1)} %collective-permute-done.35.refs_3_, ...), custom_call_target="tpu_custom_call" | custom-call | bytes 1024 | tf_op jit(solution)/shard_map/pallas_call | solution.py:119
  307.5 2.4 shard_map.66
  (134 shorter events, 55.7 us)
Async XLA Ops:
  3.8 22.1 %collective-permute-start.7 = (bf16[320,1280]{1,0:T(8,128)(2,1)S(1)}, bf16[320,1280]{1,0:T(8,128)(2,1)S(1)}, u32[]{:S(2)}, u32[]{:S(2)}) collective-permute-start(bf16[320,1280]{1,0:T(8,128)(2,1)S(1)} %get-tuple-element.43.refs_1_.refs_17_), channel_id=1, source_target_pairs={{2,0},{4,2},{6,4},{7,6},{5,7},{3,5},{1,3},{0,1},{10,8},{12,10},{14... | collective-permute-start | bytes 2457608 | tf_op jit(solution)/shard_map/ppermute | solution.py:307
  6.8 21.2 %collective-permute-start.6 = (bf16[320,1280]{1,0:T(8,128)(2,1)S(1)}, bf16[320,1280]{1,0:T(8,128)(2,1)S(1)}, u32[]{:S(2)}, u32[]{:S(2)}) collective-permute-start(bf16[320,1280]{1,0:T(8,128)(2,1)S(1)} %get-tuple-element.43.refs_1_.refs_17_), channel_id=1, source_target_pairs={{0,2},{2,4},{4,6},{6,7},{7,5},{5,3},{3,1},{1,0},{8,10},{10,12},{12... | collective-permute-start | bytes 2457608 | tf_op jit(solution)/shard_map/ppermute | solution.py:306
  12.3 31.2 %collective-permute-start.1 = (bf16[320,1280]{1,0:T(8,128)(2,1)}, bf16[320,1280]{1,0:T(8,128)(2,1)S(1)}, u32[]{:S(2)}, u32[]{:S(2)}) collective-permute-start(bf16[320,1280]{1,0:T(8,128)(2,1)} %get-tuple-element.37.refs_0_.refs_16_), channel_id=1, source_target_pairs={{2,0},{4,2},{6,4},{7,6},{5,7},{3,5},{1,3},{0,1},{10,8},{12,10},{14... | collective-permute-start | bytes 2457608 | tf_op jit(solution)/shard_map/ppermute | solution.py:307
  14.2 31.3 %collective-permute-start = (bf16[320,1280]{1,0:T(8,128)(2,1)}, bf16[320,1280]{1,0:T(8,128)(2,1)S(1)}, u32[]{:S(2)}, u32[]{:S(2)}) collective-permute-start(bf16[320,1280]{1,0:T(8,128)(2,1)} %get-tuple-element.37.refs_0_.refs_16_), channel_id=1, source_target_pairs={{0,2},{2,4},{4,6},{6,7},{7,5},{5,3},{3,1},{1,0},{8,10},{10,12},{12... | collective-permute-start | bytes 2457608 | tf_op jit(solution)/shard_map/ppermute | solution.py:306
  28.9 34.2 %collective-permute-start.8 = (bf16[320,1280]{1,0:T(8,128)(2,1)}, bf16[320,1280]{1,0:T(8,128)(2,1)S(1)}, u32[]{:S(2)}, u32[]{:S(2)}) collective-permute-start(bf16[320,1280]{1,0:T(8,128)(2,1)} %get-tuple-element.44.refs_3_.refs_19_), channel_id=1, source_target_pairs={{0,2},{2,4},{4,6},{6,7},{7,5},{5,3},{3,1},{1,0},{8,10},{10,12},{12... | collective-permute-start | bytes 2457608 | tf_op jit(solution)/shard_map/ppermute | solution.py:306
  29.8 33.3 %collective-permute-start.9 = (bf16[320,1280]{1,0:T(8,128)(2,1)}, bf16[320,1280]{1,0:T(8,128)(2,1)}, u32[]{:S(2)}, u32[]{:S(2)}) collective-permute-start(bf16[320,1280]{1,0:T(8,128)(2,1)} %get-tuple-element.45.refs_5_.refs_21_), channel_id=1, source_target_pairs={{2,0},{4,2},{6,4},{7,6},{5,7},{3,5},{1,3},{0,1},{10,8},{12,10},{14... | collective-permute-start | bytes 2457608 | tf_op jit(solution)/shard_map/ppermute | solution.py:307
  46.4 34.2 %collective-permute-start.2 = (bf16[320,1280]{1,0:T(8,128)(2,1)}, bf16[320,1280]{1,0:T(8,128)(2,1)S(1)}, u32[]{:S(2)}, u32[]{:S(2)}) collective-permute-start(bf16[320,1280]{1,0:T(8,128)(2,1)} %get-tuple-element.38.refs_2_.refs_18_), channel_id=1, source_target_pairs={{0,2},{2,4},{4,6},{6,7},{7,5},{5,3},{3,1},{1,0},{8,10},{10,12},{12... | collective-permute-start | bytes 2457608 | tf_op jit(solution)/shard_map/ppermute | solution.py:306
  47.4 33.2 %collective-permute-start.3 = (bf16[320,1280]{1,0:T(8,128)(2,1)}, bf16[320,1280]{1,0:T(8,128)(2,1)}, u32[]{:S(2)}, u32[]{:S(2)}) collective-permute-start(bf16[320,1280]{1,0:T(8,128)(2,1)} %get-tuple-element.39.refs_4_.refs_20_), channel_id=1, source_target_pairs={{2,0},{4,2},{6,4},{7,6},{5,7},{3,5},{1,3},{0,1},{10,8},{12,10},{14... | collective-permute-start | bytes 2457608 | tf_op jit(solution)/shard_map/ppermute | solution.py:307
  64.0 34.2 %collective-permute-start.10 = (bf16[320,1280]{1,0:T(8,128)(2,1)}, bf16[320,1280]{1,0:T(8,128)(2,1)S(1)}, u32[]{:S(2)}, u32[]{:S(2)}) collective-permute-start(bf16[320,1280]{1,0:T(8,128)(2,1)} %get-tuple-element.46.refs_7_.refs_23_), channel_id=1, source_target_pairs={{0,2},{2,4},{4,6},{6,7},{7,5},{5,3},{3,1},{1,0},{8,10},{10,12},{12... | collective-permute-start | bytes 2457608 | tf_op jit(solution)/shard_map/ppermute | solution.py:306
  64.1 34.1 %collective-permute-start.11 = (bf16[320,1280]{1,0:T(8,128)(2,1)}, bf16[320,1280]{1,0:T(8,128)(2,1)S(1)}, u32[]{:S(2)}, u32[]{:S(2)}) collective-permute-start(bf16[320,1280]{1,0:T(8,128)(2,1)} %get-tuple-element.47.refs_9_.refs_25_), channel_id=1, source_target_pairs={{2,0},{4,2},{6,4},{7,6},{5,7},{3,5},{1,3},{0,1},{10,8},{12,10},{14... | collective-permute-start | bytes 2457608 | tf_op jit(solution)/shard_map/ppermute | solution.py:307
  81.5 32.8 %collective-permute-start.4 = (bf16[320,1280]{1,0:T(8,128)(2,1)}, bf16[320,1280]{1,0:T(8,128)(2,1)}, u32[]{:S(2)}, u32[]{:S(2)}) collective-permute-start(bf16[320,1280]{1,0:T(8,128)(2,1)} %get-tuple-element.40.refs_6_.refs_22_), channel_id=1, source_target_pairs={{0,2},{2,4},{4,6},{6,7},{7,5},{5,3},{3,1},{1,0},{8,10},{10,12},{12... | collective-permute-start | bytes 2457608 | tf_op jit(solution)/shard_map/ppermute | solution.py:306
  81.6 32.8 %collective-permute-start.5 = (bf16[320,1280]{1,0:T(8,128)(2,1)}, bf16[320,1280]{1,0:T(8,128)(2,1)S(1)}, u32[]{:S(2)}, u32[]{:S(2)}) collective-permute-start(bf16[320,1280]{1,0:T(8,128)(2,1)} %get-tuple-element.41.refs_8_.refs_24_), channel_id=1, source_target_pairs={{2,0},{4,2},{6,4},{7,6},{5,7},{3,5},{1,3},{0,1},{10,8},{12,10},{14... | collective-permute-start | bytes 2457608 | tf_op jit(solution)/shard_map/ppermute | solution.py:307
  100.0 31.4 %collective-permute-start.15 = (bf16[320,1280]{1,0:T(8,128)(2,1)}, bf16[320,1280]{1,0:T(8,128)(2,1)}, u32[]{:S(2)}, u32[]{:S(2)}) collective-permute-start(bf16[320,1280]{1,0:T(8,128)(2,1)} %shard_map.45.refs_2_.refs_13_.refs_29_), channel_id=1, source_target_pairs={{2,0},{4,2},{6,4},{7,6},{5,7},{3,5},{1,3},{0,1},{10,8},{12,10},{14... | collective-permute-start | bytes 2457608 | tf_op jit(solution)/shard_map/ppermute | solution.py:312
  115.3 21.5 %collective-permute-start.14 = (bf16[320,1280]{1,0:T(8,128)(2,1)}, bf16[320,1280]{1,0:T(8,128)(2,1)}, u32[]{:S(2)}, u32[]{:S(2)}) collective-permute-start(bf16[320,1280]{1,0:T(8,128)(2,1)} %shard_map.40.refs_1_.refs_10_.refs_26_), channel_id=1, source_target_pairs={{0,2},{2,4},{4,6},{6,7},{7,5},{5,3},{3,1},{1,0},{8,10},{10,12},{12... | collective-permute-start | bytes 2457608 | tf_op jit(solution)/shard_map/ppermute | solution.py:312
  116.7 36.5 %collective-permute-start.13 = (bf16[320,1152]{1,0:T(8,128)(2,1)}, bf16[320,1152]{1,0:T(8,128)(2,1)}, u32[]{:S(2)}, u32[]{:S(2)}) collective-permute-start(bf16[320,1152]{1,0:T(8,128)(2,1)} %shard_map.41.refs_0_), channel_id=1, source_target_pairs={{2,0},{4,2},{6,4},{7,6},{5,7},{3,5},{1,3},{0,1},{10,8},{12,10},{14... | collective-permute-start | bytes 2211848 | tf_op jit(solution)/shard_map/ppermute | solution.py:307
  117.4 35.8 %collective-permute-start.12 = (bf16[320,1152]{1,0:T(8,128)(2,1)}, bf16[320,1152]{1,0:T(8,128)(2,1)}, u32[]{:S(2)}, u32[]{:S(2)}) collective-permute-start(bf16[320,1152]{1,0:T(8,128)(2,1)} %shard_map.41.refs_0_), channel_id=1, source_target_pairs={{0,2},{2,4},{4,6},{6,7},{7,5},{5,3},{3,1},{1,0},{8,10},{10,12},{12... | collective-permute-start | bytes 2211848 | tf_op jit(solution)/shard_map/ppermute | solution.py:306
  118.8 43.3 %collective-permute-start.17 = (bf16[320,1152]{1,0:T(8,128)(2,1)}, bf16[320,1152]{1,0:T(8,128)(2,1)}, u32[]{:S(2)}, u32[]{:S(2)}) collective-permute-start(bf16[320,1152]{1,0:T(8,128)(2,1)} %shard_map.46.refs_1_), channel_id=1, source_target_pairs={{2,0},{4,2},{6,4},{7,6},{5,7},{3,5},{1,3},{0,1},{10,8},{12,10},{14... | collective-permute-start | bytes 2211848 | tf_op jit(solution)/shard_map/ppermute | solution.py:307
  131.4 37.0 %collective-permute-start.16 = (bf16[320,1152]{1,0:T(8,128)(2,1)}, bf16[320,1152]{1,0:T(8,128)(2,1)}, u32[]{:S(2)}, u32[]{:S(2)}) collective-permute-start(bf16[320,1152]{1,0:T(8,128)(2,1)} %shard_map.46.refs_1_), channel_id=1, source_target_pairs={{0,2},{2,4},{4,6},{6,7},{7,5},{5,3},{3,1},{1,0},{8,10},{10,12},{12... | collective-permute-start | bytes 2211848 | tf_op jit(solution)/shard_map/ppermute | solution.py:306
  153.3 48.7 %collective-permute-start.24 = (bf16[640,768]{1,0:T(8,128)(2,1)}, bf16[640,768]{1,0:T(8,128)(2,1)}, u32[]{:S(2)}, u32[]{:S(2)}) collective-permute-start(bf16[640,768]{1,0:T(8,128)(2,1)} %shard_map.52), channel_id=1, source_target_pairs={{0,8},{8,0},{16,24},{24,16},{1,9},{9,1},{17,25},{25,17},{2,10},{10... | collective-permute-start | bytes 2949128 | tf_op jit(solution)/shard_map/ppermute | solution.py:336
  153.8 30.4 %collective-permute-start.18 = (bf16[320,1152]{1,0:T(8,128)(2,1)}, bf16[320,1152]{1,0:T(8,128)(2,1)}, u32[]{:S(2)}, u32[]{:S(2)}) collective-permute-start(bf16[320,1152]{1,0:T(8,128)(2,1)} %get-tuple-element.49.refs_1_.refs_2_), channel_id=1, source_target_pairs={{0,2},{2,4},{4,6},{6,7},{7,5},{5,3},{3,1},{1,0},{8,10},{10,12},{12... | collective-permute-start | bytes 2211848 | tf_op jit(solution)/shard_map/ppermute | solution.py:306
  162.1 23.6 %collective-permute-start.19 = (bf16[320,1152]{1,0:T(8,128)(2,1)}, bf16[320,1152]{1,0:T(8,128)(2,1)}, u32[]{:S(2)}, u32[]{:S(2)}) collective-permute-start(bf16[320,1152]{1,0:T(8,128)(2,1)} %get-tuple-element.51.refs_2_.refs_4_), channel_id=1, source_target_pairs={{2,0},{4,2},{6,4},{7,6},{5,7},{3,5},{1,3},{0,1},{10,8},{12,10},{14... | collective-permute-start | bytes 2211848 | tf_op jit(solution)/shard_map/ppermute | solution.py:307
  168.4 31.6 %collective-permute-start.20 = (bf16[320,1152]{1,0:T(8,128)(2,1)}, bf16[320,1152]{1,0:T(8,128)(2,1)}, u32[]{:S(2)}, u32[]{:S(2)}) collective-permute-start(bf16[320,1152]{1,0:T(8,128)(2,1)} %get-tuple-element.50.refs_3_), channel_id=1, source_target_pairs={{0,2},{2,4},{4,6},{6,7},{7,5},{5,3},{3,1},{1,0},{8,10},{10,12},{12... | collective-permute-start | bytes 2211848 | tf_op jit(solution)/shard_map/ppermute | solution.py:306
  169.8 31.8 %collective-permute-start.21 = (bf16[320,1152]{1,0:T(8,128)(2,1)}, bf16[320,1152]{1,0:T(8,128)(2,1)}, u32[]{:S(2)}, u32[]{:S(2)}) collective-permute-start(bf16[320,1152]{1,0:T(8,128)(2,1)} %get-tuple-element.52.refs_5_), channel_id=1, source_target_pairs={{2,0},{4,2},{6,4},{7,6},{5,7},{3,5},{1,3},{0,1},{10,8},{12,10},{14... | collective-permute-start | bytes 2211848 | tf_op jit(solution)/shard_map/ppermute | solution.py:307
  184.2 22.1 %collective-permute-start.28 = (bf16[640,512]{1,0:T(8,128)(2,1)}, bf16[640,512]{1,0:T(8,128)(2,1)}, u32[]{:S(2)}, u32[]{:S(2)}) collective-permute-start(bf16[640,512]{1,0:T(8,128)(2,1)} %add_convert_fusion.3.refs_3_), channel_id=1, source_target_pairs={{0,16},{8,24},{16,0},{24,8},{1,17},{9,25},{17,1},{25,9},{2,18},{10... | collective-permute-start | bytes 1966088 | tf_op jit(solution)/shard_map/ppermute | solution.py:339
  185.7 30.1 %collective-permute-start.22 = (bf16[320,1152]{1,0:T(8,128)(2,1)}, bf16[320,1152]{1,0:T(8,128)(2,1)}, u32[]{:S(2)}, u32[]{:S(2)}) collective-permute-start(bf16[320,1152]{1,0:T(8,128)(2,1)} %get-tuple-element.53.refs_6_), channel_id=1, source_target_pairs={{0,2},{2,4},{4,6},{6,7},{7,5},{5,3},{3,1},{1,0},{8,10},{10,12},{12... | collective-permute-start | bytes 2211848 | tf_op jit(solution)/shard_map/ppermute | solution.py:306
  200.0 19.7 %collective-permute-start.23 = (bf16[320,1152]{1,0:T(8,128)(2,1)}, bf16[320,1152]{1,0:T(8,128)(2,1)}, u32[]{:S(2)}, u32[]{:S(2)}) collective-permute-start(bf16[320,1152]{1,0:T(8,128)(2,1)} %get-tuple-element.55.refs_8_), channel_id=1, source_target_pairs={{2,0},{4,2},{6,4},{7,6},{5,7},{3,5},{1,3},{0,1},{10,8},{12,10},{14... | collective-permute-start | bytes 2211848 | tf_op jit(solution)/shard_map/ppermute | solution.py:307
  201.6 30.0 %collective-permute-start.26 = (bf16[320,1152]{1,0:T(8,128)(2,1)}, bf16[320,1152]{1,0:T(8,128)(2,1)}, u32[]{:S(2)}, u32[]{:S(2)}) collective-permute-start(bf16[320,1152]{1,0:T(8,128)(2,1)} %get-tuple-element.54.refs_7_), channel_id=1, source_target_pairs={{0,2},{2,4},{4,6},{6,7},{7,5},{5,3},{3,1},{1,0},{8,10},{10,12},{12... | collective-permute-start | bytes 2211848 | tf_op jit(solution)/shard_map/ppermute | solution.py:306
  202.0 29.6 %collective-permute-start.27 = (bf16[320,1152]{1,0:T(8,128)(2,1)}, bf16[320,1152]{1,0:T(8,128)(2,1)}, u32[]{:S(2)}, u32[]{:S(2)}) collective-permute-start(bf16[320,1152]{1,0:T(8,128)(2,1)} %get-tuple-element.56.refs_9_), channel_id=1, source_target_pairs={{2,0},{4,2},{6,4},{7,6},{5,7},{3,5},{1,3},{0,1},{10,8},{12,10},{14... | collective-permute-start | bytes 2211848 | tf_op jit(solution)/shard_map/ppermute | solution.py:307
  206.3 39.3 %collective-permute-start.31 = (bf16[640,768]{1,0:T(8,128)(2,1)}, bf16[640,768]{1,0:T(8,128)(2,1)}, u32[]{:S(2)}, u32[]{:S(2)}) collective-permute-start(bf16[640,768]{1,0:T(8,128)(2,1)} %add_convert_fusion.1.refs_2_), channel_id=1, source_target_pairs={{0,16},{8,24},{16,0},{24,8},{1,17},{9,25},{17,1},{25,9},{2,18},{10... | collective-permute-start | bytes 2949128 | tf_op jit(solution)/shard_map/ppermute | solution.py:339
  219.7 25.9 %collective-permute-start.29 = (bf16[320,1152]{1,0:T(8,128)(2,1)}, bf16[320,1152]{1,0:T(8,128)(2,1)}, u32[]{:S(2)}, u32[]{:S(2)}) collective-permute-start(bf16[320,1152]{1,0:T(8,128)(2,1)} %shard_map.54.refs_32_.refs_10_), channel_id=1, source_target_pairs={{0,2},{2,4},{4,6},{6,7},{7,5},{5,3},{3,1},{1,0},{8,10},{10,12},{12... | collective-permute-start | bytes 2211848 | tf_op jit(solution)/shard_map/ppermute | solution.py:312
  260.2 27.0 %collective-permute-start.36 = (bf16[640,768]{1,0:T(8,128)(2,1)S(1)}, bf16[640,768]{1,0:T(8,128)(2,1)S(1)}, u32[]{:S(2)}, u32[]{:S(2)}) collective-permute-start(bf16[640,768]{1,0:T(8,128)(2,1)S(1)} %add_convert_fusion.refs_32_), channel_id=1, source_target_pairs={{0,16},{8,24},{16,0},{24,8},{1,17},{9,25},{17,1},{25,9},{2,18},{10... | collective-permute-start | bytes 2949128 | tf_op jit(solution)/shard_map/ppermute | solution.py:339
  276.6 22.8 %collective-permute-start.35 = (bf16[640,1280]{1,0:T(8,128)(2,1)}, bf16[640,1280]{1,0:T(8,128)(2,1)}, u32[]{:S(2)}, u32[]{:S(2)}) collective-permute-start(bf16[640,1280]{1,0:T(8,128)(2,1)} %get-tuple-element.65), channel_id=1, source_target_pairs={{0,8},{8,0},{16,24},{24,16},{1,9},{9,1},{17,25},{25,17},{2,10},{10... | collective-permute-start | bytes 4915208 | tf_op jit(solution)/shard_map/ppermute | solution.py:336
  (33 other events, 429.9 us)

commit v11 on v10

--- a/solution.py
+++ b/solution.py
@@ -206,24 +206,26 @@
     own_rows[:, body:] = jnp.where(kept, own_rows[:, body:].astype(jnp.float32), 0.0).astype(jnp.bfloat16)
 
     limit = clip_limit * duration
-    width = products_a.shape[1]
+    widest = products_a.shape[1]
     tiles = []
     for n, out_ref in enumerate(out_refs):
-        tiles += [(n + 1, k, out_ref) for k in range(0, out_ref.shape[1], width)]
+        columns = out_ref.shape[1]
+        tiles += [(n + 1, k, min(widest, columns - k), out_ref) for k in range(0, columns, widest)]
     buffers = (products_a, products_b)
 
     def multiply(i):
-        n, k, _ = tiles[i]
+        n, k, width, _ = tiles[i]
         if k == 0:
             arrived(n)
-        buffers[i % 2][...] = lax.dot_general(
+        buffers[i % 2][:, :width] = lax.dot_general(
             own_rows[...], wanted[n][1][pl.ds(k, width)], (((1,), (1,)), ((), ())), preferred_element_type=jnp.float32
         )
 
     def score(i):
-        products = jnp.clip(buffers[i % 2][...], -limit, limit)
+        _, k, width, out_ref = tiles[i]
+        products = jnp.clip(buffers[i % 2][:, :width], -limit, limit)
         fisher = 0.5 * (jnp.log(duration + products) - jnp.log(duration - products))
-        tiles[i][2][:, pl.ds(tiles[i][1], width)] = fisher.astype(jnp.bfloat16)
+        out_ref[:, pl.ds(k, width)] = fisher.astype(jnp.bfloat16)
 
     multiply(0)
     for i in range(1, len(tiles)):
@@ -238,7 +240,7 @@
     chunk = window // (2 * chips)
     sizes = [columns for _, _, _, columns in targets]
     granule = math.gcd(*cuts, *sizes, *(first for _, _, first, _ in targets), block_rows)
-    width = math.gcd(*sizes, 256)
+    widest = min(512, *sizes)
     padded = tails[0].shape[1]
     smem = pl.BlockSpec(memory_space=pltpu.SMEM)
     return pl.pallas_call(
@@ -259,8 +261,8 @@
         scratch_shapes=[pltpu.VMEM((columns, padded), jnp.bfloat16) for columns in sizes]
         + [
             pltpu.VMEM((slab, padded), jnp.bfloat16),
-            pltpu.VMEM((slab, width), jnp.float32),
-            pltpu.VMEM((slab, width), jnp.float32),
+            pltpu.VMEM((slab, widest), jnp.float32),
+            pltpu.VMEM((slab, widest), jnp.float32),
             pltpu.SMEM((block_start.shape[0],), jnp.int32),
             pltpu.SemaphoreType.DMA((1 + len(targets),)),
         ],

time: 309 us -> 309 us (level)
  starting transfers between devices: 44.3 us -> 38.8 us
    ppermute x4, starting transfers between devices: 9.66 us -> 3.34 us  [send(): lax.ppermute(summed, 'subj', [(s, (s + 2 * d) % subjs) for s in range(sub...]
  transfers between devices with their start and end apart: 38 -> 38, of which waited for: 20 -> 22; matrix products, arithmetic and copies ran while one was open for 2% -> 2% of each run, Pallas kernels for 18% -> 18%
where the time goes in v11:
time: 309 us
  waiting for transfers between devices  173 us (56%)
  Pallas kernels  72 us (23%)
  starting transfers between devices  38.8 us (13%)
  local copies, waits for them, and re-layouts  16.7 us (5%)
  other arithmetic  7.57 us (2%)
    ppermute x12, waiting for transfers between devices, gather(): got[-2][half] = lax.ppermute(ahead[half], SLABS, onward)  108 us
    pallas_call x5, Pallas kernels, scores(): pl.pallas_call(functools.partial(scores_kernel, subject=subject, targets=...  55.2 us
    ppermute x12, waiting for transfers between devices, gather(): got[-1][half] = lax.ppermute(behind[half], SLABS, backward)  35.8 us
    ppermute x12, starting transfers between devices, gather(): got[-1][half] = lax.ppermute(behind[half], SLABS, backward)  17.8 us
    unnamed x54, local copies, waits for them, and re-layouts  16 us
    ppermute x4, waiting for transfers between devices, gather(): last.append(lax.ppermute(got[side][half], SLABS, way))  14.6 us
    ppermute x12, starting transfers between devices, gather(): got[-2][half] = lax.ppermute(ahead[half], SLABS, onward)  10.3 us
    ppermute x4, waiting for transfers between devices, send(): lax.ppermute(summed, 'subj', [(s, (s + 2 * d) % subjs) for s in range(sub...  10 us
  transfers between devices with their start and end apart: 38, of which 22 were waited for; matrix products, arithmetic and copies ran while one was open for 2% of the time, Pallas kernels for 18%

profile of v11, /device:TPU:0, one launch (start us, length us, event | category | flops | bytes accessed | tf_op | source)
XLA Modules:
  0.0 308.7 jit_solution(6014528992285369983)
XLA Ops:
  0.0 3.7 %shard_map.42 = (bf16[320,1280]{1,0:T(8,128)(2,1)S(1)}, bf16[320,1152]{1,0:T(8,128)(2,1)S(1)}) custom-call(f32[2,1200,640]{2,1,0:T(8,128)} %bitcast.5), custom_call_target="tpu_custom_call" | custom-call | bytes 1024 | tf_op jit(solution)/shard_map/pallas_call | solution.py:76
  3.8 3.0 collective-permute-start.7
  6.9 4.5 %shard_map.37 = (bf16[320,1280]{1,0:T(8,128)(2,1)}, bf16[320,1152]{1,0:T(8,128)(2,1)S(1)}) custom-call(f32[2,1200,640]{2,1,0:T(8,128)} %bitcast.6), custom_call_target="tpu_custom_call" | custom-call | bytes 1024 | tf_op jit(solution)/shard_map/pallas_call | solution.py:76
  14.3 11.6 %collective-permute-done.7.refs_1_ = bf16[320,1280]{1,0:T(8,128)(2,1)S(1)} collective-permute-done((bf16[320,1280]{1,0:T(8,128)(2,1)S(1)}, bf16[320,1280]{1,0:T(8,128)(2,1)S(1)}, u32[]{:S(2)}, u32[]{:S(2)}) %collective-permute-start.7) | collective-permute-done | bytes 819232 | tf_op jit(solution)/shard_map/ppermute | solution.py:309
  30.9 12.6 %collective-permute-done.1.refs_1_ = bf16[320,1280]{1,0:T(8,128)(2,1)S(1)} collective-permute-done((bf16[320,1280]{1,0:T(8,128)(2,1)}, bf16[320,1280]{1,0:T(8,128)(2,1)S(1)}, u32[]{:S(2)}, u32[]{:S(2)}) %collective-permute-start.1) | collective-permute-done | bytes 819232 | tf_op jit(solution)/shard_map/ppermute | solution.py:309
  43.5 2.0 collective-permute-done.refs_0_
  48.5 14.6 %collective-permute-done.8.refs_0_ = bf16[320,1280]{1,0:T(8,128)(2,1)S(1)} collective-permute-done((bf16[320,1280]{1,0:T(8,128)(2,1)}, bf16[320,1280]{1,0:T(8,128)(2,1)S(1)}, u32[]{:S(2)}, u32[]{:S(2)}) %collective-permute-start.8) | collective-permute-done | bytes 819232 | tf_op jit(solution)/shard_map/ppermute | solution.py:308
  64.1 1.9 collective-permute-start.11
  66.0 14.6 %collective-permute-done.2.refs_0_ = bf16[320,1280]{1,0:T(8,128)(2,1)S(1)} collective-permute-done((bf16[320,1280]{1,0:T(8,128)(2,1)}, bf16[320,1280]{1,0:T(8,128)(2,1)S(1)}, u32[]{:S(2)}, u32[]{:S(2)}) %collective-permute-start.2) | collective-permute-done | bytes 819232 | tf_op jit(solution)/shard_map/ppermute | solution.py:308
  83.6 14.6 %collective-permute-done.10.refs_1_.refs_11_.refs_27_ = bf16[320,1280]{1,0:T(8,128)(2,1)S(1)} collective-permute-done((bf16[320,1280]{1,0:T(8,128)(2,1)}, bf16[320,1280]{1,0:T(8,128)(2,1)S(1)}, u32[]{:S(2)}, u32[]{:S(2)}) %collective-permute-start.10) | collective-permute-done | bytes 819232 | tf_op jit(solution)/shard_map/ppermute | solution.py:308
  101.6 12.8 %collective-permute-done.4.refs_0_ = bf16[320,1280]{1,0:T(8,128)(2,1)} collective-permute-done((bf16[320,1280]{1,0:T(8,128)(2,1)}, bf16[320,1280]{1,0:T(8,128)(2,1)}, u32[]{:S(2)}, u32[]{:S(2)}) %collective-permute-start.4) | collective-permute-done | bytes 819232 | tf_op jit(solution)/shard_map/ppermute | solution.py:308
  119.5 11.9 %collective-permute-done.15.refs_15_.refs_31_ = bf16[320,1280]{1,0:T(8,128)(2,1)} collective-permute-done((bf16[320,1280]{1,0:T(8,128)(2,1)}, bf16[320,1280]{1,0:T(8,128)(2,1)}, u32[]{:S(2)}, u32[]{:S(2)}) %collective-permute-start.15) | collective-permute-done | bytes 819232 | tf_op jit(solution)/shard_map/ppermute | solution.py:314
  131.4 2.1 collective-permute-start.16
  134.1 2.7 collective-permute-done.14.refs_14_.refs_30_
  136.8 12.9 %shard_map.47 = (bf16[640,768]{1,0:T(8,128)(2,1)}, bf16[640,768]{1,0:T(8,128)(2,1)}, bf16[640,512]{1,0:T(8,128)(2,1)S(1)}, bf16[640,512]{1,0:T(8,128)(2,1)S(1)}) custom-call(s32[8]{0:T(128)S(1)} %dynamic-slice_bitcast_fusion.source_ref, s32[5]{0:T(128)S(1)} %copy-done.17, s32[2]{0:T(128)S(1)} %pad_add_fusion.place_ref, ...), custom_call_target="tpu_custom_call" | custom-call | bytes 1024 | tf_op jit(solution)/shard_map/pallas_call | solution.py:246
  154.5 7.6 %collective-permute-done.17.refs_1_ = bf16[320,1152]{1,0:T(8,128)(2,1)} collective-permute-done((bf16[320,1152]{1,0:T(8,128)(2,1)}, bf16[320,1152]{1,0:T(8,128)(2,1)}, u32[]{:S(2)}, u32[]{:S(2)}) %collective-permute-start.17) | collective-permute-done | bytes 737312 | tf_op jit(solution)/shard_map/ppermute | solution.py:309
  163.8 4.6 %collective-permute-done.16.refs_0_ = bf16[320,1152]{1,0:T(8,128)(2,1)} collective-permute-done((bf16[320,1152]{1,0:T(8,128)(2,1)}, bf16[320,1152]{1,0:T(8,128)(2,1)}, u32[]{:S(2)}, u32[]{:S(2)}) %collective-permute-start.16) | collective-permute-done | bytes 737312 | tf_op jit(solution)/shard_map/ppermute | solution.py:308
  170.4 2.3 add_convert_fusion.3.refs_3_
  172.8 11.4 %collective-permute-done.18.refs_0_ = bf16[320,1152]{1,0:T(8,128)(2,1)} collective-permute-done((bf16[320,1152]{1,0:T(8,128)(2,1)}, bf16[320,1152]{1,0:T(8,128)(2,1)}, u32[]{:S(2)}, u32[]{:S(2)}) %collective-permute-start.18) | collective-permute-done | bytes 737312 | tf_op jit(solution)/shard_map/ppermute | solution.py:308
  187.1 12.9 %collective-permute-done.20.refs_0_ = bf16[320,1152]{1,0:T(8,128)(2,1)} collective-permute-done((bf16[320,1152]{1,0:T(8,128)(2,1)}, bf16[320,1152]{1,0:T(8,128)(2,1)}, u32[]{:S(2)}, u32[]{:S(2)}) %collective-permute-start.20) | collective-permute-done | bytes 737312 | tf_op jit(solution)/shard_map/ppermute | solution.py:308
  203.6 2.7 add_convert_fusion.1.refs_2_
  207.8 8.0 %collective-permute-done.22.refs_0_ = bf16[320,1152]{1,0:T(8,128)(2,1)} collective-permute-done((bf16[320,1152]{1,0:T(8,128)(2,1)}, bf16[320,1152]{1,0:T(8,128)(2,1)}, u32[]{:S(2)}, u32[]{:S(2)}) %collective-permute-start.22) | collective-permute-done | bytes 737312 | tf_op jit(solution)/shard_map/ppermute | solution.py:308
  215.8 3.9 %collective-permute-done.23.refs_1_.refs_12_ = bf16[320,1152]{1,0:T(8,128)(2,1)} collective-permute-done((bf16[320,1152]{1,0:T(8,128)(2,1)}, bf16[320,1152]{1,0:T(8,128)(2,1)}, u32[]{:S(2)}, u32[]{:S(2)}) %collective-permute-start.23) | collective-permute-done | bytes 737312 | tf_op jit(solution)/shard_map/ppermute | solution.py:309
  221.1 10.5 %collective-permute-done.26.refs_1_.refs_11_ = bf16[320,1152]{1,0:T(8,128)(2,1)} collective-permute-done((bf16[320,1152]{1,0:T(8,128)(2,1)}, bf16[320,1152]{1,0:T(8,128)(2,1)}, u32[]{:S(2)}, u32[]{:S(2)}) %collective-permute-start.26) | collective-permute-done | bytes 737312 | tf_op jit(solution)/shard_map/ppermute | solution.py:308
  233.2 15.2 %shard_map.58 = (bf16[640,1280]{1,0:T(8,128)(2,1)}, bf16[640,1280]{1,0:T(8,128)(2,1)}) custom-call(s32[8]{0:T(128)S(1)} %dynamic-slice_bitcast_fusion.source_ref, s32[5]{0:T(128)S(1)} %copy-done.17, s32[2]{0:T(128)S(1)} %pad_add_fusion.place_ref, bf16[320,1280]{1,0:T(8,128)(2,1)} %get-tuple-element.37.refs_0_.refs_16_, ...), custom_call_target="tpu_custom_call" | custom-call | bytes 1024 | tf_op jit(solution)/shard_map/pallas_call | solution.py:246
  249.7 9.3 %shard_map.59 = (bf16[640,768]{1,0:T(8,128)(2,1)}, bf16[640,768]{1,0:T(8,128)(2,1)}) custom-call(s32[8]{0:T(128)S(1)} %dynamic-slice_bitcast_fusion.source_ref, s32[5]{0:T(128)S(1)} %copy-done.17, s32[2]{0:T(128)S(1)} %pad_add_fusion.place_ref, bf16[320,1152]{1,0:T(8,128)(2,1)S(1)} %copy-done.10, bf16[320,1152]{1,0:T(8,128)(2,1)S(1)} %copy-done.8, ...), custom_call_target="tpu_custom_call" | custom-call | bytes 1024 | tf_op jit(solution)/shard_map/pallas_call | solution.py:246
  259.1 2.8 collective-permute-done.32
  264.3 11.0 %shard_map.60 = (bf16[640,512]{1,0:T(8,128)(2,1)S(1)}, bf16[640,512]{1,0:T(8,128)(2,1)S(1)}, bf16[640,1280]{1,0:T(8,128)(2,1)}) custom-call(s32[8]{0:T(128)S(1)} %dynamic-slice_bitcast_fusion.source_ref, s32[5]{0:T(128)S(1)} %copy-done.17, s32[2]{0:T(128)S(1)} %pad_add_fusion.place_ref, bf16[320,1152]{1,0:T(8,128)(2,1)S(1)} %copy-done.10, ...), custom_call_target="tpu_custom_call" | custom-call | bytes 1024 | tf_op jit(solution)/shard_map/pallas_call | solution.py:246
  278.9 8.3 %collective-permute-done.36.refs_0_ = bf16[640,768]{1,0:T(8,128)(2,1)S(1)} collective-permute-done((bf16[640,768]{1,0:T(8,128)(2,1)S(1)}, bf16[640,768]{1,0:T(8,128)(2,1)S(1)}, u32[]{:S(2)}, u32[]{:S(2)}) %collective-permute-start.36) | collective-permute-done | bytes 983072 | tf_op jit(solution)/shard_map/ppermute | solution.py:341
  289.6 6.8 %shard_map.61.refs_4_ = bf16[640,1280]{1,0:T(8,128)(2,1)} custom-call(s32[8]{0:T(128)S(1)} %dynamic-slice_bitcast_fusion.source_ref, s32[5]{0:T(128)S(1)} %copy-done.17, s32[2]{0:T(128)S(1)} %pad_add_fusion.place_ref, bf16[320,1152]{1,0:T(8,128)(2,1)S(1)} %copy-done.10, bf16[320,1152]{1,0:T(8,128)(2,1)S(1)} %copy-done.8, ...), custom_call_target="tpu_custom_call" | custom-call | bytes 1024 | tf_op jit(solution)/shard_map/pallas_call | solution.py:246
  297.6 6.1 %shard_map.64.refs_1_.before_ref = f32[640,1280]{1,0:T(8,128)} custom-call(bf16[640,768]{1,0:T(8,128)(2,1)} %shard_map.57.refs_32_.refs_0_, bf16[640,512]{1,0:T(8,128)(2,1)} %shard_map.55.refs_4_.refs_33_.refs_1_, bf16[640,1280]{1,0:T(8,128)(2,1)S(1)} %copy-done.13, bf16[640,1280]{1,0:T(8,128)(2,1)} %collective-permute-done.35.refs_3_, ...), custom_call_target="tpu_custom_call" | custom-call | bytes 1024 | tf_op jit(solution)/shard_map/pallas_call | solution.py:119
  306.3 2.4 shard_map.66
  (134 shorter events, 56.9 us)
Async XLA Ops:
  3.8 22.1 %collective-permute-start.7 = (bf16[320,1280]{1,0:T(8,128)(2,1)S(1)}, bf16[320,1280]{1,0:T(8,128)(2,1)S(1)}, u32[]{:S(2)}, u32[]{:S(2)}) collective-permute-start(bf16[320,1280]{1,0:T(8,128)(2,1)S(1)} %get-tuple-element.43.refs_1_.refs_17_), channel_id=1, source_target_pairs={{2,0},{4,2},{6,4},{7,6},{5,7},{3,5},{1,3},{0,1},{10,8},{12,10},{14... | collective-permute-start | bytes 2457608 | tf_op jit(solution)/shard_map/ppermute | solution.py:309
  6.8 21.2 %collective-permute-start.6 = (bf16[320,1280]{1,0:T(8,128)(2,1)S(1)}, bf16[320,1280]{1,0:T(8,128)(2,1)S(1)}, u32[]{:S(2)}, u32[]{:S(2)}) collective-permute-start(bf16[320,1280]{1,0:T(8,128)(2,1)S(1)} %get-tuple-element.43.refs_1_.refs_17_), channel_id=1, source_target_pairs={{0,2},{2,4},{4,6},{6,7},{7,5},{5,3},{3,1},{1,0},{8,10},{10,12},{12... | collective-permute-start | bytes 2457608 | tf_op jit(solution)/shard_map/ppermute | solution.py:308
  12.3 31.2 %collective-permute-start.1 = (bf16[320,1280]{1,0:T(8,128)(2,1)}, bf16[320,1280]{1,0:T(8,128)(2,1)S(1)}, u32[]{:S(2)}, u32[]{:S(2)}) collective-permute-start(bf16[320,1280]{1,0:T(8,128)(2,1)} %get-tuple-element.37.refs_0_.refs_16_), channel_id=1, source_target_pairs={{2,0},{4,2},{6,4},{7,6},{5,7},{3,5},{1,3},{0,1},{10,8},{12,10},{14... | collective-permute-start | bytes 2457608 | tf_op jit(solution)/shard_map/ppermute | solution.py:309
  14.2 31.3 %collective-permute-start = (bf16[320,1280]{1,0:T(8,128)(2,1)}, bf16[320,1280]{1,0:T(8,128)(2,1)S(1)}, u32[]{:S(2)}, u32[]{:S(2)}) collective-permute-start(bf16[320,1280]{1,0:T(8,128)(2,1)} %get-tuple-element.37.refs_0_.refs_16_), channel_id=1, source_target_pairs={{0,2},{2,4},{4,6},{6,7},{7,5},{5,3},{3,1},{1,0},{8,10},{10,12},{12... | collective-permute-start | bytes 2457608 | tf_op jit(solution)/shard_map/ppermute | solution.py:308
  28.9 34.2 %collective-permute-start.8 = (bf16[320,1280]{1,0:T(8,128)(2,1)}, bf16[320,1280]{1,0:T(8,128)(2,1)S(1)}, u32[]{:S(2)}, u32[]{:S(2)}) collective-permute-start(bf16[320,1280]{1,0:T(8,128)(2,1)} %get-tuple-element.44.refs_3_.refs_19_), channel_id=1, source_target_pairs={{0,2},{2,4},{4,6},{6,7},{7,5},{5,3},{3,1},{1,0},{8,10},{10,12},{12... | collective-permute-start | bytes 2457608 | tf_op jit(solution)/shard_map/ppermute | solution.py:308
  29.8 33.3 %collective-permute-start.9 = (bf16[320,1280]{1,0:T(8,128)(2,1)}, bf16[320,1280]{1,0:T(8,128)(2,1)}, u32[]{:S(2)}, u32[]{:S(2)}) collective-permute-start(bf16[320,1280]{1,0:T(8,128)(2,1)} %get-tuple-element.45.refs_5_.refs_21_), channel_id=1, source_target_pairs={{2,0},{4,2},{6,4},{7,6},{5,7},{3,5},{1,3},{0,1},{10,8},{12,10},{14... | collective-permute-start | bytes 2457608 | tf_op jit(solution)/shard_map/ppermute | solution.py:309
  46.4 34.2 %collective-permute-start.2 = (bf16[320,1280]{1,0:T(8,128)(2,1)}, bf16[320,1280]{1,0:T(8,128)(2,1)S(1)}, u32[]{:S(2)}, u32[]{:S(2)}) collective-permute-start(bf16[320,1280]{1,0:T(8,128)(2,1)} %get-tuple-element.38.refs_2_.refs_18_), channel_id=1, source_target_pairs={{0,2},{2,4},{4,6},{6,7},{7,5},{5,3},{3,1},{1,0},{8,10},{10,12},{12... | collective-permute-start | bytes 2457608 | tf_op jit(solution)/shard_map/ppermute | solution.py:308
  47.4 33.2 %collective-permute-start.3 = (bf16[320,1280]{1,0:T(8,128)(2,1)}, bf16[320,1280]{1,0:T(8,128)(2,1)}, u32[]{:S(2)}, u32[]{:S(2)}) collective-permute-start(bf16[320,1280]{1,0:T(8,128)(2,1)} %get-tuple-element.39.refs_4_.refs_20_), channel_id=1, source_target_pairs={{2,0},{4,2},{6,4},{7,6},{5,7},{3,5},{1,3},{0,1},{10,8},{12,10},{14... | collective-permute-start | bytes 2457608 | tf_op jit(solution)/shard_map/ppermute | solution.py:309
  64.0 34.2 %collective-permute-start.10 = (bf16[320,1280]{1,0:T(8,128)(2,1)}, bf16[320,1280]{1,0:T(8,128)(2,1)S(1)}, u32[]{:S(2)}, u32[]{:S(2)}) collective-permute-start(bf16[320,1280]{1,0:T(8,128)(2,1)} %get-tuple-element.46.refs_7_.refs_23_), channel_id=1, source_target_pairs={{0,2},{2,4},{4,6},{6,7},{7,5},{5,3},{3,1},{1,0},{8,10},{10,12},{12... | collective-permute-start | bytes 2457608 | tf_op jit(solution)/shard_map/ppermute | solution.py:308
  64.1 34.1 %collective-permute-start.11 = (bf16[320,1280]{1,0:T(8,128)(2,1)}, bf16[320,1280]{1,0:T(8,128)(2,1)S(1)}, u32[]{:S(2)}, u32[]{:S(2)}) collective-permute-start(bf16[320,1280]{1,0:T(8,128)(2,1)} %get-tuple-element.47.refs_9_.refs_25_), channel_id=1, source_target_pairs={{2,0},{4,2},{6,4},{7,6},{5,7},{3,5},{1,3},{0,1},{10,8},{12,10},{14... | collective-permute-start | bytes 2457608 | tf_op jit(solution)/shard_map/ppermute | solution.py:309
  81.5 32.8 %collective-permute-start.4 = (bf16[320,1280]{1,0:T(8,128)(2,1)}, bf16[320,1280]{1,0:T(8,128)(2,1)}, u32[]{:S(2)}, u32[]{:S(2)}) collective-permute-start(bf16[320,1280]{1,0:T(8,128)(2,1)} %get-tuple-element.40.refs_6_.refs_22_), channel_id=1, source_target_pairs={{0,2},{2,4},{4,6},{6,7},{7,5},{5,3},{3,1},{1,0},{8,10},{10,12},{12... | collective-permute-start | bytes 2457608 | tf_op jit(solution)/shard_map/ppermute | solution.py:308
  81.6 32.8 %collective-permute-start.5 = (bf16[320,1280]{1,0:T(8,128)(2,1)}, bf16[320,1280]{1,0:T(8,128)(2,1)S(1)}, u32[]{:S(2)}, u32[]{:S(2)}) collective-permute-start(bf16[320,1280]{1,0:T(8,128)(2,1)} %get-tuple-element.41.refs_8_.refs_24_), channel_id=1, source_target_pairs={{2,0},{4,2},{6,4},{7,6},{5,7},{3,5},{1,3},{0,1},{10,8},{12,10},{14... | collective-permute-start | bytes 2457608 | tf_op jit(solution)/shard_map/ppermute | solution.py:309
  100.0 31.4 %collective-permute-start.15 = (bf16[320,1280]{1,0:T(8,128)(2,1)}, bf16[320,1280]{1,0:T(8,128)(2,1)}, u32[]{:S(2)}, u32[]{:S(2)}) collective-permute-start(bf16[320,1280]{1,0:T(8,128)(2,1)} %shard_map.45.refs_2_.refs_13_.refs_29_), channel_id=1, source_target_pairs={{2,0},{4,2},{6,4},{7,6},{5,7},{3,5},{1,3},{0,1},{10,8},{12,10},{14... | collective-permute-start | bytes 2457608 | tf_op jit(solution)/shard_map/ppermute | solution.py:314
  115.3 21.5 %collective-permute-start.14 = (bf16[320,1280]{1,0:T(8,128)(2,1)}, bf16[320,1280]{1,0:T(8,128)(2,1)}, u32[]{:S(2)}, u32[]{:S(2)}) collective-permute-start(bf16[320,1280]{1,0:T(8,128)(2,1)} %shard_map.40.refs_1_.refs_10_.refs_26_), channel_id=1, source_target_pairs={{0,2},{2,4},{4,6},{6,7},{7,5},{5,3},{3,1},{1,0},{8,10},{10,12},{12... | collective-permute-start | bytes 2457608 | tf_op jit(solution)/shard_map/ppermute | solution.py:314
  116.7 34.7 %collective-permute-start.13 = (bf16[320,1152]{1,0:T(8,128)(2,1)}, bf16[320,1152]{1,0:T(8,128)(2,1)}, u32[]{:S(2)}, u32[]{:S(2)}) collective-permute-start(bf16[320,1152]{1,0:T(8,128)(2,1)} %shard_map.41.refs_0_), channel_id=1, source_target_pairs={{2,0},{4,2},{6,4},{7,6},{5,7},{3,5},{1,3},{0,1},{10,8},{12,10},{14... | collective-permute-start | bytes 2211848 | tf_op jit(solution)/shard_map/ppermute | solution.py:309
  117.4 35.2 %collective-permute-start.12 = (bf16[320,1152]{1,0:T(8,128)(2,1)}, bf16[320,1152]{1,0:T(8,128)(2,1)}, u32[]{:S(2)}, u32[]{:S(2)}) collective-permute-start(bf16[320,1152]{1,0:T(8,128)(2,1)} %shard_map.41.refs_0_), channel_id=1, source_target_pairs={{0,2},{2,4},{4,6},{6,7},{7,5},{5,3},{3,1},{1,0},{8,10},{10,12},{12... | collective-permute-start | bytes 2211848 | tf_op jit(solution)/shard_map/ppermute | solution.py:308
  118.8 43.3 %collective-permute-start.17 = (bf16[320,1152]{1,0:T(8,128)(2,1)}, bf16[320,1152]{1,0:T(8,128)(2,1)}, u32[]{:S(2)}, u32[]{:S(2)}) collective-permute-start(bf16[320,1152]{1,0:T(8,128)(2,1)} %shard_map.46.refs_1_), channel_id=1, source_target_pairs={{2,0},{4,2},{6,4},{7,6},{5,7},{3,5},{1,3},{0,1},{10,8},{12,10},{14... | collective-permute-start | bytes 2211848 | tf_op jit(solution)/shard_map/ppermute | solution.py:309
  131.4 37.0 %collective-permute-start.16 = (bf16[320,1152]{1,0:T(8,128)(2,1)}, bf16[320,1152]{1,0:T(8,128)(2,1)}, u32[]{:S(2)}, u32[]{:S(2)}) collective-permute-start(bf16[320,1152]{1,0:T(8,128)(2,1)} %shard_map.46.refs_1_), channel_id=1, source_target_pairs={{0,2},{2,4},{4,6},{6,7},{7,5},{5,3},{3,1},{1,0},{8,10},{10,12},{12... | collective-permute-start | bytes 2211848 | tf_op jit(solution)/shard_map/ppermute | solution.py:308
  152.6 49.4 %collective-permute-start.24 = (bf16[640,768]{1,0:T(8,128)(2,1)}, bf16[640,768]{1,0:T(8,128)(2,1)}, u32[]{:S(2)}, u32[]{:S(2)}) collective-permute-start(bf16[640,768]{1,0:T(8,128)(2,1)} %shard_map.52), channel_id=1, source_target_pairs={{0,8},{8,0},{16,24},{24,16},{1,9},{9,1},{17,25},{25,17},{2,10},{10... | collective-permute-start | bytes 2949128 | tf_op jit(solution)/shard_map/ppermute | solution.py:338
  153.1 31.1 %collective-permute-start.18 = (bf16[320,1152]{1,0:T(8,128)(2,1)}, bf16[320,1152]{1,0:T(8,128)(2,1)}, u32[]{:S(2)}, u32[]{:S(2)}) collective-permute-start(bf16[320,1152]{1,0:T(8,128)(2,1)} %get-tuple-element.49.refs_1_.refs_2_), channel_id=1, source_target_pairs={{0,2},{2,4},{4,6},{6,7},{7,5},{5,3},{3,1},{1,0},{8,10},{10,12},{12... | collective-permute-start | bytes 2211848 | tf_op jit(solution)/shard_map/ppermute | solution.py:308
  162.1 23.6 %collective-permute-start.19 = (bf16[320,1152]{1,0:T(8,128)(2,1)}, bf16[320,1152]{1,0:T(8,128)(2,1)}, u32[]{:S(2)}, u32[]{:S(2)}) collective-permute-start(bf16[320,1152]{1,0:T(8,128)(2,1)} %get-tuple-element.51.refs_2_.refs_4_), channel_id=1, source_target_pairs={{2,0},{4,2},{6,4},{7,6},{5,7},{3,5},{1,3},{0,1},{10,8},{12,10},{14... | collective-permute-start | bytes 2211848 | tf_op jit(solution)/shard_map/ppermute | solution.py:309
  168.4 31.6 %collective-permute-start.20 = (bf16[320,1152]{1,0:T(8,128)(2,1)}, bf16[320,1152]{1,0:T(8,128)(2,1)}, u32[]{:S(2)}, u32[]{:S(2)}) collective-permute-start(bf16[320,1152]{1,0:T(8,128)(2,1)} %get-tuple-element.50.refs_3_), channel_id=1, source_target_pairs={{0,2},{2,4},{4,6},{6,7},{7,5},{5,3},{3,1},{1,0},{8,10},{10,12},{12... | collective-permute-start | bytes 2211848 | tf_op jit(solution)/shard_map/ppermute | solution.py:308
  169.8 31.8 %collective-permute-start.21 = (bf16[320,1152]{1,0:T(8,128)(2,1)}, bf16[320,1152]{1,0:T(8,128)(2,1)}, u32[]{:S(2)}, u32[]{:S(2)}) collective-permute-start(bf16[320,1152]{1,0:T(8,128)(2,1)} %get-tuple-element.52.refs_5_), channel_id=1, source_target_pairs={{2,0},{4,2},{6,4},{7,6},{5,7},{3,5},{1,3},{0,1},{10,8},{12,10},{14... | collective-permute-start | bytes 2211848 | tf_op jit(solution)/shard_map/ppermute | solution.py:309
  184.2 22.1 %collective-permute-start.28 = (bf16[640,512]{1,0:T(8,128)(2,1)}, bf16[640,512]{1,0:T(8,128)(2,1)}, u32[]{:S(2)}, u32[]{:S(2)}) collective-permute-start(bf16[640,512]{1,0:T(8,128)(2,1)} %add_convert_fusion.3.refs_3_), channel_id=1, source_target_pairs={{0,16},{8,24},{16,0},{24,8},{1,17},{9,25},{17,1},{25,9},{2,18},{10... | collective-permute-start | bytes 1966088 | tf_op jit(solution)/shard_map/ppermute | solution.py:341
  185.7 30.1 %collective-permute-start.22 = (bf16[320,1152]{1,0:T(8,128)(2,1)}, bf16[320,1152]{1,0:T(8,128)(2,1)}, u32[]{:S(2)}, u32[]{:S(2)}) collective-permute-start(bf16[320,1152]{1,0:T(8,128)(2,1)} %get-tuple-element.53.refs_6_), channel_id=1, source_target_pairs={{0,2},{2,4},{4,6},{6,7},{7,5},{5,3},{3,1},{1,0},{8,10},{10,12},{12... | collective-permute-start | bytes 2211848 | tf_op jit(solution)/shard_map/ppermute | solution.py:308
  200.0 19.7 %collective-permute-start.23 = (bf16[320,1152]{1,0:T(8,128)(2,1)}, bf16[320,1152]{1,0:T(8,128)(2,1)}, u32[]{:S(2)}, u32[]{:S(2)}) collective-permute-start(bf16[320,1152]{1,0:T(8,128)(2,1)} %get-tuple-element.55.refs_8_), channel_id=1, source_target_pairs={{2,0},{4,2},{6,4},{7,6},{5,7},{3,5},{1,3},{0,1},{10,8},{12,10},{14... | collective-permute-start | bytes 2211848 | tf_op jit(solution)/shard_map/ppermute | solution.py:309
  201.6 30.0 %collective-permute-start.26 = (bf16[320,1152]{1,0:T(8,128)(2,1)}, bf16[320,1152]{1,0:T(8,128)(2,1)}, u32[]{:S(2)}, u32[]{:S(2)}) collective-permute-start(bf16[320,1152]{1,0:T(8,128)(2,1)} %get-tuple-element.54.refs_7_), channel_id=1, source_target_pairs={{0,2},{2,4},{4,6},{6,7},{7,5},{5,3},{3,1},{1,0},{8,10},{10,12},{12... | collective-permute-start | bytes 2211848 | tf_op jit(solution)/shard_map/ppermute | solution.py:308
  202.0 29.6 %collective-permute-start.27 = (bf16[320,1152]{1,0:T(8,128)(2,1)}, bf16[320,1152]{1,0:T(8,128)(2,1)}, u32[]{:S(2)}, u32[]{:S(2)}) collective-permute-start(bf16[320,1152]{1,0:T(8,128)(2,1)} %get-tuple-element.56.refs_9_), channel_id=1, source_target_pairs={{2,0},{4,2},{6,4},{7,6},{5,7},{3,5},{1,3},{0,1},{10,8},{12,10},{14... | collective-permute-start | bytes 2211848 | tf_op jit(solution)/shard_map/ppermute | solution.py:309
  206.3 42.1 %collective-permute-start.31 = (bf16[640,768]{1,0:T(8,128)(2,1)}, bf16[640,768]{1,0:T(8,128)(2,1)}, u32[]{:S(2)}, u32[]{:S(2)}) collective-permute-start(bf16[640,768]{1,0:T(8,128)(2,1)} %add_convert_fusion.1.refs_2_), channel_id=1, source_target_pairs={{0,16},{8,24},{16,0},{24,8},{1,17},{9,25},{17,1},{25,9},{2,18},{10... | collective-permute-start | bytes 2949128 | tf_op jit(solution)/shard_map/ppermute | solution.py:341
  219.7 28.7 %collective-permute-start.29 = (bf16[320,1152]{1,0:T(8,128)(2,1)}, bf16[320,1152]{1,0:T(8,128)(2,1)}, u32[]{:S(2)}, u32[]{:S(2)}) collective-permute-start(bf16[320,1152]{1,0:T(8,128)(2,1)} %shard_map.54.refs_32_.refs_10_), channel_id=1, source_target_pairs={{0,2},{2,4},{4,6},{6,7},{7,5},{5,3},{3,1},{1,0},{8,10},{10,12},{12... | collective-permute-start | bytes 2211848 | tf_op jit(solution)/shard_map/ppermute | solution.py:314
  263.3 23.9 %collective-permute-start.36 = (bf16[640,768]{1,0:T(8,128)(2,1)S(1)}, bf16[640,768]{1,0:T(8,128)(2,1)S(1)}, u32[]{:S(2)}, u32[]{:S(2)}) collective-permute-start(bf16[640,768]{1,0:T(8,128)(2,1)S(1)} %add_convert_fusion.refs_32_), channel_id=1, source_target_pairs={{0,16},{8,24},{16,0},{24,8},{1,17},{9,25},{17,1},{25,9},{2,18},{10... | collective-permute-start | bytes 2949128 | tf_op jit(solution)/shard_map/ppermute | solution.py:341
  276.0 20.5 %collective-permute-start.35 = (bf16[640,1280]{1,0:T(8,128)(2,1)}, bf16[640,1280]{1,0:T(8,128)(2,1)}, u32[]{:S(2)}, u32[]{:S(2)}) collective-permute-start(bf16[640,1280]{1,0:T(8,128)(2,1)} %get-tuple-element.65), channel_id=1, source_target_pairs={{0,8},{8,0},{16,24},{24,16},{1,9},{9,1},{17,25},{25,17},{2,10},{10... | collective-permute-start | bytes 4915208 | tf_op jit(solution)/shard_map/ppermute | solution.py:338
  (33 other events, 419.6 us)

commit v12 on v11

--- a/solution.py
+++ b/solution.py
@@ -101,23 +101,20 @@
     )(*pieces, *others)
 
 
-def combine_kernel(*refs, starts, scale):
+def combine_kernel(*refs, starts, width, scale):
     *in_refs, out_ref = refs
-    total = jnp.zeros(out_ref.shape, jnp.float32)
-    for ref, start in zip(in_refs, starts):
-        if start is None:
-            total = total + ref[...].astype(jnp.float32)
-    out_ref[...] = total * scale
-    for ref, start in zip(in_refs, starts):
-        if start is not None:
-            here = pl.ds(start, ref.shape[1])
-            out_ref[:, here] = out_ref[:, here] + ref[...].astype(jnp.float32) * scale
-
-
-def combine(terms, starts, slab, columns, scale):
+    for k in range(0, out_ref.shape[1], width):
+        total = jnp.zeros((out_ref.shape[0], width), jnp.float32)
+        for ref, start in zip(in_refs, starts):
+            if start <= k < start + ref.shape[1]:
+                total = total + ref[:, pl.ds(k - start, width)].astype(jnp.float32)
+        out_ref[:, pl.ds(k, width)] = total * scale
+
+
+def combine(terms, starts, slab, columns, width, scale):
     step = max(d for d in range(16, 161, 16) if slab % d == 0)
     return pl.pallas_call(
-        functools.partial(combine_kernel, starts=starts, scale=scale),
+        functools.partial(combine_kernel, starts=starts, width=width, scale=scale),
         grid=(slab // step,),
         in_specs=[pl.BlockSpec((step, term.shape[1]), lambda i: (i, 0)) for term in terms],
         out_specs=pl.BlockSpec((step, columns), lambda i: (i, 0)),
@@ -344,7 +341,7 @@
     def added(same, crossed):
         return (same.astype(jnp.float32) + crossed.astype(jnp.float32)).astype(jnp.bfloat16)
 
-    terms, starts = [], []
+    terms, starts, pending = [], [], []
     for a in range(1, local_subjects):
         shares, sums, gone = [], [], []
 
@@ -372,8 +369,9 @@
         terms += gone
         same, other = share(a - 1, [(0, flip, 0, chunk) for flip in (0, 1)], [everything[a][-3][0], everything[a][-2][1]])
         gone.append(same)
-        terms += [same, cross(other)]
-        starts += [None, None]
+        pending.append(other)
+        terms.append(same)
+        starts.append(0)
     last = local_subjects - 1
     scale = 1 / (local_subjects * subjs)
     late = gone
@@ -381,18 +379,24 @@
         same, other = share(last, [(d, 0, 0, chunk), (d, 1, 0, chunk)], late)
         late = [added(same, cross(other))]
         terms.append(send(late[0], d, LONG))
-        starts.append(None)
+        starts.append(0)
     d = aways[-2]
     same, other = share(last, [(d, 0, 0, early), (d, 1, 0, early)], late)
     leading = added(same, cross(other))
-    rest = chunk - early
-    other, same, others = share(last, [(d, 1, early, rest), (d, 0, early, rest), (0, 1, 0, chunk)], [leading])
-    summed = added(same, cross(other))
+    pieces = [(d, 1, k, width) for k in range(early, chunk, width)]
+    ends = [*range(0, chunk - width, 2 * width), chunk - width, chunk]
+    others = [(0, 1, k, end - k) for k, end in zip(ends, ends[1:])]
+    arrays = share(last, [*pieces, (d, 0, early, chunk - early), *others], [leading])
+    crossed = jnp.concatenate([cross(array) for array in arrays[: len(pieces)]], axis=1)
+    summed = added(arrays[len(pieces)], crossed)
     (same,) = share(last, [(0, 0, 0, chunk)], [summed])
-    there = send(leading, d, LONG)
-    terms += [same, cross(others, [there, summed]), there]
-    starts += [None, None, 0]
-    out = combine(terms, starts, slab, chunk, scale)
+    there = send(leading, d, LONG, [same])
+    terms += [same, there, *(cross(other, [summed]) for other in pending)]
+    starts += [0 for _ in terms[len(starts) :]]
+    for array, (_, _, start, _) in zip(arrays[len(pieces) + 1 :], others):
+        terms.append(cross(array, [there] if start == others[-1][2] else ()))
+        starts.append(start)
+    out = combine(terms, starts, slab, chunk, width, scale)
     return finish(send(summed, d, LONG, [out]), out, early, scale)
 
 

time: 309 us -> 322 us (1.042)
  waiting for transfers between devices: 173 us -> 180 us
  starting transfers between devices: 38.8 us -> 44.4 us
    ppermute x4, waiting for transfers between devices: 10 us -> 17.9 us  [send(): lax.ppermute(summed, 'subj', [(s, (s + 2 * d) % subjs) for s in range(sub...]
    ppermute x4, starting transfers between devices: 3.34 us -> 8.16 us  [send(): lax.ppermute(summed, 'subj', [(s, (s + 2 * d) % subjs) for s in range(sub...]
  transfers between devices with their start and end apart: 38 -> 41, of which waited for: 22 -> 23; matrix products, arithmetic and copies ran while one was open for 2% -> 2% of each run, Pallas kernels for 18% -> 14%
where the time goes in v12:
time: 322 us
  waiting for transfers between devices  180 us (56%)
  Pallas kernels  73.3 us (23%)
  starting transfers between devices  44.4 us (14%)
  local copies, waits for them, and re-layouts  15.1 us (5%)
  other arithmetic  8.45 us (3%)
    ppermute x12, waiting for transfers between devices, gather(): got[-2][half] = lax.ppermute(ahead[half], SLABS, onward)  107 us
    pallas_call x5, Pallas kernels, scores(): pl.pallas_call(functools.partial(scores_kernel, subject=subject, targets=...  57.2 us
    ppermute x12, waiting for transfers between devices, gather(): got[-1][half] = lax.ppermute(behind[half], SLABS, backward)  34.2 us
    ppermute x12, starting transfers between devices, gather(): got[-1][half] = lax.ppermute(behind[half], SLABS, backward)  18 us
    ppermute x4, waiting for transfers between devices, send(): lax.ppermute(summed, 'subj', [(s, (s + 2 * d) % subjs) for s in range(sub...  17.9 us
    ppermute x4, waiting for transfers between devices, gather(): last.append(lax.ppermute(got[side][half], SLABS, way))  14.5 us
    unnamed x54, local copies, waits for them, and re-layouts  14.4 us
    ppermute x12, starting transfers between devices, gather(): got[-2][half] = lax.ppermute(ahead[half], SLABS, onward)  10.1 us
  transfers between devices with their start and end apart: 41, of which 23 were waited for; matrix products, arithmetic and copies ran while one was open for 2% of the time, Pallas kernels for 14%

profile of v12, /device:TPU:0, one launch (start us, length us, event | category | flops | bytes accessed | tf_op | source)
XLA Modules:
  0.0 321.8 jit_solution(13808209099916246733)
XLA Ops:
  0.0 3.7 %shard_map.42 = (bf16[320,1280]{1,0:T(8,128)(2,1)S(1)}, bf16[320,1152]{1,0:T(8,128)(2,1)S(1)}) custom-call(f32[2,1200,640]{2,1,0:T(8,128)} %bitcast.5), custom_call_target="tpu_custom_call" | custom-call | bytes 1024 | tf_op jit(solution)/shard_map/pallas_call | solution.py:76
  4.6 3.0 collective-permute-start.7
  7.7 4.6 %shard_map.37 = (bf16[320,1280]{1,0:T(8,128)(2,1)}, bf16[320,1152]{1,0:T(8,128)(2,1)S(1)}) custom-call(f32[2,1200,640]{2,1,0:T(8,128)} %bitcast.6), custom_call_target="tpu_custom_call" | custom-call | bytes 1024 | tf_op jit(solution)/shard_map/pallas_call | solution.py:76
  15.2 11.5 %collective-permute-done.7.refs_1_ = bf16[320,1280]{1,0:T(8,128)(2,1)S(1)} collective-permute-done((bf16[320,1280]{1,0:T(8,128)(2,1)S(1)}, bf16[320,1280]{1,0:T(8,128)(2,1)S(1)}, u32[]{:S(2)}, u32[]{:S(2)}) %collective-permute-start.7) | collective-permute-done | bytes 819232 | tf_op jit(solution)/shard_map/ppermute | solution.py:306
  31.8 12.5 %collective-permute-done.1.refs_1_ = bf16[320,1280]{1,0:T(8,128)(2,1)S(1)} collective-permute-done((bf16[320,1280]{1,0:T(8,128)(2,1)}, bf16[320,1280]{1,0:T(8,128)(2,1)S(1)}, u32[]{:S(2)}, u32[]{:S(2)}) %collective-permute-start.1) | collective-permute-done | bytes 819232 | tf_op jit(solution)/shard_map/ppermute | solution.py:306
  49.3 14.6 %collective-permute-done.8.refs_0_ = bf16[320,1280]{1,0:T(8,128)(2,1)S(1)} collective-permute-done((bf16[320,1280]{1,0:T(8,128)(2,1)}, bf16[320,1280]{1,0:T(8,128)(2,1)S(1)}, u32[]{:S(2)}, u32[]{:S(2)}) %collective-permute-start.8) | collective-permute-done | bytes 819232 | tf_op jit(solution)/shard_map/ppermute | solution.py:305
  66.8 14.6 %collective-permute-done.2.refs_0_ = bf16[320,1280]{1,0:T(8,128)(2,1)S(1)} collective-permute-done((bf16[320,1280]{1,0:T(8,128)(2,1)}, bf16[320,1280]{1,0:T(8,128)(2,1)S(1)}, u32[]{:S(2)}, u32[]{:S(2)}) %collective-permute-start.2) | collective-permute-done | bytes 819232 | tf_op jit(solution)/shard_map/ppermute | solution.py:305
  84.4 14.6 %collective-permute-done.10.refs_1_.refs_11_.refs_27_ = bf16[320,1280]{1,0:T(8,128)(2,1)S(1)} collective-permute-done((bf16[320,1280]{1,0:T(8,128)(2,1)}, bf16[320,1280]{1,0:T(8,128)(2,1)S(1)}, u32[]{:S(2)}, u32[]{:S(2)}) %collective-permute-start.10) | collective-permute-done | bytes 819232 | tf_op jit(solution)/shard_map/ppermute | solution.py:305
  102.3 12.9 %collective-permute-done.4.refs_0_ = bf16[320,1280]{1,0:T(8,128)(2,1)} collective-permute-done((bf16[320,1280]{1,0:T(8,128)(2,1)}, bf16[320,1280]{1,0:T(8,128)(2,1)}, u32[]{:S(2)}, u32[]{:S(2)}) %collective-permute-start.4) | collective-permute-done | bytes 819232 | tf_op jit(solution)/shard_map/ppermute | solution.py:305
  120.3 11.9 %collective-permute-done.15.refs_15_.refs_31_ = bf16[320,1280]{1,0:T(8,128)(2,1)} collective-permute-done((bf16[320,1280]{1,0:T(8,128)(2,1)}, bf16[320,1280]{1,0:T(8,128)(2,1)}, u32[]{:S(2)}, u32[]{:S(2)}) %collective-permute-start.15) | collective-permute-done | bytes 819232 | tf_op jit(solution)/shard_map/ppermute | solution.py:311
  134.9 2.7 collective-permute-done.14.refs_14_.refs_30_
  137.6 15.4 %shard_map.47 = (bf16[640,768]{1,0:T(8,128)(2,1)}, bf16[640,768]{1,0:T(8,128)(2,1)}, bf16[640,512]{1,0:T(8,128)(2,1)S(1)}, bf16[640,512]{1,0:T(8,128)(2,1)S(1)}) custom-call(s32[8]{0:T(128)S(1)} %dynamic-slice_bitcast_fusion.source_ref, s32[5]{0:T(128)S(1)} %copy-done.18, s32[2]{0:T(128)S(1)} %pad_add_fusion.place_ref, ...), custom_call_target="tpu_custom_call" | custom-call | bytes 1024 | tf_op jit(solution)/shard_map/pallas_call | solution.py:243
  156.7 6.2 %collective-permute-done.17.refs_1_ = bf16[320,1152]{1,0:T(8,128)(2,1)} collective-permute-done((bf16[320,1152]{1,0:T(8,128)(2,1)}, bf16[320,1152]{1,0:T(8,128)(2,1)}, u32[]{:S(2)}, u32[]{:S(2)}) %collective-permute-start.17) | collective-permute-done | bytes 737312 | tf_op jit(solution)/shard_map/ppermute | solution.py:306
  164.6 4.6 %collective-permute-done.16.refs_0_ = bf16[320,1152]{1,0:T(8,128)(2,1)} collective-permute-done((bf16[320,1152]{1,0:T(8,128)(2,1)}, bf16[320,1152]{1,0:T(8,128)(2,1)}, u32[]{:S(2)}, u32[]{:S(2)}) %collective-permute-start.16) | collective-permute-done | bytes 737312 | tf_op jit(solution)/shard_map/ppermute | solution.py:305
  171.2 2.3 add_convert_fusion.3.refs_3_
  173.5 11.5 %collective-permute-done.18.refs_0_ = bf16[320,1152]{1,0:T(8,128)(2,1)} collective-permute-done((bf16[320,1152]{1,0:T(8,128)(2,1)}, bf16[320,1152]{1,0:T(8,128)(2,1)}, u32[]{:S(2)}, u32[]{:S(2)}) %collective-permute-start.18) | collective-permute-done | bytes 737312 | tf_op jit(solution)/shard_map/ppermute | solution.py:305
  187.9 12.9 %collective-permute-done.20.refs_0_ = bf16[320,1152]{1,0:T(8,128)(2,1)} collective-permute-done((bf16[320,1152]{1,0:T(8,128)(2,1)}, bf16[320,1152]{1,0:T(8,128)(2,1)}, u32[]{:S(2)}, u32[]{:S(2)}) %collective-permute-start.20) | collective-permute-done | bytes 737312 | tf_op jit(solution)/shard_map/ppermute | solution.py:305
  204.4 2.7 add_convert_fusion.1.refs_2_
  208.6 8.0 %collective-permute-done.22.refs_0_ = bf16[320,1152]{1,0:T(8,128)(2,1)} collective-permute-done((bf16[320,1152]{1,0:T(8,128)(2,1)}, bf16[320,1152]{1,0:T(8,128)(2,1)}, u32[]{:S(2)}, u32[]{:S(2)}) %collective-permute-start.22) | collective-permute-done | bytes 737312 | tf_op jit(solution)/shard_map/ppermute | solution.py:305
  216.6 3.9 %collective-permute-done.23.refs_1_.refs_12_ = bf16[320,1152]{1,0:T(8,128)(2,1)} collective-permute-done((bf16[320,1152]{1,0:T(8,128)(2,1)}, bf16[320,1152]{1,0:T(8,128)(2,1)}, u32[]{:S(2)}, u32[]{:S(2)}) %collective-permute-start.23) | collective-permute-done | bytes 737312 | tf_op jit(solution)/shard_map/ppermute | solution.py:306
  221.9 10.5 %collective-permute-done.26.refs_1_.refs_11_ = bf16[320,1152]{1,0:T(8,128)(2,1)} collective-permute-done((bf16[320,1152]{1,0:T(8,128)(2,1)}, bf16[320,1152]{1,0:T(8,128)(2,1)}, u32[]{:S(2)}, u32[]{:S(2)}) %collective-permute-start.26) | collective-permute-done | bytes 737312 | tf_op jit(solution)/shard_map/ppermute | solution.py:305
  234.0 12.4 %shard_map.58 = (bf16[640,1280]{1,0:T(8,128)(2,1)}, bf16[640,1280]{1,0:T(8,128)(2,1)}) custom-call(s32[8]{0:T(128)S(1)} %dynamic-slice_bitcast_fusion.source_ref, s32[5]{0:T(128)S(1)} %copy-done.18, s32[2]{0:T(128)S(1)} %pad_add_fusion.place_ref, bf16[320,1280]{1,0:T(8,128)(2,1)} %get-tuple-element.40.refs_0_.refs_16_, ...), custom_call_target="tpu_custom_call" | custom-call | bytes 1024 | tf_op jit(solution)/shard_map/pallas_call | solution.py:243
  247.8 9.1 %shard_map.59 = (bf16[640,768]{1,0:T(8,128)(2,1)}, bf16[640,768]{1,0:T(8,128)(2,1)}) custom-call(s32[8]{0:T(128)S(1)} %dynamic-slice_bitcast_fusion.source_ref, s32[5]{0:T(128)S(1)} %copy-done.18, s32[2]{0:T(128)S(1)} %pad_add_fusion.place_ref, bf16[320,1152]{1,0:T(8,128)(2,1)S(1)} %copy-done.10, bf16[320,1152]{1,0:T(8,128)(2,1)S(1)} %copy-done.8, ...), custom_call_target="tpu_custom_call" | custom-call | bytes 1024 | tf_op jit(solution)/shard_map/pallas_call | solution.py:243
  257.0 2.8 collective-permute-done.32
  259.7 2.4 add_convert_fusion.refs_32_
  262.1 12.0 %shard_map.60 = (bf16[640,256]{1,0:T(8,128)(2,1)S(1)}, bf16[640,256]{1,0:T(8,128)(2,1)S(1)}, bf16[640,512]{1,0:T(8,128)(2,1)S(1)}, bf16[640,512]{1,0:T(8,128)(2,...) custom-call(s32[8]{0:T(128)S(1)} %dynamic-slice_bitcast_fusion.source_ref, s32[5]{0:T(128)S(1)} %copy-done.18, ...), custom_call_target="tpu_custom_call" | custom-call | bytes 1024 | tf_op jit(solution)/shard_map/pallas_call | solution.py:243
  277.9 5.0 %collective-permute-start.36 = (bf16[640,768]{1,0:T(8,128)(2,1)}, bf16[640,768]{1,0:T(8,128)(2,1)S(1)}, u32[]{:S(2)}, u32[]{:S(2)}) collective-permute-start(bf16[640,768]{1,0:T(8,128)(2,1)} %add_convert_fusion.refs_32_), channel_id=1, source_target_pairs={{0,16},{8,24},{16,0},{24,8},{1,17},{9,25},{17,1},{25,9},{2,18},{10... | collective-permute-start | bytes 2949128 | tf_op jit(solution)/shard_map/ppermute | solution.py:338
  283.6 8.3 %shard_map.61.refs_1_.refs_3_ = bf16[640,1280]{1,0:T(8,128)(2,1)} custom-call(s32[8]{0:T(128)S(1)} %dynamic-slice_bitcast_fusion.source_ref, s32[5]{0:T(128)S(1)} %copy-done.18, s32[2]{0:T(128)S(1)} %pad_add_fusion.place_ref, bf16[320,1152]{1,0:T(8,128)(2,1)S(1)} %copy-done.10, bf16[320,1152]{1,0:T(8,128)(2,1)S(1)} %copy-done.8, ...), custom_call_target="tpu_custom_call" | custom-call | bytes 1024 | tf_op jit(solution)/shard_map/pallas_call | solution.py:243
  291.9 13.8 %collective-permute-done.36.refs_0_ = bf16[640,768]{1,0:T(8,128)(2,1)S(1)} collective-permute-done((bf16[640,768]{1,0:T(8,128)(2,1)}, bf16[640,768]{1,0:T(8,128)(2,1)S(1)}, u32[]{:S(2)}, u32[]{:S(2)}) %collective-permute-start.36) | collective-permute-done | bytes 983072 | tf_op jit(solution)/shard_map/ppermute | solution.py:338
  309.9 5.3 %shard_map.65.refs_1_.before_ref = f32[640,1280]{1,0:T(8,128)} custom-call(bf16[640,768]{1,0:T(8,128)(2,1)} %shard_map.57.refs_32_.refs_0_, bf16[640,512]{1,0:T(8,128)(2,1)} %shard_map.55.refs_4_.refs_33_.refs_1_, bf16[640,1280]{1,0:T(8,128)(2,1)S(1)} %copy-done.13, bf16[640,1280]{1,0:T(8,128)(2,1)} %shard_map.61.refs_1_.refs_3_, ...), custom_call_target="tpu_custom_call" | custom-call | bytes 1024 | tf_op jit(solution)/shard_map/pallas_call | solution.py:116
  315.3 4.1 %collective-permute-done.35.refs_0_ = bf16[640,512]{1,0:T(8,128)(2,1)} collective-permute-done((bf16[640,512]{1,0:T(8,128)(2,1)S(1)}, bf16[640,512]{1,0:T(8,128)(2,1)}, u32[]{:S(2)}, u32[]{:S(2)}) %collective-permute-start.35) | collective-permute-done | bytes 655392 | tf_op jit(solution)/shard_map/ppermute | solution.py:338
  319.4 2.4 shard_map.67
  (141 shorter events, 59.2 us)
Async XLA Ops:
  4.6 22.1 %collective-permute-start.7 = (bf16[320,1280]{1,0:T(8,128)(2,1)S(1)}, bf16[320,1280]{1,0:T(8,128)(2,1)S(1)}, u32[]{:S(2)}, u32[]{:S(2)}) collective-permute-start(bf16[320,1280]{1,0:T(8,128)(2,1)S(1)} %get-tuple-element.46.refs_1_.refs_17_), channel_id=1, source_target_pairs={{2,0},{4,2},{6,4},{7,6},{5,7},{3,5},{1,3},{0,1},{10,8},{12,10},{14... | collective-permute-start | bytes 2457608 | tf_op jit(solution)/shard_map/ppermute | solution.py:306
  13.2 31.1 %collective-permute-start.1 = (bf16[320,1280]{1,0:T(8,128)(2,1)}, bf16[320,1280]{1,0:T(8,128)(2,1)S(1)}, u32[]{:S(2)}, u32[]{:S(2)}) collective-permute-start(bf16[320,1280]{1,0:T(8,128)(2,1)} %get-tuple-element.40.refs_0_.refs_16_), channel_id=1, source_target_pairs={{2,0},{4,2},{6,4},{7,6},{5,7},{3,5},{1,3},{0,1},{10,8},{12,10},{14... | collective-permute-start | bytes 2457608 | tf_op jit(solution)/shard_map/ppermute | solution.py:306
  15.1 31.2 %collective-permute-start = (bf16[320,1280]{1,0:T(8,128)(2,1)}, bf16[320,1280]{1,0:T(8,128)(2,1)S(1)}, u32[]{:S(2)}, u32[]{:S(2)}) collective-permute-start(bf16[320,1280]{1,0:T(8,128)(2,1)} %get-tuple-element.40.refs_0_.refs_16_), channel_id=1, source_target_pairs={{0,2},{2,4},{4,6},{6,7},{7,5},{5,3},{3,1},{1,0},{8,10},{10,12},{12... | collective-permute-start | bytes 2457608 | tf_op jit(solution)/shard_map/ppermute | solution.py:305
  29.7 34.2 %collective-permute-start.8 = (bf16[320,1280]{1,0:T(8,128)(2,1)}, bf16[320,1280]{1,0:T(8,128)(2,1)S(1)}, u32[]{:S(2)}, u32[]{:S(2)}) collective-permute-start(bf16[320,1280]{1,0:T(8,128)(2,1)} %get-tuple-element.47.refs_3_.refs_19_), channel_id=1, source_target_pairs={{0,2},{2,4},{4,6},{6,7},{7,5},{5,3},{3,1},{1,0},{8,10},{10,12},{12... | collective-permute-start | bytes 2457608 | tf_op jit(solution)/shard_map/ppermute | solution.py:305
  30.7 33.2 %collective-permute-start.9 = (bf16[320,1280]{1,0:T(8,128)(2,1)}, bf16[320,1280]{1,0:T(8,128)(2,1)}, u32[]{:S(2)}, u32[]{:S(2)}) collective-permute-start(bf16[320,1280]{1,0:T(8,128)(2,1)} %get-tuple-element.48.refs_5_.refs_21_), channel_id=1, source_target_pairs={{2,0},{4,2},{6,4},{7,6},{5,7},{3,5},{1,3},{0,1},{10,8},{12,10},{14... | collective-permute-start | bytes 2457608 | tf_op jit(solution)/shard_map/ppermute | solution.py:306
  47.2 34.2 %collective-permute-start.2 = (bf16[320,1280]{1,0:T(8,128)(2,1)}, bf16[320,1280]{1,0:T(8,128)(2,1)S(1)}, u32[]{:S(2)}, u32[]{:S(2)}) collective-permute-start(bf16[320,1280]{1,0:T(8,128)(2,1)} %get-tuple-element.41.refs_2_.refs_18_), channel_id=1, source_target_pairs={{0,2},{2,4},{4,6},{6,7},{7,5},{5,3},{3,1},{1,0},{8,10},{10,12},{12... | collective-permute-start | bytes 2457608 | tf_op jit(solution)/shard_map/ppermute | solution.py:305
  48.2 33.3 %collective-permute-start.3 = (bf16[320,1280]{1,0:T(8,128)(2,1)}, bf16[320,1280]{1,0:T(8,128)(2,1)}, u32[]{:S(2)}, u32[]{:S(2)}) collective-permute-start(bf16[320,1280]{1,0:T(8,128)(2,1)} %get-tuple-element.42.refs_4_.refs_20_), channel_id=1, source_target_pairs={{2,0},{4,2},{6,4},{7,6},{5,7},{3,5},{1,3},{0,1},{10,8},{12,10},{14... | collective-permute-start | bytes 2457608 | tf_op jit(solution)/shard_map/ppermute | solution.py:306
  64.8 34.2 %collective-permute-start.10 = (bf16[320,1280]{1,0:T(8,128)(2,1)}, bf16[320,1280]{1,0:T(8,128)(2,1)S(1)}, u32[]{:S(2)}, u32[]{:S(2)}) collective-permute-start(bf16[320,1280]{1,0:T(8,128)(2,1)} %get-tuple-element.49.refs_7_.refs_23_), channel_id=1, source_target_pairs={{0,2},{2,4},{4,6},{6,7},{7,5},{5,3},{3,1},{1,0},{8,10},{10,12},{12... | collective-permute-start | bytes 2457608 | tf_op jit(solution)/shard_map/ppermute | solution.py:305
  64.8 34.2 %collective-permute-start.11 = (bf16[320,1280]{1,0:T(8,128)(2,1)}, bf16[320,1280]{1,0:T(8,128)(2,1)S(1)}, u32[]{:S(2)}, u32[]{:S(2)}) collective-permute-start(bf16[320,1280]{1,0:T(8,128)(2,1)} %get-tuple-element.50.refs_9_.refs_25_), channel_id=1, source_target_pairs={{2,0},{4,2},{6,4},{7,6},{5,7},{3,5},{1,3},{0,1},{10,8},{12,10},{14... | collective-permute-start | bytes 2457608 | tf_op jit(solution)/shard_map/ppermute | solution.py:306
  82.3 32.8 %collective-permute-start.4 = (bf16[320,1280]{1,0:T(8,128)(2,1)}, bf16[320,1280]{1,0:T(8,128)(2,1)}, u32[]{:S(2)}, u32[]{:S(2)}) collective-permute-start(bf16[320,1280]{1,0:T(8,128)(2,1)} %get-tuple-element.43.refs_6_.refs_22_), channel_id=1, source_target_pairs={{0,2},{2,4},{4,6},{6,7},{7,5},{5,3},{3,1},{1,0},{8,10},{10,12},{12... | collective-permute-start | bytes 2457608 | tf_op jit(solution)/shard_map/ppermute | solution.py:305
  82.4 32.8 %collective-permute-start.5 = (bf16[320,1280]{1,0:T(8,128)(2,1)}, bf16[320,1280]{1,0:T(8,128)(2,1)S(1)}, u32[]{:S(2)}, u32[]{:S(2)}) collective-permute-start(bf16[320,1280]{1,0:T(8,128)(2,1)} %get-tuple-element.44.refs_8_.refs_24_), channel_id=1, source_target_pairs={{2,0},{4,2},{6,4},{7,6},{5,7},{3,5},{1,3},{0,1},{10,8},{12,10},{14... | collective-permute-start | bytes 2457608 | tf_op jit(solution)/shard_map/ppermute | solution.py:306
  100.8 31.4 %collective-permute-start.15 = (bf16[320,1280]{1,0:T(8,128)(2,1)}, bf16[320,1280]{1,0:T(8,128)(2,1)}, u32[]{:S(2)}, u32[]{:S(2)}) collective-permute-start(bf16[320,1280]{1,0:T(8,128)(2,1)} %shard_map.45.refs_2_.refs_13_.refs_29_), channel_id=1, source_target_pairs={{2,0},{4,2},{6,4},{7,6},{5,7},{3,5},{1,3},{0,1},{10,8},{12,10},{14... | collective-permute-start | bytes 2457608 | tf_op jit(solution)/shard_map/ppermute | solution.py:311
  117.5 37.2 %collective-permute-start.13 = (bf16[320,1152]{1,0:T(8,128)(2,1)}, bf16[320,1152]{1,0:T(8,128)(2,1)}, u32[]{:S(2)}, u32[]{:S(2)}) collective-permute-start(bf16[320,1152]{1,0:T(8,128)(2,1)} %shard_map.41.refs_0_), channel_id=1, source_target_pairs={{2,0},{4,2},{6,4},{7,6},{5,7},{3,5},{1,3},{0,1},{10,8},{12,10},{14... | collective-permute-start | bytes 2211848 | tf_op jit(solution)/shard_map/ppermute | solution.py:306
  118.2 36.5 %collective-permute-start.12 = (bf16[320,1152]{1,0:T(8,128)(2,1)}, bf16[320,1152]{1,0:T(8,128)(2,1)}, u32[]{:S(2)}, u32[]{:S(2)}) collective-permute-start(bf16[320,1152]{1,0:T(8,128)(2,1)} %shard_map.41.refs_0_), channel_id=1, source_target_pairs={{0,2},{2,4},{4,6},{6,7},{7,5},{5,3},{3,1},{1,0},{8,10},{10,12},{12... | collective-permute-start | bytes 2211848 | tf_op jit(solution)/shard_map/ppermute | solution.py:305
  119.6 43.3 %collective-permute-start.17 = (bf16[320,1152]{1,0:T(8,128)(2,1)}, bf16[320,1152]{1,0:T(8,128)(2,1)}, u32[]{:S(2)}, u32[]{:S(2)}) collective-permute-start(bf16[320,1152]{1,0:T(8,128)(2,1)} %shard_map.46.refs_1_), channel_id=1, source_target_pairs={{2,0},{4,2},{6,4},{7,6},{5,7},{3,5},{1,3},{0,1},{10,8},{12,10},{14... | collective-permute-start | bytes 2211848 | tf_op jit(solution)/shard_map/ppermute | solution.py:306
  132.2 37.0 %collective-permute-start.16 = (bf16[320,1152]{1,0:T(8,128)(2,1)}, bf16[320,1152]{1,0:T(8,128)(2,1)}, u32[]{:S(2)}, u32[]{:S(2)}) collective-permute-start(bf16[320,1152]{1,0:T(8,128)(2,1)} %shard_map.46.refs_1_), channel_id=1, source_target_pairs={{0,2},{2,4},{4,6},{6,7},{7,5},{5,3},{3,1},{1,0},{8,10},{10,12},{12... | collective-permute-start | bytes 2211848 | tf_op jit(solution)/shard_map/ppermute | solution.py:305
  154.8 48.1 %collective-permute-start.24 = (bf16[640,768]{1,0:T(8,128)(2,1)}, bf16[640,768]{1,0:T(8,128)(2,1)}, u32[]{:S(2)}, u32[]{:S(2)}) collective-permute-start(bf16[640,768]{1,0:T(8,128)(2,1)} %shard_map.52), channel_id=1, source_target_pairs={{0,8},{8,0},{16,24},{24,16},{1,9},{9,1},{17,25},{25,17},{2,10},{10... | collective-permute-start | bytes 2949128 | tf_op jit(solution)/shard_map/ppermute | solution.py:335
  155.3 29.7 %collective-permute-start.18 = (bf16[320,1152]{1,0:T(8,128)(2,1)}, bf16[320,1152]{1,0:T(8,128)(2,1)}, u32[]{:S(2)}, u32[]{:S(2)}) collective-permute-start(bf16[320,1152]{1,0:T(8,128)(2,1)} %get-tuple-element.52.refs_1_.refs_2_), channel_id=1, source_target_pairs={{0,2},{2,4},{4,6},{6,7},{7,5},{5,3},{3,1},{1,0},{8,10},{10,12},{12... | collective-permute-start | bytes 2211848 | tf_op jit(solution)/shard_map/ppermute | solution.py:305
  162.9 23.6 %collective-permute-start.19 = (bf16[320,1152]{1,0:T(8,128)(2,1)}, bf16[320,1152]{1,0:T(8,128)(2,1)}, u32[]{:S(2)}, u32[]{:S(2)}) collective-permute-start(bf16[320,1152]{1,0:T(8,128)(2,1)} %get-tuple-element.54.refs_2_.refs_4_), channel_id=1, source_target_pairs={{2,0},{4,2},{6,4},{7,6},{5,7},{3,5},{1,3},{0,1},{10,8},{12,10},{14... | collective-permute-start | bytes 2211848 | tf_op jit(solution)/shard_map/ppermute | solution.py:306
  169.2 31.6 %collective-permute-start.20 = (bf16[320,1152]{1,0:T(8,128)(2,1)}, bf16[320,1152]{1,0:T(8,128)(2,1)}, u32[]{:S(2)}, u32[]{:S(2)}) collective-permute-start(bf16[320,1152]{1,0:T(8,128)(2,1)} %get-tuple-element.53.refs_3_), channel_id=1, source_target_pairs={{0,2},{2,4},{4,6},{6,7},{7,5},{5,3},{3,1},{1,0},{8,10},{10,12},{12... | collective-permute-start | bytes 2211848 | tf_op jit(solution)/shard_map/ppermute | solution.py:305
  170.6 31.8 %collective-permute-start.21 = (bf16[320,1152]{1,0:T(8,128)(2,1)}, bf16[320,1152]{1,0:T(8,128)(2,1)}, u32[]{:S(2)}, u32[]{:S(2)}) collective-permute-start(bf16[320,1152]{1,0:T(8,128)(2,1)} %get-tuple-element.55.refs_5_), channel_id=1, source_target_pairs={{2,0},{4,2},{6,4},{7,6},{5,7},{3,5},{1,3},{0,1},{10,8},{12,10},{14... | collective-permute-start | bytes 2211848 | tf_op jit(solution)/shard_map/ppermute | solution.py:306
  185.0 22.1 %collective-permute-start.28 = (bf16[640,512]{1,0:T(8,128)(2,1)}, bf16[640,512]{1,0:T(8,128)(2,1)}, u32[]{:S(2)}, u32[]{:S(2)}) collective-permute-start(bf16[640,512]{1,0:T(8,128)(2,1)} %add_convert_fusion.3.refs_3_), channel_id=1, source_target_pairs={{0,16},{8,24},{16,0},{24,8},{1,17},{9,25},{17,1},{25,9},{2,18},{10... | collective-permute-start | bytes 1966088 | tf_op jit(solution)/shard_map/ppermute | solution.py:338
  186.5 30.1 %collective-permute-start.22 = (bf16[320,1152]{1,0:T(8,128)(2,1)}, bf16[320,1152]{1,0:T(8,128)(2,1)}, u32[]{:S(2)}, u32[]{:S(2)}) collective-permute-start(bf16[320,1152]{1,0:T(8,128)(2,1)} %get-tuple-element.56.refs_6_), channel_id=1, source_target_pairs={{0,2},{2,4},{4,6},{6,7},{7,5},{5,3},{3,1},{1,0},{8,10},{10,12},{12... | collective-permute-start | bytes 2211848 | tf_op jit(solution)/shard_map/ppermute | solution.py:305
  202.4 30.0 %collective-permute-start.26 = (bf16[320,1152]{1,0:T(8,128)(2,1)}, bf16[320,1152]{1,0:T(8,128)(2,1)}, u32[]{:S(2)}, u32[]{:S(2)}) collective-permute-start(bf16[320,1152]{1,0:T(8,128)(2,1)} %get-tuple-element.57.refs_7_), channel_id=1, source_target_pairs={{0,2},{2,4},{4,6},{6,7},{7,5},{5,3},{3,1},{1,0},{8,10},{10,12},{12... | collective-permute-start | bytes 2211848 | tf_op jit(solution)/shard_map/ppermute | solution.py:305
  202.8 29.6 %collective-permute-start.27 = (bf16[320,1152]{1,0:T(8,128)(2,1)}, bf16[320,1152]{1,0:T(8,128)(2,1)}, u32[]{:S(2)}, u32[]{:S(2)}) collective-permute-start(bf16[320,1152]{1,0:T(8,128)(2,1)} %get-tuple-element.59.refs_9_), channel_id=1, source_target_pairs={{2,0},{4,2},{6,4},{7,6},{5,7},{3,5},{1,3},{0,1},{10,8},{12,10},{14... | collective-permute-start | bytes 2211848 | tf_op jit(solution)/shard_map/ppermute | solution.py:306
  207.1 39.3 %collective-permute-start.31 = (bf16[640,768]{1,0:T(8,128)(2,1)}, bf16[640,768]{1,0:T(8,128)(2,1)}, u32[]{:S(2)}, u32[]{:S(2)}) collective-permute-start(bf16[640,768]{1,0:T(8,128)(2,1)} %add_convert_fusion.1.refs_2_), channel_id=1, source_target_pairs={{0,16},{8,24},{16,0},{24,8},{1,17},{9,25},{17,1},{25,9},{2,18},{10... | collective-permute-start | bytes 2949128 | tf_op jit(solution)/shard_map/ppermute | solution.py:338
  220.5 25.9 %collective-permute-start.29 = (bf16[320,1152]{1,0:T(8,128)(2,1)}, bf16[320,1152]{1,0:T(8,128)(2,1)}, u32[]{:S(2)}, u32[]{:S(2)}) collective-permute-start(bf16[320,1152]{1,0:T(8,128)(2,1)} %shard_map.54.refs_32_.refs_10_), channel_id=1, source_target_pairs={{0,2},{2,4},{4,6},{6,7},{7,5},{5,3},{3,1},{1,0},{8,10},{10,12},{12... | collective-permute-start | bytes 2211848 | tf_op jit(solution)/shard_map/ppermute | solution.py:311
  277.5 31.0 %collective-permute-start.37 = (bf16[640,1280]{1,0:T(8,128)(2,1)}, bf16[640,1280]{1,0:T(8,128)(2,1)}, u32[]{:S(2)}, u32[]{:S(2)}) collective-permute-start(bf16[640,1280]{1,0:T(8,128)(2,1)} %shard_map.63), channel_id=1, source_target_pairs={{0,8},{8,0},{16,24},{24,16},{1,9},{9,1},{17,25},{25,17},{2,10},{10... | collective-permute-start | bytes 4915208 | tf_op jit(solution)/shard_map/ppermute | solution.py:335
  277.9 27.8 %collective-permute-start.36 = (bf16[640,768]{1,0:T(8,128)(2,1)}, bf16[640,768]{1,0:T(8,128)(2,1)S(1)}, u32[]{:S(2)}, u32[]{:S(2)}) collective-permute-start(bf16[640,768]{1,0:T(8,128)(2,1)} %add_convert_fusion.refs_32_), channel_id=1, source_target_pairs={{0,16},{8,24},{16,0},{24,8},{1,17},{9,25},{17,1},{25,9},{2,18},{10... | collective-permute-start | bytes 2949128 | tf_op jit(solution)/shard_map/ppermute | solution.py:338
  282.9 23.7 %collective-permute-start.38 = (bf16[640,512]{1,0:T(8,128)(2,1)}, bf16[640,512]{1,0:T(8,128)(2,1)}, u32[]{:S(2)}, u32[]{:S(2)}) collective-permute-start(bf16[640,512]{1,0:T(8,128)(2,1)} %copy-done.20), channel_id=1, source_target_pairs={{0,8},{8,0},{16,24},{24,16},{1,9},{9,1},{17,25},{25,17},{2,10},{10... | collective-permute-start | bytes 1966088 | tf_op jit(solution)/shard_map/ppermute | solution.py:335
  282.9 23.7 %collective-permute-start.39 = (bf16[640,512]{1,0:T(8,128)(2,1)}, bf16[640,512]{1,0:T(8,128)(2,1)}, u32[]{:S(2)}, u32[]{:S(2)}) collective-permute-start(bf16[640,512]{1,0:T(8,128)(2,1)} %copy-done.19), channel_id=1, source_target_pairs={{0,8},{8,0},{16,24},{24,16},{1,9},{9,1},{17,25},{25,17},{2,10},{10... | collective-permute-start | bytes 1966088 | tf_op jit(solution)/shard_map/ppermute | solution.py:335
  283.5 35.9 %collective-permute-start.35 = (bf16[640,512]{1,0:T(8,128)(2,1)S(1)}, bf16[640,512]{1,0:T(8,128)(2,1)}, u32[]{:S(2)}, u32[]{:S(2)}) collective-permute-start(bf16[640,512]{1,0:T(8,128)(2,1)S(1)} %copy-done.14), channel_id=1, source_target_pairs={{0,16},{8,24},{16,0},{24,8},{1,17},{9,25},{17,1},{25,9},{2,18},{10... | collective-permute-start | bytes 1966088 | tf_op jit(solution)/shard_map/ppermute | solution.py:338
  (36 other events, 445.7 us)

commit v13 on v12

--- a/solution.py
+++ b/solution.py
@@ -341,7 +341,7 @@
     def added(same, crossed):
         return (same.astype(jnp.float32) + crossed.astype(jnp.float32)).astype(jnp.bfloat16)
 
-    terms, starts, pending = [], [], []
+    terms, starts = [], []
     for a in range(1, local_subjects):
         shares, sums, gone = [], [], []
 
@@ -369,9 +369,8 @@
         terms += gone
         same, other = share(a - 1, [(0, flip, 0, chunk) for flip in (0, 1)], [everything[a][-3][0], everything[a][-2][1]])
         gone.append(same)
-        pending.append(other)
-        terms.append(same)
-        starts.append(0)
+        terms += [same, cross(other)]
+        starts += [0, 0]
     last = local_subjects - 1
     scale = 1 / (local_subjects * subjs)
     late = gone
@@ -391,8 +390,8 @@
     summed = added(arrays[len(pieces)], crossed)
     (same,) = share(last, [(0, 0, 0, chunk)], [summed])
     there = send(leading, d, LONG, [same])
-    terms += [same, there, *(cross(other, [summed]) for other in pending)]
-    starts += [0 for _ in terms[len(starts) :]]
+    terms += [same, there]
+    starts += [0, 0]
     for array, (_, _, start, _) in zip(arrays[len(pieces) + 1 :], others):
         terms.append(cross(array, [there] if start == others[-1][2] else ()))
         starts.append(start)

time: 322 us -> 304 us (0.944)
  waiting for transfers between devices: 180 us -> 166 us
    ppermute x4, waiting for transfers between devices: 17.9 us -> 3.68 us  [send(): lax.ppermute(summed, 'subj', [(s, (s + 2 * d) % subjs) for s in range(sub...]
    unnamed x54 -> x50, local copies, waits for them, and re-layouts: 14.4 us -> 13.6 us
  transfers between devices with their start and end apart: 41 -> 41, of which waited for: 23 -> 22; matrix products, arithmetic and copies ran while one was open for 2% -> 2% of each run, Pallas kernels for 14% -> 20%
where the time goes in v13:
time: 304 us; the launch traced here: 303 us
  waiting for transfers between devices  166 us (55%)
  Pallas kernels  74.2 us (24%)
  starting transfers between devices  41.3 us (14%)
  local copies, waits for them, and re-layouts  14.3 us (5%)
  other arithmetic  6.64 us (2%)
    ppermute x12, waiting for transfers between devices, gather(): got[-2][half] = lax.ppermute(ahead[half], SLABS, onward)  107 us
    pallas_call x5, Pallas kernels, scores(): pl.pallas_call(functools.partial(scores_kernel, subject=subject, targets=...  58.1 us
    ppermute x12, waiting for transfers between devices, gather(): got[-1][half] = lax.ppermute(behind[half], SLABS, backward)  35.1 us
    ppermute x12, starting transfers between devices, gather(): got[-1][half] = lax.ppermute(behind[half], SLABS, backward)  17.8 us
    ppermute x4, waiting for transfers between devices, gather(): last.append(lax.ppermute(got[side][half], SLABS, way))  14.6 us
    unnamed x50, local copies, waits for them, and re-layouts  13.6 us
    ppermute x12, starting transfers between devices, gather(): got[-2][half] = lax.ppermute(ahead[half], SLABS, onward)  9.88 us
    pallas_call x2, Pallas kernels, normalize(): pl.pallas_call(functools.partial(normalize_kernel, begin=low, lead=begin...  8.32 us
  transfers between devices with their start and end apart: 41, of which 22 were waited for; matrix products, arithmetic and copies ran while one was open for 2% of the time, Pallas kernels for 20%

profile of v13, /device:TPU:0, one launch (start us, length us, event | category | flops | bytes accessed | tf_op | source)
XLA Modules:
  0.0 303.2 jit_solution(8601014767710160796)
XLA Ops:
  0.0 3.7 %shard_map.42 = (bf16[320,1280]{1,0:T(8,128)(2,1)S(1)}, bf16[320,1152]{1,0:T(8,128)(2,1)S(1)}) custom-call(f32[2,1200,640]{2,1,0:T(8,128)} %bitcast.5), custom_call_target="tpu_custom_call" | custom-call | bytes 1024 | tf_op jit(solution)/shard_map/pallas_call | solution.py:76
  3.8 3.0 collective-permute-start.7
  6.9 4.6 %shard_map.37 = (bf16[320,1280]{1,0:T(8,128)(2,1)}, bf16[320,1152]{1,0:T(8,128)(2,1)S(1)}) custom-call(f32[2,1200,640]{2,1,0:T(8,128)} %bitcast.6), custom_call_target="tpu_custom_call" | custom-call | bytes 1024 | tf_op jit(solution)/shard_map/pallas_call | solution.py:76
  14.4 11.5 %collective-permute-done.7.refs_1_ = bf16[320,1280]{1,0:T(8,128)(2,1)S(1)} collective-permute-done((bf16[320,1280]{1,0:T(8,128)(2,1)S(1)}, bf16[320,1280]{1,0:T(8,128)(2,1)S(1)}, u32[]{:S(2)}, u32[]{:S(2)}) %collective-permute-start.7) | collective-permute-done | bytes 819232 | tf_op jit(solution)/shard_map/ppermute | solution.py:306
  30.9 12.6 %collective-permute-done.1.refs_1_ = bf16[320,1280]{1,0:T(8,128)(2,1)S(1)} collective-permute-done((bf16[320,1280]{1,0:T(8,128)(2,1)}, bf16[320,1280]{1,0:T(8,128)(2,1)S(1)}, u32[]{:S(2)}, u32[]{:S(2)}) %collective-permute-start.1) | collective-permute-done | bytes 819232 | tf_op jit(solution)/shard_map/ppermute | solution.py:306
  43.5 2.0 collective-permute-done.refs_0_
  48.4 14.6 %collective-permute-done.8.refs_0_ = bf16[320,1280]{1,0:T(8,128)(2,1)S(1)} collective-permute-done((bf16[320,1280]{1,0:T(8,128)(2,1)}, bf16[320,1280]{1,0:T(8,128)(2,1)S(1)}, u32[]{:S(2)}, u32[]{:S(2)}) %collective-permute-start.8) | collective-permute-done | bytes 819232 | tf_op jit(solution)/shard_map/ppermute | solution.py:305
  66.1 14.6 %collective-permute-done.2.refs_0_ = bf16[320,1280]{1,0:T(8,128)(2,1)S(1)} collective-permute-done((bf16[320,1280]{1,0:T(8,128)(2,1)}, bf16[320,1280]{1,0:T(8,128)(2,1)S(1)}, u32[]{:S(2)}, u32[]{:S(2)}) %collective-permute-start.2) | collective-permute-done | bytes 819232 | tf_op jit(solution)/shard_map/ppermute | solution.py:305
  83.5 14.6 %collective-permute-done.10.refs_1_.refs_11_.refs_27_ = bf16[320,1280]{1,0:T(8,128)(2,1)S(1)} collective-permute-done((bf16[320,1280]{1,0:T(8,128)(2,1)}, bf16[320,1280]{1,0:T(8,128)(2,1)S(1)}, u32[]{:S(2)}, u32[]{:S(2)}) %collective-permute-start.10) | collective-permute-done | bytes 819232 | tf_op jit(solution)/shard_map/ppermute | solution.py:305
  101.6 12.8 %collective-permute-done.4.refs_0_ = bf16[320,1280]{1,0:T(8,128)(2,1)} collective-permute-done((bf16[320,1280]{1,0:T(8,128)(2,1)}, bf16[320,1280]{1,0:T(8,128)(2,1)}, u32[]{:S(2)}, u32[]{:S(2)}) %collective-permute-start.4) | collective-permute-done | bytes 819232 | tf_op jit(solution)/shard_map/ppermute | solution.py:305
  119.5 11.9 %collective-permute-done.15.refs_15_.refs_31_ = bf16[320,1280]{1,0:T(8,128)(2,1)} collective-permute-done((bf16[320,1280]{1,0:T(8,128)(2,1)}, bf16[320,1280]{1,0:T(8,128)(2,1)}, u32[]{:S(2)}, u32[]{:S(2)}) %collective-permute-start.15) | collective-permute-done | bytes 819232 | tf_op jit(solution)/shard_map/ppermute | solution.py:311
  131.4 2.1 collective-permute-start.16
  134.1 2.6 collective-permute-done.14.refs_14_.refs_30_
  136.8 15.0 %shard_map.47 = (bf16[640,768]{1,0:T(8,128)(2,1)}, bf16[640,768]{1,0:T(8,128)(2,1)}, bf16[640,512]{1,0:T(8,128)(2,1)S(1)}, bf16[640,512]{1,0:T(8,128)(2,1)S(1)}) custom-call(s32[8]{0:T(128)S(1)} %dynamic-slice_bitcast_fusion.source_ref, s32[5]{0:T(128)S(1)} %copy-done.17, s32[2]{0:T(128)S(1)} %pad_add_fusion.place_ref, ...), custom_call_target="tpu_custom_call" | custom-call | bytes 1024 | tf_op jit(solution)/shard_map/pallas_call | solution.py:243
  155.1 7.1 %collective-permute-done.17.refs_1_ = bf16[320,1152]{1,0:T(8,128)(2,1)} collective-permute-done((bf16[320,1152]{1,0:T(8,128)(2,1)}, bf16[320,1152]{1,0:T(8,128)(2,1)}, u32[]{:S(2)}, u32[]{:S(2)}) %collective-permute-start.17) | collective-permute-done | bytes 737312 | tf_op jit(solution)/shard_map/ppermute | solution.py:306
  163.8 4.5 %collective-permute-done.16.refs_0_ = bf16[320,1152]{1,0:T(8,128)(2,1)} collective-permute-done((bf16[320,1152]{1,0:T(8,128)(2,1)}, bf16[320,1152]{1,0:T(8,128)(2,1)}, u32[]{:S(2)}, u32[]{:S(2)}) %collective-permute-start.16) | collective-permute-done | bytes 737312 | tf_op jit(solution)/shard_map/ppermute | solution.py:305
  170.4 2.3 add_convert_fusion.3.refs_3_
  172.7 11.5 %collective-permute-done.18.refs_0_ = bf16[320,1152]{1,0:T(8,128)(2,1)} collective-permute-done((bf16[320,1152]{1,0:T(8,128)(2,1)}, bf16[320,1152]{1,0:T(8,128)(2,1)}, u32[]{:S(2)}, u32[]{:S(2)}) %collective-permute-start.18) | collective-permute-done | bytes 737312 | tf_op jit(solution)/shard_map/ppermute | solution.py:305
  187.0 12.9 %collective-permute-done.20.refs_0_ = bf16[320,1152]{1,0:T(8,128)(2,1)} collective-permute-done((bf16[320,1152]{1,0:T(8,128)(2,1)}, bf16[320,1152]{1,0:T(8,128)(2,1)}, u32[]{:S(2)}, u32[]{:S(2)}) %collective-permute-start.20) | collective-permute-done | bytes 737312 | tf_op jit(solution)/shard_map/ppermute | solution.py:305
  203.6 2.7 add_convert_fusion.1.refs_2_
  207.7 8.0 %collective-permute-done.22.refs_0_ = bf16[320,1152]{1,0:T(8,128)(2,1)} collective-permute-done((bf16[320,1152]{1,0:T(8,128)(2,1)}, bf16[320,1152]{1,0:T(8,128)(2,1)}, u32[]{:S(2)}, u32[]{:S(2)}) %collective-permute-start.22) | collective-permute-done | bytes 737312 | tf_op jit(solution)/shard_map/ppermute | solution.py:305
  215.8 3.9 %collective-permute-done.23.refs_1_.refs_12_ = bf16[320,1152]{1,0:T(8,128)(2,1)} collective-permute-done((bf16[320,1152]{1,0:T(8,128)(2,1)}, bf16[320,1152]{1,0:T(8,128)(2,1)}, u32[]{:S(2)}, u32[]{:S(2)}) %collective-permute-start.23) | collective-permute-done | bytes 737312 | tf_op jit(solution)/shard_map/ppermute | solution.py:306
  221.1 10.5 %collective-permute-done.26.refs_1_.refs_11_ = bf16[320,1152]{1,0:T(8,128)(2,1)} collective-permute-done((bf16[320,1152]{1,0:T(8,128)(2,1)}, bf16[320,1152]{1,0:T(8,128)(2,1)}, u32[]{:S(2)}, u32[]{:S(2)}) %collective-permute-start.26) | collective-permute-done | bytes 737312 | tf_op jit(solution)/shard_map/ppermute | solution.py:305
  233.1 14.1 %shard_map.58 = (bf16[640,1280]{1,0:T(8,128)(2,1)}, bf16[640,1280]{1,0:T(8,128)(2,1)}) custom-call(s32[8]{0:T(128)S(1)} %dynamic-slice_bitcast_fusion.source_ref, s32[5]{0:T(128)S(1)} %copy-done.17, s32[2]{0:T(128)S(1)} %pad_add_fusion.place_ref, bf16[320,1280]{1,0:T(8,128)(2,1)} %get-tuple-element.40.refs_0_.refs_16_, ...), custom_call_target="tpu_custom_call" | custom-call | bytes 1024 | tf_op jit(solution)/shard_map/pallas_call | solution.py:243
  248.6 8.7 %shard_map.59 = (bf16[640,768]{1,0:T(8,128)(2,1)}, bf16[640,768]{1,0:T(8,128)(2,1)}) custom-call(s32[8]{0:T(128)S(1)} %dynamic-slice_bitcast_fusion.source_ref, s32[5]{0:T(128)S(1)} %copy-done.17, s32[2]{0:T(128)S(1)} %pad_add_fusion.place_ref, bf16[320,1152]{1,0:T(8,128)(2,1)S(1)} %copy-done.10, bf16[320,1152]{1,0:T(8,128)(2,1)S(1)} %copy-done.8, ...), custom_call_target="tpu_custom_call" | custom-call | bytes 1024 | tf_op jit(solution)/shard_map/pallas_call | solution.py:243
  257.9 2.9 collective-permute-done.32
  262.2 2.4 collective-permute-start.37
  264.6 12.8 %shard_map.60 = (bf16[640,256]{1,0:T(8,128)(2,1)S(1)}, bf16[640,256]{1,0:T(8,128)(2,1)S(1)}, bf16[640,512]{1,0:T(8,128)(2,1)S(1)}, bf16[640,512]{1,0:T(8,128)(2,...) custom-call(s32[8]{0:T(128)S(1)} %dynamic-slice_bitcast_fusion.source_ref, s32[5]{0:T(128)S(1)} %copy-done.17, ...), custom_call_target="tpu_custom_call" | custom-call | bytes 1024 | tf_op jit(solution)/shard_map/pallas_call | solution.py:243
  280.0 7.5 %shard_map.61.refs_1_.refs_4_ = bf16[640,1280]{1,0:T(8,128)(2,1)} custom-call(s32[8]{0:T(128)S(1)} %dynamic-slice_bitcast_fusion.source_ref, s32[5]{0:T(128)S(1)} %copy-done.17, s32[2]{0:T(128)S(1)} %pad_add_fusion.place_ref, bf16[320,1152]{1,0:T(8,128)(2,1)S(1)} %copy-done.10, bf16[320,1152]{1,0:T(8,128)(2,1)S(1)} %copy-done.8, ...), custom_call_target="tpu_custom_call" | custom-call | bytes 1024 | tf_op jit(solution)/shard_map/pallas_call | solution.py:243
  291.8 5.3 %shard_map.64.refs_1_.before_ref = f32[640,1280]{1,0:T(8,128)} custom-call(bf16[640,768]{1,0:T(8,128)(2,1)} %shard_map.57.refs_32_.refs_0_, bf16[640,512]{1,0:T(8,128)(2,1)} %shard_map.55.refs_4_.refs_33_.refs_1_, bf16[640,1280]{1,0:T(8,128)(2,1)S(1)} %copy-done.13, bf16[640,1280]{1,0:T(8,128)(2,1)} %collective-permute-done.36.refs_3_, ...), custom_call_target="tpu_custom_call" | custom-call | bytes 1024 | tf_op jit(solution)/shard_map/pallas_call | solution.py:116
  297.1 3.7 %collective-permute-done.35.refs_0_ = bf16[640,512]{1,0:T(8,128)(2,1)} collective-permute-done((bf16[640,512]{1,0:T(8,128)(2,1)S(1)}, bf16[640,512]{1,0:T(8,128)(2,1)}, u32[]{:S(2)}, u32[]{:S(2)}) %collective-permute-start.35) | collective-permute-done | bytes 655392 | tf_op jit(solution)/shard_map/ppermute | solution.py:338
  300.8 2.4 shard_map.66
  (136 shorter events, 54.0 us)
Async XLA Ops:
  3.8 22.1 %collective-permute-start.7 = (bf16[320,1280]{1,0:T(8,128)(2,1)S(1)}, bf16[320,1280]{1,0:T(8,128)(2,1)S(1)}, u32[]{:S(2)}, u32[]{:S(2)}) collective-permute-start(bf16[320,1280]{1,0:T(8,128)(2,1)S(1)} %get-tuple-element.46.refs_1_.refs_17_), channel_id=1, source_target_pairs={{2,0},{4,2},{6,4},{7,6},{5,7},{3,5},{1,3},{0,1},{10,8},{12,10},{14... | collective-permute-start | bytes 2457608 | tf_op jit(solution)/shard_map/ppermute | solution.py:306
  6.8 21.2 %collective-permute-start.6 = (bf16[320,1280]{1,0:T(8,128)(2,1)S(1)}, bf16[320,1280]{1,0:T(8,128)(2,1)S(1)}, u32[]{:S(2)}, u32[]{:S(2)}) collective-permute-start(bf16[320,1280]{1,0:T(8,128)(2,1)S(1)} %get-tuple-element.46.refs_1_.refs_17_), channel_id=1, source_target_pairs={{0,2},{2,4},{4,6},{6,7},{7,5},{5,3},{3,1},{1,0},{8,10},{10,12},{12... | collective-permute-start | bytes 2457608 | tf_op jit(solution)/shard_map/ppermute | solution.py:305
  12.4 31.1 %collective-permute-start.1 = (bf16[320,1280]{1,0:T(8,128)(2,1)}, bf16[320,1280]{1,0:T(8,128)(2,1)S(1)}, u32[]{:S(2)}, u32[]{:S(2)}) collective-permute-start(bf16[320,1280]{1,0:T(8,128)(2,1)} %get-tuple-element.40.refs_0_.refs_16_), channel_id=1, source_target_pairs={{2,0},{4,2},{6,4},{7,6},{5,7},{3,5},{1,3},{0,1},{10,8},{12,10},{14... | collective-permute-start | bytes 2457608 | tf_op jit(solution)/shard_map/ppermute | solution.py:306
  14.3 31.2 %collective-permute-start = (bf16[320,1280]{1,0:T(8,128)(2,1)}, bf16[320,1280]{1,0:T(8,128)(2,1)S(1)}, u32[]{:S(2)}, u32[]{:S(2)}) collective-permute-start(bf16[320,1280]{1,0:T(8,128)(2,1)} %get-tuple-element.40.refs_0_.refs_16_), channel_id=1, source_target_pairs={{0,2},{2,4},{4,6},{6,7},{7,5},{5,3},{3,1},{1,0},{8,10},{10,12},{12... | collective-permute-start | bytes 2457608 | tf_op jit(solution)/shard_map/ppermute | solution.py:305
  28.9 34.2 %collective-permute-start.8 = (bf16[320,1280]{1,0:T(8,128)(2,1)}, bf16[320,1280]{1,0:T(8,128)(2,1)S(1)}, u32[]{:S(2)}, u32[]{:S(2)}) collective-permute-start(bf16[320,1280]{1,0:T(8,128)(2,1)} %get-tuple-element.47.refs_3_.refs_19_), channel_id=1, source_target_pairs={{0,2},{2,4},{4,6},{6,7},{7,5},{5,3},{3,1},{1,0},{8,10},{10,12},{12... | collective-permute-start | bytes 2457608 | tf_op jit(solution)/shard_map/ppermute | solution.py:305
  29.8 33.3 %collective-permute-start.9 = (bf16[320,1280]{1,0:T(8,128)(2,1)}, bf16[320,1280]{1,0:T(8,128)(2,1)}, u32[]{:S(2)}, u32[]{:S(2)}) collective-permute-start(bf16[320,1280]{1,0:T(8,128)(2,1)} %get-tuple-element.48.refs_5_.refs_21_), channel_id=1, source_target_pairs={{2,0},{4,2},{6,4},{7,6},{5,7},{3,5},{1,3},{0,1},{10,8},{12,10},{14... | collective-permute-start | bytes 2457608 | tf_op jit(solution)/shard_map/ppermute | solution.py:306
  46.4 34.2 %collective-permute-start.2 = (bf16[320,1280]{1,0:T(8,128)(2,1)}, bf16[320,1280]{1,0:T(8,128)(2,1)S(1)}, u32[]{:S(2)}, u32[]{:S(2)}) collective-permute-start(bf16[320,1280]{1,0:T(8,128)(2,1)} %get-tuple-element.41.refs_2_.refs_18_), channel_id=1, source_target_pairs={{0,2},{2,4},{4,6},{6,7},{7,5},{5,3},{3,1},{1,0},{8,10},{10,12},{12... | collective-permute-start | bytes 2457608 | tf_op jit(solution)/shard_map/ppermute | solution.py:305
  47.4 33.3 %collective-permute-start.3 = (bf16[320,1280]{1,0:T(8,128)(2,1)}, bf16[320,1280]{1,0:T(8,128)(2,1)}, u32[]{:S(2)}, u32[]{:S(2)}) collective-permute-start(bf16[320,1280]{1,0:T(8,128)(2,1)} %get-tuple-element.42.refs_4_.refs_20_), channel_id=1, source_target_pairs={{2,0},{4,2},{6,4},{7,6},{5,7},{3,5},{1,3},{0,1},{10,8},{12,10},{14... | collective-permute-start | bytes 2457608 | tf_op jit(solution)/shard_map/ppermute | solution.py:306
  64.0 34.1 %collective-permute-start.10 = (bf16[320,1280]{1,0:T(8,128)(2,1)}, bf16[320,1280]{1,0:T(8,128)(2,1)S(1)}, u32[]{:S(2)}, u32[]{:S(2)}) collective-permute-start(bf16[320,1280]{1,0:T(8,128)(2,1)} %get-tuple-element.49.refs_7_.refs_23_), channel_id=1, source_target_pairs={{0,2},{2,4},{4,6},{6,7},{7,5},{5,3},{3,1},{1,0},{8,10},{10,12},{12... | collective-permute-start | bytes 2457608 | tf_op jit(solution)/shard_map/ppermute | solution.py:305
  64.1 34.1 %collective-permute-start.11 = (bf16[320,1280]{1,0:T(8,128)(2,1)}, bf16[320,1280]{1,0:T(8,128)(2,1)S(1)}, u32[]{:S(2)}, u32[]{:S(2)}) collective-permute-start(bf16[320,1280]{1,0:T(8,128)(2,1)} %get-tuple-element.50.refs_9_.refs_25_), channel_id=1, source_target_pairs={{2,0},{4,2},{6,4},{7,6},{5,7},{3,5},{1,3},{0,1},{10,8},{12,10},{14... | collective-permute-start | bytes 2457608 | tf_op jit(solution)/shard_map/ppermute | solution.py:306
  81.5 32.9 %collective-permute-start.4 = (bf16[320,1280]{1,0:T(8,128)(2,1)}, bf16[320,1280]{1,0:T(8,128)(2,1)}, u32[]{:S(2)}, u32[]{:S(2)}) collective-permute-start(bf16[320,1280]{1,0:T(8,128)(2,1)} %get-tuple-element.43.refs_6_.refs_22_), channel_id=1, source_target_pairs={{0,2},{2,4},{4,6},{6,7},{7,5},{5,3},{3,1},{1,0},{8,10},{10,12},{12... | collective-permute-start | bytes 2457608 | tf_op jit(solution)/shard_map/ppermute | solution.py:305
  81.6 32.8 %collective-permute-start.5 = (bf16[320,1280]{1,0:T(8,128)(2,1)}, bf16[320,1280]{1,0:T(8,128)(2,1)S(1)}, u32[]{:S(2)}, u32[]{:S(2)}) collective-permute-start(bf16[320,1280]{1,0:T(8,128)(2,1)} %get-tuple-element.44.refs_8_.refs_24_), channel_id=1, source_target_pairs={{2,0},{4,2},{6,4},{7,6},{5,7},{3,5},{1,3},{0,1},{10,8},{12,10},{14... | collective-permute-start | bytes 2457608 | tf_op jit(solution)/shard_map/ppermute | solution.py:306
  100.0 31.3 %collective-permute-start.15 = (bf16[320,1280]{1,0:T(8,128)(2,1)}, bf16[320,1280]{1,0:T(8,128)(2,1)}, u32[]{:S(2)}, u32[]{:S(2)}) collective-permute-start(bf16[320,1280]{1,0:T(8,128)(2,1)} %shard_map.45.refs_2_.refs_13_.refs_29_), channel_id=1, source_target_pairs={{2,0},{4,2},{6,4},{7,6},{5,7},{3,5},{1,3},{0,1},{10,8},{12,10},{14... | collective-permute-start | bytes 2457608 | tf_op jit(solution)/shard_map/ppermute | solution.py:311
  115.3 21.5 %collective-permute-start.14 = (bf16[320,1280]{1,0:T(8,128)(2,1)}, bf16[320,1280]{1,0:T(8,128)(2,1)}, u32[]{:S(2)}, u32[]{:S(2)}) collective-permute-start(bf16[320,1280]{1,0:T(8,128)(2,1)} %shard_map.40.refs_1_.refs_10_.refs_26_), channel_id=1, source_target_pairs={{0,2},{2,4},{4,6},{6,7},{7,5},{5,3},{3,1},{1,0},{8,10},{10,12},{12... | collective-permute-start | bytes 2457608 | tf_op jit(solution)/shard_map/ppermute | solution.py:311
  116.6 36.9 %collective-permute-start.13 = (bf16[320,1152]{1,0:T(8,128)(2,1)}, bf16[320,1152]{1,0:T(8,128)(2,1)}, u32[]{:S(2)}, u32[]{:S(2)}) collective-permute-start(bf16[320,1152]{1,0:T(8,128)(2,1)} %shard_map.41.refs_0_), channel_id=1, source_target_pairs={{2,0},{4,2},{6,4},{7,6},{5,7},{3,5},{1,3},{0,1},{10,8},{12,10},{14... | collective-permute-start | bytes 2211848 | tf_op jit(solution)/shard_map/ppermute | solution.py:306
  117.4 36.2 %collective-permute-start.12 = (bf16[320,1152]{1,0:T(8,128)(2,1)}, bf16[320,1152]{1,0:T(8,128)(2,1)}, u32[]{:S(2)}, u32[]{:S(2)}) collective-permute-start(bf16[320,1152]{1,0:T(8,128)(2,1)} %shard_map.41.refs_0_), channel_id=1, source_target_pairs={{0,2},{2,4},{4,6},{6,7},{7,5},{5,3},{3,1},{1,0},{8,10},{10,12},{12... | collective-permute-start | bytes 2211848 | tf_op jit(solution)/shard_map/ppermute | solution.py:305
  118.8 43.3 %collective-permute-start.17 = (bf16[320,1152]{1,0:T(8,128)(2,1)}, bf16[320,1152]{1,0:T(8,128)(2,1)}, u32[]{:S(2)}, u32[]{:S(2)}) collective-permute-start(bf16[320,1152]{1,0:T(8,128)(2,1)} %shard_map.46.refs_1_), channel_id=1, source_target_pairs={{2,0},{4,2},{6,4},{7,6},{5,7},{3,5},{1,3},{0,1},{10,8},{12,10},{14... | collective-permute-start | bytes 2211848 | tf_op jit(solution)/shard_map/ppermute | solution.py:306
  131.4 37.0 %collective-permute-start.16 = (bf16[320,1152]{1,0:T(8,128)(2,1)}, bf16[320,1152]{1,0:T(8,128)(2,1)}, u32[]{:S(2)}, u32[]{:S(2)}) collective-permute-start(bf16[320,1152]{1,0:T(8,128)(2,1)} %shard_map.46.refs_1_), channel_id=1, source_target_pairs={{0,2},{2,4},{4,6},{6,7},{7,5},{5,3},{3,1},{1,0},{8,10},{10,12},{12... | collective-permute-start | bytes 2211848 | tf_op jit(solution)/shard_map/ppermute | solution.py:305
  153.6 48.4 %collective-permute-start.24 = (bf16[640,768]{1,0:T(8,128)(2,1)}, bf16[640,768]{1,0:T(8,128)(2,1)}, u32[]{:S(2)}, u32[]{:S(2)}) collective-permute-start(bf16[640,768]{1,0:T(8,128)(2,1)} %shard_map.52), channel_id=1, source_target_pairs={{0,8},{8,0},{16,24},{24,16},{1,9},{9,1},{17,25},{25,17},{2,10},{10... | collective-permute-start | bytes 2949128 | tf_op jit(solution)/shard_map/ppermute | solution.py:335
  154.1 30.1 %collective-permute-start.18 = (bf16[320,1152]{1,0:T(8,128)(2,1)}, bf16[320,1152]{1,0:T(8,128)(2,1)}, u32[]{:S(2)}, u32[]{:S(2)}) collective-permute-start(bf16[320,1152]{1,0:T(8,128)(2,1)} %get-tuple-element.52.refs_1_.refs_2_), channel_id=1, source_target_pairs={{0,2},{2,4},{4,6},{6,7},{7,5},{5,3},{3,1},{1,0},{8,10},{10,12},{12... | collective-permute-start | bytes 2211848 | tf_op jit(solution)/shard_map/ppermute | solution.py:305
  162.1 23.5 %collective-permute-start.19 = (bf16[320,1152]{1,0:T(8,128)(2,1)}, bf16[320,1152]{1,0:T(8,128)(2,1)}, u32[]{:S(2)}, u32[]{:S(2)}) collective-permute-start(bf16[320,1152]{1,0:T(8,128)(2,1)} %get-tuple-element.54.refs_2_.refs_4_), channel_id=1, source_target_pairs={{2,0},{4,2},{6,4},{7,6},{5,7},{3,5},{1,3},{0,1},{10,8},{12,10},{14... | collective-permute-start | bytes 2211848 | tf_op jit(solution)/shard_map/ppermute | solution.py:306
  168.4 31.6 %collective-permute-start.20 = (bf16[320,1152]{1,0:T(8,128)(2,1)}, bf16[320,1152]{1,0:T(8,128)(2,1)}, u32[]{:S(2)}, u32[]{:S(2)}) collective-permute-start(bf16[320,1152]{1,0:T(8,128)(2,1)} %get-tuple-element.53.refs_3_), channel_id=1, source_target_pairs={{0,2},{2,4},{4,6},{6,7},{7,5},{5,3},{3,1},{1,0},{8,10},{10,12},{12... | collective-permute-start | bytes 2211848 | tf_op jit(solution)/shard_map/ppermute | solution.py:305
  169.7 31.8 %collective-permute-start.21 = (bf16[320,1152]{1,0:T(8,128)(2,1)}, bf16[320,1152]{1,0:T(8,128)(2,1)}, u32[]{:S(2)}, u32[]{:S(2)}) collective-permute-start(bf16[320,1152]{1,0:T(8,128)(2,1)} %get-tuple-element.55.refs_5_), channel_id=1, source_target_pairs={{2,0},{4,2},{6,4},{7,6},{5,7},{3,5},{1,3},{0,1},{10,8},{12,10},{14... | collective-permute-start | bytes 2211848 | tf_op jit(solution)/shard_map/ppermute | solution.py:306
  184.2 22.1 %collective-permute-start.28 = (bf16[640,512]{1,0:T(8,128)(2,1)}, bf16[640,512]{1,0:T(8,128)(2,1)}, u32[]{:S(2)}, u32[]{:S(2)}) collective-permute-start(bf16[640,512]{1,0:T(8,128)(2,1)} %add_convert_fusion.3.refs_3_), channel_id=1, source_target_pairs={{0,16},{8,24},{16,0},{24,8},{1,17},{9,25},{17,1},{25,9},{2,18},{10... | collective-permute-start | bytes 1966088 | tf_op jit(solution)/shard_map/ppermute | solution.py:338
  185.6 30.1 %collective-permute-start.22 = (bf16[320,1152]{1,0:T(8,128)(2,1)}, bf16[320,1152]{1,0:T(8,128)(2,1)}, u32[]{:S(2)}, u32[]{:S(2)}) collective-permute-start(bf16[320,1152]{1,0:T(8,128)(2,1)} %get-tuple-element.56.refs_6_), channel_id=1, source_target_pairs={{0,2},{2,4},{4,6},{6,7},{7,5},{5,3},{3,1},{1,0},{8,10},{10,12},{12... | collective-permute-start | bytes 2211848 | tf_op jit(solution)/shard_map/ppermute | solution.py:305
  201.5 30.0 %collective-permute-start.26 = (bf16[320,1152]{1,0:T(8,128)(2,1)}, bf16[320,1152]{1,0:T(8,128)(2,1)}, u32[]{:S(2)}, u32[]{:S(2)}) collective-permute-start(bf16[320,1152]{1,0:T(8,128)(2,1)} %get-tuple-element.57.refs_7_), channel_id=1, source_target_pairs={{0,2},{2,4},{4,6},{6,7},{7,5},{5,3},{3,1},{1,0},{8,10},{10,12},{12... | collective-permute-start | bytes 2211848 | tf_op jit(solution)/shard_map/ppermute | solution.py:305
  202.0 29.6 %collective-permute-start.27 = (bf16[320,1152]{1,0:T(8,128)(2,1)}, bf16[320,1152]{1,0:T(8,128)(2,1)}, u32[]{:S(2)}, u32[]{:S(2)}) collective-permute-start(bf16[320,1152]{1,0:T(8,128)(2,1)} %get-tuple-element.59.refs_9_), channel_id=1, source_target_pairs={{2,0},{4,2},{6,4},{7,6},{5,7},{3,5},{1,3},{0,1},{10,8},{12,10},{14... | collective-permute-start | bytes 2211848 | tf_op jit(solution)/shard_map/ppermute | solution.py:306
  206.2 41.0 %collective-permute-start.31 = (bf16[640,768]{1,0:T(8,128)(2,1)}, bf16[640,768]{1,0:T(8,128)(2,1)}, u32[]{:S(2)}, u32[]{:S(2)}) collective-permute-start(bf16[640,768]{1,0:T(8,128)(2,1)} %add_convert_fusion.1.refs_2_), channel_id=1, source_target_pairs={{0,16},{8,24},{16,0},{24,8},{1,17},{9,25},{17,1},{25,9},{2,18},{10... | collective-permute-start | bytes 2949128 | tf_op jit(solution)/shard_map/ppermute | solution.py:338
  219.7 27.6 %collective-permute-start.29 = (bf16[320,1152]{1,0:T(8,128)(2,1)}, bf16[320,1152]{1,0:T(8,128)(2,1)}, u32[]{:S(2)}, u32[]{:S(2)}) collective-permute-start(bf16[320,1152]{1,0:T(8,128)(2,1)} %shard_map.54.refs_32_.refs_10_), channel_id=1, source_target_pairs={{0,2},{2,4},{4,6},{6,7},{7,5},{5,3},{3,1},{1,0},{8,10},{10,12},{12... | collective-permute-start | bytes 2211848 | tf_op jit(solution)/shard_map/ppermute | solution.py:311
  257.4 31.3 %collective-permute-start.36 = (bf16[640,1280]{1,0:T(8,128)(2,1)}, bf16[640,1280]{1,0:T(8,128)(2,1)}, u32[]{:S(2)}, u32[]{:S(2)}) collective-permute-start(bf16[640,1280]{1,0:T(8,128)(2,1)} %get-tuple-element.69), channel_id=1, source_target_pairs={{0,8},{8,0},{16,24},{24,16},{1,9},{9,1},{17,25},{25,17},{2,10},{10... | collective-permute-start | bytes 4915208 | tf_op jit(solution)/shard_map/ppermute | solution.py:335
  262.2 25.2 %collective-permute-start.37 = (bf16[640,768]{1,0:T(8,128)(2,1)S(1)}, bf16[640,768]{1,0:T(8,128)(2,1)S(1)}, u32[]{:S(2)}, u32[]{:S(2)}) collective-permute-start(bf16[640,768]{1,0:T(8,128)(2,1)S(1)} %add_convert_fusion.refs_32_), channel_id=1, source_target_pairs={{0,16},{8,24},{16,0},{24,8},{1,17},{9,25},{17,1},{25,9},{2,18},{10... | collective-permute-start | bytes 2949128 | tf_op jit(solution)/shard_map/ppermute | solution.py:338
  279.8 21.0 %collective-permute-start.35 = (bf16[640,512]{1,0:T(8,128)(2,1)S(1)}, bf16[640,512]{1,0:T(8,128)(2,1)}, u32[]{:S(2)}, u32[]{:S(2)}) collective-permute-start(bf16[640,512]{1,0:T(8,128)(2,1)S(1)} %add_convert_fusion.2.refs_32_), channel_id=1, source_target_pairs={{0,16},{8,24},{16,0},{24,8},{1,17},{9,25},{17,1},{25,9},{2,18},{10... | collective-permute-start | bytes 1966088 | tf_op jit(solution)/shard_map/ppermute | solution.py:338
  (34 other events, 429.8 us)

commit v14 on v13

--- a/solution.py
+++ b/solution.py
@@ -220,9 +220,11 @@
 
     def score(i):
         _, k, width, out_ref = tiles[i]
-        products = jnp.clip(buffers[i % 2][:, :width], -limit, limit)
-        fisher = 0.5 * (jnp.log(duration + products) - jnp.log(duration - products))
-        out_ref[:, pl.ds(k, width)] = fisher.astype(jnp.bfloat16)
+        step = math.gcd(slab, 64)
+        for r in range(0, slab, step):
+            products = jnp.clip(buffers[i % 2][r : r + step, :width], -limit, limit)
+            fisher = jnp.log(duration + products) - jnp.log(duration - products)
+            out_ref[r : r + step, pl.ds(k, width)] = fisher.astype(jnp.bfloat16)
 
     multiply(0)
     for i in range(1, len(tiles)):
@@ -372,7 +374,7 @@
         terms += [same, cross(other)]
         starts += [0, 0]
     last = local_subjects - 1
-    scale = 1 / (local_subjects * subjs)
+    scale = 0.5 / (local_subjects * subjs)
     late = gone
     for d in aways[:-2]:
         same, other = share(last, [(d, 0, 0, chunk), (d, 1, 0, chunk)], late)

time: 304 us -> 304 us (level)
  Pallas kernels: 74.2 us -> 71.1 us
    pallas_call x5, Pallas kernels: 58.1 us -> 55 us  [scores(): pl.pallas_call(functools.partial(scores_kernel, subject=subject, targets=...]
  transfers between devices with their start and end apart: 41 -> 41, of which waited for: 22 -> 24; matrix products, arithmetic and copies ran while one was open for 2% -> 2% of each run, Pallas kernels for 20% -> 19%
where the time goes in v14:
time: 304 us; the launch traced here: 303 us
  waiting for transfers between devices  169 us (56%)
  Pallas kernels  71.1 us (23%)
  starting transfers between devices  41.1 us (14%)
  local copies, waits for them, and re-layouts  14.3 us (5%)
  other arithmetic  6.64 us (2%)
    ppermute x12, waiting for transfers between devices, gather(): got[-2][half] = lax.ppermute(ahead[half], SLABS, onward)  108 us
    pallas_call x5, Pallas kernels, scores(): pl.pallas_call(functools.partial(scores_kernel, subject=subject, targets=...  55 us
    ppermute x12, waiting for transfers between devices, gather(): got[-1][half] = lax.ppermute(behind[half], SLABS, backward)  35.7 us
    ppermute x12, starting transfers between devices, gather(): got[-1][half] = lax.ppermute(behind[half], SLABS, backward)  17.8 us
    ppermute x4, waiting for transfers between devices, gather(): last.append(lax.ppermute(got[side][half], SLABS, way))  14.6 us
    unnamed x50, local copies, waits for them, and re-layouts  13.6 us
    ppermute x12, starting transfers between devices, gather(): got[-2][half] = lax.ppermute(ahead[half], SLABS, onward)  10.3 us
    pallas_call x2, Pallas kernels, normalize(): pl.pallas_call(functools.partial(normalize_kernel, begin=low, lead=begin...  8.32 us
  transfers between devices with their start and end apart: 41, of which 24 were waited for; matrix products, arithmetic and copies ran while one was open for 2% of the time, Pallas kernels for 19%

profile of v14, /device:TPU:0, one launch (start us, length us, event | category | flops | bytes accessed | tf_op | source)
XLA Modules:
  0.0 302.5 jit_solution(8636898286347819764)
XLA Ops:
  0.0 3.7 %shard_map.42 = (bf16[320,1280]{1,0:T(8,128)(2,1)S(1)}, bf16[320,1152]{1,0:T(8,128)(2,1)S(1)}) custom-call(f32[2,1200,640]{2,1,0:T(8,128)} %bitcast.5), custom_call_target="tpu_custom_call" | custom-call | bytes 1024 | tf_op jit(solution)/shard_map/pallas_call | solution.py:76
  3.8 3.0 collective-permute-start.7
  6.9 4.6 %shard_map.37 = (bf16[320,1280]{1,0:T(8,128)(2,1)}, bf16[320,1152]{1,0:T(8,128)(2,1)S(1)}) custom-call(f32[2,1200,640]{2,1,0:T(8,128)} %bitcast.6), custom_call_target="tpu_custom_call" | custom-call | bytes 1024 | tf_op jit(solution)/shard_map/pallas_call | solution.py:76
  14.4 11.5 %collective-permute-done.7.refs_1_ = bf16[320,1280]{1,0:T(8,128)(2,1)S(1)} collective-permute-done((bf16[320,1280]{1,0:T(8,128)(2,1)S(1)}, bf16[320,1280]{1,0:T(8,128)(2,1)S(1)}, u32[]{:S(2)}, u32[]{:S(2)}) %collective-permute-start.7) | collective-permute-done | bytes 819232 | tf_op jit(solution)/shard_map/ppermute | solution.py:308
  30.9 12.6 %collective-permute-done.1.refs_1_ = bf16[320,1280]{1,0:T(8,128)(2,1)S(1)} collective-permute-done((bf16[320,1280]{1,0:T(8,128)(2,1)}, bf16[320,1280]{1,0:T(8,128)(2,1)S(1)}, u32[]{:S(2)}, u32[]{:S(2)}) %collective-permute-start.1) | collective-permute-done | bytes 819232 | tf_op jit(solution)/shard_map/ppermute | solution.py:308
  43.5 2.0 collective-permute-done.refs_0_
  48.4 14.6 %collective-permute-done.8.refs_0_ = bf16[320,1280]{1,0:T(8,128)(2,1)S(1)} collective-permute-done((bf16[320,1280]{1,0:T(8,128)(2,1)}, bf16[320,1280]{1,0:T(8,128)(2,1)S(1)}, u32[]{:S(2)}, u32[]{:S(2)}) %collective-permute-start.8) | collective-permute-done | bytes 819232 | tf_op jit(solution)/shard_map/ppermute | solution.py:307
  64.1 1.9 collective-permute-start.11
  66.1 14.6 %collective-permute-done.2.refs_0_ = bf16[320,1280]{1,0:T(8,128)(2,1)S(1)} collective-permute-done((bf16[320,1280]{1,0:T(8,128)(2,1)}, bf16[320,1280]{1,0:T(8,128)(2,1)S(1)}, u32[]{:S(2)}, u32[]{:S(2)}) %collective-permute-start.2) | collective-permute-done | bytes 819232 | tf_op jit(solution)/shard_map/ppermute | solution.py:307
  83.5 14.6 %collective-permute-done.10.refs_1_.refs_11_.refs_27_ = bf16[320,1280]{1,0:T(8,128)(2,1)S(1)} collective-permute-done((bf16[320,1280]{1,0:T(8,128)(2,1)}, bf16[320,1280]{1,0:T(8,128)(2,1)S(1)}, u32[]{:S(2)}, u32[]{:S(2)}) %collective-permute-start.10) | collective-permute-done | bytes 819232 | tf_op jit(solution)/shard_map/ppermute | solution.py:307
  101.6 12.8 %collective-permute-done.4.refs_0_ = bf16[320,1280]{1,0:T(8,128)(2,1)} collective-permute-done((bf16[320,1280]{1,0:T(8,128)(2,1)}, bf16[320,1280]{1,0:T(8,128)(2,1)}, u32[]{:S(2)}, u32[]{:S(2)}) %collective-permute-start.4) | collective-permute-done | bytes 819232 | tf_op jit(solution)/shard_map/ppermute | solution.py:307
  119.5 11.9 %collective-permute-done.15.refs_15_.refs_31_ = bf16[320,1280]{1,0:T(8,128)(2,1)} collective-permute-done((bf16[320,1280]{1,0:T(8,128)(2,1)}, bf16[320,1280]{1,0:T(8,128)(2,1)}, u32[]{:S(2)}, u32[]{:S(2)}) %collective-permute-start.15) | collective-permute-done | bytes 819232 | tf_op jit(solution)/shard_map/ppermute | solution.py:313
  131.4 2.1 collective-permute-start.16
  134.1 2.6 collective-permute-done.14.refs_14_.refs_30_
  136.8 13.0 %shard_map.47 = (bf16[640,768]{1,0:T(8,128)(2,1)}, bf16[640,768]{1,0:T(8,128)(2,1)}, bf16[640,512]{1,0:T(8,128)(2,1)S(1)}, bf16[640,512]{1,0:T(8,128)(2,1)S(1)}) custom-call(s32[8]{0:T(128)S(1)} %dynamic-slice_bitcast_fusion.source_ref, s32[5]{0:T(128)S(1)} %copy-done.17, s32[2]{0:T(128)S(1)} %pad_add_fusion.place_ref, ...), custom_call_target="tpu_custom_call" | custom-call | bytes 1024 | tf_op jit(solution)/shard_map/pallas_call | solution.py:245
  154.4 7.7 %collective-permute-done.17.refs_1_ = bf16[320,1152]{1,0:T(8,128)(2,1)} collective-permute-done((bf16[320,1152]{1,0:T(8,128)(2,1)}, bf16[320,1152]{1,0:T(8,128)(2,1)}, u32[]{:S(2)}, u32[]{:S(2)}) %collective-permute-start.17) | collective-permute-done | bytes 737312 | tf_op jit(solution)/shard_map/ppermute | solution.py:308
  163.8 4.5 %collective-permute-done.16.refs_0_ = bf16[320,1152]{1,0:T(8,128)(2,1)} collective-permute-done((bf16[320,1152]{1,0:T(8,128)(2,1)}, bf16[320,1152]{1,0:T(8,128)(2,1)}, u32[]{:S(2)}, u32[]{:S(2)}) %collective-permute-start.16) | collective-permute-done | bytes 737312 | tf_op jit(solution)/shard_map/ppermute | solution.py:307
  170.4 2.3 add_convert_fusion.3.refs_3_
  172.7 11.5 %collective-permute-done.18.refs_0_ = bf16[320,1152]{1,0:T(8,128)(2,1)} collective-permute-done((bf16[320,1152]{1,0:T(8,128)(2,1)}, bf16[320,1152]{1,0:T(8,128)(2,1)}, u32[]{:S(2)}, u32[]{:S(2)}) %collective-permute-start.18) | collective-permute-done | bytes 737312 | tf_op jit(solution)/shard_map/ppermute | solution.py:307
  187.0 12.9 %collective-permute-done.20.refs_0_ = bf16[320,1152]{1,0:T(8,128)(2,1)} collective-permute-done((bf16[320,1152]{1,0:T(8,128)(2,1)}, bf16[320,1152]{1,0:T(8,128)(2,1)}, u32[]{:S(2)}, u32[]{:S(2)}) %collective-permute-start.20) | collective-permute-done | bytes 737312 | tf_op jit(solution)/shard_map/ppermute | solution.py:307
  203.6 2.7 add_convert_fusion.1.refs_2_
  207.7 8.0 %collective-permute-done.22.refs_0_ = bf16[320,1152]{1,0:T(8,128)(2,1)} collective-permute-done((bf16[320,1152]{1,0:T(8,128)(2,1)}, bf16[320,1152]{1,0:T(8,128)(2,1)}, u32[]{:S(2)}, u32[]{:S(2)}) %collective-permute-start.22) | collective-permute-done | bytes 737312 | tf_op jit(solution)/shard_map/ppermute | solution.py:307
  215.8 3.9 %collective-permute-done.23.refs_1_.refs_12_ = bf16[320,1152]{1,0:T(8,128)(2,1)} collective-permute-done((bf16[320,1152]{1,0:T(8,128)(2,1)}, bf16[320,1152]{1,0:T(8,128)(2,1)}, u32[]{:S(2)}, u32[]{:S(2)}) %collective-permute-start.23) | collective-permute-done | bytes 737312 | tf_op jit(solution)/shard_map/ppermute | solution.py:308
  221.1 10.5 %collective-permute-done.26.refs_1_.refs_11_ = bf16[320,1152]{1,0:T(8,128)(2,1)} collective-permute-done((bf16[320,1152]{1,0:T(8,128)(2,1)}, bf16[320,1152]{1,0:T(8,128)(2,1)}, u32[]{:S(2)}, u32[]{:S(2)}) %collective-permute-start.26) | collective-permute-done | bytes 737312 | tf_op jit(solution)/shard_map/ppermute | solution.py:307
  233.1 14.0 %shard_map.58 = (bf16[640,1280]{1,0:T(8,128)(2,1)}, bf16[640,1280]{1,0:T(8,128)(2,1)}) custom-call(s32[8]{0:T(128)S(1)} %dynamic-slice_bitcast_fusion.source_ref, s32[5]{0:T(128)S(1)} %copy-done.17, s32[2]{0:T(128)S(1)} %pad_add_fusion.place_ref, bf16[320,1280]{1,0:T(8,128)(2,1)} %get-tuple-element.40.refs_0_.refs_16_, ...), custom_call_target="tpu_custom_call" | custom-call | bytes 1024 | tf_op jit(solution)/shard_map/pallas_call | solution.py:245
  248.5 8.7 %shard_map.59 = (bf16[640,768]{1,0:T(8,128)(2,1)}, bf16[640,768]{1,0:T(8,128)(2,1)}) custom-call(s32[8]{0:T(128)S(1)} %dynamic-slice_bitcast_fusion.source_ref, s32[5]{0:T(128)S(1)} %copy-done.17, s32[2]{0:T(128)S(1)} %pad_add_fusion.place_ref, bf16[320,1152]{1,0:T(8,128)(2,1)S(1)} %copy-done.10, bf16[320,1152]{1,0:T(8,128)(2,1)S(1)} %copy-done.8, ...), custom_call_target="tpu_custom_call" | custom-call | bytes 1024 | tf_op jit(solution)/shard_map/pallas_call | solution.py:245
  257.8 2.9 collective-permute-done.32
  263.2 11.8 %shard_map.60 = (bf16[640,256]{1,0:T(8,128)(2,1)S(1)}, bf16[640,256]{1,0:T(8,128)(2,1)S(1)}, bf16[640,512]{1,0:T(8,128)(2,1)S(1)}, bf16[640,512]{1,0:T(8,128)(2,...) custom-call(s32[8]{0:T(128)S(1)} %dynamic-slice_bitcast_fusion.source_ref, s32[5]{0:T(128)S(1)} %copy-done.17, ...), custom_call_target="tpu_custom_call" | custom-call | bytes 1024 | tf_op jit(solution)/shard_map/pallas_call | solution.py:245
  278.4 7.5 %shard_map.61.refs_1_.refs_4_ = bf16[640,1280]{1,0:T(8,128)(2,1)} custom-call(s32[8]{0:T(128)S(1)} %dynamic-slice_bitcast_fusion.source_ref, s32[5]{0:T(128)S(1)} %copy-done.17, s32[2]{0:T(128)S(1)} %pad_add_fusion.place_ref, bf16[320,1152]{1,0:T(8,128)(2,1)S(1)} %copy-done.10, bf16[320,1152]{1,0:T(8,128)(2,1)S(1)} %copy-done.8, ...), custom_call_target="tpu_custom_call" | custom-call | bytes 1024 | tf_op jit(solution)/shard_map/pallas_call | solution.py:245
  291.1 5.3 %shard_map.64.refs_1_.before_ref = f32[640,1280]{1,0:T(8,128)} custom-call(bf16[640,768]{1,0:T(8,128)(2,1)} %shard_map.57.refs_32_.refs_0_, bf16[640,512]{1,0:T(8,128)(2,1)} %shard_map.55.refs_4_.refs_33_.refs_1_, bf16[640,1280]{1,0:T(8,128)(2,1)S(1)} %copy-done.13, bf16[640,1280]{1,0:T(8,128)(2,1)} %collective-permute-done.36.refs_3_, ...), custom_call_target="tpu_custom_call" | custom-call | bytes 1024 | tf_op jit(solution)/shard_map/pallas_call | solution.py:116
  296.4 3.7 %collective-permute-done.35.refs_0_ = bf16[640,512]{1,0:T(8,128)(2,1)} collective-permute-done((bf16[640,512]{1,0:T(8,128)(2,1)S(1)}, bf16[640,512]{1,0:T(8,128)(2,1)}, u32[]{:S(2)}, u32[]{:S(2)}) %collective-permute-start.35) | collective-permute-done | bytes 655392 | tf_op jit(solution)/shard_map/ppermute | solution.py:340
  300.1 2.4 shard_map.66
  (136 shorter events, 56.2 us)
Async XLA Ops:
  3.8 22.1 %collective-permute-start.7 = (bf16[320,1280]{1,0:T(8,128)(2,1)S(1)}, bf16[320,1280]{1,0:T(8,128)(2,1)S(1)}, u32[]{:S(2)}, u32[]{:S(2)}) collective-permute-start(bf16[320,1280]{1,0:T(8,128)(2,1)S(1)} %get-tuple-element.46.refs_1_.refs_17_), channel_id=1, source_target_pairs={{2,0},{4,2},{6,4},{7,6},{5,7},{3,5},{1,3},{0,1},{10,8},{12,10},{14... | collective-permute-start | bytes 2457608 | tf_op jit(solution)/shard_map/ppermute | solution.py:308
  6.8 21.2 %collective-permute-start.6 = (bf16[320,1280]{1,0:T(8,128)(2,1)S(1)}, bf16[320,1280]{1,0:T(8,128)(2,1)S(1)}, u32[]{:S(2)}, u32[]{:S(2)}) collective-permute-start(bf16[320,1280]{1,0:T(8,128)(2,1)S(1)} %get-tuple-element.46.refs_1_.refs_17_), channel_id=1, source_target_pairs={{0,2},{2,4},{4,6},{6,7},{7,5},{5,3},{3,1},{1,0},{8,10},{10,12},{12... | collective-permute-start | bytes 2457608 | tf_op jit(solution)/shard_map/ppermute | solution.py:307
  12.4 31.1 %collective-permute-start.1 = (bf16[320,1280]{1,0:T(8,128)(2,1)}, bf16[320,1280]{1,0:T(8,128)(2,1)S(1)}, u32[]{:S(2)}, u32[]{:S(2)}) collective-permute-start(bf16[320,1280]{1,0:T(8,128)(2,1)} %get-tuple-element.40.refs_0_.refs_16_), channel_id=1, source_target_pairs={{2,0},{4,2},{6,4},{7,6},{5,7},{3,5},{1,3},{0,1},{10,8},{12,10},{14... | collective-permute-start | bytes 2457608 | tf_op jit(solution)/shard_map/ppermute | solution.py:308
  14.3 31.2 %collective-permute-start = (bf16[320,1280]{1,0:T(8,128)(2,1)}, bf16[320,1280]{1,0:T(8,128)(2,1)S(1)}, u32[]{:S(2)}, u32[]{:S(2)}) collective-permute-start(bf16[320,1280]{1,0:T(8,128)(2,1)} %get-tuple-element.40.refs_0_.refs_16_), channel_id=1, source_target_pairs={{0,2},{2,4},{4,6},{6,7},{7,5},{5,3},{3,1},{1,0},{8,10},{10,12},{12... | collective-permute-start | bytes 2457608 | tf_op jit(solution)/shard_map/ppermute | solution.py:307
  28.9 34.2 %collective-permute-start.8 = (bf16[320,1280]{1,0:T(8,128)(2,1)}, bf16[320,1280]{1,0:T(8,128)(2,1)S(1)}, u32[]{:S(2)}, u32[]{:S(2)}) collective-permute-start(bf16[320,1280]{1,0:T(8,128)(2,1)} %get-tuple-element.47.refs_3_.refs_19_), channel_id=1, source_target_pairs={{0,2},{2,4},{4,6},{6,7},{7,5},{5,3},{3,1},{1,0},{8,10},{10,12},{12... | collective-permute-start | bytes 2457608 | tf_op jit(solution)/shard_map/ppermute | solution.py:307
  29.8 33.3 %collective-permute-start.9 = (bf16[320,1280]{1,0:T(8,128)(2,1)}, bf16[320,1280]{1,0:T(8,128)(2,1)}, u32[]{:S(2)}, u32[]{:S(2)}) collective-permute-start(bf16[320,1280]{1,0:T(8,128)(2,1)} %get-tuple-element.48.refs_5_.refs_21_), channel_id=1, source_target_pairs={{2,0},{4,2},{6,4},{7,6},{5,7},{3,5},{1,3},{0,1},{10,8},{12,10},{14... | collective-permute-start | bytes 2457608 | tf_op jit(solution)/shard_map/ppermute | solution.py:308
  46.4 34.2 %collective-permute-start.2 = (bf16[320,1280]{1,0:T(8,128)(2,1)}, bf16[320,1280]{1,0:T(8,128)(2,1)S(1)}, u32[]{:S(2)}, u32[]{:S(2)}) collective-permute-start(bf16[320,1280]{1,0:T(8,128)(2,1)} %get-tuple-element.41.refs_2_.refs_18_), channel_id=1, source_target_pairs={{0,2},{2,4},{4,6},{6,7},{7,5},{5,3},{3,1},{1,0},{8,10},{10,12},{12... | collective-permute-start | bytes 2457608 | tf_op jit(solution)/shard_map/ppermute | solution.py:307
  47.4 33.3 %collective-permute-start.3 = (bf16[320,1280]{1,0:T(8,128)(2,1)}, bf16[320,1280]{1,0:T(8,128)(2,1)}, u32[]{:S(2)}, u32[]{:S(2)}) collective-permute-start(bf16[320,1280]{1,0:T(8,128)(2,1)} %get-tuple-element.42.refs_4_.refs_20_), channel_id=1, source_target_pairs={{2,0},{4,2},{6,4},{7,6},{5,7},{3,5},{1,3},{0,1},{10,8},{12,10},{14... | collective-permute-start | bytes 2457608 | tf_op jit(solution)/shard_map/ppermute | solution.py:308
  64.0 34.1 %collective-permute-start.10 = (bf16[320,1280]{1,0:T(8,128)(2,1)}, bf16[320,1280]{1,0:T(8,128)(2,1)S(1)}, u32[]{:S(2)}, u32[]{:S(2)}) collective-permute-start(bf16[320,1280]{1,0:T(8,128)(2,1)} %get-tuple-element.49.refs_7_.refs_23_), channel_id=1, source_target_pairs={{0,2},{2,4},{4,6},{6,7},{7,5},{5,3},{3,1},{1,0},{8,10},{10,12},{12... | collective-permute-start | bytes 2457608 | tf_op jit(solution)/shard_map/ppermute | solution.py:307
  64.1 34.1 %collective-permute-start.11 = (bf16[320,1280]{1,0:T(8,128)(2,1)}, bf16[320,1280]{1,0:T(8,128)(2,1)S(1)}, u32[]{:S(2)}, u32[]{:S(2)}) collective-permute-start(bf16[320,1280]{1,0:T(8,128)(2,1)} %get-tuple-element.50.refs_9_.refs_25_), channel_id=1, source_target_pairs={{2,0},{4,2},{6,4},{7,6},{5,7},{3,5},{1,3},{0,1},{10,8},{12,10},{14... | collective-permute-start | bytes 2457608 | tf_op jit(solution)/shard_map/ppermute | solution.py:308
  81.5 32.9 %collective-permute-start.4 = (bf16[320,1280]{1,0:T(8,128)(2,1)}, bf16[320,1280]{1,0:T(8,128)(2,1)}, u32[]{:S(2)}, u32[]{:S(2)}) collective-permute-start(bf16[320,1280]{1,0:T(8,128)(2,1)} %get-tuple-element.43.refs_6_.refs_22_), channel_id=1, source_target_pairs={{0,2},{2,4},{4,6},{6,7},{7,5},{5,3},{3,1},{1,0},{8,10},{10,12},{12... | collective-permute-start | bytes 2457608 | tf_op jit(solution)/shard_map/ppermute | solution.py:307
  81.6 32.8 %collective-permute-start.5 = (bf16[320,1280]{1,0:T(8,128)(2,1)}, bf16[320,1280]{1,0:T(8,128)(2,1)S(1)}, u32[]{:S(2)}, u32[]{:S(2)}) collective-permute-start(bf16[320,1280]{1,0:T(8,128)(2,1)} %get-tuple-element.44.refs_8_.refs_24_), channel_id=1, source_target_pairs={{2,0},{4,2},{6,4},{7,6},{5,7},{3,5},{1,3},{0,1},{10,8},{12,10},{14... | collective-permute-start | bytes 2457608 | tf_op jit(solution)/shard_map/ppermute | solution.py:308
  100.0 31.3 %collective-permute-start.15 = (bf16[320,1280]{1,0:T(8,128)(2,1)}, bf16[320,1280]{1,0:T(8,128)(2,1)}, u32[]{:S(2)}, u32[]{:S(2)}) collective-permute-start(bf16[320,1280]{1,0:T(8,128)(2,1)} %shard_map.45.refs_2_.refs_13_.refs_29_), channel_id=1, source_target_pairs={{2,0},{4,2},{6,4},{7,6},{5,7},{3,5},{1,3},{0,1},{10,8},{12,10},{14... | collective-permute-start | bytes 2457608 | tf_op jit(solution)/shard_map/ppermute | solution.py:313
  115.3 21.5 %collective-permute-start.14 = (bf16[320,1280]{1,0:T(8,128)(2,1)}, bf16[320,1280]{1,0:T(8,128)(2,1)}, u32[]{:S(2)}, u32[]{:S(2)}) collective-permute-start(bf16[320,1280]{1,0:T(8,128)(2,1)} %shard_map.40.refs_1_.refs_10_.refs_26_), channel_id=1, source_target_pairs={{0,2},{2,4},{4,6},{6,7},{7,5},{5,3},{3,1},{1,0},{8,10},{10,12},{12... | collective-permute-start | bytes 2457608 | tf_op jit(solution)/shard_map/ppermute | solution.py:313
  116.6 34.8 %collective-permute-start.13 = (bf16[320,1152]{1,0:T(8,128)(2,1)}, bf16[320,1152]{1,0:T(8,128)(2,1)}, u32[]{:S(2)}, u32[]{:S(2)}) collective-permute-start(bf16[320,1152]{1,0:T(8,128)(2,1)} %shard_map.41.refs_0_), channel_id=1, source_target_pairs={{2,0},{4,2},{6,4},{7,6},{5,7},{3,5},{1,3},{0,1},{10,8},{12,10},{14... | collective-permute-start | bytes 2211848 | tf_op jit(solution)/shard_map/ppermute | solution.py:308
  117.4 35.2 %collective-permute-start.12 = (bf16[320,1152]{1,0:T(8,128)(2,1)}, bf16[320,1152]{1,0:T(8,128)(2,1)}, u32[]{:S(2)}, u32[]{:S(2)}) collective-permute-start(bf16[320,1152]{1,0:T(8,128)(2,1)} %shard_map.41.refs_0_), channel_id=1, source_target_pairs={{0,2},{2,4},{4,6},{6,7},{7,5},{5,3},{3,1},{1,0},{8,10},{10,12},{12... | collective-permute-start | bytes 2211848 | tf_op jit(solution)/shard_map/ppermute | solution.py:307
  118.8 43.3 %collective-permute-start.17 = (bf16[320,1152]{1,0:T(8,128)(2,1)}, bf16[320,1152]{1,0:T(8,128)(2,1)}, u32[]{:S(2)}, u32[]{:S(2)}) collective-permute-start(bf16[320,1152]{1,0:T(8,128)(2,1)} %shard_map.46.refs_1_), channel_id=1, source_target_pairs={{2,0},{4,2},{6,4},{7,6},{5,7},{3,5},{1,3},{0,1},{10,8},{12,10},{14... | collective-permute-start | bytes 2211848 | tf_op jit(solution)/shard_map/ppermute | solution.py:308
  131.4 37.0 %collective-permute-start.16 = (bf16[320,1152]{1,0:T(8,128)(2,1)}, bf16[320,1152]{1,0:T(8,128)(2,1)}, u32[]{:S(2)}, u32[]{:S(2)}) collective-permute-start(bf16[320,1152]{1,0:T(8,128)(2,1)} %shard_map.46.refs_1_), channel_id=1, source_target_pairs={{0,2},{2,4},{4,6},{6,7},{7,5},{5,3},{3,1},{1,0},{8,10},{10,12},{12... | collective-permute-start | bytes 2211848 | tf_op jit(solution)/shard_map/ppermute | solution.py:307
  152.6 49.4 %collective-permute-start.24 = (bf16[640,768]{1,0:T(8,128)(2,1)}, bf16[640,768]{1,0:T(8,128)(2,1)}, u32[]{:S(2)}, u32[]{:S(2)}) collective-permute-start(bf16[640,768]{1,0:T(8,128)(2,1)} %shard_map.52), channel_id=1, source_target_pairs={{0,8},{8,0},{16,24},{24,16},{1,9},{9,1},{17,25},{25,17},{2,10},{10... | collective-permute-start | bytes 2949128 | tf_op jit(solution)/shard_map/ppermute | solution.py:337
  153.1 31.1 %collective-permute-start.18 = (bf16[320,1152]{1,0:T(8,128)(2,1)}, bf16[320,1152]{1,0:T(8,128)(2,1)}, u32[]{:S(2)}, u32[]{:S(2)}) collective-permute-start(bf16[320,1152]{1,0:T(8,128)(2,1)} %get-tuple-element.52.refs_1_.refs_2_), channel_id=1, source_target_pairs={{0,2},{2,4},{4,6},{6,7},{7,5},{5,3},{3,1},{1,0},{8,10},{10,12},{12... | collective-permute-start | bytes 2211848 | tf_op jit(solution)/shard_map/ppermute | solution.py:307
  162.1 23.5 %collective-permute-start.19 = (bf16[320,1152]{1,0:T(8,128)(2,1)}, bf16[320,1152]{1,0:T(8,128)(2,1)}, u32[]{:S(2)}, u32[]{:S(2)}) collective-permute-start(bf16[320,1152]{1,0:T(8,128)(2,1)} %get-tuple-element.54.refs_2_.refs_4_), channel_id=1, source_target_pairs={{2,0},{4,2},{6,4},{7,6},{5,7},{3,5},{1,3},{0,1},{10,8},{12,10},{14... | collective-permute-start | bytes 2211848 | tf_op jit(solution)/shard_map/ppermute | solution.py:308
  168.4 31.6 %collective-permute-start.20 = (bf16[320,1152]{1,0:T(8,128)(2,1)}, bf16[320,1152]{1,0:T(8,128)(2,1)}, u32[]{:S(2)}, u32[]{:S(2)}) collective-permute-start(bf16[320,1152]{1,0:T(8,128)(2,1)} %get-tuple-element.53.refs_3_), channel_id=1, source_target_pairs={{0,2},{2,4},{4,6},{6,7},{7,5},{5,3},{3,1},{1,0},{8,10},{10,12},{12... | collective-permute-start | bytes 2211848 | tf_op jit(solution)/shard_map/ppermute | solution.py:307
  169.7 31.8 %collective-permute-start.21 = (bf16[320,1152]{1,0:T(8,128)(2,1)}, bf16[320,1152]{1,0:T(8,128)(2,1)}, u32[]{:S(2)}, u32[]{:S(2)}) collective-permute-start(bf16[320,1152]{1,0:T(8,128)(2,1)} %get-tuple-element.55.refs_5_), channel_id=1, source_target_pairs={{2,0},{4,2},{6,4},{7,6},{5,7},{3,5},{1,3},{0,1},{10,8},{12,10},{14... | collective-permute-start | bytes 2211848 | tf_op jit(solution)/shard_map/ppermute | solution.py:308
  184.2 22.1 %collective-permute-start.28 = (bf16[640,512]{1,0:T(8,128)(2,1)}, bf16[640,512]{1,0:T(8,128)(2,1)}, u32[]{:S(2)}, u32[]{:S(2)}) collective-permute-start(bf16[640,512]{1,0:T(8,128)(2,1)} %add_convert_fusion.3.refs_3_), channel_id=1, source_target_pairs={{0,16},{8,24},{16,0},{24,8},{1,17},{9,25},{17,1},{25,9},{2,18},{10... | collective-permute-start | bytes 1966088 | tf_op jit(solution)/shard_map/ppermute | solution.py:340
  185.6 30.1 %collective-permute-start.22 = (bf16[320,1152]{1,0:T(8,128)(2,1)}, bf16[320,1152]{1,0:T(8,128)(2,1)}, u32[]{:S(2)}, u32[]{:S(2)}) collective-permute-start(bf16[320,1152]{1,0:T(8,128)(2,1)} %get-tuple-element.56.refs_6_), channel_id=1, source_target_pairs={{0,2},{2,4},{4,6},{6,7},{7,5},{5,3},{3,1},{1,0},{8,10},{10,12},{12... | collective-permute-start | bytes 2211848 | tf_op jit(solution)/shard_map/ppermute | solution.py:307
  201.5 30.0 %collective-permute-start.26 = (bf16[320,1152]{1,0:T(8,128)(2,1)}, bf16[320,1152]{1,0:T(8,128)(2,1)}, u32[]{:S(2)}, u32[]{:S(2)}) collective-permute-start(bf16[320,1152]{1,0:T(8,128)(2,1)} %get-tuple-element.57.refs_7_), channel_id=1, source_target_pairs={{0,2},{2,4},{4,6},{6,7},{7,5},{5,3},{3,1},{1,0},{8,10},{10,12},{12... | collective-permute-start | bytes 2211848 | tf_op jit(solution)/shard_map/ppermute | solution.py:307
  202.0 29.6 %collective-permute-start.27 = (bf16[320,1152]{1,0:T(8,128)(2,1)}, bf16[320,1152]{1,0:T(8,128)(2,1)}, u32[]{:S(2)}, u32[]{:S(2)}) collective-permute-start(bf16[320,1152]{1,0:T(8,128)(2,1)} %get-tuple-element.59.refs_9_), channel_id=1, source_target_pairs={{2,0},{4,2},{6,4},{7,6},{5,7},{3,5},{1,3},{0,1},{10,8},{12,10},{14... | collective-permute-start | bytes 2211848 | tf_op jit(solution)/shard_map/ppermute | solution.py:308
  206.2 41.0 %collective-permute-start.31 = (bf16[640,768]{1,0:T(8,128)(2,1)}, bf16[640,768]{1,0:T(8,128)(2,1)}, u32[]{:S(2)}, u32[]{:S(2)}) collective-permute-start(bf16[640,768]{1,0:T(8,128)(2,1)} %add_convert_fusion.1.refs_2_), channel_id=1, source_target_pairs={{0,16},{8,24},{16,0},{24,8},{1,17},{9,25},{17,1},{25,9},{2,18},{10... | collective-permute-start | bytes 2949128 | tf_op jit(solution)/shard_map/ppermute | solution.py:340
  219.7 27.5 %collective-permute-start.29 = (bf16[320,1152]{1,0:T(8,128)(2,1)}, bf16[320,1152]{1,0:T(8,128)(2,1)}, u32[]{:S(2)}, u32[]{:S(2)}) collective-permute-start(bf16[320,1152]{1,0:T(8,128)(2,1)} %shard_map.54.refs_32_.refs_10_), channel_id=1, source_target_pairs={{0,2},{2,4},{4,6},{6,7},{7,5},{5,3},{3,1},{1,0},{8,10},{10,12},{12... | collective-permute-start | bytes 2211848 | tf_op jit(solution)/shard_map/ppermute | solution.py:313
  257.3 30.5 %collective-permute-start.36 = (bf16[640,1280]{1,0:T(8,128)(2,1)}, bf16[640,1280]{1,0:T(8,128)(2,1)}, u32[]{:S(2)}, u32[]{:S(2)}) collective-permute-start(bf16[640,1280]{1,0:T(8,128)(2,1)} %get-tuple-element.69), channel_id=1, source_target_pairs={{0,8},{8,0},{16,24},{24,16},{1,9},{9,1},{17,25},{25,17},{2,10},{10... | collective-permute-start | bytes 4915208 | tf_op jit(solution)/shard_map/ppermute | solution.py:337
  262.1 24.7 %collective-permute-start.37 = (bf16[640,768]{1,0:T(8,128)(2,1)S(1)}, bf16[640,768]{1,0:T(8,128)(2,1)S(1)}, u32[]{:S(2)}, u32[]{:S(2)}) collective-permute-start(bf16[640,768]{1,0:T(8,128)(2,1)S(1)} %add_convert_fusion.refs_32_), channel_id=1, source_target_pairs={{0,16},{8,24},{16,0},{24,8},{1,17},{9,25},{17,1},{25,9},{2,18},{10... | collective-permute-start | bytes 2949128 | tf_op jit(solution)/shard_map/ppermute | solution.py:340
  277.4 22.8 %collective-permute-start.35 = (bf16[640,512]{1,0:T(8,128)(2,1)S(1)}, bf16[640,512]{1,0:T(8,128)(2,1)}, u32[]{:S(2)}, u32[]{:S(2)}) collective-permute-start(bf16[640,512]{1,0:T(8,128)(2,1)S(1)} %add_convert_fusion.2.refs_32_), channel_id=1, source_target_pairs={{0,16},{8,24},{16,0},{24,8},{1,17},{9,25},{17,1},{25,9},{2,18},{10... | collective-permute-start | bytes 1966088 | tf_op jit(solution)/shard_map/ppermute | solution.py:340
  (34 other events, 433.1 us)

commit v15 on v14

--- a/solution.py
+++ b/solution.py
@@ -203,7 +203,7 @@
     own_rows[:, body:] = jnp.where(kept, own_rows[:, body:].astype(jnp.float32), 0.0).astype(jnp.bfloat16)
 
     limit = clip_limit * duration
-    widest = products_a.shape[1]
+    widest = products_a.shape[0]
     tiles = []
     for n, out_ref in enumerate(out_refs):
         columns = out_ref.shape[1]
@@ -214,17 +214,16 @@
         n, k, width, _ = tiles[i]
         if k == 0:
             arrived(n)
-        buffers[i % 2][:, :width] = lax.dot_general(
-            own_rows[...], wanted[n][1][pl.ds(k, width)], (((1,), (1,)), ((), ())), preferred_element_type=jnp.float32
+        buffers[i % 2][:width] = lax.dot_general(
+            wanted[n][1][pl.ds(k, width)], own_rows[...], (((1,), (1,)), ((), ())), preferred_element_type=jnp.float32
         )
 
     def score(i):
         _, k, width, out_ref = tiles[i]
-        step = math.gcd(slab, 64)
-        for r in range(0, slab, step):
-            products = jnp.clip(buffers[i % 2][r : r + step, :width], -limit, limit)
+        for r in range(0, width, LANES):
+            products = jnp.clip(buffers[i % 2][r : r + LANES], -limit, limit)
             fisher = jnp.log(duration + products) - jnp.log(duration - products)
-            out_ref[r : r + step, pl.ds(k, width)] = fisher.astype(jnp.bfloat16)
+            out_ref[:, pl.ds(k + r, LANES)] = fisher.T.astype(jnp.bfloat16)
 
     multiply(0)
     for i in range(1, len(tiles)):
@@ -260,8 +259,8 @@
         scratch_shapes=[pltpu.VMEM((columns, padded), jnp.bfloat16) for columns in sizes]
         + [
             pltpu.VMEM((slab, padded), jnp.bfloat16),
-            pltpu.VMEM((slab, widest), jnp.float32),
-            pltpu.VMEM((slab, widest), jnp.float32),
+            pltpu.VMEM((widest, slab), jnp.float32),
+            pltpu.VMEM((widest, slab), jnp.float32),
             pltpu.SMEM((block_start.shape[0],), jnp.int32),
             pltpu.SemaphoreType.DMA((1 + len(targets),)),
         ],

time: 304 us -> 304 us (level)
  waiting for transfers between devices: 169 us -> 164 us
  Pallas kernels: 71.1 us -> 74.8 us
    pallas_call x5, Pallas kernels: 55 us -> 58.8 us  [scores(): pl.pallas_call(functools.partial(scores_kernel, subject=subject, targets=...]
  transfers between devices with their start and end apart: 41 -> 41, of which waited for: 24 -> 22; matrix products, arithmetic and copies ran while one was open for 2% -> 2% of each run, Pallas kernels for 19% -> 20%
where the time goes in v15:
time: 304 us; the launch traced here: 303 us
  waiting for transfers between devices  164 us (54%)
  Pallas kernels  74.8 us (25%)
  starting transfers between devices  42.7 us (14%)
  local copies, waits for them, and re-layouts  14.3 us (5%)
  other arithmetic  6.64 us (2%)
    ppermute x12, waiting for transfers between devices, gather(): got[-2][half] = lax.ppermute(ahead[half], SLABS, onward)  107 us
    pallas_call x5, Pallas kernels, scores(): pl.pallas_call(functools.partial(scores_kernel, subject=subject, targets=...  58.8 us
    ppermute x12, waiting for transfers between devices, gather(): got[-1][half] = lax.ppermute(behind[half], SLABS, backward)  34.8 us
    ppermute x12, starting transfers between devices, gather(): got[-1][half] = lax.ppermute(behind[half], SLABS, backward)  17.8 us
    ppermute x4, waiting for transfers between devices, gather(): last.append(lax.ppermute(got[side][half], SLABS, way))  14.6 us
    unnamed x50, local copies, waits for them, and re-layouts  13.6 us
    ppermute x12, starting transfers between devices, gather(): got[-2][half] = lax.ppermute(ahead[half], SLABS, onward)  10.5 us
    pallas_call x2, Pallas kernels, normalize(): pl.pallas_call(functools.partial(normalize_kernel, begin=low, lead=begin...  8.32 us
  transfers between devices with their start and end apart: 41, of which 22 were waited for; matrix products, arithmetic and copies ran while one was open for 2% of the time, Pallas kernels for 20%

profile of v15, /device:TPU:0, one launch (start us, length us, event | category | flops | bytes accessed | tf_op | source)
XLA Modules:
  0.0 303.3 jit_solution(11041579900660140839)
XLA Ops:
  0.0 3.7 %shard_map.42 = (bf16[320,1280]{1,0:T(8,128)(2,1)S(1)}, bf16[320,1152]{1,0:T(8,128)(2,1)S(1)}) custom-call(f32[2,1200,640]{2,1,0:T(8,128)} %bitcast.5), custom_call_target="tpu_custom_call" | custom-call | bytes 1024 | tf_op jit(solution)/shard_map/pallas_call | solution.py:76
  3.8 3.0 collective-permute-start.7
  6.9 4.6 %shard_map.37 = (bf16[320,1280]{1,0:T(8,128)(2,1)}, bf16[320,1152]{1,0:T(8,128)(2,1)S(1)}) custom-call(f32[2,1200,640]{2,1,0:T(8,128)} %bitcast.6), custom_call_target="tpu_custom_call" | custom-call | bytes 1024 | tf_op jit(solution)/shard_map/pallas_call | solution.py:76
  14.4 11.5 %collective-permute-done.7.refs_1_ = bf16[320,1280]{1,0:T(8,128)(2,1)S(1)} collective-permute-done((bf16[320,1280]{1,0:T(8,128)(2,1)S(1)}, bf16[320,1280]{1,0:T(8,128)(2,1)S(1)}, u32[]{:S(2)}, u32[]{:S(2)}) %collective-permute-start.7) | collective-permute-done | bytes 819232 | tf_op jit(solution)/shard_map/ppermute | solution.py:307
  30.9 12.6 %collective-permute-done.1.refs_1_ = bf16[320,1280]{1,0:T(8,128)(2,1)S(1)} collective-permute-done((bf16[320,1280]{1,0:T(8,128)(2,1)}, bf16[320,1280]{1,0:T(8,128)(2,1)S(1)}, u32[]{:S(2)}, u32[]{:S(2)}) %collective-permute-start.1) | collective-permute-done | bytes 819232 | tf_op jit(solution)/shard_map/ppermute | solution.py:307
  43.5 2.0 collective-permute-done.refs_0_
  48.4 14.6 %collective-permute-done.8.refs_0_ = bf16[320,1280]{1,0:T(8,128)(2,1)S(1)} collective-permute-done((bf16[320,1280]{1,0:T(8,128)(2,1)}, bf16[320,1280]{1,0:T(8,128)(2,1)S(1)}, u32[]{:S(2)}, u32[]{:S(2)}) %collective-permute-start.8) | collective-permute-done | bytes 819232 | tf_op jit(solution)/shard_map/ppermute | solution.py:306
  66.1 14.6 %collective-permute-done.2.refs_0_ = bf16[320,1280]{1,0:T(8,128)(2,1)S(1)} collective-permute-done((bf16[320,1280]{1,0:T(8,128)(2,1)}, bf16[320,1280]{1,0:T(8,128)(2,1)S(1)}, u32[]{:S(2)}, u32[]{:S(2)}) %collective-permute-start.2) | collective-permute-done | bytes 819232 | tf_op jit(solution)/shard_map/ppermute | solution.py:306
  83.5 14.6 %collective-permute-done.10.refs_1_.refs_11_.refs_27_ = bf16[320,1280]{1,0:T(8,128)(2,1)S(1)} collective-permute-done((bf16[320,1280]{1,0:T(8,128)(2,1)}, bf16[320,1280]{1,0:T(8,128)(2,1)S(1)}, u32[]{:S(2)}, u32[]{:S(2)}) %collective-permute-start.10) | collective-permute-done | bytes 819232 | tf_op jit(solution)/shard_map/ppermute | solution.py:306
  101.6 12.8 %collective-permute-done.4.refs_0_ = bf16[320,1280]{1,0:T(8,128)(2,1)} collective-permute-done((bf16[320,1280]{1,0:T(8,128)(2,1)}, bf16[320,1280]{1,0:T(8,128)(2,1)}, u32[]{:S(2)}, u32[]{:S(2)}) %collective-permute-start.4) | collective-permute-done | bytes 819232 | tf_op jit(solution)/shard_map/ppermute | solution.py:306
  119.5 11.9 %collective-permute-done.15.refs_15_.refs_31_ = bf16[320,1280]{1,0:T(8,128)(2,1)} collective-permute-done((bf16[320,1280]{1,0:T(8,128)(2,1)}, bf16[320,1280]{1,0:T(8,128)(2,1)}, u32[]{:S(2)}, u32[]{:S(2)}) %collective-permute-start.15) | collective-permute-done | bytes 819232 | tf_op jit(solution)/shard_map/ppermute | solution.py:312
  131.4 2.1 collective-permute-start.16
  134.1 2.6 collective-permute-done.14.refs_14_.refs_30_
  136.8 14.7 %shard_map.47 = (bf16[640,768]{1,0:T(8,128)(2,1)}, bf16[640,768]{1,0:T(8,128)(2,1)}, bf16[640,512]{1,0:T(8,128)(2,1)S(1)}, bf16[640,512]{1,0:T(8,128)(2,1)S(1)}) custom-call(s32[8]{0:T(128)S(1)} %dynamic-slice_bitcast_fusion.source_ref, s32[5]{0:T(128)S(1)} %copy-done.17, s32[2]{0:T(128)S(1)} %pad_add_fusion.place_ref, ...), custom_call_target="tpu_custom_call" | custom-call | bytes 1024 | tf_op jit(solution)/shard_map/pallas_call | solution.py:244
  155.4 6.8 %collective-permute-done.17.refs_1_ = bf16[320,1152]{1,0:T(8,128)(2,1)} collective-permute-done((bf16[320,1152]{1,0:T(8,128)(2,1)}, bf16[320,1152]{1,0:T(8,128)(2,1)}, u32[]{:S(2)}, u32[]{:S(2)}) %collective-permute-start.17) | collective-permute-done | bytes 737312 | tf_op jit(solution)/shard_map/ppermute | solution.py:307
  163.8 4.5 %collective-permute-done.16.refs_0_ = bf16[320,1152]{1,0:T(8,128)(2,1)} collective-permute-done((bf16[320,1152]{1,0:T(8,128)(2,1)}, bf16[320,1152]{1,0:T(8,128)(2,1)}, u32[]{:S(2)}, u32[]{:S(2)}) %collective-permute-start.16) | collective-permute-done | bytes 737312 | tf_op jit(solution)/shard_map/ppermute | solution.py:306
  170.4 2.3 add_convert_fusion.3.refs_3_
  172.7 11.5 %collective-permute-done.18.refs_0_ = bf16[320,1152]{1,0:T(8,128)(2,1)} collective-permute-done((bf16[320,1152]{1,0:T(8,128)(2,1)}, bf16[320,1152]{1,0:T(8,128)(2,1)}, u32[]{:S(2)}, u32[]{:S(2)}) %collective-permute-start.18) | collective-permute-done | bytes 737312 | tf_op jit(solution)/shard_map/ppermute | solution.py:306
  187.0 12.9 %collective-permute-done.20.refs_0_ = bf16[320,1152]{1,0:T(8,128)(2,1)} collective-permute-done((bf16[320,1152]{1,0:T(8,128)(2,1)}, bf16[320,1152]{1,0:T(8,128)(2,1)}, u32[]{:S(2)}, u32[]{:S(2)}) %collective-permute-start.20) | collective-permute-done | bytes 737312 | tf_op jit(solution)/shard_map/ppermute | solution.py:306
  203.6 2.7 add_convert_fusion.1.refs_2_
  207.7 8.0 %collective-permute-done.22.refs_0_ = bf16[320,1152]{1,0:T(8,128)(2,1)} collective-permute-done((bf16[320,1152]{1,0:T(8,128)(2,1)}, bf16[320,1152]{1,0:T(8,128)(2,1)}, u32[]{:S(2)}, u32[]{:S(2)}) %collective-permute-start.22) | collective-permute-done | bytes 737312 | tf_op jit(solution)/shard_map/ppermute | solution.py:306
  215.8 3.9 %collective-permute-done.23.refs_1_.refs_12_ = bf16[320,1152]{1,0:T(8,128)(2,1)} collective-permute-done((bf16[320,1152]{1,0:T(8,128)(2,1)}, bf16[320,1152]{1,0:T(8,128)(2,1)}, u32[]{:S(2)}, u32[]{:S(2)}) %collective-permute-start.23) | collective-permute-done | bytes 737312 | tf_op jit(solution)/shard_map/ppermute | solution.py:307
  221.1 10.5 %collective-permute-done.26.refs_1_.refs_11_ = bf16[320,1152]{1,0:T(8,128)(2,1)} collective-permute-done((bf16[320,1152]{1,0:T(8,128)(2,1)}, bf16[320,1152]{1,0:T(8,128)(2,1)}, u32[]{:S(2)}, u32[]{:S(2)}) %collective-permute-start.26) | collective-permute-done | bytes 737312 | tf_op jit(solution)/shard_map/ppermute | solution.py:306
  233.1 13.9 %shard_map.58 = (bf16[640,1280]{1,0:T(8,128)(2,1)}, bf16[640,1280]{1,0:T(8,128)(2,1)}) custom-call(s32[8]{0:T(128)S(1)} %dynamic-slice_bitcast_fusion.source_ref, s32[5]{0:T(128)S(1)} %copy-done.17, s32[2]{0:T(128)S(1)} %pad_add_fusion.place_ref, bf16[320,1280]{1,0:T(8,128)(2,1)} %get-tuple-element.40.refs_0_.refs_16_, ...), custom_call_target="tpu_custom_call" | custom-call | bytes 1024 | tf_op jit(solution)/shard_map/pallas_call | solution.py:244
  248.4 9.2 %shard_map.59 = (bf16[640,768]{1,0:T(8,128)(2,1)}, bf16[640,768]{1,0:T(8,128)(2,1)}) custom-call(s32[8]{0:T(128)S(1)} %dynamic-slice_bitcast_fusion.source_ref, s32[5]{0:T(128)S(1)} %copy-done.17, s32[2]{0:T(128)S(1)} %pad_add_fusion.place_ref, bf16[320,1152]{1,0:T(8,128)(2,1)S(1)} %copy-done.10, bf16[320,1152]{1,0:T(8,128)(2,1)S(1)} %copy-done.8, ...), custom_call_target="tpu_custom_call" | custom-call | bytes 1024 | tf_op jit(solution)/shard_map/pallas_call | solution.py:244
  258.2 2.9 collective-permute-done.32
  262.5 2.2 collective-permute-start.37
  264.7 12.5 %shard_map.60 = (bf16[640,256]{1,0:T(8,128)(2,1)S(1)}, bf16[640,256]{1,0:T(8,128)(2,1)S(1)}, bf16[640,512]{1,0:T(8,128)(2,1)S(1)}, bf16[640,512]{1,0:T(8,128)(2,...) custom-call(s32[8]{0:T(128)S(1)} %dynamic-slice_bitcast_fusion.source_ref, s32[5]{0:T(128)S(1)} %copy-done.17, ...), custom_call_target="tpu_custom_call" | custom-call | bytes 1024 | tf_op jit(solution)/shard_map/pallas_call | solution.py:244
  280.4 8.4 %shard_map.61.refs_1_.refs_4_ = bf16[640,1280]{1,0:T(8,128)(2,1)} custom-call(s32[8]{0:T(128)S(1)} %dynamic-slice_bitcast_fusion.source_ref, s32[5]{0:T(128)S(1)} %copy-done.17, s32[2]{0:T(128)S(1)} %pad_add_fusion.place_ref, bf16[320,1152]{1,0:T(8,128)(2,1)S(1)} %copy-done.10, bf16[320,1152]{1,0:T(8,128)(2,1)S(1)} %copy-done.8, ...), custom_call_target="tpu_custom_call" | custom-call | bytes 1024 | tf_op jit(solution)/shard_map/pallas_call | solution.py:244
  293.2 5.3 %shard_map.64.refs_1_.before_ref = f32[640,1280]{1,0:T(8,128)} custom-call(bf16[640,768]{1,0:T(8,128)(2,1)} %shard_map.57.refs_32_.refs_0_, bf16[640,512]{1,0:T(8,128)(2,1)} %shard_map.55.refs_4_.refs_33_.refs_1_, bf16[640,1280]{1,0:T(8,128)(2,1)S(1)} %copy-done.13, bf16[640,1280]{1,0:T(8,128)(2,1)} %collective-permute-done.36.refs_3_, ...), custom_call_target="tpu_custom_call" | custom-call | bytes 1024 | tf_op jit(solution)/shard_map/pallas_call | solution.py:116
  298.6 2.3 collective-permute-done.35.refs_0_
  300.9 2.4 shard_map.66
  (136 shorter events, 55.3 us)
Async XLA Ops:
  3.8 22.1 %collective-permute-start.7 = (bf16[320,1280]{1,0:T(8,128)(2,1)S(1)}, bf16[320,1280]{1,0:T(8,128)(2,1)S(1)}, u32[]{:S(2)}, u32[]{:S(2)}) collective-permute-start(bf16[320,1280]{1,0:T(8,128)(2,1)S(1)} %get-tuple-element.46.refs_1_.refs_17_), channel_id=1, source_target_pairs={{2,0},{4,2},{6,4},{7,6},{5,7},{3,5},{1,3},{0,1},{10,8},{12,10},{14... | collective-permute-start | bytes 2457608 | tf_op jit(solution)/shard_map/ppermute | solution.py:307
  6.8 21.2 %collective-permute-start.6 = (bf16[320,1280]{1,0:T(8,128)(2,1)S(1)}, bf16[320,1280]{1,0:T(8,128)(2,1)S(1)}, u32[]{:S(2)}, u32[]{:S(2)}) collective-permute-start(bf16[320,1280]{1,0:T(8,128)(2,1)S(1)} %get-tuple-element.46.refs_1_.refs_17_), channel_id=1, source_target_pairs={{0,2},{2,4},{4,6},{6,7},{7,5},{5,3},{3,1},{1,0},{8,10},{10,12},{12... | collective-permute-start | bytes 2457608 | tf_op jit(solution)/shard_map/ppermute | solution.py:306
  12.4 31.1 %collective-permute-start.1 = (bf16[320,1280]{1,0:T(8,128)(2,1)}, bf16[320,1280]{1,0:T(8,128)(2,1)S(1)}, u32[]{:S(2)}, u32[]{:S(2)}) collective-permute-start(bf16[320,1280]{1,0:T(8,128)(2,1)} %get-tuple-element.40.refs_0_.refs_16_), channel_id=1, source_target_pairs={{2,0},{4,2},{6,4},{7,6},{5,7},{3,5},{1,3},{0,1},{10,8},{12,10},{14... | collective-permute-start | bytes 2457608 | tf_op jit(solution)/shard_map/ppermute | solution.py:307
  14.3 31.2 %collective-permute-start = (bf16[320,1280]{1,0:T(8,128)(2,1)}, bf16[320,1280]{1,0:T(8,128)(2,1)S(1)}, u32[]{:S(2)}, u32[]{:S(2)}) collective-permute-start(bf16[320,1280]{1,0:T(8,128)(2,1)} %get-tuple-element.40.refs_0_.refs_16_), channel_id=1, source_target_pairs={{0,2},{2,4},{4,6},{6,7},{7,5},{5,3},{3,1},{1,0},{8,10},{10,12},{12... | collective-permute-start | bytes 2457608 | tf_op jit(solution)/shard_map/ppermute | solution.py:306
  28.9 34.2 %collective-permute-start.8 = (bf16[320,1280]{1,0:T(8,128)(2,1)}, bf16[320,1280]{1,0:T(8,128)(2,1)S(1)}, u32[]{:S(2)}, u32[]{:S(2)}) collective-permute-start(bf16[320,1280]{1,0:T(8,128)(2,1)} %get-tuple-element.47.refs_3_.refs_19_), channel_id=1, source_target_pairs={{0,2},{2,4},{4,6},{6,7},{7,5},{5,3},{3,1},{1,0},{8,10},{10,12},{12... | collective-permute-start | bytes 2457608 | tf_op jit(solution)/shard_map/ppermute | solution.py:306
  29.8 33.3 %collective-permute-start.9 = (bf16[320,1280]{1,0:T(8,128)(2,1)}, bf16[320,1280]{1,0:T(8,128)(2,1)}, u32[]{:S(2)}, u32[]{:S(2)}) collective-permute-start(bf16[320,1280]{1,0:T(8,128)(2,1)} %get-tuple-element.48.refs_5_.refs_21_), channel_id=1, source_target_pairs={{2,0},{4,2},{6,4},{7,6},{5,7},{3,5},{1,3},{0,1},{10,8},{12,10},{14... | collective-permute-start | bytes 2457608 | tf_op jit(solution)/shard_map/ppermute | solution.py:307
  46.4 34.2 %collective-permute-start.2 = (bf16[320,1280]{1,0:T(8,128)(2,1)}, bf16[320,1280]{1,0:T(8,128)(2,1)S(1)}, u32[]{:S(2)}, u32[]{:S(2)}) collective-permute-start(bf16[320,1280]{1,0:T(8,128)(2,1)} %get-tuple-element.41.refs_2_.refs_18_), channel_id=1, source_target_pairs={{0,2},{2,4},{4,6},{6,7},{7,5},{5,3},{3,1},{1,0},{8,10},{10,12},{12... | collective-permute-start | bytes 2457608 | tf_op jit(solution)/shard_map/ppermute | solution.py:306
  47.4 33.3 %collective-permute-start.3 = (bf16[320,1280]{1,0:T(8,128)(2,1)}, bf16[320,1280]{1,0:T(8,128)(2,1)}, u32[]{:S(2)}, u32[]{:S(2)}) collective-permute-start(bf16[320,1280]{1,0:T(8,128)(2,1)} %get-tuple-element.42.refs_4_.refs_20_), channel_id=1, source_target_pairs={{2,0},{4,2},{6,4},{7,6},{5,7},{3,5},{1,3},{0,1},{10,8},{12,10},{14... | collective-permute-start | bytes 2457608 | tf_op jit(solution)/shard_map/ppermute | solution.py:307
  64.0 34.1 %collective-permute-start.10 = (bf16[320,1280]{1,0:T(8,128)(2,1)}, bf16[320,1280]{1,0:T(8,128)(2,1)S(1)}, u32[]{:S(2)}, u32[]{:S(2)}) collective-permute-start(bf16[320,1280]{1,0:T(8,128)(2,1)} %get-tuple-element.49.refs_7_.refs_23_), channel_id=1, source_target_pairs={{0,2},{2,4},{4,6},{6,7},{7,5},{5,3},{3,1},{1,0},{8,10},{10,12},{12... | collective-permute-start | bytes 2457608 | tf_op jit(solution)/shard_map/ppermute | solution.py:306
  64.1 34.1 %collective-permute-start.11 = (bf16[320,1280]{1,0:T(8,128)(2,1)}, bf16[320,1280]{1,0:T(8,128)(2,1)S(1)}, u32[]{:S(2)}, u32[]{:S(2)}) collective-permute-start(bf16[320,1280]{1,0:T(8,128)(2,1)} %get-tuple-element.50.refs_9_.refs_25_), channel_id=1, source_target_pairs={{2,0},{4,2},{6,4},{7,6},{5,7},{3,5},{1,3},{0,1},{10,8},{12,10},{14... | collective-permute-start | bytes 2457608 | tf_op jit(solution)/shard_map/ppermute | solution.py:307
  81.5 32.9 %collective-permute-start.4 = (bf16[320,1280]{1,0:T(8,128)(2,1)}, bf16[320,1280]{1,0:T(8,128)(2,1)}, u32[]{:S(2)}, u32[]{:S(2)}) collective-permute-start(bf16[320,1280]{1,0:T(8,128)(2,1)} %get-tuple-element.43.refs_6_.refs_22_), channel_id=1, source_target_pairs={{0,2},{2,4},{4,6},{6,7},{7,5},{5,3},{3,1},{1,0},{8,10},{10,12},{12... | collective-permute-start | bytes 2457608 | tf_op jit(solution)/shard_map/ppermute | solution.py:306
  81.6 32.8 %collective-permute-start.5 = (bf16[320,1280]{1,0:T(8,128)(2,1)}, bf16[320,1280]{1,0:T(8,128)(2,1)S(1)}, u32[]{:S(2)}, u32[]{:S(2)}) collective-permute-start(bf16[320,1280]{1,0:T(8,128)(2,1)} %get-tuple-element.44.refs_8_.refs_24_), channel_id=1, source_target_pairs={{2,0},{4,2},{6,4},{7,6},{5,7},{3,5},{1,3},{0,1},{10,8},{12,10},{14... | collective-permute-start | bytes 2457608 | tf_op jit(solution)/shard_map/ppermute | solution.py:307
  100.0 31.3 %collective-permute-start.15 = (bf16[320,1280]{1,0:T(8,128)(2,1)}, bf16[320,1280]{1,0:T(8,128)(2,1)}, u32[]{:S(2)}, u32[]{:S(2)}) collective-permute-start(bf16[320,1280]{1,0:T(8,128)(2,1)} %shard_map.45.refs_2_.refs_13_.refs_29_), channel_id=1, source_target_pairs={{2,0},{4,2},{6,4},{7,6},{5,7},{3,5},{1,3},{0,1},{10,8},{12,10},{14... | collective-permute-start | bytes 2457608 | tf_op jit(solution)/shard_map/ppermute | solution.py:312
  115.3 21.5 %collective-permute-start.14 = (bf16[320,1280]{1,0:T(8,128)(2,1)}, bf16[320,1280]{1,0:T(8,128)(2,1)}, u32[]{:S(2)}, u32[]{:S(2)}) collective-permute-start(bf16[320,1280]{1,0:T(8,128)(2,1)} %shard_map.40.refs_1_.refs_10_.refs_26_), channel_id=1, source_target_pairs={{0,2},{2,4},{4,6},{6,7},{7,5},{5,3},{3,1},{1,0},{8,10},{10,12},{12... | collective-permute-start | bytes 2457608 | tf_op jit(solution)/shard_map/ppermute | solution.py:312
  116.6 36.6 %collective-permute-start.13 = (bf16[320,1152]{1,0:T(8,128)(2,1)}, bf16[320,1152]{1,0:T(8,128)(2,1)}, u32[]{:S(2)}, u32[]{:S(2)}) collective-permute-start(bf16[320,1152]{1,0:T(8,128)(2,1)} %shard_map.41.refs_0_), channel_id=1, source_target_pairs={{2,0},{4,2},{6,4},{7,6},{5,7},{3,5},{1,3},{0,1},{10,8},{12,10},{14... | collective-permute-start | bytes 2211848 | tf_op jit(solution)/shard_map/ppermute | solution.py:307
  117.4 35.9 %collective-permute-start.12 = (bf16[320,1152]{1,0:T(8,128)(2,1)}, bf16[320,1152]{1,0:T(8,128)(2,1)}, u32[]{:S(2)}, u32[]{:S(2)}) collective-permute-start(bf16[320,1152]{1,0:T(8,128)(2,1)} %shard_map.41.refs_0_), channel_id=1, source_target_pairs={{0,2},{2,4},{4,6},{6,7},{7,5},{5,3},{3,1},{1,0},{8,10},{10,12},{12... | collective-permute-start | bytes 2211848 | tf_op jit(solution)/shard_map/ppermute | solution.py:306
  118.8 43.3 %collective-permute-start.17 = (bf16[320,1152]{1,0:T(8,128)(2,1)}, bf16[320,1152]{1,0:T(8,128)(2,1)}, u32[]{:S(2)}, u32[]{:S(2)}) collective-permute-start(bf16[320,1152]{1,0:T(8,128)(2,1)} %shard_map.46.refs_1_), channel_id=1, source_target_pairs={{2,0},{4,2},{6,4},{7,6},{5,7},{3,5},{1,3},{0,1},{10,8},{12,10},{14... | collective-permute-start | bytes 2211848 | tf_op jit(solution)/shard_map/ppermute | solution.py:307
  131.4 37.0 %collective-permute-start.16 = (bf16[320,1152]{1,0:T(8,128)(2,1)}, bf16[320,1152]{1,0:T(8,128)(2,1)}, u32[]{:S(2)}, u32[]{:S(2)}) collective-permute-start(bf16[320,1152]{1,0:T(8,128)(2,1)} %shard_map.46.refs_1_), channel_id=1, source_target_pairs={{0,2},{2,4},{4,6},{6,7},{7,5},{5,3},{3,1},{1,0},{8,10},{10,12},{12... | collective-permute-start | bytes 2211848 | tf_op jit(solution)/shard_map/ppermute | solution.py:306
  153.3 48.7 %collective-permute-start.24 = (bf16[640,768]{1,0:T(8,128)(2,1)}, bf16[640,768]{1,0:T(8,128)(2,1)}, u32[]{:S(2)}, u32[]{:S(2)}) collective-permute-start(bf16[640,768]{1,0:T(8,128)(2,1)} %shard_map.52), channel_id=1, source_target_pairs={{0,8},{8,0},{16,24},{24,16},{1,9},{9,1},{17,25},{25,17},{2,10},{10... | collective-permute-start | bytes 2949128 | tf_op jit(solution)/shard_map/ppermute | solution.py:336
  153.8 30.4 %collective-permute-start.18 = (bf16[320,1152]{1,0:T(8,128)(2,1)}, bf16[320,1152]{1,0:T(8,128)(2,1)}, u32[]{:S(2)}, u32[]{:S(2)}) collective-permute-start(bf16[320,1152]{1,0:T(8,128)(2,1)} %get-tuple-element.52.refs_1_.refs_2_), channel_id=1, source_target_pairs={{0,2},{2,4},{4,6},{6,7},{7,5},{5,3},{3,1},{1,0},{8,10},{10,12},{12... | collective-permute-start | bytes 2211848 | tf_op jit(solution)/shard_map/ppermute | solution.py:306
  162.1 23.5 %collective-permute-start.19 = (bf16[320,1152]{1,0:T(8,128)(2,1)}, bf16[320,1152]{1,0:T(8,128)(2,1)}, u32[]{:S(2)}, u32[]{:S(2)}) collective-permute-start(bf16[320,1152]{1,0:T(8,128)(2,1)} %get-tuple-element.54.refs_2_.refs_4_), channel_id=1, source_target_pairs={{2,0},{4,2},{6,4},{7,6},{5,7},{3,5},{1,3},{0,1},{10,8},{12,10},{14... | collective-permute-start | bytes 2211848 | tf_op jit(solution)/shard_map/ppermute | solution.py:307
  168.4 31.6 %collective-permute-start.20 = (bf16[320,1152]{1,0:T(8,128)(2,1)}, bf16[320,1152]{1,0:T(8,128)(2,1)}, u32[]{:S(2)}, u32[]{:S(2)}) collective-permute-start(bf16[320,1152]{1,0:T(8,128)(2,1)} %get-tuple-element.53.refs_3_), channel_id=1, source_target_pairs={{0,2},{2,4},{4,6},{6,7},{7,5},{5,3},{3,1},{1,0},{8,10},{10,12},{12... | collective-permute-start | bytes 2211848 | tf_op jit(solution)/shard_map/ppermute | solution.py:306
  169.7 31.8 %collective-permute-start.21 = (bf16[320,1152]{1,0:T(8,128)(2,1)}, bf16[320,1152]{1,0:T(8,128)(2,1)}, u32[]{:S(2)}, u32[]{:S(2)}) collective-permute-start(bf16[320,1152]{1,0:T(8,128)(2,1)} %get-tuple-element.55.refs_5_), channel_id=1, source_target_pairs={{2,0},{4,2},{6,4},{7,6},{5,7},{3,5},{1,3},{0,1},{10,8},{12,10},{14... | collective-permute-start | bytes 2211848 | tf_op jit(solution)/shard_map/ppermute | solution.py:307
  184.2 22.1 %collective-permute-start.28 = (bf16[640,512]{1,0:T(8,128)(2,1)}, bf16[640,512]{1,0:T(8,128)(2,1)}, u32[]{:S(2)}, u32[]{:S(2)}) collective-permute-start(bf16[640,512]{1,0:T(8,128)(2,1)} %add_convert_fusion.3.refs_3_), channel_id=1, source_target_pairs={{0,16},{8,24},{16,0},{24,8},{1,17},{9,25},{17,1},{25,9},{2,18},{10... | collective-permute-start | bytes 1966088 | tf_op jit(solution)/shard_map/ppermute | solution.py:339
  185.6 30.1 %collective-permute-start.22 = (bf16[320,1152]{1,0:T(8,128)(2,1)}, bf16[320,1152]{1,0:T(8,128)(2,1)}, u32[]{:S(2)}, u32[]{:S(2)}) collective-permute-start(bf16[320,1152]{1,0:T(8,128)(2,1)} %get-tuple-element.56.refs_6_), channel_id=1, source_target_pairs={{0,2},{2,4},{4,6},{6,7},{7,5},{5,3},{3,1},{1,0},{8,10},{10,12},{12... | collective-permute-start | bytes 2211848 | tf_op jit(solution)/shard_map/ppermute | solution.py:306
  201.5 30.0 %collective-permute-start.26 = (bf16[320,1152]{1,0:T(8,128)(2,1)}, bf16[320,1152]{1,0:T(8,128)(2,1)}, u32[]{:S(2)}, u32[]{:S(2)}) collective-permute-start(bf16[320,1152]{1,0:T(8,128)(2,1)} %get-tuple-element.57.refs_7_), channel_id=1, source_target_pairs={{0,2},{2,4},{4,6},{6,7},{7,5},{5,3},{3,1},{1,0},{8,10},{10,12},{12... | collective-permute-start | bytes 2211848 | tf_op jit(solution)/shard_map/ppermute | solution.py:306
  202.0 29.6 %collective-permute-start.27 = (bf16[320,1152]{1,0:T(8,128)(2,1)}, bf16[320,1152]{1,0:T(8,128)(2,1)}, u32[]{:S(2)}, u32[]{:S(2)}) collective-permute-start(bf16[320,1152]{1,0:T(8,128)(2,1)} %get-tuple-element.59.refs_9_), channel_id=1, source_target_pairs={{2,0},{4,2},{6,4},{7,6},{5,7},{3,5},{1,3},{0,1},{10,8},{12,10},{14... | collective-permute-start | bytes 2211848 | tf_op jit(solution)/shard_map/ppermute | solution.py:307
  206.2 40.8 %collective-permute-start.31 = (bf16[640,768]{1,0:T(8,128)(2,1)}, bf16[640,768]{1,0:T(8,128)(2,1)}, u32[]{:S(2)}, u32[]{:S(2)}) collective-permute-start(bf16[640,768]{1,0:T(8,128)(2,1)} %add_convert_fusion.1.refs_2_), channel_id=1, source_target_pairs={{0,16},{8,24},{16,0},{24,8},{1,17},{9,25},{17,1},{25,9},{2,18},{10... | collective-permute-start | bytes 2949128 | tf_op jit(solution)/shard_map/ppermute | solution.py:339
  219.7 27.4 %collective-permute-start.29 = (bf16[320,1152]{1,0:T(8,128)(2,1)}, bf16[320,1152]{1,0:T(8,128)(2,1)}, u32[]{:S(2)}, u32[]{:S(2)}) collective-permute-start(bf16[320,1152]{1,0:T(8,128)(2,1)} %shard_map.54.refs_32_.refs_10_), channel_id=1, source_target_pairs={{0,2},{2,4},{4,6},{6,7},{7,5},{5,3},{3,1},{1,0},{8,10},{10,12},{12... | collective-permute-start | bytes 2211848 | tf_op jit(solution)/shard_map/ppermute | solution.py:312
  257.7 32.3 %collective-permute-start.36 = (bf16[640,1280]{1,0:T(8,128)(2,1)}, bf16[640,1280]{1,0:T(8,128)(2,1)}, u32[]{:S(2)}, u32[]{:S(2)}) collective-permute-start(bf16[640,1280]{1,0:T(8,128)(2,1)} %get-tuple-element.69), channel_id=1, source_target_pairs={{0,8},{8,0},{16,24},{24,16},{1,9},{9,1},{17,25},{25,17},{2,10},{10... | collective-permute-start | bytes 4915208 | tf_op jit(solution)/shard_map/ppermute | solution.py:336
  262.5 26.4 %collective-permute-start.37 = (bf16[640,768]{1,0:T(8,128)(2,1)S(1)}, bf16[640,768]{1,0:T(8,128)(2,1)S(1)}, u32[]{:S(2)}, u32[]{:S(2)}) collective-permute-start(bf16[640,768]{1,0:T(8,128)(2,1)S(1)} %add_convert_fusion.refs_32_), channel_id=1, source_target_pairs={{0,16},{8,24},{16,0},{24,8},{1,17},{9,25},{17,1},{25,9},{2,18},{10... | collective-permute-start | bytes 2949128 | tf_op jit(solution)/shard_map/ppermute | solution.py:339
  279.7 21.2 %collective-permute-start.35 = (bf16[640,512]{1,0:T(8,128)(2,1)S(1)}, bf16[640,512]{1,0:T(8,128)(2,1)}, u32[]{:S(2)}, u32[]{:S(2)}) collective-permute-start(bf16[640,512]{1,0:T(8,128)(2,1)S(1)} %add_convert_fusion.2.refs_32_), channel_id=1, source_target_pairs={{0,16},{8,24},{16,0},{24,8},{1,17},{9,25},{17,1},{25,9},{2,18},{10... | collective-permute-start | bytes 1966088 | tf_op jit(solution)/shard_map/ppermute | solution.py:339
  (34 other events, 433.9 us)
